TPU v7x, 32 devices: a whole 2x2x4 slice. The times are simulated.
32 devices in a mesh: pack: 8 (over y, x, core), seq: 4 (over z).
Axes of the slice: x: 2, y: 2, z: 4, core: 2. Of those that a mesh axis runs over, the one named last changes fastest.
Arguments:
- patches: bfloat16 [48, 1024, 768], P('pack', 'seq'), may hold values from -6 to 6
- lengths: int32 [48, 16], P('pack'), may hold values from 1 to 128, 1024 in all within a row
- keep_mask: int32 [48, 1024], P('pack'), may hold values 0 or 1
- labels: int32 [48, 16], replicated, may hold values from 0 to 21842
- step_count: int32 [1], replicated, may hold values from 2 to 20
- embed_weight: float32 [768, 768], P(None, ('pack', 'seq')), may hold values from -0.21875 to 0.21875
- embed_first: float32 [768, 768], P(None, ('pack', 'seq')), may hold values from -0.00030517578 to 0.00030517578
- embed_second: float32 [768, 768], P(None, ('pack', 'seq')), may hold values from 1.2450748e-08 to 5.033281e-08
- qkv_weight: float32 [768, 2304], P(None, ('pack', 'seq')), may hold values from -0.21875 to 0.21875
- qkv_moment: float32 [768, 2304], P(None, ('pack', 'seq')), may hold values from -0.0029296875 to 0.0029296875
- output_weight: float32 [768, 768], P(None, ('pack', 'seq')), may hold values from -0.625 to 0.625
- output_moment: float32 [768, 768], P(None, ('pack', 'seq')), may hold values from -0.0029296875 to 0.0029296875
- up_weight: float32 [768, 3072], P(None, ('pack', 'seq')), may hold values from -0.21875 to 0.21875
- up_moment: float32 [768, 3072], P(None, ('pack', 'seq')), may hold values from -0.0029296875 to 0.0029296875
- down_weight: float32 [768, 3072], P(None, ('pack', 'seq')), may hold values from -0.109375 to 0.109375
- down_moment: float32 [768, 3072], P(None, ('pack', 'seq')), may hold values from -0.0029296875 to 0.0029296875
- small_params: float32 [15, 768], P(None, ('pack', 'seq')), may hold values from -0.5 to 1.4, as said below
- small_first: float32 [15, 768], P(None, ('pack', 'seq')), may hold values from -0.0024414062 to 0.0024414062
- small_second: float32 [15, 768], P(None, ('pack', 'seq')), may hold values from 7.9684787e-07 to 3.2213e-06
- head_weight: float32 [768, 21856], P('seq', 'pack'), may hold values from -0.21875 to 0.21875
- head_first: float32 [768, 21856], P('seq', 'pack'), may hold values from -0.00015258789 to 0.00015258789
- head_second: float32 [768, 21856], P('seq', 'pack'), may hold values from 3.1593836e-09 to 1.2518313e-08
- head_bias: float32 [21856], P(('pack', 'seq')), may hold values from -6 to 6
- bias_first: float32 [21856], P(('pack', 'seq')), may hold values from -0.00012207031 to 0.00012207031
- bias_second: float32 [21856], P(('pack', 'seq')), may hold values from 1.4313102e-09 to 5.7252407e-09
Outputs:
- loss_value: float32 [], replicated
- grad_norm: float32 [], replicated
- new_embed: float32 [768, 768], P(None, ('pack', 'seq'))
- new_embed_first: float32 [768, 768], P(None, ('pack', 'seq'))
- new_embed_second: float32 [768, 768], P(None, ('pack', 'seq'))
- new_qkv: float32 [768, 2304], P(None, ('pack', 'seq'))
- new_qkv_moment: float32 [768, 2304], P(None, ('pack', 'seq'))
- new_output: float32 [768, 768], P(None, ('pack', 'seq'))
- new_output_moment: float32 [768, 768], P(None, ('pack', 'seq'))
- new_up: float32 [768, 3072], P(None, ('pack', 'seq'))
- new_up_moment: float32 [768, 3072], P(None, ('pack', 'seq'))
- new_down: float32 [768, 3072], P(None, ('pack', 'seq'))
- new_down_moment: float32 [768, 3072], P(None, ('pack', 'seq'))
- new_small: float32 [15, 768], P(None, ('pack', 'seq'))
- new_small_first: float32 [15, 768], P(None, ('pack', 'seq'))
- new_small_second: float32 [15, 768], P(None, ('pack', 'seq'))
- new_head: float32 [768, 21856], P('seq', 'pack')
- new_head_first: float32 [768, 21856], P('seq', 'pack')
- new_head_second: float32 [768, 21856], P('seq', 'pack')
- new_bias: float32 [21856], P(('pack', 'seq'))
- new_bias_first: float32 [21856], P(('pack', 'seq'))
- new_bias_second: float32 [21856], P(('pack', 'seq'))
Inputs may be any that keep to these rules, and one draw needn't show every extreme that they name: Each pack's 16 lengths sum to 1024, and its longest is exactly 128. `small_params`: rows 0, 2 and 4 lie in [0.6, 1.4], the other rows in [-0.5, 0.5].
All inputs are finite; a program needn't handle non-finite values. No bound on the sum of `keep_mask` on one device may be relied on, other than what follows from the above.
Results may differ from a plain program's by a relative error of at most 0.00055.
The roundings to bfloat16 on the way count: a program that leaves them out, or rounds other values in their place, can miss the bound.
Values may be sent and summed in bfloat16 or wider, within the bound.
No kernel may reach another device: no remote copies, remote signals or barrier semaphores. Data moves between devices by JAX's collectives and lax.ppermute only.
A program may use at most 384 MiB of HBM per device.

v0:
```python
from functools import partial
import math

import jax
import jax.numpy as jnp
from jax import lax
from jax.sharding import PartitionSpec as P

HEAD_DIM = 64
LABELS = 21843
PACK_LEN = 1024
NS_STEPS = 2


HIGHEST_PREC = lax.Precision.HIGHEST
CLIP_NORM = 1.0
MUON_MU = 0.95
MUON_RATE = 1.0
ADAM_RATE = 0.02
BETA_ONE = 0.9
BETA_TWO = 0.95
DECAY = 0.01
COEF_ONE = 3.4445
COEF_TWO = -4.775
COEF_THREE = 2.0315


def extended(cells, sides, width):
    for axis, dim in sides:
        count = lax.axis_size(axis)
        ends = count - 1
        head = lax.slice_in_dim(cells, 0, width, axis=dim)
        tail = lax.slice_in_dim(cells, cells.shape[dim] - width, cells.shape[dim], axis=dim)
        cells = jnp.concatenate(
            [
                lax.ppermute(tail, axis, [(i, (i + 1) % count) for i in range(ends)]),
                cells,
                lax.ppermute(head, axis, [((i + 1) % count, i) for i in range(ends)]),
            ],
            axis=dim,
        )
    return cells


def passed_along(value, axis, steps):
    count = lax.axis_size(axis)
    leading, last = (max(0, -steps), min(count, count - steps))
    return lax.ppermute(value, axis, [(source, source + steps) for source in range(leading, last)])


def layer_norm(values, gain_row, bias_row):
    centre = values - jnp.mean(values, axis=-1, keepdims=True)
    spread = jnp.mean(centre * centre, axis=-1, keepdims=True)
    return centre * lax.rsqrt(spread + 1e-06) * gain_row + bias_row


def norm_back(values, gain_row, bias_row, cotangent):
    _, pullback = jax.vjp(layer_norm, values, gain_row, bias_row)
    return pullback(cotangent)


def image_index(lengths_all, positions):
    ends_at = jnp.cumsum(lengths_all, axis=-1, dtype=jnp.int32)
    starts_at = ends_at - lengths_all
    image_ids = jnp.sum(
        (positions[None, :, None] >= ends_at[:, None, :]).astype(jnp.int32), axis=2, dtype=jnp.int32
    )
    is_first = jnp.any(positions[None, :, None] == starts_at[:, None, :], axis=2)
    inside = (positions >= 0) & (positions < PACK_LEN)
    return (jnp.where(inside[None, :], image_ids, -1), is_first)


def split_heads(block_rows):
    return block_rows.reshape(block_rows.shape[0], -1, HEAD_DIM)


def pack_scores(query_rows, key_values, allowed):
    model_width = query_rows.shape[-1]
    queries = split_heads(query_rows)
    keys_part = split_heads(key_values[:, :model_width])
    values_part = split_heads(key_values[:, model_width:])
    scores = jnp.einsum(
        "she,khe->hsk", queries, keys_part, preferred_element_type=jnp.float32
    ) * HEAD_DIM ** (-0.5)
    return (queries, keys_part, values_part, jnp.where(allowed[None], scores, -1e30))


def attend_pack(operands):
    query_rows, key_values, allowed = operands
    queries, keys_part, values_part, scores = pack_scores(query_rows, key_values, allowed)
    row_max = jnp.max(scores, axis=2, keepdims=True)
    exp_scores = jnp.exp(scores - row_max)
    row_total = jnp.sum(exp_scores, axis=2, keepdims=True)
    attn_probs = (exp_scores / row_total).astype(jnp.bfloat16)
    attn_rows = jnp.einsum(
        "hsk,khe->she", attn_probs, values_part, preferred_element_type=jnp.float32
    )
    return (attn_rows.reshape(query_rows.shape), (row_max + jnp.log(row_total))[:, :, 0])


def attend_back(operands):
    query_rows, key_values, allowed, log_total, grad_rows = operands
    queries, keys_part, values_part, scores = pack_scores(query_rows, key_values, allowed)
    grad_heads = split_heads(grad_rows)
    attn_probs = jnp.exp(scores - log_total[:, :, None])
    grad_probs = jnp.einsum(
        "she,khe->hsk", grad_heads, values_part, preferred_element_type=jnp.float32
    )
    row_inner = jnp.sum(attn_probs * grad_probs, axis=2, keepdims=True)
    grad_scores = (attn_probs * (grad_probs - row_inner)).astype(jnp.bfloat16)
    grad_query = jnp.einsum(
        "hsk,khe->she", grad_scores, keys_part, preferred_element_type=jnp.float32
    ) * HEAD_DIM ** (-0.5)
    grad_key = jnp.einsum(
        "hsk,she->khe", grad_scores, queries, preferred_element_type=jnp.float32
    ) * HEAD_DIM ** (-0.5)
    grad_value = jnp.einsum(
        "hsk,she->khe",
        attn_probs.astype(jnp.bfloat16),
        grad_heads,
        preferred_element_type=jnp.float32,
    )
    key_len = key_values.shape[0]
    return (
        grad_query.reshape(query_rows.shape),
        jnp.concatenate([grad_key.reshape(key_len, -1), grad_value.reshape(key_len, -1)], axis=1),
    )


def column_sum(block_rows):
    return jnp.sum(block_rows.astype(jnp.float32), axis=(0, 1))


def hmul(left, right):
    return jnp.dot(left, right, precision=HIGHEST_PREC, preferred_element_type=jnp.float32)


def gram_of(matrix):
    return hmul(matrix, matrix.T)


def ortho_step(matrix, gram_mat):
    first_pass = hmul(gram_mat, matrix)
    second_pass = hmul(gram_mat, first_pass)
    return COEF_ONE * matrix + COEF_TWO * first_pass + COEF_THREE * second_pass


def normalize_first(iterates, gram_sums):
    scales = tuple((1.0 / (jnp.sqrt(jnp.trace(gram_mat)) + 1e-07) for gram_mat in gram_sums))
    iterates = tuple((matrix * scale_one for matrix, scale_one in zip(iterates, scales)))
    gram_sums = tuple(
        (gram_mat * scale_one * scale_one for gram_mat, scale_one in zip(gram_sums, scales))
    )
    return (iterates, gram_sums)


def muon_update(weight, iterate):
    col_ratio = math.sqrt(
        max(1.0, iterate.shape[1] * lax.axis_size(("pack", "seq")) / weight.shape[0])
    )
    return weight * (1.0 - MUON_RATE * DECAY) - MUON_RATE * col_ratio * iterate


def adam_update(weight, first_moment, second_moment, gradient, factor, count_float):
    scaled = factor * gradient
    new_first = BETA_ONE * first_moment + (1.0 - BETA_ONE) * scaled
    new_second = BETA_TWO * second_moment + (1.0 - BETA_TWO) * scaled * scaled
    first_hat = new_first / (1.0 - jnp.power(BETA_ONE, count_float))
    second_hat = new_second / (1.0 - jnp.power(BETA_TWO, count_float))
    new_weight = weight - ADAM_RATE * (first_hat / (jnp.sqrt(second_hat) + 1e-08) + DECAY * weight)
    return (new_weight, new_first, new_second)


def body(
    patches,
    lengths,
    keep_mask,
    labels,
    step_count,
    embed_weight,
    embed_first,
    embed_second,
    qkv_weight,
    qkv_moment,
    output_weight,
    output_moment,
    up_weight,
    up_moment,
    down_weight,
    down_moment,
    small_params,
    small_first,
    small_second,
    head_weight,
    head_first,
    head_second,
    head_bias,
    bias_first,
    bias_second,
):
    pack_count, shard_len, _ = patches.shape
    img_count = lengths.shape[1]
    model_width = qkv_weight.shape[0]
    seq_count = lax.axis_size("seq")
    img_group = img_count // seq_count
    seq_place = lax.axis_index("seq")
    pack_place = lax.axis_index("pack")
    qkv_full, output_full, up_full, down_full, embed_full, small_full = (
        lax.all_gather(qkv_weight.astype(jnp.bfloat16), ("pack", "seq"), axis=1, tiled=True),
        lax.all_gather(output_weight.astype(jnp.bfloat16), ("pack", "seq"), axis=1, tiled=True),
        lax.all_gather(up_weight.astype(jnp.bfloat16), ("pack", "seq"), axis=1, tiled=True),
        lax.all_gather(down_weight.astype(jnp.bfloat16), ("pack", "seq"), axis=1, tiled=True),
        lax.all_gather(embed_weight.astype(jnp.bfloat16), ("pack", "seq"), axis=1, tiled=True),
        lax.all_gather(small_params.astype(jnp.bfloat16), ("pack", "seq"), axis=1, tiled=True),
    )
    gain_bias = small_full.astype(jnp.float32)
    query_pos = seq_place * shard_len + jnp.arange(shard_len, dtype=jnp.int32)
    query_ids, query_first = image_index(lengths, query_pos)
    query_keep = (
        lax.dynamic_slice_in_dim(keep_mask, seq_place * shard_len, shard_len, 1) > 0
    ) | query_first
    embedded = (
        jnp.einsum("psi,id->psd", patches, embed_full, preferred_element_type=jnp.float32)
        + gain_bias[6]
    )
    normed_one = layer_norm(embedded, gain_bias[0], gain_bias[1]).astype(jnp.bfloat16)
    qkv_bias = jnp.concatenate([gain_bias[7], jnp.zeros_like(gain_bias[7]), gain_bias[8]])
    qkv_rows = (
        jnp.einsum("psd,de->pse", normed_one, qkv_full, preferred_element_type=jnp.float32)
        + qkv_bias
    ).astype(jnp.bfloat16)
    key_values = qkv_rows[:, :, model_width:]
    key_pos = (seq_place - 1) * shard_len + jnp.arange(3 * shard_len, dtype=jnp.int32)
    key_rows = extended(key_values, (("seq", 1),), shard_len)
    key_keep = lax.dynamic_slice_in_dim(
        jnp.pad(keep_mask, ((0, 0), (shard_len, shard_len))),
        seq_place * shard_len,
        3 * shard_len,
        1,
    )
    key_ids, key_first = image_index(lengths, key_pos)
    key_live = ((key_keep > 0) | key_first) & (key_ids >= 0)
    allowed = (query_ids[:, :, None] == key_ids[:, None, :]) & key_live[:, None, :]
    attn_rows, log_total = lax.map(attend_pack, (qkv_rows[:, :, :model_width], key_rows, allowed))
    attn_low = attn_rows.astype(jnp.bfloat16)
    after_attn = (
        embedded
        + jnp.einsum("psd,de->pse", attn_low, output_full, preferred_element_type=jnp.float32)
        + gain_bias[9]
    )
    normed_two = layer_norm(after_attn, gain_bias[2], gain_bias[3]).astype(jnp.bfloat16)
    up_rows = jnp.einsum(
        "psd,df->psf", normed_two, up_full, preferred_element_type=jnp.float32
    ) + gain_bias[11:15].reshape(-1)
    active = jax.nn.gelu(up_rows, approximate=False).astype(jnp.bfloat16)
    after_mlp = (
        after_attn
        + jnp.einsum("psf,df->psd", active, down_full, preferred_element_type=jnp.float32)
        + gain_bias[10]
    )
    final_rows = layer_norm(after_mlp, gain_bias[4], gain_bias[5])
    image_range = jnp.arange(img_count, dtype=jnp.int32)
    member = (
        (query_ids[:, None, :] == image_range[None, :, None]) & query_keep[:, None, :]
    ).astype(jnp.float32)
    pool_part = jnp.einsum(
        "pis,psd->pid",
        member,
        final_rows,
        precision=HIGHEST_PREC,
        preferred_element_type=jnp.float32,
    )
    pool_part = (
        pool_part.reshape(pack_count, img_group, seq_count, model_width)
        .transpose(2, 0, 1, 3)
        .reshape(-1, model_width)
    )
    pool_sums = lax.psum_scatter(pool_part, "seq", scatter_dimension=0, tiled=True)
    all_ids, all_first = image_index(lengths, jnp.arange(PACK_LEN, dtype=jnp.int32))
    whole_keep = (keep_mask > 0) | all_first
    counts_all = jnp.sum(
        ((all_ids[:, None, :] == image_range[None, :, None]) & whole_keep[:, None, :]).astype(
            jnp.float32
        ),
        axis=2,
    )
    own_counts = lax.dynamic_index_in_dim(
        counts_all.reshape(pack_count, img_group, seq_count), seq_place, 2, keepdims=False
    ).reshape(-1)
    pooled_low = (pool_sums / own_counts[:, None]).astype(jnp.bfloat16)
    pooled_rows = lax.all_gather(pooled_low, "pack", axis=0, tiled=True)
    head_full, bias_full = (
        lax.all_gather(head_weight.astype(jnp.bfloat16), "seq", axis=0, tiled=True),
        lax.all_gather(head_bias.astype(jnp.bfloat16), "seq", axis=0, tiled=True),
    )
    logits = jnp.dot(pooled_rows, head_full, preferred_element_type=jnp.float32) + bias_full.astype(
        jnp.float32
    )
    label_cols = head_full.shape[1]
    label_rows = lax.dynamic_index_in_dim(
        labels.reshape(lax.axis_size("pack"), pack_count, img_group, seq_count),
        seq_place,
        3,
        keepdims=False,
    ).reshape(-1)
    class_ids = pack_place * label_cols + jnp.arange(label_cols, dtype=jnp.int32)
    valid = (class_ids < LABELS).astype(jnp.float32)
    target = (label_rows[:, None] == class_ids[None, :]).astype(jnp.float32)
    image_total = labels.shape[0] * labels.shape[1]
    loss_part = jnp.sum(valid[None, :] * (jax.nn.softplus(logits) - target * logits)) / image_total
    grad_logits = (valid[None, :] * (jax.nn.sigmoid(logits) - target) / image_total).astype(
        jnp.bfloat16
    )
    head_grad, bias_grad = (
        lax.psum_scatter(
            jnp.einsum("nd,nc->dc", pooled_rows, grad_logits, preferred_element_type=jnp.float32),
            "seq",
            scatter_dimension=0,
            tiled=True,
        ),
        lax.psum_scatter(
            jnp.sum(grad_logits.astype(jnp.float32), axis=0), "seq", scatter_dimension=0, tiled=True
        ),
    )
    pooled_grad = lax.psum_scatter(
        jnp.einsum("nc,dc->nd", grad_logits, head_full, preferred_element_type=jnp.float32),
        "pack",
        scatter_dimension=0,
        tiled=True,
    )
    pooled_grad = lax.all_gather(pooled_grad / own_counts[:, None], "seq", axis=0, tiled=True)
    pooled_grad = (
        pooled_grad.reshape(seq_count, pack_count, img_group, model_width)
        .transpose(1, 2, 0, 3)
        .reshape(pack_count, img_count, model_width)
    )
    grad_final = jnp.einsum(
        "pis,pid->psd",
        member,
        pooled_grad,
        precision=HIGHEST_PREC,
        preferred_element_type=jnp.float32,
    )
    grad_mlp, grad_gain_f, grad_bias_f = norm_back(
        after_mlp, gain_bias[4], gain_bias[5], grad_final
    )
    grad_mlp_low = grad_mlp.astype(jnp.bfloat16)
    grad_down = jnp.einsum("psd,psf->df", grad_mlp_low, active, preferred_element_type=jnp.float32)
    grad_active = jnp.einsum(
        "psd,df->psf", grad_mlp_low, down_full, preferred_element_type=jnp.float32
    )
    _, gelu_pull = jax.vjp(partial(jax.nn.gelu, approximate=False), up_rows)
    grad_upper = gelu_pull(grad_active)[0].astype(jnp.bfloat16)
    grad_up = jnp.einsum("psd,psf->df", normed_two, grad_upper, preferred_element_type=jnp.float32)
    grad_two, grad_gain_2, grad_bias_2 = norm_back(
        after_attn,
        gain_bias[2],
        gain_bias[3],
        jnp.einsum("psf,df->psd", grad_upper, up_full, preferred_element_type=jnp.float32),
    )
    grad_attn = grad_mlp + grad_two
    grad_attn_low = grad_attn.astype(jnp.bfloat16)
    grad_output = jnp.einsum(
        "psd,pse->de", attn_low, grad_attn_low, preferred_element_type=jnp.float32
    )
    grad_mixed = jnp.einsum(
        "pse,de->psd", grad_attn_low, output_full, preferred_element_type=jnp.float32
    ).astype(jnp.bfloat16)
    grad_query, grad_keys = lax.map(
        attend_back, (qkv_rows[:, :, :model_width], key_rows, allowed, log_total, grad_mixed)
    )
    from_right = passed_along(grad_keys[:, :shard_len], "seq", -1)
    from_left = passed_along(grad_keys[:, 2 * shard_len :], "seq", 1)
    grad_own = grad_keys[:, shard_len : 2 * shard_len] + from_right + from_left
    grad_qkv = jnp.concatenate([grad_query, grad_own], axis=2).astype(jnp.bfloat16)
    grad_qkv_w = jnp.einsum("psd,pse->de", normed_one, grad_qkv, preferred_element_type=jnp.float32)
    qkv_bias_grad = column_sum(grad_qkv)
    grad_one, grad_gain_1, grad_bias_1 = norm_back(
        embedded,
        gain_bias[0],
        gain_bias[1],
        jnp.einsum("pse,de->psd", grad_qkv, qkv_full, preferred_element_type=jnp.float32),
    )
    grad_embed_rows = (grad_attn + grad_one).astype(jnp.bfloat16)
    grad_embed = jnp.einsum(
        "psi,psd->id", patches, grad_embed_rows, preferred_element_type=jnp.float32
    )
    small_grad = jnp.concatenate(
        [
            jnp.stack(
                [
                    grad_gain_1,
                    grad_bias_1,
                    grad_gain_2,
                    grad_bias_2,
                    grad_gain_f,
                    grad_bias_f,
                    column_sum(grad_embed_rows),
                    qkv_bias_grad[:model_width],
                    qkv_bias_grad[2 * model_width :],
                    column_sum(grad_attn_low),
                    column_sum(grad_mlp_low),
                ]
            ),
            column_sum(grad_upper).reshape(-1, model_width),
        ],
        axis=0,
    )
    qkv_share, output_share, up_share, down_share, embed_share, small_share = (
        lax.psum_scatter(grad_qkv_w, ("pack", "seq"), scatter_dimension=1, tiled=True),
        lax.psum_scatter(grad_output, ("pack", "seq"), scatter_dimension=1, tiled=True),
        lax.psum_scatter(grad_up, ("pack", "seq"), scatter_dimension=1, tiled=True),
        lax.psum_scatter(grad_down, ("pack", "seq"), scatter_dimension=1, tiled=True),
        lax.psum_scatter(grad_embed, ("pack", "seq"), scatter_dimension=1, tiled=True),
        lax.psum_scatter(small_grad, ("pack", "seq"), scatter_dimension=1, tiled=True),
    )
    shares = (
        qkv_share,
        output_share,
        up_share,
        down_share,
        embed_share,
        small_share,
        head_grad,
        bias_grad,
    )
    square_sum = sum((jnp.sum(grad_piece * grad_piece) for grad_piece in shares))
    loss_value, square_total = lax.psum((loss_part, square_sum), ("pack", "seq"))
    grad_norm = jnp.sqrt(square_total)
    factor = jnp.minimum(1.0, CLIP_NORM / (grad_norm + 1e-06))
    moments = (
        MUON_MU * qkv_moment + factor * qkv_share,
        MUON_MU * output_moment + factor * output_share,
        MUON_MU * up_moment + factor * up_share,
        MUON_MU * down_moment + factor * down_share,
    )
    iterates = moments
    for iteration in range(NS_STEPS):
        gram_sums = lax.psum(
            (
                gram_of(iterates[0]),
                gram_of(iterates[1]),
                gram_of(iterates[2]),
                gram_of(iterates[3]),
            ),
            ("pack", "seq"),
        )
        if iteration == 0:
            iterates, gram_sums = normalize_first(iterates, gram_sums)
        iterates = tuple(
            (ortho_step(matrix, gram_mat) for matrix, gram_mat in zip(iterates, gram_sums))
        )
    new_qkv = muon_update(qkv_weight, iterates[0])
    new_output = muon_update(output_weight, iterates[1])
    new_up = muon_update(up_weight, iterates[2])
    new_down = muon_update(down_weight, iterates[3])
    count_float = step_count[0].astype(jnp.float32)
    new_embed, new_embed_first, new_embed_second = adam_update(
        embed_weight, embed_first, embed_second, embed_share, factor, count_float
    )
    new_small, new_small_first, new_small_second = adam_update(
        small_params, small_first, small_second, small_share, factor, count_float
    )
    new_head, new_head_first, new_head_second = adam_update(
        head_weight, head_first, head_second, head_grad, factor, count_float
    )
    new_bias, new_bias_first, new_bias_second = adam_update(
        head_bias, bias_first, bias_second, bias_grad, factor, count_float
    )
    return (
        loss_value,
        grad_norm,
        new_embed,
        new_embed_first,
        new_embed_second,
        new_qkv,
        moments[0],
        new_output,
        moments[1],
        new_up,
        moments[2],
        new_down,
        moments[3],
        new_small,
        new_small_first,
        new_small_second,
        new_head,
        new_head_first,
        new_head_second,
        new_bias,
        new_bias_first,
        new_bias_second,
    )


def solution(mesh):
    placed = (
        P("pack", "seq", None),
        P("pack", None),
        P("pack", None),
        P(),
        P(),
        P(None, ("pack", "seq")),
        P(None, ("pack", "seq")),
        P(None, ("pack", "seq")),
        P(None, ("pack", "seq")),
        P(None, ("pack", "seq")),
        P(None, ("pack", "seq")),
        P(None, ("pack", "seq")),
        P(None, ("pack", "seq")),
        P(None, ("pack", "seq")),
        P(None, ("pack", "seq")),
        P(None, ("pack", "seq")),
        P(None, ("pack", "seq")),
        P(None, ("pack", "seq")),
        P(None, ("pack", "seq")),
        P("seq", "pack"),
        P("seq", "pack"),
        P("seq", "pack"),
        P(("pack", "seq")),
        P(("pack", "seq")),
        P(("pack", "seq")),
    )
    return jax.shard_map(
        body,
        mesh=mesh,
        in_specs=placed,
        out_specs=(
            P(),
            P(),
            P(None, ("pack", "seq")),
            P(None, ("pack", "seq")),
            P(None, ("pack", "seq")),
            P(None, ("pack", "seq")),
            P(None, ("pack", "seq")),
            P(None, ("pack", "seq")),
            P(None, ("pack", "seq")),
            P(None, ("pack", "seq")),
            P(None, ("pack", "seq")),
            P(None, ("pack", "seq")),
            P(None, ("pack", "seq")),
            P(None, ("pack", "seq")),
            P(None, ("pack", "seq")),
            P(None, ("pack", "seq")),
            P("seq", "pack"),
            P("seq", "pack"),
            P("seq", "pack"),
            P(("pack", "seq")),
            P(("pack", "seq")),
            P(("pack", "seq")),
        ),
        check_vma=False,
    )
```

profile of v0, /device:TPU:0, one launch (start us, length us, event | category | flops | bytes accessed | tf_op | source)
XLA Modules:
  0.0 2283.4 jit_solution(4549550250886097399)
XLA Ops:
  14.7 70.8 %all-gather = bf16[32,24,15]{1,2,0:T(8,128)(2,1)S(1)} all-gather(bf16[1,24,15]{1,2,0:T(8,128)(2,1)S(1)} %convert_bitcast_fusion), channel_id=1, replica_groups=mesh['pack'=8,'seq'=4] {'pack','seq'}, dimensions={0}, use_global_device_ids=true | all-gather | bytes 23760 | tf_op jit(solution)/shard_map/all_gather | solution.py:214
  93.1 37.6 %all-gather.10.cloned.1.call-done = bf16[768,2304]{0,1:T(8,128)(2,1)} async-done(((bf16[768,72]{0,1:T(8,128)(2,1)}), bf16[768,2304]{0,1:T(8,128)(2,1)}) %all-gather.10.cloned.1.call-update) | async-done | bytes 3538960 | tf_op jit(solution)/shard_map/all_gather | solution.py:209
  130.8 9.1 add_convert_fusion.1
  145.6 6.7 collective-permute-start
  159.4 4.3 copy.117
  163.7 114.0 %collective-permute-done.1 = bf16[6,256,1536]{2,1,0:T(8,128)(2,1)} collective-permute-done((bf16[6,256,1536]{2,1,0:T(8,128)(2,1)}, bf16[6,256,1536]{2,1,0:T(8,128)(2,1)}, u32[]{:S(2)}, u32[]{:S(2)}) %collective-permute-start.1) | collective-permute-done | bytes 4718624 | tf_op jit(solution)/shard_map/ppermute | solution.py:38
  278.6 12.5 pad_maximum_fusion
  291.1 18.7 copy.116
  311.4 71.4 %while.24 = (s32[]{:T(128)}, bf16[6,256,768]{1,2,0:T(8,128)(2,1)}, f32[6,12,256]{2,1,0:T(8,128)}, bf16[6,768,1536]{1,2,0:T(8,128)(2,1)}, pred[6,256,768]{2,1,0:T...) while((s32[]{:T(128)}, bf16[6,256,768]{1,2,0:T(8,128)(2,1)}, f32[6,12,256]{2,1,0:T(8,128)}, ...), condition=%wide.region_10.11_spmd, body=%wide.region_7.10_spmd.sunk | while | flops 632288256 | bytes 43552872 | solution.py:244
  382.7 6.2 fusion.140
  391.8 19.7 fusion.32
  411.5 45.6 %multiply_convert_fusion.1 = (bf16[6,256,3072]{2,1,0:T(8,128)(2,1)}, f32[6,256,3072]{2,1,0:T(8,128)}) fusion(f32[6,256,3072]{2,1,0:T(8,128)} %get-tuple-element.280, f32[3072]{0:T(1024)S(1)} %add.442, u8[256,3072]{1,0:T(8,128)(4,1)S(1)} %get-tuple-element.173, u8[256,3072]{1,0:T(8,128)(4,1)S(1)} %get-tuple-element.172), kind=kLoop, calls=%fused_computation.43 | loop fusion | flops 335020032 | bytes 48771072 | tf_op jit(solution)/shard_map/convert_element_type | solution.py:255
  457.1 12.8 fusion.141
  480.0 14.2 all-reduce.1
  499.1 9.5 all_gather.36
  508.6 72.8 %all-gather.18.cloned.1.call-done = bf16[768,2732]{1,0:T(8,128)(2,1)} async-done(((bf16[192,2732]{1,0:T(8,128)(2,1)}), bf16[768,2732]{1,0:T(8,128)(2,1)}) %all-gather.18.cloned.1.call-update) | async-done | bytes 4196368 | tf_op jit(solution)/shard_map/all_gather | solution.py:293
  581.4 5.8 convert_reduce_fusion.5
  590.6 33.0 %reduce-scatter.12.cloned.1.call-done = f32[24,768]{1,0:T(8,128)} async-done(((f32[192,768]{1,0:T(8,128)}), f32[24,768]{1,0:T(8,128)}) %reduce-scatter.12.cloned.1.call-update) | async-done | bytes 73744 | tf_op jit(solution)/shard_map/reduce_scatter | solution.py:325
  624.6 14.1 all_gather.39
  639.0 6.6 multiply_reduce_fusion.1
  650.7 24.7 %convert_reduce_fusion = (f32[3072]{0:T(1024)}, bf16[6,256,3072]{2,1,0:T(8,128)(2,1)}) fusion(f32[6,256,3072]{2,1,0:T(8,128)} %get-tuple-element.258, bf16[6,256,768]{2,1,0:T(8,128)(2,1)S(1)} %get-tuple-element.248, bf16[768,3072]{0,1:T(8,128)(2,1)} %all-gather.16.cloned.1.call-done, f32[6,256,3072]{2,1,0:T(8,128)} %get-tuple-element.280, f32[3072]{0:T(1024)S(1)} %add.442), kind=kOutput, calls=%fused_computation.41 | convolution fusion | flops 7327970304 | bytes 54288384 | tf_op jit(solution)/shard_map/psd,df->psf/dot_general | solution.py:349
  675.4 12.9 multiply_reduce_fusion.2
  692.8 3.5 convolution_convert_fusion
  697.9 133.5 %while.25 = (s32[]{:T(128)}, bf16[6,256,768]{1,2,0:T(8,128)(2,1)}, f32[6,768,1536]{1,2,0:T(8,128)}, bf16[6,768,1536]{1,2,0:T(8,128)(2,1)}, pred[6,256,768]{2,1,0...) while((s32[]{:T(128)}, bf16[6,256,768]{1,2,0:T(8,128)(2,1)}, ...), condition=%wide.region_28.29_spmd, body=%wide.region_26.28_spmd.sunk | while | flops 1547498496 | bytes 104091776 | solution.py:369
  707.8 3.8 multiply_reduce_fusion.19
  730.0 3.8 multiply_reduce_fusion.19
  752.3 3.8 multiply_reduce_fusion.19
  774.6 3.8 multiply_reduce_fusion.19
  796.8 3.8 multiply_reduce_fusion.19
  819.0 3.8 multiply_reduce_fusion.19
  831.4 13.2 fusion.137
  845.9 8.2 collective-permute-start.3
  854.1 3.6 convolution_bitcast_fusion.4
  857.9 202.3 %collective-permute-done.2 = f32[6,256,1536]{1,2,0:T(8,128)} collective-permute-done((f32[6,256,1536]{1,2,0:T(8,128)}, f32[6,256,1536]{1,2,0:T(8,128)}, u32[]{:S(2)}, u32[]{:S(2)}) %collective-permute-start.2) | collective-permute-done | bytes 9437216 | tf_op jit(solution)/shard_map/ppermute | solution.py:48
  1061.4 10.1 add_convert_fusion.2
  1071.6 12.1 fusion.125
  1089.0 3.5 convolution_bitcast_fusion.3
  1092.6 13.2 convolution_bitcast_fusion.1
  1106.5 14.5 convolution_bitcast_fusion.2
  1122.3 5.7 fusion.144
  1128.7 13.4 convolution_bitcast_fusion
  1143.6 21.6 all-reduce.3
  1167.5 4.1 convert_reduce_fusion.1
  1171.8 37.4 %all-reduce.2 = f32[15,768]{1,0:T(8,128)S(1)} all-reduce(f32[15,768]{1,0:T(8,128)S(1)} %concatenate.19), channel_id=9, replica_groups=mesh['pack'=8,'seq'=4] {'pack','seq'}, use_global_device_ids=true, to_apply=%region_52.53.clone | all-reduce | flops 11520 | bytes 92160
  1211.4 124.1 %reduce-scatter.20.cloned.1.call-done = f32[768,96]{0,1:T(8,128)} async-done(((f32[768,3072]{0,1:T(8,128)}), f32[768,96]{0,1:T(8,128)}) %reduce-scatter.20.cloned.1.call-update) | async-done | bytes 294928 | tf_op jit(solution)/shard_map/reduce_scatter | solution.py:413
  1337.2 139.9 %reduce-scatter.18.cloned.1.call-done = f32[768,96]{0,1:T(8,128)} async-done(((f32[768,3072]{0,1:T(8,128)}), f32[768,96]{0,1:T(8,128)}) %reduce-scatter.18.cloned.1.call-update) | async-done | bytes 294928 | tf_op jit(solution)/shard_map/reduce_scatter | solution.py:412
  1478.7 148.4 %reduce-scatter.24.cloned.1.call-done = f32[192,2732]{1,0:T(8,128)} async-done(((f32[768,2732]{1,0:T(8,128)}), f32[192,2732]{1,0:T(8,128)}) %reduce-scatter.24.cloned.1.call-update) | async-done | bytes 2098192 | tf_op jit(solution)/shard_map/reduce_scatter | solution.py:315
  1629.8 122.8 %reduce-scatter.14.cloned.1.call-done = f32[768,72]{0,1:T(8,128)} async-done(((f32[768,2304]{0,1:T(8,128)}), f32[768,72]{0,1:T(8,128)}) %reduce-scatter.14.cloned.1.call-update) | async-done | bytes 221200 | tf_op jit(solution)/shard_map/reduce_scatter | solution.py:410
  1759.4 40.7 %all-reduce.4 = (f32[]{:T(128)}, f32[]{:T(128)}) all-reduce(f32[]{:T(128)S(6)} %div.172, f32[]{:T(128)S(6)} %add.468), channel_id=1, replica_groups=mesh['pack'=8,'seq'=4] {'pack','seq'}, use_global_device_ids=true, to_apply=%region_20.21 | all-reduce | flops 2 | bytes 16 | tf_op jit(solution)/shard_map/psum | solution.py:428
  1802.2 3.4 fusion.154
  1805.6 3.5 fusion.151
  1810.1 3.5 fusion.145
  1813.6 3.5 fusion.148
  1817.4 191.1 %all-reduce.12.cloned.1.call-done = (f32[768,768]{1,0:T(8,128)}, f32[768,768]{1,0:T(8,128)}, f32[768,768]{1,0:T(8,128)}, f32[768,768]{1,0:T(8,128)}) async-done(((f32[768,768]{1,0:T(8,128)}, f32[768,768]{1,0:T(8,128)}, f32[768,768]{1,0:T(8,128)}, f32[768,768]{1,0:T(8,128)}), (f32[768,768]{1,0:T(8,128)}, f32[768,768]{1,0:T(8,128)}, f32[768,768]{1,0:T(8,128)}, ...) | async-done | bytes 9437200 | tf_op jit(solution)/shard_map/psum | solution.py:439
  2020.9 4.0 fusion.53
  2025.0 4.0 fusion.91
  2044.2 3.5 fusion.155
  2047.7 3.5 fusion.152
  2051.2 3.5 fusion.146
  2054.6 3.6 fusion.149
  2062.5 8.7 multiply_subtract_fusion
  2071.2 179.4 %all-reduce.10.cloned.1.call-done = (f32[768,768]{1,0:T(8,128)}, f32[768,768]{1,0:T(8,128)}, f32[768,768]{1,0:T(8,128)}, f32[768,768]{1,0:T(8,128)}) async-done(((f32[768,768]{1,0:T(8,128)}, f32[768,768]{1,0:T(8,128)}, f32[768,768]{1,0:T(8,128)}, f32[768,768]{1,0:T(8,128)}), (f32[768,768]{1,0:T(8,128)}, f32[768,768]{1,0:T(8,128)}, f32[768,768]{1,0:T(8,128)}, ...) | async-done | bytes 9437200 | tf_op jit(solution)/shard_map/psum | solution.py:439
  2250.5 3.9 fusion.150
  2254.4 4.5 fusion.93
  (542 shorter events, 314.0 us)
Async XLA Ops:
  7.2 79.5 %copy-start = (bf16[6,256,768]{2,1,0:T(8,128)(2,1)S(1)}, bf16[6,256,768]{2,1,0:T(8,128)(2,1)}, u32[]{:S(2)}) copy-start(bf16[6,256,768]{2,1,0:T(8,128)(2,1)} %param.29) | copy-start | bytes 7077892
  7.2 79.4 %all-gather.8.cloned.1.call-start = ((), (), s32[]{:S(2)}) async-start(), calls=%async_computation.8 | async-start | bytes 1216512 | tf_op jit(solution)/shard_map/all_gather | solution.py:213
  8.9 121.8 %all-gather.10.cloned.1.call-start = ((), (), s32[]{:S(2)}) async-start(), calls=%async_computation.9 | async-start | bytes 3649536 | tf_op jit(solution)/shard_map/all_gather | solution.py:209
  10.6 372.1 %all-gather.12.cloned.1.call-start = ((), (), s32[]{:S(2)}) async-start(), calls=%async_computation.10 | async-start | bytes 1216512 | tf_op jit(solution)/shard_map/all_gather | solution.py:210
  12.2 379.6 %all-gather.14.cloned.1.call-start = ((), (), s32[]{:S(2)}) async-start(), calls=%async_computation.11 | async-start | bytes 4866048 | tf_op jit(solution)/shard_map/all_gather | solution.py:211
  13.9 443.2 %all-gather.16.cloned.1.call-start = ((), (), s32[]{:S(2)}) async-start(), calls=%async_computation.12 | async-start | bytes 4866048 | tf_op jit(solution)/shard_map/all_gather | solution.py:212
  86.6 44.1 %copy-start.69 = (f32[768]{0:T(1024)}, f32[768]{0:T(1024)S(1)}, u32[]{:S(2)}) copy-start(f32[768]{0:T(1024)S(1)} %get-tuple-element.193) | copy-start | bytes 9220
  86.6 44.1 %copy-start.93 = (f32[768]{0:T(1024)}, f32[768]{0:T(1024)S(1)}, u32[]{:S(2)}) copy-start(f32[768]{0:T(1024)S(1)} %get-tuple-element.192) | copy-start | bytes 9220
  86.6 296.1 %copy-start.64 = (f32[768]{0:T(1024)}, f32[768]{0:T(1024)S(1)}, u32[]{:S(2)}) copy-start(f32[768]{0:T(1024)S(1)} %get-tuple-element.194) | copy-start | bytes 9220
  90.1 40.7 %copy-start.44 = (f32[6,256]{1,0:T(8,128)}, f32[6,256]{1,0:T(8,128)S(1)}, u32[]{:S(2)}) copy-start(f32[6,256]{1,0:T(8,128)S(1)} %broadcast_multiply_fusion.2) | copy-start | bytes 18436
  93.1 37.7 %copy-start.57 = (f32[6,256]{1,0:T(8,128)}, f32[6,256]{1,0:T(8,128)S(1)}, u32[]{:S(2)}) copy-start(f32[6,256]{1,0:T(8,128)S(1)} %multiply_reduce_fusion.9) | copy-start | bytes 18436
  93.1 37.7 %copy-start.53 = (f32[6,256]{1,0:T(8,128)}, f32[6,256]{1,0:T(8,128)S(1)}, u32[]{:S(2)}) copy-start(f32[6,256]{1,0:T(8,128)S(1)} %fusion.119) | copy-start | bytes 18436
  144.3 133.4 %collective-permute-start.1 = (bf16[6,256,1536]{2,1,0:T(8,128)(2,1)}, bf16[6,256,1536]{2,1,0:T(8,128)(2,1)}, u32[]{:S(2)}, u32[]{:S(2)}) collective-permute-start(bf16[6,256,1536]{2,1,0:T(8,128)(2,1)} %slice.101), channel_id=1, source_target_pairs={{1,0},{2,1},{3,2},{5,4},{6,5},{7,6},{9,8},{10,9},{11,10},{13,12},{... | collective-permute-start | bytes 14155784 | tf_op jit(solution)/shard_map/ppermute | solution.py:38
  145.6 133.0 %collective-permute-start = (bf16[6,256,1536]{2,1,0:T(8,128)(2,1)}, bf16[6,256,1536]{2,1,0:T(8,128)(2,1)}, u32[]{:S(2)}, u32[]{:S(2)}) collective-permute-start(bf16[6,256,1536]{2,1,0:T(8,128)(2,1)} %slice.101), channel_id=1, source_target_pairs={{0,1},{1,2},{2,3},{4,5},{5,6},{6,7},{8,9},{9,10},{10,11},{12,13},{... | collective-permute-start | bytes 14155784 | tf_op jit(solution)/shard_map/ppermute | solution.py:36
  153.0 345.2 %reduce-scatter.10.cloned.1.call-start = ((), (), s32[]{:S(2)}) async-start(), calls=%async_computation.13 | async-start | bytes 368640 | tf_op jit(solution)/shard_map/reduce_scatter | solution.py:278
  389.0 299.3 %copy-start.55 = (f32[6,256]{1,0:T(8,128)}, f32[6,256]{1,0:T(8,128)S(1)}, u32[]{:S(2)}) copy-start(f32[6,256]{1,0:T(8,128)S(1)} %broadcast_multiply_fusion.1) | copy-start | bytes 18436
  391.7 296.6 %copy-start.71 = (f32[6,256]{1,0:T(8,128)}, f32[6,256]{1,0:T(8,128)S(1)}, u32[]{:S(2)}) copy-start(f32[6,256]{1,0:T(8,128)S(1)} %fusion.120) | copy-start | bytes 18436
  411.5 45.6 %copy-start.97 = (f32[768]{0:T(1024)S(1)}, f32[768]{0:T(1024)}, u32[]{:S(2)}) copy-start(f32[768]{0:T(1024)} %get-tuple-element.186) | copy-start | bytes 9220
  472.1 22.5 copy-start.43
  472.1 23.0 %copy-start.88 = (s32[48,16]{0,1:T(8,128)S(1)}, s32[48,16]{0,1:T(8,128)}, u32[]{:S(2)}) copy-start(s32[48,16]{0,1:T(8,128)} %param.32) | copy-start | bytes 9220
  475.7 105.8 %all-gather.18.cloned.1.call-start = ((), (), s32[]{:S(2)}) async-start(), calls=%async_computation.14 | async-start | bytes 5406720 | tf_op jit(solution)/shard_map/all_gather | solution.py:293
  478.4 145.2 %reduce-scatter.12.cloned.1.call-start = ((), (), s32[]{:S(2)}) async-start(), calls=%async_computation.15 | async-start | bytes 663552 | tf_op jit(solution)/shard_map/reduce_scatter | solution.py:325
  508.6 78.6 %copy-start.35 = (bf16[192,768]{1,0:T(8,128)(2,1)}, bf16[192,768]{1,0:T(8,128)(2,1)S(1)}, u32[]{:S(2)}) copy-start(bf16[192,768]{1,0:T(8,128)(2,1)S(1)} %all_gather.36) | copy-start | bytes 884740
  590.6 575.5 %reduce-scatter.16.cloned.1.call-start = ((), (), s32[]{:S(2)}) async-start(), calls=%async_computation.17 | async-start | bytes 2433024 | tf_op jit(solution)/shard_map/reduce_scatter | solution.py:411
  647.5 42.8 %copy-start.48 = (f32[6,256]{1,0:T(8,128)}, f32[6,256]{1,0:T(8,128)S(1)}, u32[]{:S(2)}) copy-start(f32[6,256]{1,0:T(8,128)S(1)} %negate_multiply_fusion.3) | copy-start | bytes 18436
  649.6 25.8 %slice-start.8 = ((s8[4718592]{0:T(1024)(128)(4,1)}), s8[4194304]{0:T(1024)(128)(4,1)S(1)}, s32[]{:S(2)}) async-start(s8[4718592]{0:T(1024)(128)(4,1)} %bitcast.257), calls=%async_computation.32 | async-start | bytes 8388608
  650.7 24.7 %copy-start.26 = (bf16[6,256,768]{2,1,0:T(8,128)(2,1)}, bf16[6,256,768]{2,1,0:T(8,128)(2,1)S(1)}, u32[]{:S(2)}) copy-start(bf16[6,256,768]{2,1,0:T(8,128)(2,1)S(1)} %get-tuple-element.248) | copy-start | bytes 7077892
  650.7 24.7 %slice-start.9 = ((s8[4718592]{0:T(1024)(128)(4,1)}), s8[524288]{0:T(1024)(128)(4,1)S(1)}, s32[]{:S(2)}) async-start(s8[4718592]{0:T(1024)(128)(4,1)} %bitcast.257), calls=%async_computation.33 | async-start | bytes 1048576
  650.7 24.7 %copy-start.84 = (f32[768]{0:T(1024)S(1)}, f32[768]{0:T(1024)}, u32[]{:S(2)}) copy-start(f32[768]{0:T(1024)} %get-tuple-element.188) | copy-start | bytes 9220
  831.4 22.7 copy-start.25
  831.4 22.7 copy-start.28
  844.6 215.5 %collective-permute-start.2 = (f32[6,256,1536]{1,2,0:T(8,128)}, f32[6,256,1536]{1,2,0:T(8,128)}, u32[]{:S(2)}, u32[]{:S(2)}) collective-permute-start(f32[6,256,1536]{1,2,0:T(8,128)} %get-tuple-element.269), channel_id=1, source_target_pairs={{1,0},{2,1},{3,2},{5,4},{6,5},{7,6},{9,8},{10,9},{11,10},{13,12},{... | collective-permute-start | bytes 28311560 | tf_op jit(solution)/shard_map/ppermute | solution.py:48
  845.9 215.4 %collective-permute-start.3 = (f32[6,256,1536]{1,2,0:T(8,128)}, f32[6,256,1536]{1,2,0:T(8,128)}, u32[]{:S(2)}, u32[]{:S(2)}) collective-permute-start(f32[6,256,1536]{1,2,0:T(8,128)} %get-tuple-element.270), channel_id=1, source_target_pairs={{0,1},{1,2},{2,3},{4,5},{5,6},{6,7},{8,9},{9,10},{10,11},{12,13},{... | collective-permute-start | bytes 28311560 | tf_op jit(solution)/shard_map/ppermute | solution.py:48
  857.8 213.7 %copy-start.45 = (f32[6,256]{1,0:T(8,128)S(1)}, f32[6,256]{1,0:T(8,128)}, u32[]{:S(2)}) copy-start(f32[6,256]{1,0:T(8,128)} %copy-done.44) | copy-start | bytes 18436
  857.8 213.7 %copy-start.65 = (f32[768]{0:T(1024)S(1)}, f32[768]{0:T(1024)}, u32[]{:S(2)}) copy-start(f32[768]{0:T(1024)} %copy-done.64) | copy-start | bytes 9220
  857.8 213.7 %copy-start.70 = (f32[768]{0:T(1024)S(1)}, f32[768]{0:T(1024)}, u32[]{:S(2)}) copy-start(f32[768]{0:T(1024)} %copy-done.69) | copy-start | bytes 9220
  857.8 352.1 %reduce-scatter.22.cloned.1.call-start = ((), (), s32[]{:S(2)}) async-start(), calls=%async_computation.20 | async-start | bytes 2433024 | tf_op jit(solution)/shard_map/reduce_scatter | solution.py:414
  857.8 213.7 %copy-start.14 = (bf16[6,256,768]{1,2,0:T(8,128)(2,1)S(1)}, bf16[6,256,768]{1,2,0:T(8,128)(2,1)}, u32[]{:S(2)}) copy-start(bf16[6,256,768]{1,2,0:T(8,128)(2,1)} %get-tuple-element.100) | copy-start | bytes 7077892
  1061.4 24.9 %slice-start.2 = ((s8[4718592]{0:T(1024)(128)(4,1)}), s8[4194304]{0:T(1024)(128)(4,1)S(1)}, s32[]{:S(2)}) async-start(s8[4718592]{0:T(1024)(128)(4,1)} %bitcast.245), calls=%async_computation.26 | async-start | bytes 8388608
  1061.4 24.9 %slice-start.6 = ((s8[4718592]{0:T(1024)(128)(4,1)}), s8[4194304]{0:T(1024)(128)(4,1)S(1)}, s32[]{:S(2)}) async-start(s8[4718592]{0:T(1024)(128)(4,1)} %bitcast.250), calls=%async_computation.30 | async-start | bytes 8388608
  1092.5 243.0 %reduce-scatter.20.cloned.1.call-start = ((), (), s32[]{:S(2)}) async-start(), calls=%async_computation.19 | async-start | bytes 9732096 | tf_op jit(solution)/shard_map/reduce_scatter | solution.py:413
  1105.8 371.2 %reduce-scatter.18.cloned.1.call-start = ((), (), s32[]{:S(2)}) async-start(), calls=%async_computation.18 | async-start | bytes 9732096 | tf_op jit(solution)/shard_map/reduce_scatter | solution.py:412
  1121.1 505.9 %reduce-scatter.24.cloned.1.call-start = ((), (), s32[]{:S(2)}) async-start(), calls=%async_computation.21 | async-start | bytes 10813440 | tf_op jit(solution)/shard_map/reduce_scatter | solution.py:315
  1128.1 624.5 %reduce-scatter.14.cloned.1.call-start = ((), (), s32[]{:S(2)}) async-start(), calls=%async_computation.16 | async-start | bytes 7299072 | tf_op jit(solution)/shard_map/reduce_scatter | solution.py:410
  1142.2 23.7 %copy-start.77 = (f32[768]{0:T(1024)S(1)}, f32[768]{0:T(1024)}, u32[]{:S(2)}) copy-start(f32[768]{0:T(1024)} %get-tuple-element.176) | copy-start | bytes 9220
  1142.2 23.7 %copy-start.76 = (f32[768]{0:T(1024)S(1)}, f32[768]{0:T(1024)}, u32[]{:S(2)}) copy-start(f32[768]{0:T(1024)} %get-tuple-element.180) | copy-start | bytes 9220
  1142.2 23.7 %copy-start.78 = (f32[768]{0:T(1024)S(1)}, f32[768]{0:T(1024)}, u32[]{:S(2)}) copy-start(f32[768]{0:T(1024)} %get-tuple-element.247) | copy-start | bytes 9220
  1142.2 23.7 %copy-start.87 = (f32[3072]{0:T(1024)S(1)}, f32[3072]{0:T(1024)}, u32[]{:S(2)}) copy-start(f32[3072]{0:T(1024)} %get-tuple-element.286) | copy-start | bytes 36868
  1142.2 23.7 %copy-start.99 = (f32[768]{0:T(1024)S(1)}, f32[768]{0:T(1024)}, u32[]{:S(2)}) copy-start(f32[768]{0:T(1024)} %get-tuple-element.178) | copy-start | bytes 9220
  1142.2 23.7 %copy-start.98 = (f32[768]{0:T(1024)S(1)}, f32[768]{0:T(1024)}, u32[]{:S(2)}) copy-start(f32[768]{0:T(1024)} %get-tuple-element.181) | copy-start | bytes 9220
  1142.2 23.8 %copy-start.79 = (f32[768]{0:T(1024)S(1)}, f32[768]{0:T(1024)}, u32[]{:S(2)}) copy-start(f32[768]{0:T(1024)} %get-tuple-element.249) | copy-start | bytes 9220
  1142.3 866.2 %all-reduce.12.cloned.1.call-start = ((), (), s32[]{:S(2)}) async-start(), calls=%async_computation.23 | async-start | bytes 18874368 | tf_op jit(solution)/shard_map/psum | solution.py:439
  1209.2 596.4 %copy-start.52 = (f32[15,768]{1,0:T(8,128)}, f32[15,768]{1,0:T(8,128)S(1)}, u32[]{:S(2)}) copy-start(f32[15,768]{1,0:T(8,128)S(1)} %all-reduce.2) | copy-start | bytes 138244
  1752.6 56.6 %copy-start.37 = (f32[768,72]{0,1:T(8,128)S(1)}, f32[768,72]{0,1:T(8,128)}, u32[]{:S(2)}) copy-start(f32[768,72]{0,1:T(8,128)} %reduce-scatter.14.cloned.1.call-done) | copy-start | bytes 663556
  1802.1 234.3 %copy-start.17 = (f32[768,96]{0,1:T(8,128)}, f32[768,96]{0,1:T(8,128)S(1)}, u32[]{:S(2)}) copy-start(f32[768,96]{0,1:T(8,128)S(1)} %get-tuple-element.289) | copy-start | bytes 884740
  1802.2 239.6 %copy-start.16 = (f32[768,96]{0,1:T(8,128)}, f32[768,96]{0,1:T(8,128)S(1)}, u32[]{:S(2)}) copy-start(f32[768,96]{0,1:T(8,128)S(1)} %get-tuple-element.288) | copy-start | bytes 884740
  1810.1 221.4 %copy-start.19 = (f32[768,72]{0,1:T(8,128)}, f32[768,72]{0,1:T(8,128)S(1)}, u32[]{:S(2)}) copy-start(f32[768,72]{0,1:T(8,128)S(1)} %multiply_add_fusion.3) | copy-start | bytes 663556
  1813.6 211.3 %copy-start.29 = (f32[768,24]{0,1:T(8,128)}, f32[768,24]{0,1:T(8,128)S(1)}, u32[]{:S(2)}) copy-start(f32[768,24]{0,1:T(8,128)S(1)} %multiply_add_fusion.4) | copy-start | bytes 221188
  1817.1 433.4 %all-reduce.10.cloned.1.call-start = ((), (), s32[]{:S(2)}) async-start(), calls=%async_computation.22 | async-start | bytes 18874368 | tf_op jit(solution)/shard_map/psum | solution.py:439
  2029.0 25.7 %copy-start.30 = (f32[768,24]{0,1:T(8,128)}, f32[768,24]{0,1:T(8,128)S(1)}, u32[]{:S(2)}) copy-start(f32[768,24]{0,1:T(8,128)S(1)} %fusion.91) | copy-start | bytes 221188
  2062.5 188.0 %copy-start.31 = (f32[768,24]{0,1:T(8,128)S(1)}, f32[768,24]{0,1:T(8,128)}, u32[]{:S(2)}) copy-start(f32[768,24]{0,1:T(8,128)} %copy-done.30) | copy-start | bytes 221188
  2062.5 191.9 %copy-start.41 = (f32[768,24]{0,1:T(8,128)S(1)}, f32[768,24]{0,1:T(8,128)}, u32[]{:S(2)}) copy-start(f32[768,24]{0,1:T(8,128)} %param.39) | copy-start | bytes 221188
  2071.2 187.7 %copy-start.21 = (f32[768,72]{0,1:T(8,128)S(1)}, f32[768,72]{0,1:T(8,128)}, u32[]{:S(2)}) copy-start(f32[768,72]{0,1:T(8,128)} %copy-done.20) | copy-start | bytes 663556
  2071.2 190.1 %copy-start.36 = (f32[768,72]{0,1:T(8,128)S(1)}, f32[768,72]{0,1:T(8,128)}, u32[]{:S(2)}) copy-start(f32[768,72]{0,1:T(8,128)} %param.37) | copy-start | bytes 663556
  (68 other events, 407.2 us)
Sparse Core Ops, SparseCore 0:
  11.4 56.8 all-gather.7
  71.7 59.0 all-gather.9
  134.1 54.1 all-gather.11
  191.6 72.7 all-gather.13
  267.6 66.4 all-gather.15
  475.8 22.3 reduce-scatter.9
  500.3 81.0 all-gather.17
  590.7 32.9 reduce-scatter.11
  857.9 99.8 reduce-scatter.15
  1092.6 102.4 reduce-scatter.21
  1201.0 134.4 reduce-scatter.19
  1342.3 134.7 reduce-scatter.17
  1479.4 147.5 reduce-scatter.23
  1632.5 119.9 reduce-scatter.13
  1817.3 191.1 all-reduce.11
  2058.4 192.0 all-reduce.9
where the time goes:
time: 2290 us; the launch traced here: 2280 us
  waiting for transfers between devices  1370 us (60%)
  matrix products  344 us (15%)
  blocking collectives  208 us (9%)
  other arithmetic  186 us (8%)
  local copies, waits for them, and re-layouts  127 us (6%)
  between operations  28.7 us (1%)
    psum x2, waiting for transfers between devices, body(): lax.psum((gram_of(iterates[0]), gram_of(iterates[1]), gram_of(iterates[2]...  370 us
    ppermute x2, waiting for transfers between devices, passed_along(): lax.ppermute(value, axis, [(source, source + steps) for source in range(l...  204 us
    reduce_scatter x1, waiting for transfers between devices, body(): lax.psum_scatter(jnp.einsum('nd,nc->dc', pooled_rows, grad_logits, prefer...  148 us
    reduce_scatter x1, waiting for transfers between devices, body(): lax.psum_scatter(grad_up, ('pack', 'seq'), scatter_dimension=1, tiled=True)  140 us
    reduce_scatter x1, waiting for transfers between devices, body(): lax.psum_scatter(grad_down, ('pack', 'seq'), scatter_dimension=1, tiled=T...  124 us
    reduce_scatter x1, waiting for transfers between devices, body(): lax.psum_scatter(grad_qkv_w, ('pack', 'seq'), scatter_dimension=1, tiled=...  123 us
    ppermute x1, waiting for transfers between devices, extended(): lax.ppermute(head, axis, [((i + 1) % count, i) for i in range(ends)])  114 us
    dot_general x24, matrix products, hmul(): jnp.dot(left, right, precision=HIGHEST_PREC, preferred_element_type=jnp.f...  75.9 us
  transfers between devices with their start and end apart: 20, of which 14 were waited for; matrix products, arithmetic and copies ran while one was open for 14% of the time, Pallas kernels for 0%

commit v1 on v0

v1 whole, which is shorter than its diff:
```python
import math

import jax
import jax.numpy as jnp
from jax import lax
from jax.experimental import pallas as pl
from jax.experimental.pallas import tpu as pltpu
from jax.sharding import PartitionSpec as P

HEAD_DIM = 64
LABELS = 21843
PACK_LEN = 1024
MAXLEN = 128
NS_STEPS = 2
BLOCK = 128
PAIR = 2 * HEAD_DIM

HIGHEST_PREC = lax.Precision.HIGHEST
NS_PREC = lax.Precision.HIGH
CLIP_NORM = 1.0
MUON_MU = 0.95
MUON_RATE = 1.0
ADAM_RATE = 0.02
BETA_ONE = 0.9
BETA_TWO = 0.95
DECAY = 0.01
COEF_ONE = 3.4445
COEF_TWO = -4.775
COEF_THREE = 2.0315
SCALE = HEAD_DIM ** (-0.5)
LOW = jnp.bfloat16
F32 = jnp.float32
NEG = -1e30


def swap(value, axis, bit):
    return lax.ppermute(value, axis, [(i, i ^ bit) for i in range(lax.axis_size(axis))])


def pick(value, index, dim=0):
    return lax.dynamic_index_in_dim(value, index, dim, keepdims=False)


def tree_sum(parts):
    while len(parts) > 1:
        parts = [parts[i] + parts[i + 1] for i in range(0, len(parts), 2)]
    return parts[0]


def relative(value, axis):
    return [value] + [swap(value, axis, k) for k in range(1, lax.axis_size(axis))]


def absolute(parts, place):
    return [_choose(parts, place, j) for j in range(len(parts))]


def _choose(parts, place, j):
    out = parts[j]
    for other in range(1, len(parts)):
        out = jnp.where(place == other, parts[j ^ other], out)
    return out


def all_sum(value, axis):
    return tree_sum(relative(value, axis))


def pack_bits(order):
    count = lax.axis_size("pack")
    bits = [1 << b for b in reversed(range(count.bit_length() - 1))]
    others = [b for b in bits if b > 1]
    return bits, (others if order == 0 else others[::-1])


def gather_rows(shard, order):
    seq_place, pack_place = lax.axis_index("seq"), lax.axis_index("pack")
    bits, others = pack_bits(order)
    whole = jnp.concatenate(absolute(relative(shard, "seq"), seq_place), axis=0)
    whole = whole.reshape((1,) * len(bits) + whole.shape)
    for bit in others + [1]:
        dim = bits.index(bit)
        other = swap(whole, "pack", bit)
        whole = jnp.where(
            (pack_place & bit) == 0,
            jnp.concatenate([whole, other], axis=dim),
            jnp.concatenate([other, whole], axis=dim),
        )
    return whole.reshape(-1, shard.shape[1])


def halve(value, bits, order):
    pack_place = lax.axis_index("pack")
    _, others = pack_bits(order)
    left = list(bits)
    for bit in [1] + others:
        dim = left.index(bit)
        mine = (pack_place & bit) // bit
        value = pick(value, mine, dim) + swap(pick(value, 1 - mine, dim), "pack", bit)
        left.remove(bit)
    return value


def scatter_rows(grad, order):
    seq_count, seq_place = lax.axis_size("seq"), lax.axis_index("seq")
    bits, _ = pack_bits(order)
    count = lax.axis_size("pack") * seq_count
    value = grad.reshape((2,) * len(bits) + (seq_count, grad.shape[0] // count, grad.shape[1]))
    value = halve(value, bits, order)
    parts = [pick(value, seq_place)]
    parts += [swap(pick(value, seq_place ^ k), "seq", k) for k in range(1, seq_count)]
    return tree_sum(parts)


def pack_sum(value, order):
    pack_place = lax.axis_index("pack")
    bits, others = pack_bits(order)
    rows = value.shape[0] >> len(bits)
    part = halve(value.reshape((2,) * len(bits) + (rows, value.shape[1])), bits, order)
    part = part.reshape((1,) * len(bits) + part.shape)
    for bit in others[::-1] + [1]:
        dim = bits.index(bit)
        other = swap(part, "pack", bit)
        part = jnp.where(
            (pack_place & bit) == 0,
            jnp.concatenate([part, other], axis=dim),
            jnp.concatenate([other, part], axis=dim),
        )
    return part.reshape(value.shape)


def _dot(left, right, dims):
    return lax.dot_general(left, right, (dims, ((), ())), preferred_element_type=F32)


NT = ((1,), (1,))
TN = ((0,), (0,))
NN = ((1,), (0,))


def _window(ref, block, blocks, column):
    places = (jnp.maximum(block - 1, 0), block, jnp.minimum(block + 1, blocks - 1))
    return jnp.concatenate(
        [ref[pl.ds(pl.multiple_of(place * BLOCK, BLOCK), BLOCK), column : column + PAIR] for place in places],
        axis=0,
    )


def _halves(value):
    lane = lax.broadcasted_iota(jnp.int32, value.shape, 1)
    zero = jnp.zeros_like(value)
    return jnp.where(lane < HEAD_DIM, value, zero), jnp.where(lane < HEAD_DIM, zero, value)


def _merge(low, high):
    return jnp.concatenate([low[:HEAD_DIM], high[HEAD_DIM:]], axis=0).T


def attend_kernel(width, blocks, rows_ref, query_id_ref, key_id_ref, out_ref, log_ref):
    block = pl.program_id(0)
    allowed = key_id_ref[pl.ds(pl.multiple_of(block * BLOCK, BLOCK), 3 * BLOCK), :] == query_id_ref[0]
    here = pl.ds(pl.multiple_of(block * BLOCK, BLOCK), BLOCK)
    for pair in range(width // PAIR):
        column = pair * PAIR
        queries = _halves(rows_ref[here, column : column + PAIR] * SCALE)
        keys = _window(rows_ref, block, blocks, width + column)
        values = _window(rows_ref, block, blocks, 2 * width + column)
        mixed = []
        for half in range(2):
            scores = jnp.where(allowed, _dot(keys, queries[half], NT), NEG)
            top = jnp.max(scores, axis=0, keepdims=True)
            raised = jnp.exp(scores - top)
            total = jnp.sum(raised, axis=0, keepdims=True)
            probs = (raised * (1.0 / total)).astype(LOW)
            mixed.append(_dot(values, probs, TN))
            log_ref[0, 2 * pair + half : 2 * pair + half + 1, :] = top + jnp.log(total)
        out_ref[:, column : column + PAIR] = _merge(*mixed).astype(LOW)


def attend_back_kernel(
    width, blocks, rows_ref, grad_ref, log_ref, query_id_ref, key_id_ref, out_ref, key_sum, value_sum
):
    block = pl.program_id(0)

    @pl.when(block == 0)
    def _():
        key_sum[...] = jnp.zeros_like(key_sum)
        value_sum[...] = jnp.zeros_like(value_sum)

    span = pl.ds(pl.multiple_of(block * BLOCK, BLOCK), 3 * BLOCK)
    here = pl.ds(pl.multiple_of(block * BLOCK, BLOCK), BLOCK)
    allowed = key_id_ref[span, :] == query_id_ref[0]
    for pair in range(width // PAIR):
        column = pair * PAIR
        queries = _halves(rows_ref[here, column : column + PAIR] * SCALE)
        grads = _halves(grad_ref[here, column : column + PAIR])
        keys = _window(rows_ref, block, blocks, width + column)
        values = _window(rows_ref, block, blocks, 2 * width + column)
        probs_low, grad_scores, query_grads = [], [], []
        for half in range(2):
            scores = jnp.where(allowed, _dot(keys, queries[half], NT), NEG)
            probs = jnp.exp(scores - log_ref[0, 2 * pair + half : 2 * pair + half + 1, :])
            grad_probs = _dot(values, grads[half], NT)
            inner = jnp.sum(probs * grad_probs, axis=0, keepdims=True)
            grad_score = (probs * (grad_probs - inner)).astype(LOW)
            probs_low.append(probs.astype(LOW))
            grad_scores.append(grad_score)
            query_grads.append(_dot(keys, grad_score, TN))
        out_ref[here, column : column + PAIR] = (_merge(*query_grads) * SCALE).astype(LOW)
        lanes = slice(column, column + PAIR)
        key_sum[span, lanes] += _dot(
            jnp.concatenate(grad_scores, axis=1), jnp.concatenate(queries, axis=0), NN
        )
        value_sum[span, lanes] += _dot(
            jnp.concatenate(probs_low, axis=1), jnp.concatenate(grads, axis=0), NN
        )

    @pl.when(block == blocks - 1)
    def _():
        def write(place, carry):
            into = pl.ds(pl.multiple_of(place * BLOCK, BLOCK), BLOCK)
            source = pl.ds(pl.multiple_of((place + 1) * BLOCK, BLOCK), BLOCK)
            out_ref[into, width : 2 * width] = key_sum[source, :].astype(LOW)
            out_ref[into, 2 * width :] = value_sum[source, :].astype(LOW)
            return carry

        lax.fori_loop(0, blocks, write, 0)


def _params():
    return pltpu.CompilerParams(dimension_semantics=("arbitrary",), vmem_limit_bytes=56 << 20)


def attend(qkv_rows, query_id, key_id):
    rows, triple = qkv_rows.shape
    width, blocks = triple // 3, rows // BLOCK
    heads = width // HEAD_DIM
    return pl.pallas_call(
        lambda *refs: attend_kernel(width, blocks, *refs),
        grid=(blocks,),
        in_specs=[
            pl.BlockSpec((rows, triple), lambda i: (0, 0)),
            pl.BlockSpec((1, 1, BLOCK), lambda i: (i, 0, 0)),
            pl.BlockSpec((rows + 2 * BLOCK, 1), lambda i: (0, 0)),
        ],
        out_specs=[
            pl.BlockSpec((BLOCK, width), lambda i: (i, 0)),
            pl.BlockSpec((1, heads, BLOCK), lambda i: (i, 0, 0)),
        ],
        out_shape=[
            jax.ShapeDtypeStruct((rows, width), LOW),
            jax.ShapeDtypeStruct((blocks, heads, BLOCK), F32),
        ],
        compiler_params=_params(),
        cost_estimate=pl.CostEstimate(
            flops=4 * rows * 3 * BLOCK * triple, bytes_accessed=8 * rows * width, transcendentals=rows * 3 * BLOCK * heads
        ),
    )(qkv_rows, query_id, key_id)


def attend_back(qkv_rows, grad_rows, log_total, query_id, key_id):
    rows, triple = qkv_rows.shape
    width, blocks = triple // 3, rows // BLOCK
    heads = width // HEAD_DIM
    return pl.pallas_call(
        lambda *refs: attend_back_kernel(width, blocks, *refs),
        grid=(blocks,),
        in_specs=[
            pl.BlockSpec((rows, triple), lambda i: (0, 0)),
            pl.BlockSpec((rows, width), lambda i: (0, 0)),
            pl.BlockSpec((1, heads, BLOCK), lambda i: (i, 0, 0)),
            pl.BlockSpec((1, 1, BLOCK), lambda i: (i, 0, 0)),
            pl.BlockSpec((rows + 2 * BLOCK, 1), lambda i: (0, 0)),
        ],
        out_specs=pl.BlockSpec((rows, triple), lambda i: (0, 0)),
        out_shape=jax.ShapeDtypeStruct((rows, triple), LOW),
        scratch_shapes=[
            pltpu.VMEM((rows + 2 * BLOCK, width), F32),
            pltpu.VMEM((rows + 2 * BLOCK, width), F32),
        ],
        compiler_params=_params(),
        cost_estimate=pl.CostEstimate(
            flops=10 * rows * 3 * BLOCK * triple, bytes_accessed=16 * rows * width, transcendentals=rows * 3 * BLOCK * heads
        ),
    )(qkv_rows, grad_rows, log_total, query_id, key_id)


def layer_norm(values, gain_row, bias_row):
    centre = values - jnp.mean(values, axis=-1, keepdims=True)
    spread = jnp.mean(centre * centre, axis=-1, keepdims=True)
    return centre * lax.rsqrt(spread + 1e-06) * gain_row + bias_row


def norm_back(values, gain_row, bias_row, cotangent):
    _, pullback = jax.vjp(layer_norm, values, gain_row, bias_row)
    return pullback(cotangent)


def gelu(values):
    return 0.5 * values * (1.0 + lax.erf(values * math.sqrt(0.5)))


def gelu_slope(values):
    return 0.5 * (1.0 + lax.erf(values * math.sqrt(0.5))) + values * (
        math.sqrt(0.5 / math.pi) * jnp.exp(-0.5 * values * values)
    )


def mm(spec, left, right):
    return jnp.einsum(spec, left, right, preferred_element_type=F32)


def column_sum(rows):
    return jnp.sum(rows.astype(F32), axis=0)


def hmul(left, right):
    return jnp.dot(left, right, precision=NS_PREC, preferred_element_type=F32)


def ortho(columns):
    gram_mat = pack_sum(
        lax.dot_general(columns, columns, (TN, ((), ())), precision=NS_PREC, preferred_element_type=F32), 0
    )
    scale = 1.0 / (jnp.sqrt(jnp.trace(gram_mat)) + 1e-07)
    iterate = columns * scale
    gram_mat = gram_mat * scale * scale
    eye = jnp.eye(gram_mat.shape[0], dtype=F32)
    for step in range(NS_STEPS):
        if step < NS_STEPS - 1:
            square = hmul(gram_mat, gram_mat)
            poly = COEF_ONE * eye + COEF_TWO * gram_mat + COEF_THREE * square
            poly_gram = COEF_ONE * gram_mat + COEF_TWO * square + COEF_THREE * hmul(square, gram_mat)
            iterate = hmul(iterate, poly)
            gram_mat = hmul(poly, poly_gram)
        else:
            first_pass = hmul(iterate, gram_mat)
            iterate = COEF_ONE * iterate + COEF_TWO * first_pass + COEF_THREE * hmul(first_pass, gram_mat)
    return iterate


def muon(moments):
    seq_count, seq_place = lax.axis_size("seq"), lax.axis_index("seq")
    most = max(m.shape[0] for m in moments)
    filled = [jnp.pad(m, ((0, most - m.shape[0]), (0, 0))) for m in moments]
    filled += [jnp.zeros_like(filled[0])] * (seq_count - len(moments))
    stacked = jnp.stack(filled)
    parts = [pick(stacked, seq_place)]
    parts += [swap(pick(stacked, seq_place ^ k), "seq", k) for k in range(1, seq_count)]
    done = ortho(jnp.concatenate(parts, axis=0)).reshape(stacked.shape)
    back = [done[0]] + [swap(done[k], "seq", k) for k in range(1, seq_count)]
    return [_choose(back, seq_place, m)[: moments[m].shape[0]] for m in range(len(moments))]


def muon_update(weight, iterate):
    col_ratio = math.sqrt(
        max(1.0, iterate.shape[1] * lax.axis_size(("pack", "seq")) / weight.shape[0])
    )
    return weight * (1.0 - MUON_RATE * DECAY) - MUON_RATE * col_ratio * iterate


def adam_update(weight, first_moment, second_moment, gradient, factor, count_float):
    scaled = factor * gradient
    new_first = BETA_ONE * first_moment + (1.0 - BETA_ONE) * scaled
    new_second = BETA_TWO * second_moment + (1.0 - BETA_TWO) * scaled * scaled
    first_hat = new_first / (1.0 - jnp.power(BETA_ONE, count_float))
    second_hat = new_second / (1.0 - jnp.power(BETA_TWO, count_float))
    new_weight = weight - ADAM_RATE * (first_hat / (jnp.sqrt(second_hat) + 1e-08) + DECAY * weight)
    return (new_weight, new_first, new_second)


def deal_rows(lengths, keep_mask, shard_len):
    packs, images = lengths.shape
    seq_count, seq_place = lax.axis_size("seq"), lax.axis_index("seq")
    image_range = jnp.arange(images, dtype=jnp.int32)
    upto = image_range[None, :] <= image_range[:, None]
    ends = jnp.sum(jnp.where(upto[None], lengths[:, None, :], 0), axis=2, dtype=jnp.int32)
    starts = ends - lengths
    cuts = jnp.arange(1, seq_count, dtype=jnp.int32) * shard_len
    straddles = (starts[:, None, :] < cuts[None, :, None]) & (ends[:, None, :] > cuts[None, :, None])
    behind = jnp.sum(jnp.where(straddles, cuts[None, :, None] - starts[:, None, :], 0), axis=2, dtype=jnp.int32)
    ahead = jnp.sum(jnp.where(straddles, ends[:, None, :] - cuts[None, :, None], 0), axis=2, dtype=jnp.int32)
    excess = jnp.zeros_like(cuts)
    moves = []
    for pack in range(packs):
        more, less = excess + ahead[pack], excess - behind[pack]
        forward = jnp.abs(more) <= jnp.abs(less)
        excess = jnp.where(forward, more, less)
        moves.append(jnp.where(forward, ahead[pack], -behind[pack]))
    borders = jnp.concatenate(
        [
            jnp.zeros((packs, 1), jnp.int32),
            cuts[None, :] + jnp.stack(moves),
            jnp.full((packs, 1), PACK_LEN, jnp.int32),
        ],
        axis=1,
    )
    first = lax.dynamic_index_in_dim(borders, seq_place, 1, keepdims=False)
    held = lax.dynamic_index_in_dim(borders, seq_place + 1, 1, keepdims=False) - first
    pack_range = jnp.arange(packs, dtype=jnp.int32)
    before = jnp.sum(jnp.where(pack_range[None, :] < pack_range[:, None], held[None, :], 0), axis=1, dtype=jnp.int32)
    row = jnp.arange(packs * shard_len + MAXLEN, dtype=jnp.int32)
    in_pack = (row[:, None] >= before[None, :]) & (row[:, None] < (before + held)[None, :])
    valid = jnp.any(in_pack, axis=1)

    def of_pack(values):
        return jnp.sum(jnp.where(in_pack, values, 0), axis=1, dtype=jnp.int32)

    pack_of = of_pack(pack_range[None, :])
    place = of_pack(row[:, None] - before[None, :] + first[None, :])
    window = shard_len + 2 * MAXLEN
    source = jnp.where(valid, pack_of * window + place - (seq_place * shard_len - MAXLEN), -1)
    row_ends = jnp.sum(jnp.where(in_pack[:, :, None], ends[None], 0), axis=1, dtype=jnp.int32)
    row_starts = jnp.sum(jnp.where(in_pack[:, :, None], starts[None], 0), axis=1, dtype=jnp.int32)
    image_of = jnp.sum((place[:, None] >= row_ends).astype(jnp.int32), axis=1, dtype=jnp.int32)
    is_first = jnp.any(place[:, None] == row_starts, axis=1)
    keep_rows = mm("rp,pj->rj", in_pack.astype(LOW), (keep_mask > 0).astype(LOW))
    spot = jnp.arange(PACK_LEN, dtype=jnp.int32)
    kept = jnp.any((place[:, None] == spot[None, :]) & (keep_rows > 0.5), axis=1)
    live = valid & (kept | is_first)
    group = jnp.where(valid, pack_of * images + image_of, -1)

    spots = jnp.arange(PACK_LEN, dtype=jnp.int32)[None, None, :]
    inside = (spots >= starts[:, :, None]) & (spots < ends[:, :, None])
    counted = inside & ((keep_mask > 0)[:, None, :] | (spots == starts[:, :, None]))
    counts = jnp.sum(counted.astype(F32), axis=2)
    return source, group, live, counts.reshape(-1)


def body(
    patches,
    lengths,
    keep_mask,
    labels,
    step_count,
    embed_weight,
    embed_first,
    embed_second,
    qkv_weight,
    qkv_moment,
    output_weight,
    output_moment,
    up_weight,
    up_moment,
    down_weight,
    down_moment,
    small_params,
    small_first,
    small_second,
    head_weight,
    head_first,
    head_second,
    head_bias,
    bias_first,
    bias_second,
):
    packs, shard_len, patch_in = patches.shape
    images = lengths.shape[1]
    width = qkv_weight.shape[0]
    seq_count, seq_place = lax.axis_size("seq"), lax.axis_index("seq")
    pack_count, pack_place = lax.axis_size("pack"), lax.axis_index("pack")
    small_rows = small_params.shape[0]

    embed_pack = jnp.concatenate(
        [embed_weight.T, jnp.pad(small_params.T, ((0, 0), (0, BLOCK - small_rows)))], axis=1
    ).astype(LOW)
    embed_pack = gather_rows(embed_pack, 0)
    embed_full, small_full = embed_pack[:, :patch_in], embed_pack[:, patch_in : patch_in + small_rows]
    gain_bias = small_full.astype(F32).T
    qkv_full = gather_rows(qkv_weight.T.astype(LOW), 1)
    output_full = gather_rows(output_weight.T.astype(LOW), 0)
    up_shard, down_shard, _ = lax.optimization_barrier(
        (up_weight.T.astype(LOW), down_weight.T.astype(LOW), qkv_full)
    )
    up_full = gather_rows(up_shard, 0)
    down_full = gather_rows(down_shard, 1)

    ends = seq_count - 1
    from_left = lax.ppermute(patches[:, shard_len - MAXLEN :], "seq", [(i, i + 1) for i in range(ends)])
    from_right = lax.ppermute(patches[:, :MAXLEN], "seq", [(i + 1, i) for i in range(ends)])
    window = jnp.concatenate([from_left, patches, from_right], axis=1).reshape(-1, patch_in)
    source, group, live, counts = deal_rows(lengths, keep_mask, shard_len)
    chosen = (source[:, None] == jnp.arange(window.shape[0], dtype=jnp.int32)[None, :]).astype(LOW)
    tokens = mm("rw,wi->ri", chosen, window).astype(LOW)
    rows = tokens.shape[0]
    query_id = group.reshape(rows // BLOCK, 1, BLOCK)
    key_id = jnp.pad(jnp.where(live, group, -2), (BLOCK, BLOCK), constant_values=-2)[:, None]
    group_count = packs * images
    member = (
        (group[None, :] == jnp.arange(group_count, dtype=jnp.int32)[:, None]) & live[None, :]
    ).astype(F32)

    head_parts = relative(head_weight.astype(LOW), "seq")
    bias_full = jnp.concatenate(absolute(relative(head_bias.astype(LOW), "seq"), seq_place), axis=0)

    embedded = mm("ri,di->rd", tokens, embed_full) + gain_bias[6]
    normed_one = layer_norm(embedded, gain_bias[0], gain_bias[1]).astype(LOW)
    qkv_bias = jnp.concatenate([gain_bias[7], jnp.zeros_like(gain_bias[7]), gain_bias[8]])
    qkv_rows = (mm("rd,ed->re", normed_one, qkv_full) + qkv_bias).astype(LOW)
    attn_low, log_total = attend(qkv_rows, query_id, key_id)
    after_attn = embedded + mm("re,de->rd", attn_low, output_full) + gain_bias[9]
    normed_two = layer_norm(after_attn, gain_bias[2], gain_bias[3]).astype(LOW)
    up_rows = mm("rd,fd->rf", normed_two, up_full) + gain_bias[11:15].reshape(-1)
    active = gelu(up_rows).astype(LOW)
    after_mlp = after_attn + mm("rf,fd->rd", active, down_full) + gain_bias[10]
    final_rows = layer_norm(after_mlp, gain_bias[4], gain_bias[5])
    pool_sums = jnp.dot(member, final_rows, precision=HIGHEST_PREC, preferred_element_type=F32)
    pooled_mine = (pool_sums / counts[:, None]).astype(LOW)

    img_share = group_count // seq_count
    split = pooled_mine.reshape(seq_count, img_share, width)
    pooled_low = tree_sum(
        [pick(split, seq_place).astype(F32)]
        + [swap(pick(split, seq_place ^ k), "seq", k).astype(F32) for k in range(1, seq_count)]
    ).astype(LOW)
    pooled_rows = jnp.concatenate(relative(pooled_low, "pack"), axis=0)
    depth = head_weight.shape[0]
    head_full = jnp.concatenate(absolute(head_parts, seq_place), axis=0)
    label_cols = head_full.shape[1]
    logits = mm("nd,dc->nc", pooled_rows, head_full) + bias_full.astype(F32)
    label_rows = jnp.take(
        pick(labels.reshape(pack_count, seq_count, img_share), seq_place, 1),
        jnp.arange(pack_count, dtype=jnp.int32) ^ pack_place,
        axis=0,
    ).reshape(-1)
    class_ids = pack_place * label_cols + jnp.arange(label_cols, dtype=jnp.int32)
    valid = (class_ids < LABELS).astype(F32)
    target = (label_rows[:, None] == class_ids[None, :]).astype(F32)
    image_total = labels.shape[0] * labels.shape[1]
    loss_part = jnp.sum(valid[None, :] * (jax.nn.softplus(logits) - target * logits)) / image_total
    grad_logits = (valid[None, :] * (jax.nn.sigmoid(logits) - target) / image_total).astype(LOW)
    pooled_part = mm("nc,dc->nd", grad_logits, head_full).reshape(pack_count, img_share, width)
    pooled_grad = tree_sum(
        [pooled_part[0]] + [swap(pooled_part[k], "pack", k) for k in range(1, pack_count)]
    )
    pooled_grad = jnp.concatenate(absolute(relative(pooled_grad, "seq"), seq_place), axis=0)
    pooled_grad = pooled_grad / counts[:, None]

    all_pooled = jnp.concatenate(
        [pick(part.reshape(-1, seq_count, depth), seq_place, 1) for part in relative(pooled_rows, "seq")], axis=0
    )
    all_logits = jnp.concatenate(relative(grad_logits, "seq"), axis=0)
    head_grad = mm("nd,nc->dc", all_pooled, all_logits)
    bias_grad = pick(column_sum(all_logits).reshape(seq_count, -1), seq_place)

    grad_final = lax.dot_general(
        member, pooled_grad, (TN, ((), ())), precision=HIGHEST_PREC, preferred_element_type=F32
    )
    grad_mlp, grad_gain_f, grad_bias_f = norm_back(after_mlp, gain_bias[4], gain_bias[5], grad_final)
    grad_mlp_low = grad_mlp.astype(LOW)
    down_share = scatter_rows(mm("rf,rd->fd", active, grad_mlp_low), 0)
    grad_upper = (mm("rd,fd->rf", grad_mlp_low, down_full) * gelu_slope(up_rows)).astype(LOW)
    up_share = scatter_rows(mm("rf,rd->fd", grad_upper, normed_two), 1)
    grad_two, grad_gain_2, grad_bias_2 = norm_back(
        after_attn, gain_bias[2], gain_bias[3], mm("rf,fd->rd", grad_upper, up_full)
    )
    grad_attn = grad_mlp + grad_two
    grad_attn_low = grad_attn.astype(LOW)
    output_share = scatter_rows(mm("rd,re->de", grad_attn_low, attn_low), 0)
    grad_mixed = mm("rd,de->re", grad_attn_low, output_full).astype(LOW)
    grad_qkv = attend_back(qkv_rows, grad_mixed, log_total, query_id, key_id)
    qkv_share = scatter_rows(mm("re,rd->ed", grad_qkv, normed_one), 1)
    qkv_bias_grad = column_sum(grad_qkv)
    grad_one, grad_gain_1, grad_bias_1 = norm_back(
        embedded, gain_bias[0], gain_bias[1], mm("re,ed->rd", grad_qkv, qkv_full)
    )
    grad_embed_rows = (grad_attn + grad_one).astype(LOW)
    small_grad = jnp.concatenate(
        [
            jnp.stack(
                [
                    grad_gain_1,
                    grad_bias_1,
                    grad_gain_2,
                    grad_bias_2,
                    grad_gain_f,
                    grad_bias_f,
                    column_sum(grad_embed_rows),
                    qkv_bias_grad[:width],
                    qkv_bias_grad[2 * width :],
                    column_sum(grad_attn_low),
                    column_sum(grad_mlp_low),
                ]
            ),
            column_sum(grad_upper).reshape(-1, width),
        ],
        axis=0,
    )
    embed_grad = jnp.concatenate(
        [
            mm("rd,ri->di", grad_embed_rows, tokens),
            jnp.pad(small_grad, ((0, BLOCK - small_rows), (0, 0))).T,
        ],
        axis=1,
    )
    embed_pack_share = scatter_rows(embed_grad, 0)
    embed_share = embed_pack_share[:, :patch_in].T
    small_share = embed_pack_share[:, patch_in : patch_in + small_rows].T

    shares = (qkv_share, output_share, up_share, down_share, embed_share, small_share, head_grad, bias_grad)
    square_sum = sum((jnp.sum(piece * piece) for piece in shares))
    sums = jnp.broadcast_to(jnp.stack([loss_part, square_sum])[:, None], (2, BLOCK))
    sums = all_sum(all_sum(sums, "pack"), "seq")
    loss_value, square_total = sums[0, 0], sums[1, 0]
    grad_norm = jnp.sqrt(square_total)
    factor = jnp.minimum(1.0, CLIP_NORM / (grad_norm + 1e-06))
    moments = (
        MUON_MU * qkv_moment.T + factor * qkv_share,
        MUON_MU * output_moment.T + factor * output_share,
        MUON_MU * up_moment.T + factor * up_share,
        MUON_MU * down_moment.T + factor * down_share,
    )
    iterates = [iterate.T for iterate in muon(moments)]
    new_qkv = muon_update(qkv_weight, iterates[0])
    new_output = muon_update(output_weight, iterates[1])
    new_up = muon_update(up_weight, iterates[2])
    new_down = muon_update(down_weight, iterates[3])
    moments = [moment.T for moment in moments]
    count_float = step_count[0].astype(F32)
    new_embed, new_embed_first, new_embed_second = adam_update(
        embed_weight, embed_first, embed_second, embed_share, factor, count_float
    )
    new_small, new_small_first, new_small_second = adam_update(
        small_params, small_first, small_second, small_share, factor, count_float
    )
    new_head, new_head_first, new_head_second = adam_update(
        head_weight, head_first, head_second, head_grad, factor, count_float
    )
    new_bias, new_bias_first, new_bias_second = adam_update(
        head_bias, bias_first, bias_second, bias_grad, factor, count_float
    )
    return (
        loss_value,
        grad_norm,
        new_embed,
        new_embed_first,
        new_embed_second,
        new_qkv,
        moments[0],
        new_output,
        moments[1],
        new_up,
        moments[2],
        new_down,
        moments[3],
        new_small,
        new_small_first,
        new_small_second,
        new_head,
        new_head_first,
        new_head_second,
        new_bias,
        new_bias_first,
        new_bias_second,
    )


def solution(mesh):
    both = P(None, ("pack", "seq"))
    head = P("seq", "pack")
    line = P(("pack", "seq"))
    return jax.shard_map(
        body,
        mesh=mesh,
        in_specs=(P("pack", "seq", None), P("pack", None), P("pack", None), P(), P())
        + (both,) * 14
        + (head,) * 3
        + (line,) * 3,
        out_specs=(P(), P()) + (both,) * 14 + (head,) * 3 + (line,) * 3,
        check_vma=False,
    )
```

time: 2290 us -> 1090 us (0.48)
  waiting for transfers between devices: 1370 us -> 413 us
  blocking collectives: 208 us -> 0 us
  matrix products: 344 us -> 201 us
  starting transfers between devices: 18.7 us -> 135 us
  Pallas kernels: 0 us -> 81.2 us
  other arithmetic: 186 us -> 140 us
    reduce_scatter x8 -> x0, waiting for transfers between devices: 571 us -> none  [the longest x1 148 us: body(): lax.psum_scatter(jnp.einsum('nd,nc->dc', pooled_rows, grad_logits, prefer...]
    psum x2 -> x0, waiting for transfers between devices: 370 us -> none  [body(): lax.psum((gram_of(iterates[0]), gram_of(iterates[1]), gram_of(iterates[2]...]
    dot_general x85 -> x28, matrix products: 344 us -> 201 us  [the longest x19 175 us: mm(): return jnp.einsum(spec, left, right, preferred_element_type=F32)]
    ppermute x4 -> x116, starting transfers between devices: 17.4 us -> 135 us  [the longest x114 128 us: swap(): lax.ppermute(value, axis, [(i, i ^ bit) for i in range(lax.axis_size(axis...]
    all_gather x6 -> x0, waiting for transfers between devices: 111 us -> none  [the longest x1 72.8 us: body(): lax.all_gather(head_weight.astype(jnp.bfloat16), 'seq', axis=0, tiled=True)]
    all_gather x3 -> x0, blocking collectives: 94.4 us -> none  [the longest x1 70.8 us: body(): lax.all_gather(small_params.astype(jnp.bfloat16), ('pack', 'seq'), axis=1...]
    ppermute x4 -> x116, waiting for transfers between devices: 318 us -> 413 us  [the longest x114 413 us: swap(): lax.ppermute(value, axis, [(i, i ^ bit) for i in range(lax.axis_size(axis...]
    pallas_call x0 -> x2, Pallas kernels: none -> 81.2 us  [the longest x1 60.1 us: attend_back(): pl.pallas_call(lambda *refs: attend_back_kernel(width, blocks, *refs), gr...]
  transfers between devices with their start and end apart: 20 -> 116, of which waited for: 14 -> 41; matrix products, arithmetic and copies ran while one was open for 14% -> 36% of each run, Pallas kernels for 0% -> 7%
where the time goes in v1:
time: 1090 us
  waiting for transfers between devices  413 us (38%)
  matrix products  201 us (18%)
  other arithmetic  140 us (13%)
  starting transfers between devices  135 us (12%)
  local copies, waits for them, and re-layouts  107 us (10%)
  Pallas kernels  81.2 us (7%)
  between operations  12.3 us (1%)
    ppermute x114, waiting for transfers between devices, swap(): lax.ppermute(value, axis, [(i, i ^ bit) for i in range(lax.axis_size(axis...  413 us
    dot_general x19, matrix products, mm(): return jnp.einsum(spec, left, right, preferred_element_type=F32)  175 us
    ppermute x114, starting transfers between devices, swap(): lax.ppermute(value, axis, [(i, i ^ bit) for i in range(lax.axis_size(axis...  128 us
    pallas_call x1, Pallas kernels, attend_back(): pl.pallas_call(lambda *refs: attend_back_kernel(width, blocks, *refs), gr...  60.1 us
    select_n x15, other arithmetic, gather_rows(): jnp.where(pack_place & bit == 0, jnp.concatenate([whole, other], axis=dim...  32.8 us
  transfers between devices with their start and end apart: 116, of which 41 were waited for; matrix products, arithmetic and copies ran while one was open for 36% of the time, Pallas kernels for 7%

profile of v1, /device:TPU:0, one launch (start us, length us, event | category | flops | bytes accessed | tf_op | source)
XLA Modules:
  0.0 1089.0 jit_solution(8599529430133012598)
XLA Ops:
  1.6 5.1 collective-permute-start.8
  32.3 5.7 collective-permute-start
  47.5 12.4 %collective-permute-done.18 = bf16[2,1,1,96,768]{4,3,2,1,0:T(8,128)(2,1)} collective-permute-done((bf16[2,1,1,96,768]{4,3,2,1,0:T(8,128)(2,1)}, bf16[2,1,1,96,768]{4,3,2,1,0:T(8,128)(2,1)}, u32[]{:S(2)}, u32[]{:S(2)}) %collective-permute-start.18) | collective-permute-done | bytes 294944 | tf_op jit(solution)/shard_map/ppermute | solution.py:37
  78.1 7.9 collective-permute-done.12
  87.8 10.3 fusion.15
  98.6 6.3 add_reduce_fusion
  104.9 4.0 maximum_select_fusion.2
  109.8 3.5 collective-permute-start.22
  113.3 4.2 collective-permute-done.20
  117.5 6.0 collective-permute-done.21
  133.2 5.5 collective-permute-done.23
  140.5 11.9 %add_convert_fusion.refs_0_ = bf16[1664,2304]{1,0:T(8,128)(2,1)} fusion(bf16[2304,768]{1,0:T(8,128)(2,1)} %bitcast.394, f32[2304]{0:T(1024)S(1)} %pad_maximum_fusion.16, f32[1664,768]{0,1:T(8,128)S(1)} %copy-done, f32[768]{0:T(1024)S(1)} %get-tuple-element.154, f32[768]{0:T(1024)S(1)} %get-tuple-element.155, f32[1664]{0:T(1024)S(1)} %fusion.126, ...), kind=kOutput, calls=%fused_computation.14 | convolution fusion | flops 5904138240 | bytes 16350208 | tf_op jit(solution)/shard_map/rd,ed->re/dot_general | solution.py:310
  156.1 11.8 %collective-permute-done.24 = bf16[2,1,1,384,768]{4,3,2,1,0:T(8,128)(2,1)S(1)} collective-permute-done((bf16[2,1,1,384,768]{4,3,2,1,0:T(8,128)(2,1)S(1)}, bf16[2,1,1,384,768]{4,3,2,1,0:T(8,128)(2,1)S(1)}, u32[]{:S(2)}, u32[]{:S(2)}) %collective-permute-start.24) | collective-permute-done | bytes 1179680 | tf_op jit(solution)/shard_map/ppermute | solution.py:37
  169.7 21.1 %shard_map.408 = (bf16[1664,768]{1,0:T(8,128)(2,1)}, f32[13,12,128]{2,1,0:T(8,128)}) custom-call(bf16[1664,2304]{1,0:T(8,128)(2,1)} %add_convert_fusion.refs_0_, s32[13,1,128]{2,1,0:T(1,128)} %select_n.1242.refs_1_.refs_3_, s32[1920,1]{1,0:T(8,128)} %broadcast_in_dim.217.refs_2_.refs_4_), custom_call_target="tpu_custom_call" | custom-call | flops 5888802816 | bytes 10223616 | tf_op jit(solution)/shard_map/pallas_call | solution.py:238
  192.6 4.1 fusion.178
  199.2 20.3 %collective-permute-done.30 = bf16[1,2,1,384,768]{4,3,2,1,0:T(8,128)(2,1)S(1)} collective-permute-done((bf16[1,2,1,384,768]{4,3,2,1,0:T(8,128)(2,1)S(1)}, bf16[1,2,1,384,768]{4,3,2,1,0:T(8,128)(2,1)S(1)}, u32[]{:S(2)}, u32[]{:S(2)}) %collective-permute-start.30) | collective-permute-done | bytes 1179680 | tf_op jit(solution)/shard_map/ppermute | solution.py:37
  221.7 7.0 maximum_select_fusion
  228.8 20.1 %multiply_convert_fusion = (bf16[1664,3072]{1,0:T(8,128)(2,1)}, f32[1664,3072]{1,0:T(8,128)}) fusion(f32[3072]{0:T(1024)S(1)} %add.733, bf16[3072,768]{1,0:T(8,128)(2,1)} %bitcast.385, f32[1664,768]{0,1:T(8,128)S(1)} %bitcast.360, f32[768]{0:T(1024)S(1)} %get-tuple-element.149, f32[768]{0:T(1024)S(1)} %get-tuple-element.150, f32[1664]{0:T(1024)S(1)} %fusion.127, ...), kind=kOutput, calls=%fused_computation.9 | convolution fusion | flops 7888797696 | bytes 40532992 | tf_op jit(solution)/shard_map/rd,fd->rf/dot_general | solution.py:310
  251.6 6.9 maximum_select_fusion.1
  258.5 15.5 %fusion.179 = (f32[1664]{0:T(1024)S(1)}, f32[1664,768]{0,1:T(8,128)}) fusion(f32[768]{0:T(1024)S(1)} %get-tuple-element.148, f32[1664,768]{0,1:T(8,128)S(1)} %bitcast.360, bf16[1664,3072]{1,0:T(8,128)(2,1)} %get-tuple-element.315, bf16[3072,768]{1,0:T(8,128)(2,1)} %bitcast.389), kind=kOutput, calls=%fused_computation.490 | convolution fusion | flops 7855569408 | bytes 25175552 | tf_op jit(solution)/shard_map/rf,fd->rd/dot_general | solution.py:310
  278.0 3.4 fusion.53
  310.1 5.8 fusion.29
  335.3 44.8 %collective-permute-done.55 = f32[24,768]{1,0:T(8,128)S(1)} collective-permute-done((f32[24,768]{1,0:T(8,128)S(1)}, f32[24,768]{1,0:T(8,128)S(1)}, u32[]{:S(2)}, u32[]{:S(2)}) %collective-permute-start.55) | collective-permute-done | bytes 73760 | tf_op jit(solution)/shard_map/ppermute | solution.py:37
  381.5 52.5 %collective-permute-done.56 = f32[24,768]{1,0:T(8,128)S(1)} collective-permute-done((f32[24,768]{1,0:T(8,128)S(1)}, f32[24,768]{1,0:T(8,128)S(1)}, u32[]{:S(2)}, u32[]{:S(2)}) %collective-permute-start.56) | collective-permute-done | bytes 73760 | tf_op jit(solution)/shard_map/ppermute | solution.py:37
  435.1 5.1 fusion.182
  440.2 6.1 copy.231
  446.2 6.1 multiply_reduce_fusion
  456.5 22.3 %convert_reduce_fusion = (f32[3072]{0:T(1024)}, bf16[1664,3072]{1,0:T(8,128)(2,1)}) fusion(f32[1664,3072]{1,0:T(8,128)} %get-tuple-element.316, f32[3072]{0:T(1024)S(1)} %copy-done.75, bf16[1664,768]{0,1:T(8,128)(2,1)S(1)} %get-tuple-element.176, bf16[3072,768]{1,0:T(8,128)(2,1)S(1)} %bitcast.392), kind=kOutput, calls=%fused_computation.8 | convolution fusion | flops 7918187520 | bytes 37969920 | tf_op jit(solution)/shard_map/rd,fd->rf/dot_general | solution.py:310
  478.9 12.6 %fusion.181 = (f32[768]{0:T(1024)S(1)}, f32[1664,768]{1,0:T(8,128)}) fusion(bf16[1664,3072]{1,0:T(8,128)(2,1)} %get-tuple-element.326, bf16[3072,768]{1,0:T(8,128)(2,1)S(1)} %bitcast.388), kind=kOutput, calls=%fused_computation.492 | convolution fusion | flops 7853014016 | bytes 20057088 | tf_op jit(solution)/shard_map/rf,fd->rd/dot_general | solution.py:310
  491.4 6.1 copy.232
  497.5 5.5 multiply_reduce_fusion.1
  507.9 3.7 convolution_convert_fusion.refs_1_
  511.6 3.7 fusion.183
  515.4 14.7 %fusion.155 = f32[3072,768]{1,0:T(8,128)} fusion(bf16[1664,3072]{1,0:T(8,128)(2,1)} %get-tuple-element.326, f32[1664,768]{0,1:T(8,128)S(1)} %bitcast.364, f32[768]{0:T(1024)S(1)} %copy-done.86, f32[768]{0:T(1024)S(1)} %get-tuple-element.150, f32[1664]{0:T(1024)S(1)} %fusion.127, f32[1664]{0:T(1024)S(1)} %broadcast_multiply_fusion.1), kind=kOutput, calls=%fused_computation.479 | convolution fusion | flops 7858126848 | bytes 24792064 | tf_op jit(solution)/shard_map/rf,rd->fd/dot_general | solution.py:310
  530.1 11.4 %fusion.184 = f32[3072,768]{1,0:T(8,128)} fusion(bf16[1664,3072]{1,0:T(8,128)(2,1)S(1)} %bitcast.418, bf16[1664,768]{0,1:T(8,128)(2,1)S(1)} %get-tuple-element.176), kind=kOutput, calls=%fused_computation.495 | convolution fusion | flops 7851737088 | bytes 22216704 | tf_op jit(solution)/shard_map/rf,rd->fd/dot_general | solution.py:310
  541.5 60.1 %shard_map.409 = bf16[1664,2304]{1,0:T(8,128)(2,1)} custom-call(bf16[1664,2304]{1,0:T(8,128)(2,1)} %add_convert_fusion.refs_0_, bf16[1664,768]{1,0:T(8,128)(2,1)} %convolution_convert_fusion.refs_1_, f32[13,12,128]{2,1,0:T(8,128)} %get-tuple-element.29.refs_2_, s32[13,1,128]{2,1,0:T(1,128)} %select_n.1242.refs_1_.refs_3_, ...), custom_call_target="tpu_custom_call" | custom-call | flops 14722007040 | bytes 20447232 | tf_op jit(solution)/shard_map/pallas_call | solution.py:265
  601.7 11.6 %fusion.157 = f32[2304,768]{1,0:T(8,128)} fusion(bf16[1664,2304]{1,0:T(8,128)(2,1)} %shard_map.409, f32[1664,768]{0,1:T(8,128)S(1)} %bitcast.352, f32[768]{0:T(1024)S(1)} %copy-done.84, f32[768]{0:T(1024)S(1)} %copy-done.64, f32[1664]{0:T(1024)S(1)} %copy-done.58, f32[1664]{0:T(1024)S(1)} %copy-done.50, f32[768]{0:T(1024)S(1)} %copy-done.53), kind=kOutput, calls=%fused_computation.481 | convolution fusion | flops 5896470528 | bytes 19879936 | tf_op jit(solution)/shard_map/re,rd->ed/dot_general | solution.py:310
  613.3 8.4 fusion.180
  621.7 6.9 constant_dynamic-slice_fusion.6
  631.2 6.1 copy.238
  637.3 5.0 multiply_reduce_fusion.3
  646.9 6.4 convert_reduce_fusion.5
  654.4 3.8 constant_dynamic-slice_fusion.8
  673.0 5.0 dynamic-slice_bitcast_fusion
  700.9 6.5 collective-permute-done.91
  708.6 5.5 multiply_reduce_fusion.9
  714.2 7.9 collective-permute-done.65
  724.8 4.9 collective-permute-done.66
  763.2 67.0 %collective-permute-done.84 = f32[4,24,896]{2,1,0:T(8,128)S(1)} collective-permute-done((f32[4,24,896]{2,1,0:T(8,128)}, f32[4,24,896]{2,1,0:T(8,128)S(1)}, u32[]{:S(2)}, u32[]{:S(2)}) %collective-permute-start.84) | collective-permute-done | bytes 344096 | tf_op jit(solution)/shard_map/ppermute | solution.py:37
  845.6 13.6 %collective-permute-done.60 = f32[4,72,768]{2,1,0:T(8,128)S(1)} collective-permute-done((f32[4,72,768]{2,1,0:T(8,128)S(1)}, f32[4,72,768]{2,1,0:T(8,128)S(1)}, u32[]{:S(2)}, u32[]{:S(2)}) %collective-permute-start.60) | collective-permute-done | bytes 884768 | tf_op jit(solution)/shard_map/ppermute | solution.py:37
  862.9 16.4 %collective-permute-done.72 = f32[4,96,768]{2,1,0:T(8,128)S(1)} collective-permute-done((f32[4,96,768]{2,1,0:T(8,128)S(1)}, f32[4,96,768]{2,1,0:T(8,128)S(1)}, u32[]{:S(2)}, u32[]{:S(2)}) %collective-permute-start.72) | collective-permute-done | bytes 1179680 | tf_op jit(solution)/shard_map/ppermute | solution.py:37
  887.6 18.1 %collective-permute-done.74 = f32[96,768]{1,0:T(8,128)S(1)} collective-permute-done((f32[96,768]{1,0:T(8,128)S(1)}, f32[96,768]{1,0:T(8,128)S(1)}, u32[]{:S(2)}, u32[]{:S(2)}) %collective-permute-start.74) | collective-permute-done | bytes 294944 | tf_op jit(solution)/shard_map/ppermute | solution.py:37
  910.2 11.9 %collective-permute-done.80 = f32[96,768]{1,0:T(8,128)} collective-permute-done((f32[96,768]{1,0:T(8,128)}, f32[96,768]{1,0:T(8,128)}, u32[]{:S(2)}, u32[]{:S(2)}) %collective-permute-start.80) | collective-permute-done | bytes 294944 | tf_op jit(solution)/shard_map/ppermute | solution.py:37
  935.9 7.5 collective-permute-start.102
  945.1 3.7 collective-permute-done.103
  957.3 7.5 collective-permute-done.106
  964.8 13.9 %collective-permute-done.105 = f32[96,768]{1,0:T(8,128)S(1)} collective-permute-done((f32[96,768]{1,0:T(8,128)S(1)}, f32[96,768]{1,0:T(8,128)S(1)}, u32[]{:S(2)}, u32[]{:S(2)}) %collective-permute-start.105) | collective-permute-done | bytes 294944 | tf_op jit(solution)/shard_map/ppermute | solution.py:37
  985.5 14.2 %collective-permute-done.108 = f32[2,96,768]{2,1,0:T(8,128)S(1)} collective-permute-done((f32[2,96,768]{2,1,0:T(8,128)S(1)}, f32[2,96,768]{2,1,0:T(8,128)S(1)}, u32[]{:S(2)}, u32[]{:S(2)}) %collective-permute-start.108) | collective-permute-done | bytes 589856 | tf_op jit(solution)/shard_map/ppermute | solution.py:37
  1000.9 7.3 collective-permute-done.109
  1009.2 6.3 collective-permute-done.110
  1017.9 10.6 collective-permute-done.111
  1030.0 6.0 multiply_subtract_fusion
  1047.7 3.5 fusion.20
  1069.9 15.4 %collective-permute-done.114 = f32[96,768]{1,0:T(8,128)S(1)} collective-permute-done((f32[96,768]{1,0:T(8,128)}, f32[96,768]{1,0:T(8,128)S(1)}, u32[]{:S(2)}, u32[]{:S(2)}) %collective-permute-start.114) | collective-permute-done | bytes 294944 | tf_op jit(solution)/shard_map/ppermute | solution.py:37
  (724 shorter events, 322.5 us)
Async XLA Ops:
  1.6 36.5 %collective-permute-start.8 = (bf16[72,768]{1,0:T(8,128)(2,1)S(1)}, bf16[72,768]{1,0:T(8,128)(2,1)S(1)}, u32[]{:S(2)}, u32[]{:S(2)}) collective-permute-start(bf16[72,768]{1,0:T(8,128)(2,1)S(1)} %convert_bitcast_fusion.2), channel_id=1, source_target_pairs={{0,3},{1,2},{2,1},{3,0},{4,7},{5,6},{6,5},{7,4},{8,11},{9,10},{10,... | collective-permute-start | bytes 331784 | tf_op jit(solution)/shard_map/ppermute | solution.py:37
  6.7 33.0 %collective-permute-start.9 = (bf16[72,768]{1,0:T(8,128)(2,1)S(1)}, bf16[72,768]{1,0:T(8,128)(2,1)S(1)}, u32[]{:S(2)}, u32[]{:S(2)}) collective-permute-start(bf16[72,768]{1,0:T(8,128)(2,1)S(1)} %convert_bitcast_fusion.2), channel_id=1, source_target_pairs={{0,2},{1,3},{2,0},{3,1},{4,6},{5,7},{6,4},{7,5},{8,10},{9,11},{10,... | collective-permute-start | bytes 331784 | tf_op jit(solution)/shard_map/ppermute | solution.py:37
  7.6 16.0 %collective-permute-start.14 = (bf16[24,768]{1,0:T(8,128)(2,1)S(1)}, bf16[24,768]{1,0:T(8,128)(2,1)S(1)}, u32[]{:S(2)}, u32[]{:S(2)}) collective-permute-start(bf16[24,768]{1,0:T(8,128)(2,1)S(1)} %convert_bitcast_fusion.4), channel_id=1, source_target_pairs={{0,3},{1,2},{2,1},{3,0},{4,7},{5,6},{6,5},{7,4},{8,11},{9,10},{10,... | collective-permute-start | bytes 110600 | tf_op jit(solution)/shard_map/ppermute | solution.py:37
  9.5 16.1 %collective-permute-start.15 = (bf16[24,768]{1,0:T(8,128)(2,1)S(1)}, bf16[24,768]{1,0:T(8,128)(2,1)S(1)}, u32[]{:S(2)}, u32[]{:S(2)}) collective-permute-start(bf16[24,768]{1,0:T(8,128)(2,1)S(1)} %convert_bitcast_fusion.4), channel_id=1, source_target_pairs={{0,2},{1,3},{2,0},{3,1},{4,6},{5,7},{6,4},{7,5},{8,10},{9,11},{10,... | collective-permute-start | bytes 110600 | tf_op jit(solution)/shard_map/ppermute | solution.py:37
  10.6 15.2 %collective-permute-start.16 = (bf16[24,768]{1,0:T(8,128)(2,1)S(1)}, bf16[24,768]{1,0:T(8,128)(2,1)S(1)}, u32[]{:S(2)}, u32[]{:S(2)}) collective-permute-start(bf16[24,768]{1,0:T(8,128)(2,1)S(1)} %convert_bitcast_fusion.4), channel_id=1, source_target_pairs={{0,1},{1,0},{2,3},{3,2},{4,5},{5,4},{6,7},{7,6},{8,9},{9,8},{10,11... | collective-permute-start | bytes 110600 | tf_op jit(solution)/shard_map/ppermute | solution.py:37
  31.0 45.3 %collective-permute-start.1 = (bf16[6,128,768]{2,1,0:T(8,128)(2,1)}, bf16[6,128,768]{2,1,0:T(8,128)(2,1)}, u32[]{:S(2)}, u32[]{:S(2)}) collective-permute-start(bf16[6,128,768]{2,1,0:T(8,128)(2,1)} %get-tuple-element.217), channel_id=1, source_target_pairs={{1,0},{2,1},{3,2},{5,4},{6,5},{7,6},{9,8},{10,9},{11,10},{13,12},{... | collective-permute-start | bytes 3538952 | tf_op jit(solution)/shard_map/ppermute | solution.py:480
  32.3 44.0 %collective-permute-start = (bf16[6,128,768]{2,1,0:T(8,128)(2,1)}, bf16[6,128,768]{2,1,0:T(8,128)(2,1)}, u32[]{:S(2)}, u32[]{:S(2)}) collective-permute-start(bf16[6,128,768]{2,1,0:T(8,128)(2,1)} %get-tuple-element.216), channel_id=1, source_target_pairs={{0,1},{1,2},{2,3},{4,5},{5,6},{6,7},{8,9},{9,10},{10,11},{12,13},{... | collective-permute-start | bytes 3538952 | tf_op jit(solution)/shard_map/ppermute | solution.py:479
  41.1 20.0 %collective-permute-start.11 = (bf16[1,1,1,288,768]{4,3,2,1,0:T(8,128)(2,1)}, bf16[1,1,1,288,768]{4,3,2,1,0:T(8,128)(2,1)}, u32[]{:S(2)}, u32[]{:S(2)}) collective-permute-start(bf16[1,1,1,288,768]{4,3,2,1,0:T(8,128)(2,1)} %get-tuple-element.265), channel_id=1, source_target_pairs={{0,8},{4,12},{8,0},{12,4},{16,24},{20,28},{24,16},{28,20},{1,9},{5... | collective-permute-start | bytes 1327112 | tf_op jit(solution)/shard_map/ppermute | solution.py:37
  44.1 15.8 %collective-permute-start.18 = (bf16[2,1,1,96,768]{4,3,2,1,0:T(8,128)(2,1)}, bf16[2,1,1,96,768]{4,3,2,1,0:T(8,128)(2,1)}, u32[]{:S(2)}, u32[]{:S(2)}) collective-permute-start(bf16[2,1,1,96,768]{4,3,2,1,0:T(8,128)(2,1)} %maximum_select_fusion.23), channel_id=1, source_target_pairs={{0,8},{4,12},{8,0},{12,4},{16,24},{20,28},{24,16},{28,20},{1,9},{5... | collective-permute-start | bytes 884744 | tf_op jit(solution)/shard_map/ppermute | solution.py:37
  46.8 25.4 %collective-permute-start.6 = (bf16[2,1,1,96,896]{4,3,2,1,0:T(8,128)(2,1)}, bf16[2,1,1,96,896]{4,3,2,1,0:T(8,128)(2,1)}, u32[]{:S(2)}, u32[]{:S(2)}) collective-permute-start(bf16[2,1,1,96,896]{4,3,2,1,0:T(8,128)(2,1)} %maximum_select_fusion.21), channel_id=1, source_target_pairs={{0,8},{4,12},{8,0},{12,4},{16,24},{20,28},{24,16},{28,20},{1,9},{5... | collective-permute-start | bytes 1032200 | tf_op jit(solution)/shard_map/ppermute | solution.py:37
  63.6 22.4 %collective-permute-start.12 = (bf16[1,2,1,288,768]{4,3,2,1,0:T(8,128)(2,1)}, bf16[1,2,1,288,768]{4,3,2,1,0:T(8,128)(2,1)}, u32[]{:S(2)}, u32[]{:S(2)}) collective-permute-start(bf16[1,2,1,288,768]{4,3,2,1,0:T(8,128)(2,1)} %maximum_select_fusion.15), channel_id=1, source_target_pairs={{0,16},{4,20},{8,24},{12,28},{16,0},{20,4},{24,8},{28,12},{1,17},{... | collective-permute-start | bytes 2654216 | tf_op jit(solution)/shard_map/ppermute | solution.py:37
  72.2 209.9 %collective-permute-start.47 = (bf16[683]{0:T(1024)(128)(2,1)S(1)}, bf16[683]{0:T(1024)(128)(2,1)}, u32[]{:S(2)}, u32[]{:S(2)}) collective-permute-start(bf16[683]{0:T(1024)(128)(2,1)S(1)} %copy-done.92), channel_id=1, source_target_pairs={{0,1},{1,0},{2,3},{3,2},{4,5},{5,4},{6,7},{7,6},{8,9},{9,8},{10,11... | collective-permute-start | bytes 4106 | tf_op jit(solution)/shard_map/ppermute | solution.py:37
  73.5 24.7 %collective-permute-start.7 = (bf16[2,2,1,96,896]{4,3,2,1,0:T(8,128)(2,1)S(1)}, bf16[2,2,1,96,896]{4,3,2,1,0:T(8,128)(2,1)S(1)}, u32[]{:S(2)}, u32[]{:S(2)}) collective-permute-start(bf16[2,2,1,96,896]{4,3,2,1,0:T(8,128)(2,1)S(1)} %maximum_select_fusion.16), channel_id=1, source_target_pairs={{0,4},{4,0},{8,12},{12,8},{16,20},{20,16},{24,28},{28,24},{1,5},{5... | collective-permute-start | bytes 2064392 | tf_op jit(solution)/shard_map/ppermute | solution.py:37
  87.7 17.2 %collective-permute-start.13 = (bf16[2,2,1,288,768]{4,3,2,1,0:T(8,128)(2,1)S(1)}, bf16[2,2,1,288,768]{4,3,2,1,0:T(8,128)(2,1)}, u32[]{:S(2)}, u32[]{:S(2)}) collective-permute-start(bf16[2,2,1,288,768]{4,3,2,1,0:T(8,128)(2,1)S(1)} %maximum_select_fusion.6), channel_id=1, source_target_pairs={{0,4},{4,0},{8,12},{12,8},{16,20},{20,16},{24,28},{28,24},{1,5},{5... | collective-permute-start | bytes 5308424 | tf_op jit(solution)/shard_map/ppermute | solution.py:37
  123.7 15.0 %collective-permute-start.23 = (bf16[1,1,1,384,768]{4,3,2,1,0:T(8,128)(2,1)S(1)}, bf16[1,1,1,384,768]{4,3,2,1,0:T(8,128)(2,1)S(1)}, u32[]{:S(2)}, u32[]{:S(2)}) collective-permute-start(bf16[1,1,1,384,768]{4,3,2,1,0:T(8,128)(2,1)S(1)} %get-tuple-element.259), channel_id=1, source_target_pairs={{0,16},{4,20},{8,24},{12,28},{16,0},{20,4},{24,8},{28,12},{1,17},{... | collective-permute-start | bytes 1769480 | tf_op jit(solution)/shard_map/ppermute | solution.py:37
  128.8 23.6 %collective-permute-start.26 = (bf16[96,768]{1,0:T(8,128)(2,1)S(1)}, bf16[96,768]{1,0:T(8,128)(2,1)S(1)}, u32[]{:S(2)}, u32[]{:S(2)}) collective-permute-start(bf16[96,768]{1,0:T(8,128)(2,1)S(1)} %copy-done.37), channel_id=1, source_target_pairs={{0,3},{1,2},{2,1},{3,0},{4,7},{5,6},{6,5},{7,4},{8,11},{9,10},{10,... | collective-permute-start | bytes 442376 | tf_op jit(solution)/shard_map/ppermute | solution.py:37
  131.4 21.5 %collective-permute-start.27 = (bf16[96,768]{1,0:T(8,128)(2,1)S(1)}, bf16[96,768]{1,0:T(8,128)(2,1)S(1)}, u32[]{:S(2)}, u32[]{:S(2)}) collective-permute-start(bf16[96,768]{1,0:T(8,128)(2,1)S(1)} %copy-done.37), channel_id=1, source_target_pairs={{0,2},{1,3},{2,0},{3,1},{4,6},{5,7},{6,4},{7,5},{8,10},{9,11},{10,... | collective-permute-start | bytes 442376 | tf_op jit(solution)/shard_map/ppermute | solution.py:37
  131.4 23.7 %collective-permute-start.28 = (bf16[96,768]{1,0:T(8,128)(2,1)S(1)}, bf16[96,768]{1,0:T(8,128)(2,1)S(1)}, u32[]{:S(2)}, u32[]{:S(2)}) collective-permute-start(bf16[96,768]{1,0:T(8,128)(2,1)S(1)} %copy-done.37), channel_id=1, source_target_pairs={{0,1},{1,0},{2,3},{3,2},{4,5},{5,4},{6,7},{7,6},{8,9},{9,8},{10,11... | collective-permute-start | bytes 442376 | tf_op jit(solution)/shard_map/ppermute | solution.py:37
  138.9 29.0 %collective-permute-start.24 = (bf16[2,1,1,384,768]{4,3,2,1,0:T(8,128)(2,1)S(1)}, bf16[2,1,1,384,768]{4,3,2,1,0:T(8,128)(2,1)S(1)}, u32[]{:S(2)}, u32[]{:S(2)}) collective-permute-start(bf16[2,1,1,384,768]{4,3,2,1,0:T(8,128)(2,1)S(1)} %maximum_select_fusion.10), channel_id=1, source_target_pairs={{0,8},{4,12},{8,0},{12,4},{16,24},{20,28},{24,16},{28,20},{1,9},{5... | collective-permute-start | bytes 3538952 | tf_op jit(solution)/shard_map/ppermute | solution.py:37
  152.4 130.9 %collective-permute-start.46 = (bf16[683]{0:T(1024)(128)(2,1)S(1)}, bf16[683]{0:T(1024)(128)(2,1)}, u32[]{:S(2)}, u32[]{:S(2)}) collective-permute-start(bf16[683]{0:T(1024)(128)(2,1)S(1)} %copy-done.92), channel_id=1, source_target_pairs={{0,2},{1,3},{2,0},{3,1},{4,6},{5,7},{6,4},{7,5},{8,10},{9,11},{10,... | collective-permute-start | bytes 4106 | tf_op jit(solution)/shard_map/ppermute | solution.py:37
  152.9 143.5 %collective-permute-start.42 = (bf16[192,2732]{1,0:T(8,128)(2,1)}, bf16[192,2732]{1,0:T(8,128)(2,1)}, u32[]{:S(2)}, u32[]{:S(2)}) collective-permute-start(bf16[192,2732]{1,0:T(8,128)(2,1)} %convert_element_type.167), channel_id=1, source_target_pairs={{0,3},{1,2},{2,1},{3,0},{4,7},{5,6},{6,5},{7,4},{8,11},{9,10},{10,... | collective-permute-start | bytes 3147272 | tf_op jit(solution)/shard_map/ppermute | solution.py:37
  155.3 35.5 %collective-permute-start.29 = (bf16[1,1,1,384,768]{4,3,2,1,0:T(8,128)(2,1)S(1)}, bf16[1,1,1,384,768]{4,3,2,1,0:T(8,128)(2,1)S(1)}, u32[]{:S(2)}, u32[]{:S(2)}) collective-permute-start(bf16[1,1,1,384,768]{4,3,2,1,0:T(8,128)(2,1)S(1)} %get-tuple-element.253), channel_id=1, source_target_pairs={{0,8},{4,12},{8,0},{12,4},{16,24},{20,28},{24,16},{28,20},{1,9},{5... | collective-permute-start | bytes 1769480 | tf_op jit(solution)/shard_map/ppermute | solution.py:37
  169.7 52.0 %collective-permute-start.25 = (bf16[2,2,1,384,768]{4,3,2,1,0:T(8,128)(2,1)}, bf16[2,2,1,384,768]{4,3,2,1,0:T(8,128)(2,1)}, u32[]{:S(2)}, u32[]{:S(2)}) collective-permute-start(bf16[2,2,1,384,768]{4,3,2,1,0:T(8,128)(2,1)} %maximum_select_fusion.3), channel_id=1, source_target_pairs={{0,4},{4,0},{8,12},{12,8},{16,20},{20,16},{24,28},{28,24},{1,5},{5... | collective-permute-start | bytes 7077896 | tf_op jit(solution)/shard_map/ppermute | solution.py:37
  191.0 28.4 %collective-permute-start.30 = (bf16[1,2,1,384,768]{4,3,2,1,0:T(8,128)(2,1)S(1)}, bf16[1,2,1,384,768]{4,3,2,1,0:T(8,128)(2,1)S(1)}, u32[]{:S(2)}, u32[]{:S(2)}) collective-permute-start(bf16[1,2,1,384,768]{4,3,2,1,0:T(8,128)(2,1)S(1)} %maximum_select_fusion.12), channel_id=1, source_target_pairs={{0,16},{4,20},{8,24},{12,28},{16,0},{20,4},{24,8},{28,12},{1,17},{... | collective-permute-start | bytes 3538952 | tf_op jit(solution)/shard_map/ppermute | solution.py:37
  219.5 76.9 %collective-permute-start.43 = (bf16[192,2732]{1,0:T(8,128)(2,1)}, bf16[192,2732]{1,0:T(8,128)(2,1)S(1)}, u32[]{:S(2)}, u32[]{:S(2)}) collective-permute-start(bf16[192,2732]{1,0:T(8,128)(2,1)} %convert_element_type.167), channel_id=1, source_target_pairs={{0,2},{1,3},{2,0},{3,1},{4,6},{5,7},{6,4},{7,5},{8,10},{9,11},{10,... | collective-permute-start | bytes 3147272 | tf_op jit(solution)/shard_map/ppermute | solution.py:37
  221.7 27.1 %collective-permute-start.31 = (bf16[2,2,1,384,768]{4,3,2,1,0:T(8,128)(2,1)}, bf16[2,2,1,384,768]{4,3,2,1,0:T(8,128)(2,1)}, u32[]{:S(2)}, u32[]{:S(2)}) collective-permute-start(bf16[2,2,1,384,768]{4,3,2,1,0:T(8,128)(2,1)} %maximum_select_fusion.4), channel_id=1, source_target_pairs={{0,4},{4,0},{8,12},{12,8},{16,20},{20,16},{24,28},{28,24},{1,5},{5... | collective-permute-start | bytes 7077896 | tf_op jit(solution)/shard_map/ppermute | solution.py:37
  248.8 47.6 %collective-permute-start.44 = (bf16[192,2732]{1,0:T(8,128)(2,1)}, bf16[192,2732]{1,0:T(8,128)(2,1)}, u32[]{:S(2)}, u32[]{:S(2)}) collective-permute-start(bf16[192,2732]{1,0:T(8,128)(2,1)} %convert_element_type.167), channel_id=1, source_target_pairs={{0,1},{1,0},{2,3},{3,2},{4,5},{5,4},{6,7},{7,6},{8,9},{9,8},{10,11... | collective-permute-start | bytes 3147272 | tf_op jit(solution)/shard_map/ppermute | solution.py:37
  326.5 351.9 %collective-permute-start.93 = (bf16[192,2732]{1,0:T(8,128)(2,1)}, bf16[192,2732]{1,0:T(8,128)(2,1)}, u32[]{:S(2)}, u32[]{:S(2)}) collective-permute-start(bf16[192,2732]{1,0:T(8,128)(2,1)} %get-tuple-element.219), channel_id=1, source_target_pairs={{0,3},{1,2},{2,1},{3,0},{4,7},{5,6},{6,5},{7,4},{8,11},{9,10},{10,... | collective-permute-start | bytes 3147272 | tf_op jit(solution)/shard_map/ppermute | solution.py:37
  327.9 353.0 %collective-permute-start.92 = (bf16[192,2732]{1,0:T(8,128)(2,1)}, bf16[192,2732]{1,0:T(8,128)(2,1)}, u32[]{:S(2)}, u32[]{:S(2)}) collective-permute-start(bf16[192,2732]{1,0:T(8,128)(2,1)} %get-tuple-element.219), channel_id=1, source_target_pairs={{0,2},{1,3},{2,0},{3,1},{4,6},{5,7},{6,4},{7,5},{8,10},{9,11},{10,... | collective-permute-start | bytes 3147272 | tf_op jit(solution)/shard_map/ppermute | solution.py:37
  329.3 50.8 %collective-permute-start.55 = (f32[24,768]{1,0:T(8,128)S(1)}, f32[24,768]{1,0:T(8,128)S(1)}, u32[]{:S(2)}, u32[]{:S(2)}) collective-permute-start(f32[24,768]{1,0:T(8,128)S(1)} %fusion.113), channel_id=1, source_target_pairs={{0,3},{1,2},{2,1},{3,0},{4,7},{5,6},{6,5},{7,4},{8,11},{9,10},{10,... | collective-permute-start | bytes 221192 | tf_op jit(solution)/shard_map/ppermute | solution.py:37
  330.7 103.3 %collective-permute-start.56 = (f32[24,768]{1,0:T(8,128)S(1)}, f32[24,768]{1,0:T(8,128)S(1)}, u32[]{:S(2)}, u32[]{:S(2)}) collective-permute-start(f32[24,768]{1,0:T(8,128)S(1)} %fusion.113), channel_id=1, source_target_pairs={{0,2},{1,3},{2,0},{3,1},{4,6},{5,7},{6,4},{7,5},{8,10},{9,11},{10,... | collective-permute-start | bytes 221192 | tf_op jit(solution)/shard_map/ppermute | solution.py:37
  332.5 102.5 %collective-permute-start.57 = (f32[24,768]{1,0:T(8,128)S(1)}, f32[24,768]{1,0:T(8,128)S(1)}, u32[]{:S(2)}, u32[]{:S(2)}) collective-permute-start(f32[24,768]{1,0:T(8,128)S(1)} %fusion.113), channel_id=1, source_target_pairs={{0,1},{1,0},{2,3},{3,2},{4,5},{5,4},{6,7},{7,6},{8,9},{9,8},{10,11... | collective-permute-start | bytes 221192 | tf_op jit(solution)/shard_map/ppermute | solution.py:37
  380.1 278.1 %collective-permute-start.90 = (bf16[192,768]{1,0:T(8,128)(2,1)}, bf16[192,768]{1,0:T(8,128)(2,1)}, u32[]{:S(2)}, u32[]{:S(2)}) collective-permute-start(bf16[192,768]{1,0:T(8,128)(2,1)} %constant_dynamic-update-slice_fusion), channel_id=1, source_target_pairs={{0,3},{1,2},{2,1},{3,0},{4,7},{5,6},{6,5},{7,4},{8,11},{9,10},{10,... | collective-permute-start | bytes 884744 | tf_op jit(solution)/shard_map/ppermute | solution.py:37
  434.0 238.8 %collective-permute-start.89 = (bf16[192,768]{1,0:T(8,128)(2,1)}, bf16[192,768]{1,0:T(8,128)(2,1)}, u32[]{:S(2)}, u32[]{:S(2)}) collective-permute-start(bf16[192,768]{1,0:T(8,128)(2,1)} %constant_dynamic-update-slice_fusion), channel_id=1, source_target_pairs={{0,2},{1,3},{2,0},{3,1},{4,6},{5,7},{6,4},{7,5},{8,10},{9,11},{10,... | collective-permute-start | bytes 884744 | tf_op jit(solution)/shard_map/ppermute | solution.py:37
  631.2 103.8 %collective-permute-start.70 = (f32[2,2,4,96,768]{4,3,2,0,1:T(8,128)}, f32[2,2,4,96,768]{4,3,2,0,1:T(8,128)}, u32[]{:S(2)}, u32[]{:S(2)}) collective-permute-start(f32[2,2,4,96,768]{4,3,2,0,1:T(8,128)} %bitcast.341), channel_id=1, source_target_pairs={{0,4},{4,0},{8,12},{12,8},{16,20},{20,16},{24,28},{28,24},{1,5},{5... | collective-permute-start | bytes 14155784 | tf_op jit(solution)/shard_map/ppermute | solution.py:37
  658.2 19.8 %collective-permute-start.88 = (bf16[192,768]{1,0:T(8,128)(2,1)}, bf16[192,768]{1,0:T(8,128)(2,1)}, u32[]{:S(2)}, u32[]{:S(2)}) collective-permute-start(bf16[192,768]{1,0:T(8,128)(2,1)} %constant_dynamic-update-slice_fusion), channel_id=1, source_target_pairs={{0,1},{1,0},{2,3},{3,2},{4,5},{5,4},{6,7},{7,6},{8,9},{9,8},{10,11... | collective-permute-start | bytes 884744 | tf_op jit(solution)/shard_map/ppermute | solution.py:37
  672.8 57.0 %collective-permute-start.58 = (f32[2,2,4,72,768]{4,3,2,0,1:T(8,128)}, f32[2,2,4,72,768]{4,3,2,0,1:T(8,128)}, u32[]{:S(2)}, u32[]{:S(2)}) collective-permute-start(f32[2,2,4,72,768]{4,3,2,0,1:T(8,128)} %bitcast.396), channel_id=1, source_target_pairs={{0,4},{4,0},{8,12},{12,8},{16,20},{20,16},{24,28},{28,24},{1,5},{5... | collective-permute-start | bytes 10616840 | tf_op jit(solution)/shard_map/ppermute | solution.py:37
  678.0 20.9 %collective-permute-start.64 = (f32[2,2,4,24,768]{4,3,2,1,0:T(8,128)}, f32[2,2,4,24,768]{4,3,2,1,0:T(8,128)}, u32[]{:S(2)}, u32[]{:S(2)}) collective-permute-start(f32[2,2,4,24,768]{4,3,2,1,0:T(8,128)} %dynamic-slice_bitcast_fusion.8), channel_id=1, source_target_pairs={{0,4},{4,0},{8,12},{12,8},{16,20},{20,16},{24,28},{28,24},{1,5},{5... | collective-permute-start | bytes 3538952 | tf_op jit(solution)/shard_map/ppermute | solution.py:37
  678.3 64.2 %collective-permute-start.76 = (f32[2,2,4,96,768]{4,3,2,1,0:T(8,128)}, f32[2,2,4,96,768]{4,3,2,1,0:T(8,128)}, u32[]{:S(2)}, u32[]{:S(2)}) collective-permute-start(f32[2,2,4,96,768]{4,3,2,1,0:T(8,128)} %dynamic-slice_bitcast_fusion), channel_id=1, source_target_pairs={{0,4},{4,0},{8,12},{12,8},{16,20},{20,16},{24,28},{28,24},{1,5},{5... | collective-permute-start | bytes 14155784 | tf_op jit(solution)/shard_map/ppermute | solution.py:37
  680.9 26.4 %collective-permute-start.91 = (bf16[192,2732]{1,0:T(8,128)(2,1)}, bf16[192,2732]{1,0:T(8,128)(2,1)}, u32[]{:S(2)}, u32[]{:S(2)}) collective-permute-start(bf16[192,2732]{1,0:T(8,128)(2,1)} %get-tuple-element.219), channel_id=1, source_target_pairs={{0,1},{1,0},{2,3},{3,2},{4,5},{5,4},{6,7},{7,6},{8,9},{9,8},{10,11... | collective-permute-start | bytes 3147272 | tf_op jit(solution)/shard_map/ppermute | solution.py:37
  698.9 24.4 %collective-permute-start.82 = (f32[2,2,4,24,896]{4,3,2,1,0:T(8,128)}, f32[2,2,4,24,896]{4,3,2,1,0:T(8,128)S(1)}, u32[]{:S(2)}, u32[]{:S(2)}) collective-permute-start(f32[2,2,4,24,896]{4,3,2,1,0:T(8,128)} %dynamic-slice_bitcast_fusion.4), channel_id=1, source_target_pairs={{0,4},{4,0},{8,12},{12,8},{16,20},{20,16},{24,28},{28,24},{1,5},{5... | collective-permute-start | bytes 4128776 | tf_op jit(solution)/shard_map/ppermute | solution.py:37
  707.4 14.7 %collective-permute-start.65 = (f32[2,4,24,768]{3,2,1,0:T(8,128)S(1)}, f32[2,4,24,768]{3,2,1,0:T(8,128)S(1)}, u32[]{:S(2)}, u32[]{:S(2)}) collective-permute-start(f32[2,4,24,768]{3,2,1,0:T(8,128)S(1)} %dynamic-slice_bitcast_fusion.12), channel_id=1, source_target_pairs={{0,16},{4,20},{8,24},{12,28},{16,0},{20,4},{24,8},{28,12},{1,17},{... | collective-permute-start | bytes 1769480 | tf_op jit(solution)/shard_map/ppermute | solution.py:37
  723.6 26.7 %collective-permute-start.83 = (f32[2,4,24,896]{3,2,1,0:T(8,128)S(1)}, f32[2,4,24,896]{3,2,1,0:T(8,128)S(1)}, u32[]{:S(2)}, u32[]{:S(2)}) collective-permute-start(f32[2,4,24,896]{3,2,1,0:T(8,128)S(1)} %dynamic-slice_bitcast_fusion.10), channel_id=1, source_target_pairs={{0,16},{4,20},{8,24},{12,28},{16,0},{20,4},{24,8},{28,12},{1,17},{... | collective-permute-start | bytes 2064392 | tf_op jit(solution)/shard_map/ppermute | solution.py:37
  733.9 98.3 %collective-permute-start.59 = (f32[2,4,72,768]{3,2,1,0:T(8,128)}, f32[2,4,72,768]{3,2,1,0:T(8,128)S(1)}, u32[]{:S(2)}, u32[]{:S(2)}) collective-permute-start(f32[2,4,72,768]{3,2,1,0:T(8,128)} %dynamic-slice_bitcast_fusion.3), channel_id=1, source_target_pairs={{0,8},{4,12},{8,0},{12,4},{16,24},{20,28},{24,16},{28,20},{1,9},{5... | collective-permute-start | bytes 5308424 | tf_op jit(solution)/shard_map/ppermute | solution.py:37
  741.6 94.8 %collective-permute-start.71 = (f32[2,4,96,768]{3,2,1,0:T(8,128)}, f32[2,4,96,768]{3,2,1,0:T(8,128)}, u32[]{:S(2)}, u32[]{:S(2)}) collective-permute-start(f32[2,4,96,768]{3,2,1,0:T(8,128)} %dynamic-slice_bitcast_fusion.2), channel_id=1, source_target_pairs={{0,8},{4,12},{8,0},{12,4},{16,24},{20,28},{24,16},{28,20},{1,9},{5... | collective-permute-start | bytes 7077896 | tf_op jit(solution)/shard_map/ppermute | solution.py:37
  748.4 91.4 %collective-permute-start.77 = (f32[2,4,96,768]{3,2,1,0:T(8,128)}, f32[2,4,96,768]{3,2,1,0:T(8,128)}, u32[]{:S(2)}, u32[]{:S(2)}) collective-permute-start(f32[2,4,96,768]{3,2,1,0:T(8,128)} %dynamic-slice_bitcast_fusion.1), channel_id=1, source_target_pairs={{0,16},{4,20},{8,24},{12,28},{16,0},{20,4},{24,8},{28,12},{1,17},{... | collective-permute-start | bytes 7077896 | tf_op jit(solution)/shard_map/ppermute | solution.py:37
  756.6 73.5 %collective-permute-start.84 = (f32[4,24,896]{2,1,0:T(8,128)}, f32[4,24,896]{2,1,0:T(8,128)S(1)}, u32[]{:S(2)}, u32[]{:S(2)}) collective-permute-start(f32[4,24,896]{2,1,0:T(8,128)} %dynamic-slice_bitcast_fusion.13), channel_id=1, source_target_pairs={{0,8},{4,12},{8,0},{12,4},{16,24},{20,28},{24,16},{28,20},{1,9},{5... | collective-permute-start | bytes 1032200 | tf_op jit(solution)/shard_map/ppermute | solution.py:37
  836.5 22.6 %collective-permute-start.60 = (f32[4,72,768]{2,1,0:T(8,128)S(1)}, f32[4,72,768]{2,1,0:T(8,128)S(1)}, u32[]{:S(2)}, u32[]{:S(2)}) collective-permute-start(f32[4,72,768]{2,1,0:T(8,128)S(1)} %dynamic-slice_bitcast_fusion.9), channel_id=1, source_target_pairs={{0,16},{4,20},{8,24},{12,28},{16,0},{20,4},{24,8},{28,12},{1,17},{... | collective-permute-start | bytes 2654216 | tf_op jit(solution)/shard_map/ppermute | solution.py:37
  839.8 39.4 %collective-permute-start.72 = (f32[4,96,768]{2,1,0:T(8,128)S(1)}, f32[4,96,768]{2,1,0:T(8,128)S(1)}, u32[]{:S(2)}, u32[]{:S(2)}) collective-permute-start(f32[4,96,768]{2,1,0:T(8,128)S(1)} %dynamic-slice_bitcast_fusion.7), channel_id=1, source_target_pairs={{0,16},{4,20},{8,24},{12,28},{16,0},{20,4},{24,8},{28,12},{1,17},{... | collective-permute-start | bytes 3538952 | tf_op jit(solution)/shard_map/ppermute | solution.py:37
  843.0 37.3 %collective-permute-start.78 = (f32[4,96,768]{2,1,0:T(8,128)S(1)}, f32[4,96,768]{2,1,0:T(8,128)S(1)}, u32[]{:S(2)}, u32[]{:S(2)}) collective-permute-start(f32[4,96,768]{2,1,0:T(8,128)S(1)} %dynamic-slice_bitcast_fusion.6), channel_id=1, source_target_pairs={{0,8},{4,12},{8,0},{12,4},{16,24},{20,28},{24,16},{28,20},{1,9},{5... | collective-permute-start | bytes 3538952 | tf_op jit(solution)/shard_map/ppermute | solution.py:37
  859.3 22.9 %collective-permute-start.62 = (f32[72,768]{1,0:T(8,128)S(1)}, f32[72,768]{1,0:T(8,128)S(1)}, u32[]{:S(2)}, u32[]{:S(2)}) collective-permute-start(f32[72,768]{1,0:T(8,128)S(1)} %get-tuple-element.240), channel_id=1, source_target_pairs={{0,2},{1,3},{2,0},{3,1},{4,6},{5,7},{6,4},{7,5},{8,10},{9,11},{10,... | collective-permute-start | bytes 663560 | tf_op jit(solution)/shard_map/ppermute | solution.py:37
  859.5 25.4 %collective-permute-start.63 = (f32[72,768]{1,0:T(8,128)S(1)}, f32[72,768]{1,0:T(8,128)S(1)}, u32[]{:S(2)}, u32[]{:S(2)}) collective-permute-start(f32[72,768]{1,0:T(8,128)S(1)} %get-tuple-element.239), channel_id=1, source_target_pairs={{0,3},{1,2},{2,1},{3,0},{4,7},{5,6},{6,5},{7,4},{8,11},{9,10},{10,... | collective-permute-start | bytes 663560 | tf_op jit(solution)/shard_map/ppermute | solution.py:37
  861.0 24.8 %collective-permute-start.61 = (f32[72,768]{1,0:T(8,128)S(1)}, f32[72,768]{1,0:T(8,128)S(1)}, u32[]{:S(2)}, u32[]{:S(2)}) collective-permute-start(f32[72,768]{1,0:T(8,128)S(1)} %get-tuple-element.238), channel_id=1, source_target_pairs={{0,1},{1,0},{2,3},{3,2},{4,5},{5,4},{6,7},{7,6},{8,9},{9,8},{10,11... | collective-permute-start | bytes 663560 | tf_op jit(solution)/shard_map/ppermute | solution.py:37
  880.2 25.6 %collective-permute-start.74 = (f32[96,768]{1,0:T(8,128)S(1)}, f32[96,768]{1,0:T(8,128)S(1)}, u32[]{:S(2)}, u32[]{:S(2)}) collective-permute-start(f32[96,768]{1,0:T(8,128)S(1)} %get-tuple-element.235), channel_id=1, source_target_pairs={{0,2},{1,3},{2,0},{3,1},{4,6},{5,7},{6,4},{7,5},{8,10},{9,11},{10,... | collective-permute-start | bytes 884744 | tf_op jit(solution)/shard_map/ppermute | solution.py:37
  880.3 27.4 %collective-permute-start.75 = (f32[96,768]{1,0:T(8,128)}, f32[96,768]{1,0:T(8,128)}, u32[]{:S(2)}, u32[]{:S(2)}) collective-permute-start(f32[96,768]{1,0:T(8,128)} %get-tuple-element.234), channel_id=1, source_target_pairs={{0,3},{1,2},{2,1},{3,0},{4,7},{5,6},{6,5},{7,4},{8,11},{9,10},{10,... | collective-permute-start | bytes 884744 | tf_op jit(solution)/shard_map/ppermute | solution.py:37
  882.2 25.5 %collective-permute-start.73 = (f32[96,768]{1,0:T(8,128)S(1)}, f32[96,768]{1,0:T(8,128)}, u32[]{:S(2)}, u32[]{:S(2)}) collective-permute-start(f32[96,768]{1,0:T(8,128)S(1)} %get-tuple-element.233), channel_id=1, source_target_pairs={{0,1},{1,0},{2,3},{3,2},{4,5},{5,4},{6,7},{7,6},{8,9},{9,8},{10,11... | collective-permute-start | bytes 884744 | tf_op jit(solution)/shard_map/ppermute | solution.py:37
  884.9 37.3 %collective-permute-start.80 = (f32[96,768]{1,0:T(8,128)}, f32[96,768]{1,0:T(8,128)}, u32[]{:S(2)}, u32[]{:S(2)}) collective-permute-start(f32[96,768]{1,0:T(8,128)} %get-tuple-element.232), channel_id=1, source_target_pairs={{0,2},{1,3},{2,0},{3,1},{4,6},{5,7},{6,4},{7,5},{8,10},{9,11},{10,... | collective-permute-start | bytes 884744 | tf_op jit(solution)/shard_map/ppermute | solution.py:37
  885.9 36.2 %collective-permute-start.81 = (f32[96,768]{1,0:T(8,128)}, f32[96,768]{1,0:T(8,128)}, u32[]{:S(2)}, u32[]{:S(2)}) collective-permute-start(f32[96,768]{1,0:T(8,128)} %get-tuple-element.231), channel_id=1, source_target_pairs={{0,3},{1,2},{2,1},{3,0},{4,7},{5,6},{6,5},{7,4},{8,11},{9,10},{10,... | collective-permute-start | bytes 884744 | tf_op jit(solution)/shard_map/ppermute | solution.py:37
  905.7 16.4 %collective-permute-start.79 = (f32[96,768]{1,0:T(8,128)}, f32[96,768]{1,0:T(8,128)}, u32[]{:S(2)}, u32[]{:S(2)}) collective-permute-start(f32[96,768]{1,0:T(8,128)} %get-tuple-element.230), channel_id=1, source_target_pairs={{0,1},{1,0},{2,3},{3,2},{4,5},{5,4},{6,7},{7,6},{8,9},{9,8},{10,11... | collective-permute-start | bytes 884744 | tf_op jit(solution)/shard_map/ppermute | solution.py:37
  955.0 23.8 %collective-permute-start.105 = (f32[96,768]{1,0:T(8,128)S(1)}, f32[96,768]{1,0:T(8,128)S(1)}, u32[]{:S(2)}, u32[]{:S(2)}) collective-permute-start(f32[96,768]{1,0:T(8,128)S(1)} %get-tuple-element.228), channel_id=1, source_target_pairs={{0,2},{1,3},{2,0},{3,1},{4,6},{5,7},{6,4},{7,5},{8,10},{9,11},{10,... | collective-permute-start | bytes 884744 | tf_op jit(solution)/shard_map/ppermute | solution.py:37
  955.0 23.8 %collective-permute-start.104 = (f32[96,768]{1,0:T(8,128)S(1)}, f32[96,768]{1,0:T(8,128)S(1)}, u32[]{:S(2)}, u32[]{:S(2)}) collective-permute-start(f32[96,768]{1,0:T(8,128)S(1)} %get-tuple-element.229), channel_id=1, source_target_pairs={{0,1},{1,0},{2,3},{3,2},{4,5},{5,4},{6,7},{7,6},{8,9},{9,8},{10,11... | collective-permute-start | bytes 884744 | tf_op jit(solution)/shard_map/ppermute | solution.py:37
  984.3 15.4 %collective-permute-start.108 = (f32[2,96,768]{2,1,0:T(8,128)S(1)}, f32[2,96,768]{2,1,0:T(8,128)S(1)}, u32[]{:S(2)}, u32[]{:S(2)}) collective-permute-start(f32[2,96,768]{2,1,0:T(8,128)S(1)} %dynamic-slice_bitcast_fusion.11), channel_id=1, source_target_pairs={{0,16},{4,20},{8,24},{12,28},{16,0},{20,4},{24,8},{28,12},{1,17},{... | collective-permute-start | bytes 1769480 | tf_op jit(solution)/shard_map/ppermute | solution.py:37
  1060.1 25.2 %collective-permute-start.114 = (f32[96,768]{1,0:T(8,128)}, f32[96,768]{1,0:T(8,128)S(1)}, u32[]{:S(2)}, u32[]{:S(2)}) collective-permute-start(f32[96,768]{1,0:T(8,128)} %get-tuple-element.224), channel_id=1, source_target_pairs={{0,2},{1,3},{2,0},{3,1},{4,6},{5,7},{6,4},{7,5},{8,10},{9,11},{10,... | collective-permute-start | bytes 884744 | tf_op jit(solution)/shard_map/ppermute | solution.py:37
  1060.1 25.2 %collective-permute-start.115 = (f32[96,768]{1,0:T(8,128)}, f32[96,768]{1,0:T(8,128)S(1)}, u32[]{:S(2)}, u32[]{:S(2)}) collective-permute-start(f32[96,768]{1,0:T(8,128)} %get-tuple-element.222), channel_id=1, source_target_pairs={{0,1},{1,0},{2,3},{3,2},{4,5},{5,4},{6,7},{7,6},{8,9},{9,8},{10,11... | collective-permute-start | bytes 884744 | tf_op jit(solution)/shard_map/ppermute | solution.py:37
  (182 other events, 2739.9 us)

commit v2 on v1

--- a/solution.py
+++ b/solution.py
@@ -66,67 +66,164 @@
     return tree_sum(relative(value, axis))
 
 
-def pack_bits(order):
+def hold(*values):
+    return lax.optimization_barrier(values)
+
+
+def other_chips():
+    return list(range(2, lax.axis_size("pack"), 2))
+
+
+def relative_packs():
+    same = [0] + other_chips()
+    return jnp.array(same + [k + 1 for k in same], jnp.int32)
+
+
+def relative_slots():
     count = lax.axis_size("pack")
-    bits = [1 << b for b in reversed(range(count.bit_length() - 1))]
-    others = [b for b in bits if b > 1]
-    return bits, (others if order == 0 else others[::-1])
-
-
-def gather_rows(shard, order):
-    seq_place, pack_place = lax.axis_index("seq"), lax.axis_index("pack")
-    bits, others = pack_bits(order)
-    whole = jnp.concatenate(absolute(relative(shard, "seq"), seq_place), axis=0)
-    whole = whole.reshape((1,) * len(bits) + whole.shape)
-    for bit in others + [1]:
-        dim = bits.index(bit)
-        other = swap(whole, "pack", bit)
-        whole = jnp.where(
-            (pack_place & bit) == 0,
-            jnp.concatenate([whole, other], axis=dim),
-            jnp.concatenate([other, whole], axis=dim),
-        )
-    return whole.reshape(-1, shard.shape[1])
-
-
-def halve(value, bits, order):
-    pack_place = lax.axis_index("pack")
-    _, others = pack_bits(order)
-    left = list(bits)
-    for bit in [1] + others:
-        dim = left.index(bit)
-        mine = (pack_place & bit) // bit
-        value = pick(value, mine, dim) + swap(pick(value, 1 - mine, dim), "pack", bit)
-        left.remove(bit)
-    return value
-
-
-def scatter_rows(grad, order):
-    seq_count, seq_place = lax.axis_size("seq"), lax.axis_index("seq")
-    bits, _ = pack_bits(order)
-    count = lax.axis_size("pack") * seq_count
-    value = grad.reshape((2,) * len(bits) + (seq_count, grad.shape[0] // count, grad.shape[1]))
-    value = halve(value, bits, order)
-    parts = [pick(value, seq_place)]
-    parts += [swap(pick(value, seq_place ^ k), "seq", k) for k in range(1, seq_count)]
+    offset = lax.axis_index("pack") ^ jnp.arange(count, dtype=jnp.int32)
+    return (offset >> 1) + (offset & 1) * (count // 2)
+
+
+def gather_blocks(block):
+    own = jnp.stack([block] + [swap(block, "pack", k) for k in other_chips()])
+    return own, swap(own, "pack", 1)
+
+
+def by_index(parts, place):
+    if len(parts) <= 8:
+        return jnp.stack(absolute(parts, place))
+    value = jnp.stack(parts)
+    shape, bit = value.shape, 1
+    while bit < len(parts):
+        value = value.reshape((-1, 2, bit) + shape[1:])
+        turned = jnp.concatenate([value[:, 1:], value[:, :1]], axis=1)
+        value = jnp.where((place & bit) == 0, value, turned)
+        bit *= 2
+    return value.reshape(shape)
+
+
+def by_core(own, other, dim):
+    return jnp.where(
+        (lax.axis_index("pack") & 1) == 0, jnp.stack([own, other], axis=dim), jnp.stack([other, own], axis=dim)
+    )
+
+
+class Gather:
+    def __init__(self, shard):
+        self.shard = shard
+
+    def along_seq(self):
+        self.block = by_index(relative(self.shard, "seq"), lax.axis_index("seq"))
+        return self.block
+
+    def in_plane(self):
+        self.parts = list(hold(self.block, *[swap(self.block, "pack", k) for k in other_chips()]))
+        return self.parts[-1]
+
+    def whole(self):
+        mine = by_index(self.parts, lax.axis_index("pack") >> 1)
+        cells = by_core(mine, swap(mine, "pack", 1), 1)
+        return cells.reshape((-1,) + self.shard.shape)
+
+    def halves(self):
+        own = jnp.stack(self.parts)
+        return own, swap(own, "pack", 1)
+
+
+class Scatter:
+    def __init__(self, order, width, relative=False):
+        count = lax.axis_size("pack")
+        self.left = [1 << b for b in reversed(range(count.bit_length() - 1))]
+        chips = [b for b in self.left if b > 1]
+        self.order = [1] + (chips if order == 0 else chips[::-1])
+        self.relative, self.width = relative, width
+
+    def start(self, grad):
+        self.value = grad.reshape((2,) * len(self.left) + (lax.axis_size("seq"), -1, self.width))
+        return self.send()
+
+    def start_halves(self, keep, send):
+        self.left.remove(1)
+        self.order.remove(1)
+        shape = (2,) * len(self.left) + (lax.axis_size("seq"), -1, self.width)
+        self.bit, self.keep = 1, keep.reshape(shape)
+        return send.reshape(shape)
+
+    def start_joined(self, value):
+        self.left.remove(1)
+        self.order.remove(1)
+        self.value = value
+        return self.send()
+
+    def send(self):
+        self.bit = self.order.pop(0)
+        dim = self.left.index(self.bit)
+        self.left.remove(self.bit)
+        if self.relative:
+            self.keep = lax.index_in_dim(self.value, 0, dim, keepdims=False)
+            return lax.index_in_dim(self.value, 1, dim, keepdims=False)
+        mine = (lax.axis_index("pack") & self.bit) // self.bit
+        self.keep = pick(self.value, mine, dim)
+        return pick(self.value, 1 - mine, dim)
+
+    def join(self, sent):
+        self.value = self.keep + swap(sent, "pack", self.bit)
+
+    def step(self, sent):
+        self.join(sent)
+        return self.send() if self.order else None
+
+    def finish(self):
+        value, count = self.value, lax.axis_size("seq")
+        tail = value.shape[1:]
+        bit = 1
+        while bit < count:
+            mine = (lax.axis_index("seq") & bit) // bit
+            value = value.reshape((-1, 2) + tail)
+            value = pick(value, mine, 1) + swap(pick(value, 1 - mine, 1), "seq", bit)
+            bit *= 2
+        return value.reshape(tail)
+
+
+def late_halves(qkv_grad, output_grad):
+    seq_count, pack_count = lax.axis_size("seq"), lax.axis_size("pack")
+    chips = (2,) * (pack_count.bit_length() - 2)
+    core = lax.axis_index("pack") & 1
+
+    def half(which):
+        pieces = [
+            pick(grad.reshape(chips + (2, seq_count, -1, grad.shape[1])), which, len(chips))
+            for grad in (qkv_grad, output_grad)
+        ]
+        return jnp.concatenate(pieces, axis=-2)
+
+    return half(core), half(1 - core)
+
+
+def pack_scatter(value):
+    half = value.shape[0] // 2
+    mine = value[:half] + swap(value[half:], "pack", 1)
+    parts = [mine[0]] + [swap(mine[k // 2], "pack", k) for k in other_chips()]
     return tree_sum(parts)
 
 
-def pack_sum(value, order):
-    pack_place = lax.axis_index("pack")
-    bits, others = pack_bits(order)
-    rows = value.shape[0] >> len(bits)
-    part = halve(value.reshape((2,) * len(bits) + (rows, value.shape[1])), bits, order)
-    part = part.reshape((1,) * len(bits) + part.shape)
-    for bit in others[::-1] + [1]:
-        dim = bits.index(bit)
-        other = swap(part, "pack", bit)
-        part = jnp.where(
-            (pack_place & bit) == 0,
-            jnp.concatenate([part, other], axis=dim),
-            jnp.concatenate([other, part], axis=dim),
-        )
-    return part.reshape(value.shape)
+def pack_sum(value):
+    pack_place, count = lax.axis_index("pack"), lax.axis_size("pack")
+    core = pack_place & 1
+    split = value.reshape(count // 2, 2, -1, value.shape[1])
+    mine = pick(split, core, 1) + swap(pick(split, 1 - core, 1), "pack", 1)
+    chip = pack_place >> 1
+    parts = [pick(mine, chip)] + [swap(pick(mine, chip ^ (k // 2)), "pack", k) for k in other_chips()]
+    total = tree_sum(parts)
+    mine = by_index([total] + [swap(total, "pack", k) for k in other_chips()], chip)
+    return by_core(mine, swap(mine, "pack", 1), 1).reshape(value.shape)
+
+
+def sum_all(value):
+    value = value + swap(value, "pack", 1)
+    value = tree_sum([value] + [swap(value, "pack", k) for k in other_chips()])
+    return all_sum(value, "seq")
 
 
 def _dot(left, right, dims):
@@ -306,6 +403,17 @@
     )
 
 
+def as_rows(value, width):
+    flat = value.reshape(1, -1)
+    return jnp.pad(flat, ((0, 7), (0, width - flat.shape[1])))
+
+
+def from_rows(cells, shape):
+    rows, columns = shape
+    flat = cells[:, 0, : rows * columns].reshape(-1, rows, columns)
+    return flat.transpose(1, 0, 2).reshape(rows, -1)
+
+
 def mm(spec, left, right):
     return jnp.einsum(spec, left, right, preferred_element_type=F32)
 
@@ -320,7 +428,7 @@
 
 def ortho(columns):
     gram_mat = pack_sum(
-        lax.dot_general(columns, columns, (TN, ((), ())), precision=NS_PREC, preferred_element_type=F32), 0
+        lax.dot_general(columns, columns, (TN, ((), ())), precision=NS_PREC, preferred_element_type=F32)
     )
     scale = 1.0 / (jnp.sqrt(jnp.trace(gram_mat)) + 1e-07)
     iterate = columns * scale
@@ -339,17 +447,20 @@
     return iterate
 
 
-def muon(moments):
+def to_planes(shards):
     seq_count, seq_place = lax.axis_size("seq"), lax.axis_index("seq")
-    most = max(m.shape[0] for m in moments)
-    filled = [jnp.pad(m, ((0, most - m.shape[0]), (0, 0))) for m in moments]
-    filled += [jnp.zeros_like(filled[0])] * (seq_count - len(moments))
+    most = max(m.shape[0] for m in shards)
+    filled = [jnp.pad(m, ((0, most - m.shape[0]), (0, 0))) for m in shards]
+    filled += [jnp.zeros_like(filled[0])] * (seq_count - len(shards))
     stacked = jnp.stack(filled)
     parts = [pick(stacked, seq_place)]
     parts += [swap(pick(stacked, seq_place ^ k), "seq", k) for k in range(1, seq_count)]
-    done = ortho(jnp.concatenate(parts, axis=0)).reshape(stacked.shape)
-    back = [done[0]] + [swap(done[k], "seq", k) for k in range(1, seq_count)]
-    return [_choose(back, seq_place, m)[: moments[m].shape[0]] for m in range(len(moments))]
+    return jnp.stack(parts)
+
+
+def from_planes(value, counts):
+    back = [value[0]] + [swap(value[k], "seq", k) for k in range(1, lax.axis_size("seq"))]
+    return [_choose(back, lax.axis_index("seq"), m)[:count] for m, count in enumerate(counts)]
 
 
 def muon_update(weight, iterate):
@@ -461,19 +572,43 @@
     pack_count, pack_place = lax.axis_size("pack"), lax.axis_index("pack")
     small_rows = small_params.shape[0]
 
-    embed_pack = jnp.concatenate(
-        [embed_weight.T, jnp.pad(small_params.T, ((0, 0), (0, BLOCK - small_rows)))], axis=1
-    ).astype(LOW)
-    embed_pack = gather_rows(embed_pack, 0)
-    embed_full, small_full = embed_pack[:, :patch_in], embed_pack[:, patch_in : patch_in + small_rows]
-    gain_bias = small_full.astype(F32).T
-    qkv_full = gather_rows(qkv_weight.T.astype(LOW), 1)
-    output_full = gather_rows(output_weight.T.astype(LOW), 0)
-    up_shard, down_shard, _ = lax.optimization_barrier(
-        (up_weight.T.astype(LOW), down_weight.T.astype(LOW), qkv_full)
-    )
-    up_full = gather_rows(up_shard, 0)
-    down_full = gather_rows(down_shard, 1)
+    bundle = [embed_weight.T, qkv_weight.T, as_rows(small_params, width), as_rows(head_bias, width)]
+    spots = [0]
+    for piece in bundle:
+        spots.append(spots[-1] + piece.shape[0])
+    first = Gather(jnp.concatenate([piece.astype(LOW) for piece in bundle]))
+    first_block = first.along_seq()
+    patches, first_there = hold(patches, first_block)
+    first_plane = first.in_plane()
+    second_shard, _ = hold(
+        jnp.concatenate([up_weight.T.astype(LOW), output_weight.T.astype(LOW)]), first_there
+    )
+    second = Gather(second_shard)
+    second.along_seq()
+    second.block, _ = hold(second.block, first_plane)
+    cells = first.whole()
+    embed_full, qkv_full, small_full, bias_full = (
+        cells[:, here:there] for here, there in zip(spots[:-1], spots[1:])
+    )
+    embed_full, qkv_full = embed_full.reshape(-1, width), qkv_full.reshape(-1, width)
+    gain_bias = from_rows(small_full, small_params.shape).astype(F32)
+    bias_full = lax.dynamic_slice_in_dim(bias_full, pack_place * seq_count, seq_count, 0)
+    bias_full = bias_full[:, 0, : head_bias.shape[0]].reshape(-1)
+    third_shard, _ = hold(down_weight.T.astype(LOW), second.block)
+    third = Gather(third_shard)
+    third_block = third.along_seq()
+    second_plane = second.in_plane()
+    third.block, _ = hold(third.block, second_plane)
+    head_shard, _ = hold(head_weight.astype(LOW), third_block)
+    head_full = lax.all_gather(head_shard, "seq", axis=0, tiled=True)
+    hidden = up_weight.shape[1]
+    own, other = second.halves()
+    up_full = [half[:, :, :hidden].reshape(-1, width) for half in (own, other)]
+    by_chip = by_index([own[k, :, hidden:] for k in range(own.shape[0])], pack_place >> 1)
+    other_chip = by_index([other[k, :, hidden:] for k in range(own.shape[0])], pack_place >> 1)
+    output_full = by_core(by_chip, other_chip, 1).reshape(-1, width)
+    third.in_plane()
+    down_full = [half.reshape(-1, width) for half in third.halves()]
 
     ends = seq_count - 1
     from_left = lax.ppermute(patches[:, shard_len - MAXLEN :], "seq", [(i, i + 1) for i in range(ends)])
@@ -490,9 +625,6 @@
         (group[None, :] == jnp.arange(group_count, dtype=jnp.int32)[:, None]) & live[None, :]
     ).astype(F32)
 
-    head_parts = relative(head_weight.astype(LOW), "seq")
-    bias_full = jnp.concatenate(absolute(relative(head_bias.astype(LOW), "seq"), seq_place), axis=0)
-
     embedded = mm("ri,di->rd", tokens, embed_full) + gain_bias[6]
     normed_one = layer_norm(embedded, gain_bias[0], gain_bias[1]).astype(LOW)
     qkv_bias = jnp.concatenate([gain_bias[7], jnp.zeros_like(gain_bias[7]), gain_bias[8]])
@@ -500,9 +632,16 @@
     attn_low, log_total = attend(qkv_rows, query_id, key_id)
     after_attn = embedded + mm("re,de->rd", attn_low, output_full) + gain_bias[9]
     normed_two = layer_norm(after_attn, gain_bias[2], gain_bias[3]).astype(LOW)
-    up_rows = mm("rd,fd->rf", normed_two, up_full) + gain_bias[11:15].reshape(-1)
-    active = gelu(up_rows).astype(LOW)
-    after_mlp = after_attn + mm("rf,fd->rd", active, down_full) + gain_bias[10]
+    up_bias = jnp.take(
+        gain_bias[11:15].reshape(pack_count, -1), relative_packs() ^ pack_place, axis=0
+    ).reshape(2, -1)
+    up_rows = [mm("rd,fd->rf", normed_two, up_full[half]) + up_bias[half] for half in range(2)]
+    active = [gelu(rows).astype(LOW) for rows in up_rows]
+    after_mlp = (
+        after_attn
+        + (mm("rf,fd->rd", active[0], down_full[0]) + mm("rf,fd->rd", active[1], down_full[1]))
+        + gain_bias[10]
+    )
     final_rows = layer_norm(after_mlp, gain_bias[4], gain_bias[5])
     pool_sums = jnp.dot(member, final_rows, precision=HIGHEST_PREC, preferred_element_type=F32)
     pooled_mine = (pool_sums / counts[:, None]).astype(LOW)
@@ -513,14 +652,13 @@
         [pick(split, seq_place).astype(F32)]
         + [swap(pick(split, seq_place ^ k), "seq", k).astype(F32) for k in range(1, seq_count)]
     ).astype(LOW)
-    pooled_rows = jnp.concatenate(relative(pooled_low, "pack"), axis=0)
+    pooled_rows = jnp.concatenate(gather_blocks(pooled_low), axis=0).reshape(-1, width)
     depth = head_weight.shape[0]
-    head_full = jnp.concatenate(absolute(head_parts, seq_place), axis=0)
     label_cols = head_full.shape[1]
     logits = mm("nd,dc->nc", pooled_rows, head_full) + bias_full.astype(F32)
     label_rows = jnp.take(
         pick(labels.reshape(pack_count, seq_count, img_share), seq_place, 1),
-        jnp.arange(pack_count, dtype=jnp.int32) ^ pack_place,
+        relative_packs() ^ pack_place,
         axis=0,
     ).reshape(-1)
     class_ids = pack_place * label_cols + jnp.arange(label_cols, dtype=jnp.int32)
@@ -530,40 +668,59 @@
     loss_part = jnp.sum(valid[None, :] * (jax.nn.softplus(logits) - target * logits)) / image_total
     grad_logits = (valid[None, :] * (jax.nn.sigmoid(logits) - target) / image_total).astype(LOW)
     pooled_part = mm("nc,dc->nd", grad_logits, head_full).reshape(pack_count, img_share, width)
-    pooled_grad = tree_sum(
-        [pooled_part[0]] + [swap(pooled_part[k], "pack", k) for k in range(1, pack_count)]
-    )
+    pooled_grad = pack_scatter(pooled_part)
     pooled_grad = jnp.concatenate(absolute(relative(pooled_grad, "seq"), seq_place), axis=0)
     pooled_grad = pooled_grad / counts[:, None]
 
-    all_pooled = jnp.concatenate(
-        [pick(part.reshape(-1, seq_count, depth), seq_place, 1) for part in relative(pooled_rows, "seq")], axis=0
-    )
-    all_logits = jnp.concatenate(relative(grad_logits, "seq"), axis=0)
-    head_grad = mm("nd,nc->dc", all_pooled, all_logits)
-    bias_grad = pick(column_sum(all_logits).reshape(seq_count, -1), seq_place)
+    traded, pooled_grad = hold(jnp.concatenate([pooled_rows, grad_logits], axis=1), pooled_grad)
+    traded = lax.all_gather(traded, "seq", axis=0, tiled=True)
 
     grad_final = lax.dot_general(
         member, pooled_grad, (TN, ((), ())), precision=HIGHEST_PREC, preferred_element_type=F32
     )
     grad_mlp, grad_gain_f, grad_bias_f = norm_back(after_mlp, gain_bias[4], gain_bias[5], grad_final)
     grad_mlp_low = grad_mlp.astype(LOW)
-    down_share = scatter_rows(mm("rf,rd->fd", active, grad_mlp_low), 0)
-    grad_upper = (mm("rd,fd->rf", grad_mlp_low, down_full) * gelu_slope(up_rows)).astype(LOW)
-    up_share = scatter_rows(mm("rf,rd->fd", grad_upper, normed_two), 1)
-    grad_two, grad_gain_2, grad_bias_2 = norm_back(
-        after_attn, gain_bias[2], gain_bias[3], mm("rf,fd->rd", grad_upper, up_full)
-    )
+    down_sum, up_sum = Scatter(0, width, True), Scatter(1, width, True)
+    half = width // 2
+    late_sums = [Scatter(0, half), Scatter(1, half)]
+    last_sum = Scatter(0, width)
+    down_out = mm("rf,rd->fd", active[1], grad_mlp_low)
+    down_keep = mm("rf,rd->fd", active[0], grad_mlp_low)
+    grad_mlp_low, down_out, down_keep = hold(grad_mlp_low, down_out, down_keep)
+    down_out = down_sum.start_halves(down_keep, down_out)
+    grad_upper = [
+        (mm("rd,fd->rf", grad_mlp_low, down_full[side]) * gelu_slope(up_rows[side])).astype(LOW)
+        for side in range(2)
+    ]
+    up_out = mm("rf,rd->fd", grad_upper[1], normed_two)
+    up_keep = mm("rf,rd->fd", grad_upper[0], normed_two)
+    grad_upper[0], grad_upper[1], up_out, up_keep = hold(*grad_upper, up_out, up_keep)
+    up_out = up_sum.start_halves(up_keep, up_out)
+    grad_normed = mm("rf,fd->rd", grad_upper[0], up_full[0]) + mm("rf,fd->rd", grad_upper[1], up_full[1])
+    down_out = down_sum.step(down_out)
+    grad_normed, down_out = hold(grad_normed, down_out)
+    grad_two, grad_gain_2, grad_bias_2 = norm_back(after_attn, gain_bias[2], gain_bias[3], grad_normed)
     grad_attn = grad_mlp + grad_two
     grad_attn_low = grad_attn.astype(LOW)
-    output_share = scatter_rows(mm("rd,re->de", grad_attn_low, attn_low), 0)
     grad_mixed = mm("rd,de->re", grad_attn_low, output_full).astype(LOW)
+    output_grad = mm("rd,re->de", grad_attn_low, attn_low)
+    up_out = up_sum.step(up_out)
+    muon_moments = [m.T for m in (qkv_moment, output_moment, up_moment, down_moment)]
+    grad_mixed, up_out, *muon_moments = hold(grad_mixed, up_out, *muon_moments)
+    old_columns = to_planes(muon_moments)
     grad_qkv = attend_back(qkv_rows, grad_mixed, log_total, query_id, key_id)
-    qkv_share = scatter_rows(mm("re,rd->ed", grad_qkv, normed_one), 1)
+    grad_qkv, traded, old_columns = hold(grad_qkv, traded, old_columns)
+    late_keep, late_out = late_halves(mm("re,rd->ed", grad_qkv, normed_one), output_grad)
+    down_out, up_out = down_sum.step(down_out), up_sum.step(up_out)
+    grad_qkv, late_out, down_out, up_out = hold(grad_qkv, late_out, down_out, up_out)
     qkv_bias_grad = column_sum(grad_qkv)
-    grad_one, grad_gain_1, grad_bias_1 = norm_back(
-        embedded, gain_bias[0], gain_bias[1], mm("re,ed->rd", grad_qkv, qkv_full)
-    )
+    grad_normed = mm("re,ed->rd", grad_qkv, qkv_full)
+    late = late_keep + swap(late_out, "pack", 1)
+    late_outs = [
+        each.start_joined(part) for each, part in zip(late_sums, (late[..., :half], late[..., half:]))
+    ]
+    grad_normed, *late_outs = hold(grad_normed, *late_outs)
+    grad_one, grad_gain_1, grad_bias_1 = norm_back(embedded, gain_bias[0], gain_bias[1], grad_normed)
     grad_embed_rows = (grad_attn + grad_one).astype(LOW)
     small_grad = jnp.concatenate(
         [
@@ -582,40 +739,62 @@
                     column_sum(grad_mlp_low),
                 ]
             ),
-            column_sum(grad_upper).reshape(-1, width),
+            jnp.take(
+                jnp.concatenate([column_sum(half) for half in grad_upper]).reshape(pack_count, -1),
+                relative_slots(),
+                axis=0,
+            ).reshape(-1, width),
         ],
         axis=0,
     )
-    embed_grad = jnp.concatenate(
+    devices = pack_count * seq_count
+    small_cells = small_grad.reshape(small_rows, devices, -1).transpose(1, 0, 2).reshape(devices, 1, -1)
+    last_cells = jnp.concatenate(
         [
-            mm("rd,ri->di", grad_embed_rows, tokens),
-            jnp.pad(small_grad, ((0, BLOCK - small_rows), (0, 0))).T,
+            mm("rd,ri->di", grad_embed_rows, tokens).reshape(devices, -1, width),
+            jnp.pad(small_cells, ((0, 0), (0, 7), (0, width - small_cells.shape[2]))),
         ],
         axis=1,
     )
-    embed_pack_share = scatter_rows(embed_grad, 0)
-    embed_share = embed_pack_share[:, :patch_in].T
-    small_share = embed_pack_share[:, patch_in : patch_in + small_rows].T
+    all_pooled = pick(traded[:, :width].reshape(-1, seq_count, head_weight.shape[0]), seq_place, 1)
+    all_logits = traded[:, width:]
+    head_grad = mm("nd,nc->dc", all_pooled, all_logits)
+    bias_grad = pick(column_sum(all_logits).reshape(seq_count, -1), seq_place)
+    going = [
+        (down_sum, down_out),
+        (up_sum, up_out),
+        (late_sums[0], late_outs[0]),
+        (late_sums[1], late_outs[1]),
+        (last_sum, last_sum.start(last_cells)),
+    ]
+    while going:
+        going = [(each, each.step(sent)) for each, sent in going]
+        going = [(each, sent) for each, sent in going if sent is not None]
+    down_share, up_share = down_sum.finish(), up_sum.finish()
+    late_share = jnp.concatenate([each.finish() for each in late_sums], axis=1)
+    qkv_share, output_share = late_share[: qkv_weight.shape[1]], late_share[qkv_weight.shape[1] :]
+    last_share = last_sum.finish()
+    embed_share = last_share[: embed_weight.shape[1]].T
+    small_share = last_share[embed_weight.shape[1], : small_params.size].reshape(small_params.shape)
 
     shares = (qkv_share, output_share, up_share, down_share, embed_share, small_share, head_grad, bias_grad)
     square_sum = sum((jnp.sum(piece * piece) for piece in shares))
     sums = jnp.broadcast_to(jnp.stack([loss_part, square_sum])[:, None], (2, BLOCK))
-    sums = all_sum(all_sum(sums, "pack"), "seq")
+    sums = sum_all(sums)
     loss_value, square_total = sums[0, 0], sums[1, 0]
     grad_norm = jnp.sqrt(square_total)
     factor = jnp.minimum(1.0, CLIP_NORM / (grad_norm + 1e-06))
-    moments = (
-        MUON_MU * qkv_moment.T + factor * qkv_share,
-        MUON_MU * output_moment.T + factor * output_share,
-        MUON_MU * up_moment.T + factor * up_share,
-        MUON_MU * down_moment.T + factor * down_share,
-    )
-    iterates = [iterate.T for iterate in muon(moments)]
+    muon_shares = (qkv_share, output_share, up_share, down_share)
+    columns = MUON_MU * old_columns + factor * to_planes(muon_shares)
+    iterates = ortho(columns.reshape(-1, width)).reshape(columns.shape)
+    iterates = [iterate.T for iterate in from_planes(iterates, [m.shape[0] for m in muon_moments])]
+    moments = [
+        (MUON_MU * moment + factor * share).T for moment, share in zip(muon_moments, muon_shares)
+    ]
     new_qkv = muon_update(qkv_weight, iterates[0])
     new_output = muon_update(output_weight, iterates[1])
     new_up = muon_update(up_weight, iterates[2])
     new_down = muon_update(down_weight, iterates[3])
-    moments = [moment.T for moment in moments]
     count_float = step_count[0].astype(F32)
     new_embed, new_embed_first, new_embed_second = adam_update(
         embed_weight, embed_first, embed_second, embed_share, factor, count_float

time: 1090 us -> 872 us (0.80)
  waiting for transfers between devices: 413 us -> 219 us
  starting transfers between devices: 135 us -> 106 us
  local copies, waits for them, and re-layouts: 107 us -> 84.4 us
  between operations: 12.3 us -> 26.4 us
    ppermute x114 -> x83, waiting for transfers between devices: 413 us -> 219 us  [swap(): lax.ppermute(value, axis, [(i, i ^ bit) for i in range(lax.axis_size(axis...]
    select_n x17 -> x5, other arithmetic: 34.2 us -> 1.07 us  [the longest x2 0.92 us: by_core(): jnp.where(lax.axis_index('pack') & 1 == 0, jnp.stack([own, other], axis=d...]
    ppermute x114 -> x83, starting transfers between devices: 128 us -> 101 us  [swap(): lax.ppermute(value, axis, [(i, i ^ bit) for i in range(lax.axis_size(axis...]
    dynamic_slice x9 -> x3, local copies, waits for them, and re-layouts: 18.1 us -> 1.03 us  [pick(): return lax.dynamic_index_in_dim(value, index, dim, keepdims=False)]
    slice x4 -> x13, local copies, waits for them, and re-layouts: 1.01 us -> 15.9 us  [the longest x2 6.86 us: body(): up_full = [half[:, :, :hidden].reshape(-1, width) for half in (own, other)]]
    reduce_sum x5 -> x7, other arithmetic: 12.5 us -> 25.8 us  [column_sum(): return jnp.sum(rows.astype(F32), axis=0)]
    another operation x1 -> x20, other arithmetic: 0.09 us -> 12.7 us  [the longest x2 4.73 us: halves(): own = jnp.stack(self.parts)]
    add x19 -> x26, other arithmetic: 18.4 us -> 27.2 us  [the longest x13 21.1 us: join(): self.value = self.keep + swap(sent, 'pack', self.bit)]
  transfers between devices with their start and end apart: 116 -> 87, of which waited for: 41 -> 46; matrix products, arithmetic and copies ran while one was open for 36% -> 34% of each run, Pallas kernels for 7% -> 9%
where the time goes in v2:
time: 872 us; the launch traced here: 865 us
  waiting for transfers between devices  219 us (25%)
  matrix products  209 us (24%)
  other arithmetic  139 us (16%)
  starting transfers between devices  106 us (12%)
  local copies, waits for them, and re-layouts  84.4 us (10%)
  Pallas kernels  81.2 us (9%)
  between operations  26.4 us (3%)
    ppermute x83, waiting for transfers between devices, swap(): lax.ppermute(value, axis, [(i, i ^ bit) for i in range(lax.axis_size(axis...  219 us
    dot_general x25, matrix products, mm(): return jnp.einsum(spec, left, right, preferred_element_type=F32)  183 us
    ppermute x83, starting transfers between devices, swap(): lax.ppermute(value, axis, [(i, i ^ bit) for i in range(lax.axis_size(axis...  101 us
    pallas_call x1, Pallas kernels, attend_back(): pl.pallas_call(lambda *refs: attend_back_kernel(width, blocks, *refs), gr...  59.9 us
    reduce_sum x7, other arithmetic, column_sum(): return jnp.sum(rows.astype(F32), axis=0)  25.8 us
    unnamed x293, local copies, waits for them, and re-layouts  21.4 us
    pallas_call x1, Pallas kernels, attend(): pl.pallas_call(lambda *refs: attend_kernel(width, blocks, *refs), grid=(b...  21.3 us
    add x13, other arithmetic, join(): self.value = self.keep + swap(sent, 'pack', self.bit)  21.1 us
  transfers between devices with their start and end apart: 87, of which 46 were waited for; matrix products, arithmetic and copies ran while one was open for 34% of the time, Pallas kernels for 9%

profile of v2, /device:TPU:0, one launch (start us, length us, event | category | flops | bytes accessed | tf_op | source)
XLA Modules:
  0.0 864.8 jit_solution(2810840821667304594)
XLA Ops:
  11.3 5.0 collective-permute-start
  39.5 4.5 collective-permute-done.10
  54.8 13.1 %collective-permute-done.6 = bf16[4,112,768]{2,1,0:T(8,128)(2,1)S(1)} collective-permute-done((bf16[4,112,768]{2,1,0:T(8,128)(2,1)S(1)}, bf16[4,112,768]{2,1,0:T(8,128)(2,1)S(1)}, u32[]{:S(2)}, u32[]{:S(2)}) %collective-permute-start.6) | collective-permute-done | bytes 688160 | tf_op jit(solution)/shard_map/ppermute | solution.py:37
  72.7 13.8 %collective-permute-done.16 = bf16[96,768]{1,0:T(8,128)(2,1)S(1)} collective-permute-done((bf16[96,768]{1,0:T(8,128)(2,1)S(1)}, bf16[96,768]{1,0:T(8,128)(2,1)S(1)}, u32[]{:S(2)}, u32[]{:S(2)}) %collective-permute-start.16) | collective-permute-done | bytes 147488 | tf_op jit(solution)/shard_map/ppermute | solution.py:37
  86.9 4.5 collective-permute-done.17
  99.5 6.1 collective-permute-done.12
  105.6 15.2 %collective-permute-done.13 = bf16[4,120,768]{2,1,0:T(8,128)(2,1)} collective-permute-done((bf16[4,120,768]{2,1,0:T(8,128)(2,1)S(1)}, bf16[4,120,768]{2,1,0:T(8,128)(2,1)}, u32[]{:S(2)}, u32[]{:S(2)}) %collective-permute-start.13) | collective-permute-done | bytes 737312 | tf_op jit(solution)/shard_map/ppermute | solution.py:37
  124.3 10.3 %fusion.23 = bf16[1664,768]{1,0:T(8,128)(2,1)} fusion(bf16[3072,768]{1,0:T(8,128)(2,1)S(1)} %bitcast.429, s32[1664]{0:T(1024)S(1)} %get-tuple-element.256), kind=kOutput, calls=%fused_computation.75 | convolution fusion | flops 7858126848 | bytes 7281152 | tf_op jit(solution)/shard_map/rw,wi->ri/dot_general | solution.py:418
  153.2 4.1 add_reduce_fusion
  161.3 13.6 %add_convert_fusion.refs_0_ = bf16[1664,2304]{1,0:T(8,128)(2,1)} fusion(bf16[2304,768]{1,0:T(8,128)(2,1)} %bitcast.439, f32[2304]{0:T(1024)S(1)} %pad_maximum_fusion.16, f32[1664,768]{0,1:T(8,128)} %copy-done, f32[768]{0:T(1024)S(1)} %add.717, f32[768]{0:T(1024)S(1)} %mul.720, f32[1664]{0:T(1024)S(1)} %fusion.108, f32[1664]{0:T(1024)S(1)} %broadcast_multiply_fusion.2, ...), kind=kOutput, calls=%fused_computation.8 | convolution fusion | flops 5904138240 | bytes 16350208 | tf_op jit(solution)/shard_map/rd,ed->re/dot_general | solution.py:418
  175.0 21.3 %shard_map.426 = (bf16[1664,768]{1,0:T(8,128)(2,1)}, f32[13,12,128]{2,1,0:T(8,128)}) custom-call(bf16[1664,2304]{1,0:T(8,128)(2,1)} %add_convert_fusion.refs_0_, s32[13,1,128]{2,1,0:T(1,128)} %select_n.909.refs_1_.refs_3_, s32[1920,1]{1,0:T(8,128)} %broadcast_in_dim.236.refs_2_.refs_4_), custom_call_target="tpu_custom_call" | custom-call | flops 5888802816 | bytes 10223616 | tf_op jit(solution)/shard_map/pallas_call | solution.py:335
  205.6 7.8 multiply_convert_fusion.1
  213.4 3.6 slice.385
  217.0 9.5 %fusion.153 = f32[1664,768]{0,1:T(8,128)} fusion(bf16[1664,1536]{1,0:T(8,128)(2,1)S(1)} %get-tuple-element.270, bf16[1536,768]{1,0:T(8,128)(2,1)} %bitcast.42), kind=kOutput, calls=%fused_computation.478 | convolution fusion | flops 3925868544 | bytes 12582912 | tf_op jit(solution)/shard_map/rf,fd->rd/dot_general | solution.py:418
  226.5 9.8 %multiply_convert_fusion = (bf16[1664,1536]{1,0:T(8,128)(2,1)}, f32[1664,1536]{1,0:T(8,128)}) fusion(f32[1536]{0:T(1024)S(1)} %add.734, bf16[1664,768]{0,1:T(8,128)(2,1)S(1)} %add_convert_fusion.2, bf16[1536,768]{1,0:T(8,128)(2,1)S(1)} %bitcast.446), kind=kOutput, calls=%fused_computation.23 | convolution fusion | flops 3941203968 | bytes 20256768 | tf_op jit(solution)/shard_map/rd,fd->rf/dot_general | solution.py:418
  236.3 10.1 %fusion.151 = (f32[1664]{0:T(1024)S(1)}, f32[1664,768]{0,1:T(8,128)S(1)}) fusion(f32[768]{0:T(1024)S(1)} %add.740, f32[1664,768]{0,1:T(8,128)S(1)} %get-tuple-element.269, f32[1664,768]{0,1:T(8,128)} %fusion.153, bf16[1664,1536]{1,0:T(8,128)(2,1)} %get-tuple-element.272, bf16[1536,768]{1,0:T(8,128)(2,1)} %bitcast.44), kind=kOutput, calls=%fused_computation.476 | convolution fusion | flops 3930978816 | bytes 22816256 | tf_op jit(solution)/shard_map/rf,fd->rd/dot_general | solution.py:418
  248.7 3.4 fusion.66
  252.3 4.3 collective-permute-start.25
  267.1 5.6 fusion.39
  293.0 4.5 fusion.152
  297.5 6.1 copy.83
  303.5 5.5 multiply_reduce_fusion
  314.2 9.6 %fusion.156 = f32[1536,768]{1,0:T(8,128)} fusion(bf16[1664,1536]{1,0:T(8,128)(2,1)} %copy-done.114, bf16[1664,768]{0,1:T(8,128)(2,1)S(1)} %add_convert_fusion.4), kind=kOutput, calls=%fused_computation.481 | convolution fusion | flops 3925868544 | bytes 12386304 | tf_op jit(solution)/shard_map/rf,rd->fd/dot_general | solution.py:418
  323.8 6.4 fusion.155
  330.3 9.7 %fusion.6 = bf16[1664,1536]{1,0:T(8,128)(2,1)S(1)} fusion(bf16[1664,768]{0,1:T(8,128)(2,1)S(1)} %add_convert_fusion.4, bf16[1536,768]{1,0:T(8,128)(2,1)} %bitcast.42, f32[1664,1536]{1,0:T(8,128)S(1)} %bitcast.492, f32[1536]{0:T(1024)S(1)} %add.730), kind=kOutput, calls=%fused_computation.14 | convolution fusion | flops 3953983488 | bytes 20256768 | tf_op jit(solution)/shard_map/rd,fd->rf/dot_general | solution.py:418
  339.9 6.2 fusion.158
  346.2 9.5 %fusion.12 = bf16[1664,1536]{1,0:T(8,128)(2,1)S(1)} fusion(bf16[1664,768]{0,1:T(8,128)(2,1)S(1)} %add_convert_fusion.4, bf16[1536,768]{1,0:T(8,128)(2,1)} %bitcast.44, f32[1664,1536]{1,0:T(8,128)S(1)} %bitcast.494, f32[1536]{0:T(1024)S(1)} %add.734), kind=kOutput, calls=%fused_computation.20 | convolution fusion | flops 3953983488 | bytes 20256768 | tf_op jit(solution)/shard_map/rd,fd->rf/dot_general | solution.py:418
  355.8 6.6 fusion.157
  366.9 3.4 convert_reduce_fusion.1
  370.3 8.9 %fusion.159 = f32[1664,768]{0,1:T(8,128)S(1)} fusion(bf16[1664,1536]{1,0:T(8,128)(2,1)} %copy-done.18, bf16[1536,768]{1,0:T(8,128)(2,1)} %bitcast.444), kind=kOutput, calls=%fused_computation.484 | convolution fusion | flops 3925868544 | bytes 12582912 | tf_op jit(solution)/shard_map/rf,fd->rd/dot_general | solution.py:418
  379.3 8.9 %convolution_add_fusion.1 = f32[1664,768]{0,1:T(8,128)} fusion(f32[1664,768]{0,1:T(8,128)S(1)} %fusion.159, bf16[1664,1536]{1,0:T(8,128)(2,1)} %copy-done.19, bf16[1536,768]{1,0:T(8,128)(2,1)S(1)} %bitcast.447), kind=kOutput, calls=%fused_computation.71 | convolution fusion | flops 3927146496 | bytes 17694720 | tf_op jit(solution)/shard_map/rf,fd->rd/dot_general | solution.py:418
  392.0 4.7 add.767
  400.6 3.8 add.769
  412.8 3.6 convolution_convert_fusion.refs_1_
  423.4 59.9 %shard_map.427 = bf16[1664,2304]{1,0:T(8,128)(2,1)} custom-call(bf16[1664,2304]{1,0:T(8,128)(2,1)} %add_convert_fusion.refs_0_, bf16[1664,768]{1,0:T(8,128)(2,1)} %convolution_convert_fusion.refs_1_, f32[13,12,128]{2,1,0:T(8,128)} %get-tuple-element.97.refs_2_, s32[13,1,128]{2,1,0:T(1,128)} %select_n.909.refs_1_.refs_3_, ...), custom_call_target="tpu_custom_call" | custom-call | flops 14722007040 | bytes 20447232 | tf_op jit(solution)/shard_map/pallas_call | solution.py:362
  483.3 5.5 fusion.160
  504.2 11.3 %fusion.132 = f32[2304,768]{1,0:T(8,128)S(1)} fusion(bf16[1664,2304]{1,0:T(8,128)(2,1)} %shard_map.427, f32[1664,768]{0,1:T(8,128)} %copy-done, f32[768]{0:T(1024)S(1)} %copy-done.107, f32[768]{0:T(1024)S(1)} %copy-done.88, f32[1664]{0:T(1024)S(1)} %copy-done.77, f32[1664]{0:T(1024)S(1)} %copy-done.68, f32[768]{0:T(1024)S(1)} %copy-done.74), kind=kOutput, calls=%fused_computation.465 | convolution fusion | flops 5896470528 | bytes 19879936 | tf_op jit(solution)/shard_map/re,rd->ed/dot_general | solution.py:418
  522.1 9.8 %fusion.161 = f32[1664,768]{1,0:T(8,128)} fusion(bf16[1664,2304]{1,0:T(8,128)(2,1)} %shard_map.427, bf16[2304,768]{1,0:T(8,128)(2,1)S(1)} %bitcast.440), kind=kOutput, calls=%fused_computation.486 | convolution fusion | flops 5888802816 | bytes 16318464 | tf_op jit(solution)/shard_map/re,ed->rd/dot_general | solution.py:418
  537.0 4.3 convert_reduce_fusion
  544.7 3.5 collective-permute-done.56
  553.6 5.3 multiply_reduce_fusion.9
  558.9 7.4 collective-permute-done.57
  568.0 15.9 %collective-permute-done.54 = f32[2,96,768]{2,1,0:T(8,128)S(1)} collective-permute-done((f32[2,96,768]{2,1,0:T(8,128)S(1)}, f32[2,96,768]{2,1,0:T(8,128)S(1)}, u32[]{:S(2)}, u32[]{:S(2)}) %collective-permute-start.54) | collective-permute-done | bytes 589856 | tf_op jit(solution)/shard_map/ppermute | solution.py:37
  592.8 6.1 copy.92
  601.8 5.0 multiply_reduce_fusion.3
  607.0 4.2 multiply_reduce_fusion.2
  611.4 10.1 %convert_reduce_fusion.6 = (f32[768]{0:T(1024)S(1)}, bf16[1664,768]{0,1:T(8,128)(2,1)}) fusion(f32[1664]{0:T(1024)S(1)} %negate_multiply_fusion, f32[1664]{0:T(1024)S(1)} %multiply_multiply_fusion.6, f32[1664]{0:T(1024)S(1)} %copy-done.68, f32[1664,768]{0,1:T(8,128)} %copy-done, f32[768]{0:T(1024)S(1)} %copy-done.75, f32[1664]{0:T(1024)S(1)} %copy-done.78, ...), kind=kLoop, calls=%fused_computation.39 | loop fusion | flops 19168512 | bytes 23052288 | tf_op jit(solution)/shard_map/reduce_sum | solution.py:422
  621.7 4.8 fusion.162
  638.4 14.9 %collective-permute-done.45 = f32[2,4,96,384]{3,2,1,0:T(8,128)} collective-permute-done((f32[2,4,96,384]{3,2,1,0:T(8,128)}, f32[2,4,96,384]{3,2,1,0:T(8,128)}, u32[]{:S(2)}, u32[]{:S(2)}) %collective-permute-start.45) | collective-permute-done | bytes 1179680 | tf_op jit(solution)/shard_map/ppermute | solution.py:37
  663.7 6.8 collective-permute-done.46
  683.6 5.3 collective-permute-done.51
  693.0 4.4 collective-permute-done.52
  703.8 3.6 collective-permute-done.62
  736.5 6.2 collective-permute-done.71
  742.6 12.1 %collective-permute-done.72 = f32[96,768]{1,0:T(8,128)S(1)} collective-permute-done((f32[96,768]{1,0:T(8,128)S(1)}, f32[96,768]{1,0:T(8,128)S(1)}, u32[]{:S(2)}, u32[]{:S(2)}) %collective-permute-start.72) | collective-permute-done | bytes 294944 | tf_op jit(solution)/shard_map/ppermute | solution.py:37
  772.0 5.0 collective-permute-done.75
  777.0 5.9 collective-permute-done.76
  787.5 6.5 collective-permute-done.78
  793.9 3.8 collective-permute-done.79
  800.0 5.6 multiply_subtract_fusion
  814.4 3.7 fusion.30
  825.6 3.6 collective-permute-start.83
  830.6 5.0 collective-permute-done.82
  835.6 18.4 %collective-permute-done.83 = f32[96,768]{1,0:T(8,128)S(1)} collective-permute-done((f32[96,768]{1,0:T(8,128)S(1)}, f32[96,768]{1,0:T(8,128)S(1)}, u32[]{:S(2)}, u32[]{:S(2)}) %collective-permute-start.83) | collective-permute-done | bytes 294944 | tf_op jit(solution)/shard_map/ppermute | solution.py:37
  (719 shorter events, 311.8 us)
Async XLA Ops:
  7.2 259.9 %all-gather.3.cloned.1.call-start = ((), (), s32[]{:S(2)}) async-start(), calls=%async_computation | async-start | bytes 5406720 | tf_op jit(solution)/shard_map/all_gather | solution.py:603
  11.3 23.4 %collective-permute-start = (bf16[112,768]{1,0:T(8,128)(2,1)}, bf16[112,768]{1,0:T(8,128)(2,1)S(1)}, u32[]{:S(2)}, u32[]{:S(2)}) collective-permute-start(bf16[112,768]{1,0:T(8,128)(2,1)} %fusion.93), channel_id=1, source_target_pairs={{0,3},{1,2},{2,1},{3,0},{4,7},{5,6},{6,5},{7,4},{8,11},{9,10},{10,... | collective-permute-start | bytes 516104 | tf_op jit(solution)/shard_map/ppermute | solution.py:37
  16.3 19.7 %collective-permute-start.1 = (bf16[112,768]{1,0:T(8,128)(2,1)}, bf16[112,768]{1,0:T(8,128)(2,1)S(1)}, u32[]{:S(2)}, u32[]{:S(2)}) collective-permute-start(bf16[112,768]{1,0:T(8,128)(2,1)} %fusion.93), channel_id=1, source_target_pairs={{0,2},{1,3},{2,0},{3,1},{4,6},{5,7},{6,4},{7,5},{8,10},{9,11},{10,... | collective-permute-start | bytes 516104 | tf_op jit(solution)/shard_map/ppermute | solution.py:37
  16.3 19.7 %collective-permute-start.2 = (bf16[112,768]{1,0:T(8,128)(2,1)}, bf16[112,768]{1,0:T(8,128)(2,1)S(1)}, u32[]{:S(2)}, u32[]{:S(2)}) collective-permute-start(bf16[112,768]{1,0:T(8,128)(2,1)} %fusion.93), channel_id=1, source_target_pairs={{0,1},{1,0},{2,3},{3,2},{4,5},{5,4},{6,7},{7,6},{8,9},{9,8},{10,11... | collective-permute-start | bytes 516104 | tf_op jit(solution)/shard_map/ppermute | solution.py:37
  18.8 25.3 %collective-permute-start.10 = (bf16[120,768]{1,0:T(8,128)(2,1)S(1)}, bf16[120,768]{1,0:T(8,128)(2,1)}, u32[]{:S(2)}, u32[]{:S(2)}) collective-permute-start(bf16[120,768]{1,0:T(8,128)(2,1)S(1)} %pad_maximum_fusion.13), channel_id=1, source_target_pairs={{0,2},{1,3},{2,0},{3,1},{4,6},{5,7},{6,4},{7,5},{8,10},{9,11},{10,... | collective-permute-start | bytes 552968 | tf_op jit(solution)/shard_map/ppermute | solution.py:37
  21.2 26.8 %collective-permute-start.11 = (bf16[120,768]{1,0:T(8,128)(2,1)S(1)}, bf16[120,768]{1,0:T(8,128)(2,1)}, u32[]{:S(2)}, u32[]{:S(2)}) collective-permute-start(bf16[120,768]{1,0:T(8,128)(2,1)S(1)} %pad_maximum_fusion.13), channel_id=1, source_target_pairs={{0,1},{1,0},{2,3},{3,2},{4,5},{5,4},{6,7},{7,6},{8,9},{9,8},{10,11... | collective-permute-start | bytes 552968 | tf_op jit(solution)/shard_map/ppermute | solution.py:37
  34.7 16.2 %collective-permute-start.9 = (bf16[120,768]{1,0:T(8,128)(2,1)S(1)}, bf16[120,768]{1,0:T(8,128)(2,1)S(1)}, u32[]{:S(2)}, u32[]{:S(2)}) collective-permute-start(bf16[120,768]{1,0:T(8,128)(2,1)S(1)} %pad_maximum_fusion.13), channel_id=1, source_target_pairs={{0,3},{1,2},{2,1},{3,0},{4,7},{5,6},{6,5},{7,4},{8,11},{9,10},{10,... | collective-permute-start | bytes 552968 | tf_op jit(solution)/shard_map/ppermute | solution.py:37
  36.4 18.4 %collective-permute-start.5 = (bf16[4,112,768]{2,1,0:T(8,128)(2,1)S(1)}, bf16[4,112,768]{2,1,0:T(8,128)(2,1)S(1)}, u32[]{:S(2)}, u32[]{:S(2)}) collective-permute-start(bf16[4,112,768]{2,1,0:T(8,128)(2,1)S(1)} %pad_maximum_fusion.11), channel_id=1, source_target_pairs={{0,8},{4,12},{8,0},{12,4},{16,24},{20,28},{24,16},{28,20},{1,9},{5... | collective-permute-start | bytes 2064392 | tf_op jit(solution)/shard_map/ppermute | solution.py:37
  38.0 30.0 %collective-permute-start.6 = (bf16[4,112,768]{2,1,0:T(8,128)(2,1)S(1)}, bf16[4,112,768]{2,1,0:T(8,128)(2,1)S(1)}, u32[]{:S(2)}, u32[]{:S(2)}) collective-permute-start(bf16[4,112,768]{2,1,0:T(8,128)(2,1)S(1)} %pad_maximum_fusion.11), channel_id=1, source_target_pairs={{0,16},{4,20},{8,24},{12,28},{16,0},{20,4},{24,8},{28,12},{1,17},{... | collective-permute-start | bytes 2064392 | tf_op jit(solution)/shard_map/ppermute | solution.py:37
  44.0 23.9 %collective-permute-start.7 = (bf16[4,112,768]{2,1,0:T(8,128)(2,1)S(1)}, bf16[4,112,768]{2,1,0:T(8,128)(2,1)S(1)}, u32[]{:S(2)}, u32[]{:S(2)}) collective-permute-start(bf16[4,112,768]{2,1,0:T(8,128)(2,1)S(1)} %pad_maximum_fusion.11), channel_id=1, source_target_pairs={{0,24},{4,28},{8,16},{12,20},{16,8},{20,12},{24,0},{28,4},{1,25},{... | collective-permute-start | bytes 2064392 | tf_op jit(solution)/shard_map/ppermute | solution.py:37
  48.0 48.8 %collective-permute-start.3 = (bf16[6,128,768]{2,1,0:T(8,128)(2,1)}, bf16[6,128,768]{2,1,0:T(8,128)(2,1)}, u32[]{:S(2)}, u32[]{:S(2)}) collective-permute-start(bf16[6,128,768]{2,1,0:T(8,128)(2,1)} %get-tuple-element.202), channel_id=1, source_target_pairs={{0,1},{1,2},{2,3},{4,5},{5,6},{6,7},{8,9},{9,10},{10,11},{12,13},{... | collective-permute-start | bytes 3538952 | tf_op jit(solution)/shard_map/ppermute | solution.py:614
  50.9 46.1 %collective-permute-start.4 = (bf16[6,128,768]{2,1,0:T(8,128)(2,1)}, bf16[6,128,768]{2,1,0:T(8,128)(2,1)}, u32[]{:S(2)}, u32[]{:S(2)}) collective-permute-start(bf16[6,128,768]{2,1,0:T(8,128)(2,1)} %get-tuple-element.203), channel_id=1, source_target_pairs={{1,0},{2,1},{3,2},{5,4},{6,5},{7,6},{9,8},{10,9},{11,10},{13,12},{... | collective-permute-start | bytes 3538952 | tf_op jit(solution)/shard_map/ppermute | solution.py:615
  68.0 18.4 %collective-permute-start.16 = (bf16[96,768]{1,0:T(8,128)(2,1)S(1)}, bf16[96,768]{1,0:T(8,128)(2,1)S(1)}, u32[]{:S(2)}, u32[]{:S(2)}) collective-permute-start(bf16[96,768]{1,0:T(8,128)(2,1)S(1)} %copy-done.60), channel_id=1, source_target_pairs={{0,3},{1,2},{2,1},{3,0},{4,7},{5,6},{6,5},{7,4},{8,11},{9,10},{10,... | collective-permute-start | bytes 442376 | tf_op jit(solution)/shard_map/ppermute | solution.py:37
  70.4 21.0 %collective-permute-start.17 = (bf16[96,768]{1,0:T(8,128)(2,1)S(1)}, bf16[96,768]{1,0:T(8,128)(2,1)S(1)}, u32[]{:S(2)}, u32[]{:S(2)}) collective-permute-start(bf16[96,768]{1,0:T(8,128)(2,1)S(1)} %copy-done.60), channel_id=1, source_target_pairs={{0,2},{1,3},{2,0},{3,1},{4,6},{5,7},{6,4},{7,5},{8,10},{9,11},{10,... | collective-permute-start | bytes 442376 | tf_op jit(solution)/shard_map/ppermute | solution.py:37
  70.4 21.5 %collective-permute-start.18 = (bf16[96,768]{1,0:T(8,128)(2,1)S(1)}, bf16[96,768]{1,0:T(8,128)(2,1)S(1)}, u32[]{:S(2)}, u32[]{:S(2)}) collective-permute-start(bf16[96,768]{1,0:T(8,128)(2,1)S(1)} %copy-done.60), channel_id=1, source_target_pairs={{0,1},{1,0},{2,3},{3,2},{4,5},{5,4},{6,7},{7,6},{8,9},{9,8},{10,11... | collective-permute-start | bytes 442376 | tf_op jit(solution)/shard_map/ppermute | solution.py:37
  86.4 19.2 %collective-permute-start.12 = (bf16[4,120,768]{2,1,0:T(8,128)(2,1)S(1)}, bf16[4,120,768]{2,1,0:T(8,128)(2,1)}, u32[]{:S(2)}, u32[]{:S(2)}) collective-permute-start(bf16[4,120,768]{2,1,0:T(8,128)(2,1)S(1)} %pad_maximum_fusion.10), channel_id=1, source_target_pairs={{0,8},{4,12},{8,0},{12,4},{16,24},{20,28},{24,16},{28,20},{1,9},{5... | collective-permute-start | bytes 2211848 | tf_op jit(solution)/shard_map/ppermute | solution.py:37
  91.5 29.3 %collective-permute-start.13 = (bf16[4,120,768]{2,1,0:T(8,128)(2,1)S(1)}, bf16[4,120,768]{2,1,0:T(8,128)(2,1)}, u32[]{:S(2)}, u32[]{:S(2)}) collective-permute-start(bf16[4,120,768]{2,1,0:T(8,128)(2,1)S(1)} %pad_maximum_fusion.10), channel_id=1, source_target_pairs={{0,16},{4,20},{8,24},{12,28},{16,0},{20,4},{24,8},{28,12},{1,17},{... | collective-permute-start | bytes 2211848 | tf_op jit(solution)/shard_map/ppermute | solution.py:37
  92.0 28.8 %collective-permute-start.14 = (bf16[4,120,768]{2,1,0:T(8,128)(2,1)S(1)}, bf16[4,120,768]{2,1,0:T(8,128)(2,1)}, u32[]{:S(2)}, u32[]{:S(2)}) collective-permute-start(bf16[4,120,768]{2,1,0:T(8,128)(2,1)S(1)} %pad_maximum_fusion.10), channel_id=1, source_target_pairs={{0,24},{4,28},{8,16},{12,20},{16,8},{20,12},{24,0},{28,4},{1,25},{... | collective-permute-start | bytes 2211848 | tf_op jit(solution)/shard_map/ppermute | solution.py:37
  96.3 407.8 %all-gather.5.cloned.1.call-start = ((), (), s32[]{:S(2)}) async-start(), calls=%async_computation.1 | async-start | bytes 6881280 | tf_op jit(solution)/shard_map/all_gather | solution.py:676
  96.9 50.2 %collective-permute-start.8 = (bf16[4,4,112,768]{3,2,1,0:T(8,128)(2,1)}, bf16[4,4,112,768]{3,2,1,0:T(8,128)(2,1)S(1)}, u32[]{:S(2)}, u32[]{:S(2)}) collective-permute-start(bf16[4,4,112,768]{3,2,1,0:T(8,128)(2,1)} %get-tuple-element.195), channel_id=1, source_target_pairs={{0,4},{4,0},{8,12},{12,8},{16,20},{20,16},{24,28},{28,24},{1,5},{5... | collective-permute-start | bytes 8257544 | tf_op jit(solution)/shard_map/ppermute | solution.py:37
  120.8 21.9 %collective-permute-start.19 = (bf16[4,96,768]{2,1,0:T(8,128)(2,1)S(1)}, bf16[4,96,768]{2,1,0:T(8,128)(2,1)S(1)}, u32[]{:S(2)}, u32[]{:S(2)}) collective-permute-start(bf16[4,96,768]{2,1,0:T(8,128)(2,1)S(1)} %copy-done.33), channel_id=1, source_target_pairs={{0,8},{4,12},{8,0},{12,4},{16,24},{20,28},{24,16},{28,20},{1,9},{5... | collective-permute-start | bytes 1769480 | tf_op jit(solution)/shard_map/ppermute | solution.py:37
  120.8 24.6 %collective-permute-start.20 = (bf16[4,96,768]{2,1,0:T(8,128)(2,1)S(1)}, bf16[4,96,768]{2,1,0:T(8,128)(2,1)S(1)}, u32[]{:S(2)}, u32[]{:S(2)}) collective-permute-start(bf16[4,96,768]{2,1,0:T(8,128)(2,1)S(1)} %copy-done.33), channel_id=1, source_target_pairs={{0,16},{4,20},{8,24},{12,28},{16,0},{20,4},{24,8},{28,12},{1,17},{... | collective-permute-start | bytes 1769480 | tf_op jit(solution)/shard_map/ppermute | solution.py:37
  121.6 23.8 %collective-permute-start.21 = (bf16[4,96,768]{2,1,0:T(8,128)(2,1)S(1)}, bf16[4,96,768]{2,1,0:T(8,128)(2,1)S(1)}, u32[]{:S(2)}, u32[]{:S(2)}) collective-permute-start(bf16[4,96,768]{2,1,0:T(8,128)(2,1)S(1)} %copy-done.33), channel_id=1, source_target_pairs={{0,24},{4,28},{8,16},{12,20},{16,8},{20,12},{24,0},{28,4},{1,25},{... | collective-permute-start | bytes 1769480 | tf_op jit(solution)/shard_map/ppermute | solution.py:37
  137.5 58.7 %collective-permute-start.15 = (bf16[4,4,120,768]{3,2,1,0:T(8,128)(2,1)}, bf16[4,4,120,768]{3,2,1,0:T(8,128)(2,1)}, u32[]{:S(2)}, u32[]{:S(2)}) collective-permute-start(bf16[4,4,120,768]{3,2,1,0:T(8,128)(2,1)} %pad_maximum_fusion.2), channel_id=1, source_target_pairs={{0,4},{4,0},{8,12},{12,8},{16,20},{20,16},{24,28},{28,24},{1,5},{5... | collective-permute-start | bytes 8847368 | tf_op jit(solution)/shard_map/ppermute | solution.py:37
  147.1 89.2 %collective-permute-start.22 = (bf16[4,4,96,768]{3,2,1,0:T(8,128)(2,1)}, bf16[4,4,96,768]{3,2,1,0:T(8,128)(2,1)}, u32[]{:S(2)}, u32[]{:S(2)}) collective-permute-start(bf16[4,4,96,768]{3,2,1,0:T(8,128)(2,1)} %pad_maximum_fusion.4), channel_id=1, source_target_pairs={{0,4},{4,0},{8,12},{12,8},{16,20},{20,16},{24,28},{28,24},{1,5},{5... | collective-permute-start | bytes 7077896 | tf_op jit(solution)/shard_map/ppermute | solution.py:37
  355.7 36.3 %collective-permute-start.37 = (f32[2,2,4,96,768]{4,3,2,1,0:T(8,128)}, f32[2,2,4,96,768]{4,3,2,1,0:T(8,128)}, u32[]{:S(2)}, u32[]{:S(2)}) collective-permute-start(f32[2,2,4,96,768]{4,3,2,1,0:T(8,128)} %bitcast.64), channel_id=1, source_target_pairs={{0,4},{4,0},{8,12},{12,8},{16,20},{20,16},{24,28},{28,24},{1,5},{5... | collective-permute-start | bytes 14155784 | tf_op jit(solution)/shard_map/ppermute | solution.py:37
  362.4 38.2 %collective-permute-start.38 = (f32[2,2,4,96,768]{4,3,2,1,0:T(8,128)}, f32[2,2,4,96,768]{4,3,2,1,0:T(8,128)}, u32[]{:S(2)}, u32[]{:S(2)}) collective-permute-start(f32[2,2,4,96,768]{4,3,2,1,0:T(8,128)} %bitcast.67), channel_id=1, source_target_pairs={{0,4},{4,0},{8,12},{12,8},{16,20},{20,16},{24,28},{28,24},{1,5},{5... | collective-permute-start | bytes 14155784 | tf_op jit(solution)/shard_map/ppermute | solution.py:37
  416.5 79.5 %collective-permute-start.43 = (f32[2,4,96,768]{3,2,1,0:T(8,128)}, f32[2,4,96,768]{3,2,1,0:T(8,128)S(1)}, u32[]{:S(2)}, u32[]{:S(2)}) collective-permute-start(f32[2,4,96,768]{3,2,1,0:T(8,128)} %slice_bitcast_fusion.2), channel_id=1, source_target_pairs={{0,8},{4,12},{8,0},{12,4},{16,24},{20,28},{24,16},{28,20},{1,9},{5... | collective-permute-start | bytes 7077896 | tf_op jit(solution)/shard_map/ppermute | solution.py:37
  418.2 76.5 %collective-permute-start.39 = (f32[96,768]{1,0:T(8,128)}, f32[96,768]{1,0:T(8,128)S(1)}, u32[]{:S(2)}, u32[]{:S(2)}) collective-permute-start(f32[96,768]{1,0:T(8,128)} %get-tuple-element.228), channel_id=1, source_target_pairs={{0,1},{1,0},{2,3},{3,2},{4,5},{5,4},{6,7},{7,6},{8,9},{9,8},{10,11... | collective-permute-start | bytes 884744 | tf_op jit(solution)/shard_map/ppermute | solution.py:37
  418.8 75.9 %collective-permute-start.40 = (f32[96,768]{1,0:T(8,128)}, f32[96,768]{1,0:T(8,128)S(1)}, u32[]{:S(2)}, u32[]{:S(2)}) collective-permute-start(f32[96,768]{1,0:T(8,128)} %get-tuple-element.227), channel_id=1, source_target_pairs={{0,2},{1,3},{2,0},{3,1},{4,6},{5,7},{6,4},{7,5},{8,10},{9,11},{10,... | collective-permute-start | bytes 884744 | tf_op jit(solution)/shard_map/ppermute | solution.py:37
  420.8 74.0 %collective-permute-start.41 = (f32[96,768]{1,0:T(8,128)}, f32[96,768]{1,0:T(8,128)S(1)}, u32[]{:S(2)}, u32[]{:S(2)}) collective-permute-start(f32[96,768]{1,0:T(8,128)} %get-tuple-element.226), channel_id=1, source_target_pairs={{0,3},{1,2},{2,1},{3,0},{4,7},{5,6},{6,5},{7,4},{8,11},{9,10},{10,... | collective-permute-start | bytes 884744 | tf_op jit(solution)/shard_map/ppermute | solution.py:37
  422.6 77.0 %collective-permute-start.42 = (f32[2,4,96,768]{3,2,1,0:T(8,128)}, f32[2,4,96,768]{3,2,1,0:T(8,128)}, u32[]{:S(2)}, u32[]{:S(2)}) collective-permute-start(f32[2,4,96,768]{3,2,1,0:T(8,128)} %slice_bitcast_fusion.3), channel_id=1, source_target_pairs={{0,16},{4,20},{8,24},{12,28},{16,0},{20,4},{24,8},{28,12},{1,17},{... | collective-permute-start | bytes 7077896 | tf_op jit(solution)/shard_map/ppermute | solution.py:37
  519.4 65.9 %collective-permute-start.44 = (f32[2,2,4,96,768]{4,3,2,1,0:T(8,128)}, f32[2,2,4,96,768]{4,3,2,1,0:T(8,128)}, u32[]{:S(2)}, u32[]{:S(2)}) collective-permute-start(f32[2,2,4,96,768]{4,3,2,1,0:T(8,128)} %pad_maximum_fusion.1), channel_id=1, source_target_pairs={{0,4},{4,0},{8,12},{12,8},{16,20},{20,16},{24,28},{28,24},{1,5},{5... | collective-permute-start | bytes 14155784 | tf_op jit(solution)/shard_map/ppermute | solution.py:37
  519.4 28.7 %collective-permute-start.56 = (f32[4,96,768]{2,1,0:T(8,128)}, f32[4,96,768]{2,1,0:T(8,128)}, u32[]{:S(2)}, u32[]{:S(2)}) collective-permute-start(f32[4,96,768]{2,1,0:T(8,128)} %slice_bitcast_fusion.7), channel_id=1, source_target_pairs={{0,8},{4,12},{8,0},{12,4},{16,24},{20,28},{24,16},{28,20},{1,9},{5... | collective-permute-start | bytes 3538952 | tf_op jit(solution)/shard_map/ppermute | solution.py:37
  520.8 29.3 %collective-permute-start.53 = (f32[4,96,768]{2,1,0:T(8,128)}, f32[4,96,768]{2,1,0:T(8,128)}, u32[]{:S(2)}, u32[]{:S(2)}) collective-permute-start(f32[4,96,768]{2,1,0:T(8,128)} %slice_bitcast_fusion.6), channel_id=1, source_target_pairs={{0,16},{4,20},{8,24},{12,28},{16,0},{20,4},{24,8},{28,12},{1,17},{... | collective-permute-start | bytes 3538952 | tf_op jit(solution)/shard_map/ppermute | solution.py:37
  550.0 16.3 %collective-permute-start.57 = (f32[2,96,768]{2,1,0:T(8,128)S(1)}, f32[2,96,768]{2,1,0:T(8,128)S(1)}, u32[]{:S(2)}, u32[]{:S(2)}) collective-permute-start(f32[2,96,768]{2,1,0:T(8,128)S(1)} %dynamic-slice_bitcast_fusion.8), channel_id=1, source_target_pairs={{0,1},{1,0},{2,3},{3,2},{4,5},{5,4},{6,7},{7,6},{8,9},{9,8},{10,11... | collective-permute-start | bytes 1769480 | tf_op jit(solution)/shard_map/ppermute | solution.py:37
  551.5 32.4 %collective-permute-start.54 = (f32[2,96,768]{2,1,0:T(8,128)S(1)}, f32[2,96,768]{2,1,0:T(8,128)S(1)}, u32[]{:S(2)}, u32[]{:S(2)}) collective-permute-start(f32[2,96,768]{2,1,0:T(8,128)S(1)} %dynamic-slice_bitcast_fusion.9), channel_id=1, source_target_pairs={{0,1},{1,0},{2,3},{3,2},{4,5},{5,4},{6,7},{7,6},{8,9},{9,8},{10,11... | collective-permute-start | bytes 1769480 | tf_op jit(solution)/shard_map/ppermute | solution.py:37
  567.1 67.1 %collective-permute-start.58 = (f32[1,96,768]{2,1,0:T(8,128)}, f32[1,96,768]{2,1,0:T(8,128)}, u32[]{:S(2)}, u32[]{:S(2)}) collective-permute-start(f32[1,96,768]{2,1,0:T(8,128)} %constant_dynamic-slice_fusion.3), channel_id=1, source_target_pairs={{0,2},{1,3},{2,0},{3,1},{4,6},{5,7},{6,4},{7,5},{8,10},{9,11},{10,... | collective-permute-start | bytes 884744 | tf_op jit(solution)/shard_map/ppermute | solution.py:37
  584.8 51.8 %collective-permute-start.55 = (f32[1,96,768]{2,1,0:T(8,128)}, f32[1,96,768]{2,1,0:T(8,128)}, u32[]{:S(2)}, u32[]{:S(2)}) collective-permute-start(f32[1,96,768]{2,1,0:T(8,128)} %constant_dynamic-slice_fusion.4), channel_id=1, source_target_pairs={{0,2},{1,3},{2,0},{3,1},{4,6},{5,7},{6,4},{7,5},{8,10},{9,11},{10,... | collective-permute-start | bytes 884744 | tf_op jit(solution)/shard_map/ppermute | solution.py:37
  626.5 26.8 %collective-permute-start.45 = (f32[2,4,96,384]{3,2,1,0:T(8,128)}, f32[2,4,96,384]{3,2,1,0:T(8,128)}, u32[]{:S(2)}, u32[]{:S(2)}) collective-permute-start(f32[2,4,96,384]{3,2,1,0:T(8,128)} %dynamic-slice_bitcast_fusion.4), channel_id=1, source_target_pairs={{0,16},{4,20},{8,24},{12,28},{16,0},{20,4},{24,8},{28,12},{1,17},{... | collective-permute-start | bytes 3538952 | tf_op jit(solution)/shard_map/ppermute | solution.py:37
  629.3 31.9 %collective-permute-start.59 = (f32[2,2,4,32,768]{4,3,2,1,0:T(8,128)}, f32[2,2,4,32,768]{4,3,2,1,0:T(8,128)}, u32[]{:S(2)}, u32[]{:S(2)}) collective-permute-start(f32[2,2,4,32,768]{4,3,2,1,0:T(8,128)} %fusion.47), channel_id=1, source_target_pairs={{0,4},{4,0},{8,12},{12,8},{16,20},{20,16},{24,28},{28,24},{1,5},{5... | collective-permute-start | bytes 4718600 | tf_op jit(solution)/shard_map/ppermute | solution.py:37
  629.3 29.1 %collective-permute-start.49 = (f32[2,4,96,384]{3,2,1,0:T(8,128)}, f32[2,4,96,384]{3,2,1,0:T(8,128)}, u32[]{:S(2)}, u32[]{:S(2)}) collective-permute-start(f32[2,4,96,384]{3,2,1,0:T(8,128)} %dynamic-slice_bitcast_fusion.3), channel_id=1, source_target_pairs={{0,8},{4,12},{8,0},{12,4},{16,24},{20,28},{24,16},{28,20},{1,9},{5... | collective-permute-start | bytes 3538952 | tf_op jit(solution)/shard_map/ppermute | solution.py:37
  655.1 15.4 %collective-permute-start.46 = (f32[4,96,384]{2,1,0:T(8,128)S(1)}, f32[4,96,384]{2,1,0:T(8,128)S(1)}, u32[]{:S(2)}, u32[]{:S(2)}) collective-permute-start(f32[4,96,384]{2,1,0:T(8,128)S(1)} %dynamic-slice_bitcast_fusion.11), channel_id=1, source_target_pairs={{0,8},{4,12},{8,0},{12,4},{16,24},{20,28},{24,16},{28,20},{1,9},{5... | collective-permute-start | bytes 1769480 | tf_op jit(solution)/shard_map/ppermute | solution.py:37
  659.9 16.3 %collective-permute-start.50 = (f32[4,96,384]{2,1,0:T(8,128)S(1)}, f32[4,96,384]{2,1,0:T(8,128)S(1)}, u32[]{:S(2)}, u32[]{:S(2)}) collective-permute-start(f32[4,96,384]{2,1,0:T(8,128)S(1)} %dynamic-slice_bitcast_fusion.10), channel_id=1, source_target_pairs={{0,16},{4,20},{8,24},{12,28},{16,0},{20,4},{24,8},{28,12},{1,17},{... | collective-permute-start | bytes 1769480 | tf_op jit(solution)/shard_map/ppermute | solution.py:37
  662.9 28.5 %collective-permute-start.60 = (f32[2,4,32,768]{3,2,1,0:T(8,128)S(1)}, f32[2,4,32,768]{3,2,1,0:T(8,128)S(1)}, u32[]{:S(2)}, u32[]{:S(2)}) collective-permute-start(f32[2,4,32,768]{3,2,1,0:T(8,128)S(1)} %dynamic-slice_bitcast_fusion.7), channel_id=1, source_target_pairs={{0,16},{4,20},{8,24},{12,28},{16,0},{20,4},{24,8},{28,12},{1,17},{... | collective-permute-start | bytes 2359304 | tf_op jit(solution)/shard_map/ppermute | solution.py:37
  670.6 10.5 %collective-permute-start.47 = (f32[2,96,384]{2,1,0:T(8,128)S(1)}, f32[2,96,384]{2,1,0:T(8,128)S(1)}, u32[]{:S(2)}, u32[]{:S(2)}) collective-permute-start(f32[2,96,384]{2,1,0:T(8,128)S(1)} %dynamic-slice_bitcast_fusion.20), channel_id=1, source_target_pairs={{0,1},{1,0},{2,3},{3,2},{4,5},{5,4},{6,7},{7,6},{8,9},{9,8},{10,11... | collective-permute-start | bytes 884744 | tf_op jit(solution)/shard_map/ppermute | solution.py:37
  676.3 12.7 %collective-permute-start.51 = (f32[2,96,384]{2,1,0:T(8,128)S(1)}, f32[2,96,384]{2,1,0:T(8,128)S(1)}, u32[]{:S(2)}, u32[]{:S(2)}) collective-permute-start(f32[2,96,384]{2,1,0:T(8,128)S(1)} %dynamic-slice_bitcast_fusion.19), channel_id=1, source_target_pairs={{0,1},{1,0},{2,3},{3,2},{4,5},{5,4},{6,7},{7,6},{8,9},{9,8},{10,11... | collective-permute-start | bytes 884744 | tf_op jit(solution)/shard_map/ppermute | solution.py:37
  681.2 11.8 %collective-permute-start.48 = (f32[1,96,384]{2,1,0:T(8,128)S(1)}, f32[1,96,384]{2,1,0:T(8,128)S(1)}, u32[]{:S(2)}, u32[]{:S(2)}) collective-permute-start(f32[1,96,384]{2,1,0:T(8,128)S(1)} %constant_dynamic-slice_fusion.6), channel_id=1, source_target_pairs={{0,2},{1,3},{2,0},{3,1},{4,6},{5,7},{6,4},{7,5},{8,10},{9,11},{10,... | collective-permute-start | bytes 442376 | tf_op jit(solution)/shard_map/ppermute | solution.py:37
  689.0 8.3 collective-permute-start.52
  691.5 9.5 %collective-permute-start.61 = (f32[4,32,768]{2,1,0:T(8,128)S(1)}, f32[4,32,768]{2,1,0:T(8,128)S(1)}, u32[]{:S(2)}, u32[]{:S(2)}) collective-permute-start(f32[4,32,768]{2,1,0:T(8,128)S(1)} %dynamic-slice_bitcast_fusion.12), channel_id=1, source_target_pairs={{0,8},{4,12},{8,0},{12,4},{16,24},{20,28},{24,16},{28,20},{1,9},{5... | collective-permute-start | bytes 1179656 | tf_op jit(solution)/shard_map/ppermute | solution.py:37
  725.8 8.1 collective-permute-start.68
  730.7 11.9 %collective-permute-start.71 = (f32[96,768]{1,0:T(8,128)S(1)}, f32[96,768]{1,0:T(8,128)S(1)}, u32[]{:S(2)}, u32[]{:S(2)}) collective-permute-start(f32[96,768]{1,0:T(8,128)S(1)} %get-tuple-element.224), channel_id=1, source_target_pairs={{0,1},{1,0},{2,3},{3,2},{4,5},{5,4},{6,7},{7,6},{8,9},{9,8},{10,11... | collective-permute-start | bytes 884744 | tf_op jit(solution)/shard_map/ppermute | solution.py:37
  731.9 22.8 %collective-permute-start.72 = (f32[96,768]{1,0:T(8,128)S(1)}, f32[96,768]{1,0:T(8,128)S(1)}, u32[]{:S(2)}, u32[]{:S(2)}) collective-permute-start(f32[96,768]{1,0:T(8,128)S(1)} %get-tuple-element.223), channel_id=1, source_target_pairs={{0,2},{1,3},{2,0},{3,1},{4,6},{5,7},{6,4},{7,5},{8,10},{9,11},{10,... | collective-permute-start | bytes 884744 | tf_op jit(solution)/shard_map/ppermute | solution.py:37
  733.9 20.9 %collective-permute-start.73 = (f32[96,768]{1,0:T(8,128)S(1)}, f32[96,768]{1,0:T(8,128)S(1)}, u32[]{:S(2)}, u32[]{:S(2)}) collective-permute-start(f32[96,768]{1,0:T(8,128)S(1)} %get-tuple-element.222), channel_id=1, source_target_pairs={{0,3},{1,2},{2,1},{3,0},{4,7},{5,6},{6,5},{7,4},{8,11},{9,10},{10,... | collective-permute-start | bytes 884744 | tf_op jit(solution)/shard_map/ppermute | solution.py:37
  767.1 9.9 %collective-permute-start.75 = (f32[96,768]{1,0:T(8,128)S(1)}, f32[96,768]{1,0:T(8,128)S(1)}, u32[]{:S(2)}, u32[]{:S(2)}) collective-permute-start(f32[96,768]{1,0:T(8,128)S(1)} %get-tuple-element.220), channel_id=1, source_target_pairs={{0,8},{4,12},{8,0},{12,4},{16,24},{20,28},{24,16},{28,20},{1,9},{5... | collective-permute-start | bytes 884744 | tf_op jit(solution)/shard_map/ppermute | solution.py:37
  767.8 15.1 %collective-permute-start.76 = (f32[96,768]{1,0:T(8,128)S(1)}, f32[96,768]{1,0:T(8,128)S(1)}, u32[]{:S(2)}, u32[]{:S(2)}) collective-permute-start(f32[96,768]{1,0:T(8,128)S(1)} %get-tuple-element.219), channel_id=1, source_target_pairs={{0,16},{4,20},{8,24},{12,28},{16,0},{20,4},{24,8},{28,12},{1,17},{... | collective-permute-start | bytes 884744 | tf_op jit(solution)/shard_map/ppermute | solution.py:37
  768.0 14.9 %collective-permute-start.77 = (f32[96,768]{1,0:T(8,128)S(1)}, f32[96,768]{1,0:T(8,128)S(1)}, u32[]{:S(2)}, u32[]{:S(2)}) collective-permute-start(f32[96,768]{1,0:T(8,128)S(1)} %get-tuple-element.218), channel_id=1, source_target_pairs={{0,24},{4,28},{8,16},{12,20},{16,8},{20,12},{24,0},{28,4},{1,25},{... | collective-permute-start | bytes 884744 | tf_op jit(solution)/shard_map/ppermute | solution.py:37
  783.0 10.9 %collective-permute-start.78 = (f32[96,768]{1,0:T(8,128)S(1)}, f32[96,768]{1,0:T(8,128)S(1)}, u32[]{:S(2)}, u32[]{:S(2)}) collective-permute-start(f32[96,768]{1,0:T(8,128)S(1)} %fusion.85), channel_id=1, source_target_pairs={{0,24},{4,28},{8,16},{12,20},{16,8},{20,12},{24,0},{28,4},{1,25},{... | collective-permute-start | bytes 884744 | tf_op jit(solution)/shard_map/ppermute | solution.py:37
  784.2 13.5 %collective-permute-start.79 = (f32[96,768]{1,0:T(8,128)S(1)}, f32[96,768]{1,0:T(8,128)S(1)}, u32[]{:S(2)}, u32[]{:S(2)}) collective-permute-start(f32[96,768]{1,0:T(8,128)S(1)} %fusion.85), channel_id=1, source_target_pairs={{0,16},{4,20},{8,24},{12,28},{16,0},{20,4},{24,8},{28,12},{1,17},{... | collective-permute-start | bytes 884744 | tf_op jit(solution)/shard_map/ppermute | solution.py:37
  785.9 12.3 %collective-permute-start.80 = (f32[96,768]{1,0:T(8,128)S(1)}, f32[96,768]{1,0:T(8,128)S(1)}, u32[]{:S(2)}, u32[]{:S(2)}) collective-permute-start(f32[96,768]{1,0:T(8,128)S(1)} %fusion.85), channel_id=1, source_target_pairs={{0,8},{4,12},{8,0},{12,4},{16,24},{20,28},{24,16},{28,20},{1,9},{5... | collective-permute-start | bytes 884744 | tf_op jit(solution)/shard_map/ppermute | solution.py:37
  798.5 7.1 collective-permute-start.81
  823.8 11.8 %collective-permute-start.82 = (f32[96,768]{1,0:T(8,128)S(1)}, f32[96,768]{1,0:T(8,128)S(1)}, u32[]{:S(2)}, u32[]{:S(2)}) collective-permute-start(f32[96,768]{1,0:T(8,128)S(1)} %get-tuple-element.211), channel_id=1, source_target_pairs={{0,3},{1,2},{2,1},{3,0},{4,7},{5,6},{6,5},{7,4},{8,11},{9,10},{10,... | collective-permute-start | bytes 884744 | tf_op jit(solution)/shard_map/ppermute | solution.py:37
  825.6 28.4 %collective-permute-start.83 = (f32[96,768]{1,0:T(8,128)S(1)}, f32[96,768]{1,0:T(8,128)S(1)}, u32[]{:S(2)}, u32[]{:S(2)}) collective-permute-start(f32[96,768]{1,0:T(8,128)S(1)} %get-tuple-element.210), channel_id=1, source_target_pairs={{0,2},{1,3},{2,0},{3,1},{4,6},{5,7},{6,4},{7,5},{8,10},{9,11},{10,... | collective-permute-start | bytes 884744 | tf_op jit(solution)/shard_map/ppermute | solution.py:37
  829.2 24.8 %collective-permute-start.84 = (f32[96,768]{1,0:T(8,128)S(1)}, f32[96,768]{1,0:T(8,128)S(1)}, u32[]{:S(2)}, u32[]{:S(2)}) collective-permute-start(f32[96,768]{1,0:T(8,128)S(1)} %get-tuple-element.208), channel_id=1, source_target_pairs={{0,1},{1,0},{2,3},{3,2},{4,5},{5,4},{6,7},{7,6},{8,9},{9,8},{10,11... | collective-permute-start | bytes 884744 | tf_op jit(solution)/shard_map/ppermute | solution.py:37
  (162 other events, 1614.9 us)
Sparse Core Ops, SparseCore 0:
  96.4 80.1 all-gather.2
  363.7 126.0 all-gather.4

commit v3 on v2

--- a/solution.py
+++ b/solution.py
@@ -31,6 +31,7 @@
 LOW = jnp.bfloat16
 F32 = jnp.float32
 NEG = -1e30
+NO_COST = pl.CostEstimate(flops=0, bytes_accessed=0, transcendentals=0)
 
 
 def swap(value, axis, bit):
@@ -118,13 +119,19 @@
         return self.block
 
     def in_plane(self):
-        self.parts = list(hold(self.block, *[swap(self.block, "pack", k) for k in other_chips()]))
-        return self.parts[-1]
-
-    def whole(self):
-        mine = by_index(self.parts, lax.axis_index("pack") >> 1)
-        cells = by_core(mine, swap(mine, "pack", 1), 1)
-        return cells.reshape((-1,) + self.shard.shape)
+        self.parts = [self.block] + [swap(self.block, "pack", k) for k in other_chips()]
+
+    def pieces(self, spots):
+        own = jnp.stack(self.parts)
+        other = swap(own, "pack", 1)
+        chip = lax.axis_index("pack") >> 1
+        found = []
+        for here, there in zip(spots[:-1], spots[1:]):
+            both = [
+                by_index([half[k, :, here:there] for k in range(half.shape[0])], chip) for half in (own, other)
+            ]
+            found.append(by_core(*both, 1).reshape(-1, there - here, own.shape[-1]))
+        return found
 
     def halves(self):
         own = jnp.stack(self.parts)
@@ -133,68 +140,72 @@
 
 class Scatter:
     def __init__(self, order, width, relative=False):
-        count = lax.axis_size("pack")
-        self.left = [1 << b for b in reversed(range(count.bit_length() - 1))]
+        self.left = [1 << b for b in reversed(range(lax.axis_size("pack").bit_length() - 1))]
         chips = [b for b in self.left if b > 1]
         self.order = [1] + (chips if order == 0 else chips[::-1])
         self.relative, self.width = relative, width
 
-    def start(self, grad):
-        self.value = grad.reshape((2,) * len(self.left) + (lax.axis_size("seq"), -1, self.width))
-        return self.send()
-
     def start_halves(self, keep, send):
         self.left.remove(1)
-        self.order.remove(1)
+        self.bit = self.order.pop(0)
         shape = (2,) * len(self.left) + (lax.axis_size("seq"), -1, self.width)
-        self.bit, self.keep = 1, keep.reshape(shape)
+        self.keep = keep.reshape(shape)
         return send.reshape(shape)
 
     def start_joined(self, value):
         self.left.remove(1)
-        self.order.remove(1)
+        self.order.pop(0)
         self.value = value
         return self.send()
 
     def send(self):
-        self.bit = self.order.pop(0)
-        dim = self.left.index(self.bit)
-        self.left.remove(self.bit)
+        self.bit = bit = self.order.pop(0)
+        dim = self.left.index(bit)
+        self.left.remove(bit)
         if self.relative:
             self.keep = lax.index_in_dim(self.value, 0, dim, keepdims=False)
             return lax.index_in_dim(self.value, 1, dim, keepdims=False)
-        mine = (lax.axis_index("pack") & self.bit) // self.bit
+        mine = (lax.axis_index("pack") & bit) // bit
         self.keep = pick(self.value, mine, dim)
         return pick(self.value, 1 - mine, dim)
 
-    def join(self, sent):
+    def step(self, sent):
         self.value = self.keep + swap(sent, "pack", self.bit)
+        return self.send() if self.order else None
+
+    def finish(self, sent):
+        while sent is not None:
+            sent = self.step(sent)
+
+
+class SeqScatter:
+    def __init__(self, value):
+        self.value, self.bit = value, 1
+
+    def send(self):
+        tail = self.value.shape[-2:]
+        split = self.value.reshape((-1, 2) + tail)
+        mine = (lax.axis_index("seq") & self.bit) // self.bit
+        self.keep = pick(split, mine, 1)
+        return pick(split, 1 - mine, 1)
 
     def step(self, sent):
-        self.join(sent)
-        return self.send() if self.order else None
-
-    def finish(self):
-        value, count = self.value, lax.axis_size("seq")
-        tail = value.shape[1:]
-        bit = 1
-        while bit < count:
-            mine = (lax.axis_index("seq") & bit) // bit
-            value = value.reshape((-1, 2) + tail)
-            value = pick(value, mine, 1) + swap(pick(value, 1 - mine, 1), "seq", bit)
-            bit *= 2
-        return value.reshape(tail)
-
-
-def late_halves(qkv_grad, output_grad):
+        self.value = self.keep + swap(sent, "seq", self.bit)
+        self.bit *= 2
+        return self.send() if self.bit < lax.axis_size("seq") else None
+
+    def result(self):
+        return self.value.reshape(self.value.shape[-2:])
+
+
+def late_halves(*grads):
     seq_count, pack_count = lax.axis_size("seq"), lax.axis_size("pack")
     chips = (2,) * (pack_count.bit_length() - 2)
     core = lax.axis_index("pack") & 1
 
     def half(which):
         pieces = [
-            pick(grad.reshape(chips + (2, seq_count, -1, grad.shape[1])), which, len(chips))
-            for grad in (qkv_grad, output_grad)
+            pick(grad.reshape(chips + (2, seq_count, -1, grad.shape[1])), which, len(chips)) for grad in grads
         ]
         return jnp.concatenate(pieces, axis=-2)
 
@@ -220,10 +231,9 @@
     return by_core(mine, swap(mine, "pack", 1), 1).reshape(value.shape)
 
 
-def sum_all(value):
+def sum_plane(value):
     value = value + swap(value, "pack", 1)
-    value = tree_sum([value] + [swap(value, "pack", k) for k in other_chips()])
-    return all_sum(value, "seq")
+    return tree_sum([value] + [swap(value, "pack", k) for k in other_chips()])
 
 
 def _dot(left, right, dims):
@@ -246,32 +256,34 @@
 def _halves(value):
     lane = lax.broadcasted_iota(jnp.int32, value.shape, 1)
     zero = jnp.zeros_like(value)
-    return jnp.where(lane < HEAD_DIM, value, zero), jnp.where(lane < HEAD_DIM, zero, value)
-
-
-def _merge(low, high):
-    return jnp.concatenate([low[:HEAD_DIM], high[HEAD_DIM:]], axis=0).T
+    return jnp.concatenate(
+        [jnp.where(lane < HEAD_DIM, value, zero), jnp.where(lane < HEAD_DIM, zero, value)], axis=0
+    )
+
+
+def _merge(value):
+    return jnp.concatenate([value[:HEAD_DIM, :BLOCK], value[HEAD_DIM:, BLOCK:]], axis=0).T
 
 
 def attend_kernel(width, blocks, rows_ref, query_id_ref, key_id_ref, out_ref, log_ref):
     block = pl.program_id(0)
+    here = pl.ds(pl.multiple_of(block * BLOCK, BLOCK), BLOCK)
     allowed = key_id_ref[pl.ds(pl.multiple_of(block * BLOCK, BLOCK), 3 * BLOCK), :] == query_id_ref[0]
-    here = pl.ds(pl.multiple_of(block * BLOCK, BLOCK), BLOCK)
     for pair in range(width // PAIR):
         column = pair * PAIR
         queries = _halves(rows_ref[here, column : column + PAIR] * SCALE)
         keys = _window(rows_ref, block, blocks, width + column)
         values = _window(rows_ref, block, blocks, 2 * width + column)
         mixed = []
-        for half in range(2):
-            scores = jnp.where(allowed, _dot(keys, queries[half], NT), NEG)
+        for lanes in (slice(0, BLOCK), slice(BLOCK, 2 * BLOCK)):
+            scores = jnp.where(allowed, _dot(keys, queries[lanes], NT), NEG)
             top = jnp.max(scores, axis=0, keepdims=True)
             raised = jnp.exp(scores - top)
             total = jnp.sum(raised, axis=0, keepdims=True)
             probs = (raised * (1.0 / total)).astype(LOW)
+            log_ref[0, pair : pair + 1, lanes] = top + jnp.log(total)
             mixed.append(_dot(values, probs, TN))
-            log_ref[0, 2 * pair + half : 2 * pair + half + 1, :] = top + jnp.log(total)
-        out_ref[:, column : column + PAIR] = _merge(*mixed).astype(LOW)
+        out_ref[:, column : column + PAIR] = _merge(jnp.concatenate(mixed, axis=1)).astype(LOW)
 
 
 def attend_back_kernel(
@@ -287,30 +299,22 @@
     span = pl.ds(pl.multiple_of(block * BLOCK, BLOCK), 3 * BLOCK)
     here = pl.ds(pl.multiple_of(block * BLOCK, BLOCK), BLOCK)
     allowed = key_id_ref[span, :] == query_id_ref[0]
+    allowed = jnp.concatenate([allowed, allowed], axis=1)
     for pair in range(width // PAIR):
         column = pair * PAIR
-        queries = _halves(rows_ref[here, column : column + PAIR] * SCALE)
-        grads = _halves(grad_ref[here, column : column + PAIR])
+        lanes = slice(column, column + PAIR)
+        queries = _halves(rows_ref[here, lanes] * SCALE)
+        grads = _halves(grad_ref[here, lanes])
         keys = _window(rows_ref, block, blocks, width + column)
         values = _window(rows_ref, block, blocks, 2 * width + column)
-        probs_low, grad_scores, query_grads = [], [], []
-        for half in range(2):
-            scores = jnp.where(allowed, _dot(keys, queries[half], NT), NEG)
-            probs = jnp.exp(scores - log_ref[0, 2 * pair + half : 2 * pair + half + 1, :])
-            grad_probs = _dot(values, grads[half], NT)
-            inner = jnp.sum(probs * grad_probs, axis=0, keepdims=True)
-            grad_score = (probs * (grad_probs - inner)).astype(LOW)
-            probs_low.append(probs.astype(LOW))
-            grad_scores.append(grad_score)
-            query_grads.append(_dot(keys, grad_score, TN))
-        out_ref[here, column : column + PAIR] = (_merge(*query_grads) * SCALE).astype(LOW)
-        lanes = slice(column, column + PAIR)
-        key_sum[span, lanes] += _dot(
-            jnp.concatenate(grad_scores, axis=1), jnp.concatenate(queries, axis=0), NN
-        )
-        value_sum[span, lanes] += _dot(
-            jnp.concatenate(probs_low, axis=1), jnp.concatenate(grads, axis=0), NN
-        )
+        scores = jnp.where(allowed, _dot(keys, queries, NT), NEG)
+        probs = jnp.exp(scores - log_ref[0, pair : pair + 1, :])
+        grad_probs = _dot(values, grads, NT)
+        inner = jnp.sum(probs * grad_probs, axis=0, keepdims=True)
+        grad_scores = (probs * (grad_probs - inner)).astype(LOW)
+        out_ref[here, lanes] = (_merge(_dot(keys, grad_scores, TN)) * SCALE).astype(LOW)
+        key_sum[span, lanes] += _dot(grad_scores, queries, NN)
+        value_sum[span, lanes] += _dot(probs.astype(LOW), grads, NN)
 
     @pl.when(block == blocks - 1)
     def _():
@@ -342,16 +346,14 @@
         ],
         out_specs=[
             pl.BlockSpec((BLOCK, width), lambda i: (i, 0)),
-            pl.BlockSpec((1, heads, BLOCK), lambda i: (i, 0, 0)),
+            pl.BlockSpec((1, heads // 2, 2 * BLOCK), lambda i: (i, 0, 0)),
         ],
         out_shape=[
             jax.ShapeDtypeStruct((rows, width), LOW),
-            jax.ShapeDtypeStruct((blocks, heads, BLOCK), F32),
+            jax.ShapeDtypeStruct((blocks, heads // 2, 2 * BLOCK), F32),
         ],
         compiler_params=_params(),
-        cost_estimate=pl.CostEstimate(
-            flops=4 * rows * 3 * BLOCK * triple, bytes_accessed=8 * rows * width, transcendentals=rows * 3 * BLOCK * heads
-        ),
+        cost_estimate=NO_COST,
     )(qkv_rows, query_id, key_id)
 
 
@@ -365,7 +367,7 @@
         in_specs=[
             pl.BlockSpec((rows, triple), lambda i: (0, 0)),
             pl.BlockSpec((rows, width), lambda i: (0, 0)),
-            pl.BlockSpec((1, heads, BLOCK), lambda i: (i, 0, 0)),
+            pl.BlockSpec((1, heads // 2, 2 * BLOCK), lambda i: (i, 0, 0)),
             pl.BlockSpec((1, 1, BLOCK), lambda i: (i, 0, 0)),
             pl.BlockSpec((rows + 2 * BLOCK, 1), lambda i: (0, 0)),
         ],
@@ -376,9 +378,7 @@
             pltpu.VMEM((rows + 2 * BLOCK, width), F32),
         ],
         compiler_params=_params(),
-        cost_estimate=pl.CostEstimate(
-            flops=10 * rows * 3 * BLOCK * triple, bytes_accessed=16 * rows * width, transcendentals=rows * 3 * BLOCK * heads
-        ),
+        cost_estimate=NO_COST,
     )(qkv_rows, grad_rows, log_total, query_id, key_id)
 
 
@@ -388,9 +388,93 @@
     return centre * lax.rsqrt(spread + 1e-06) * gain_row + bias_row
 
 
-def norm_back(values, gain_row, bias_row, cotangent):
-    _, pullback = jax.vjp(layer_norm, values, gain_row, bias_row)
-    return pullback(cotangent)
+def norm_back_kernel(
+    groups, keep_sum, values_ref, cot_ref, more_ref, gain_ref, low_ref, sum_ref, out_ref=None
+):
+    @pl.when(pl.program_id(0) == 0)
+    def _():
+        sum_ref[...] = jnp.zeros_like(sum_ref)
+
+    values = values_ref[...]
+    if groups:
+        group = lax.broadcasted_iota(jnp.int32, (values.shape[0], groups), 1)
+        chosen = jnp.where(more_ref[...] == group, 1.0, 0.0)
+        cot = jnp.dot(chosen, cot_ref[...], precision=HIGHEST_PREC, preferred_element_type=F32)
+    else:
+        cot = cot_ref[...]
+    centre = values - jnp.mean(values, axis=-1, keepdims=True)
+    scale = lax.rsqrt(jnp.mean(centre * centre, axis=-1, keepdims=True) + 1e-06)
+    normed = centre * scale
+    scaled = cot * gain_ref[...]
+    grad = scale * (
+        scaled
+        - jnp.mean(scaled, axis=-1, keepdims=True)
+        - normed * jnp.mean(scaled * normed, axis=-1, keepdims=True)
+    )
+    if not groups:
+        grad = grad + more_ref[...]
+    low = grad.astype(LOW)
+    if keep_sum:
+        out_ref[...] = grad
+    low_ref[...] = low
+    for row, value in enumerate((cot * normed, cot, low.astype(F32))):
+        sum_ref[row : row + 1, :] += jnp.sum(value, axis=0, keepdims=True)
+
+
+def norm_back(values, gain_row, cotangent, more, keep_sum=True):
+    rows, width = values.shape
+    groups = cotangent.shape[0] if more.shape[1] == 1 else 0
+    tile = rows // 8
+    block = pl.BlockSpec((tile, width), lambda i: (i, 0))
+    line = pl.BlockSpec((1, width), lambda i: (0, 0))
+    out_specs = [block, pl.BlockSpec((8, width), lambda i: (0, 0))]
+    out_shape = [jax.ShapeDtypeStruct((rows, width), LOW), jax.ShapeDtypeStruct((8, width), F32)]
+    if keep_sum:
+        out_specs.append(block)
+        out_shape.append(jax.ShapeDtypeStruct((rows, width), F32))
+    return pl.pallas_call(
+        lambda *refs: norm_back_kernel(groups, keep_sum, *refs),
+        grid=(8,),
+        in_specs=[
+            block,
+            pl.BlockSpec((groups, width), lambda i: (0, 0)) if groups else block,
+            pl.BlockSpec((tile, 1), lambda i: (i, 0)) if groups else block,
+            line,
+        ],
+        out_specs=out_specs,
+        out_shape=out_shape,
+        compiler_params=_params(),
+        cost_estimate=NO_COST,
+    )(values, cotangent, more, gain_row[None])
+
+
+def small_kernel(spots_ref, first_ref, second_ref, last_ref, qkv_ref, up_ref, out_ref):
+    width, slots = out_ref.shape[1], spots_ref.shape[0]
+    out_ref[...] = jnp.zeros_like(out_ref)
+    rows = [(first_ref, 0), (first_ref, 1), (second_ref, 0), (second_ref, 1), (last_ref, 0), (last_ref, 1)]
+    rows += [(first_ref, 2), (qkv_ref, 0), (qkv_ref, 2), (second_ref, 2), (last_ref, 2)]
+    for row, (ref, which) in enumerate(rows):
+        if ref is qkv_ref:
+            out_ref[row : row + 1, :] = ref[:, which * width : (which + 1) * width]
+        else:
+            out_ref[row : row + 1, :] = ref[which : which + 1, :]
+    for slot in range(slots):
+        out_ref[pl.ds(16 + spots_ref[slot], 1), :] = up_ref[slot : slot + 1, :]
+
+
+def small_sums(first, second, last, qkv_sum, up_sums):
+    width, count = first.shape[1], lax.axis_size("pack")
+    spots = relative_packs() ^ lax.axis_index("pack")
+    up_sum = jnp.concatenate(up_sums).reshape(count, -1)
+    arrays = [first, second, last, qkv_sum[None], jnp.pad(up_sum, ((0, 0), (0, width - up_sum.shape[1])))]
+    return pl.pallas_call(
+        small_kernel,
+        in_specs=[pl.BlockSpec(memory_space=pltpu.SMEM)] + [pl.BlockSpec(memory_space=pltpu.VMEM)] * len(arrays),
+        out_specs=pl.BlockSpec(memory_space=pltpu.VMEM),
+        out_shape=jax.ShapeDtypeStruct((16 + count, width), F32),
+        compiler_params=pltpu.CompilerParams(vmem_limit_bytes=16 << 20),
+        cost_estimate=NO_COST,
+    )(spots, *arrays)
 
 
 def gelu(values):
@@ -572,47 +656,37 @@
     pack_count, pack_place = lax.axis_size("pack"), lax.axis_index("pack")
     small_rows = small_params.shape[0]
 
-    bundle = [embed_weight.T, qkv_weight.T, as_rows(small_params, width), as_rows(head_bias, width)]
+    bundle = [
+        embed_weight.T,
+        qkv_weight.T,
+        output_weight.T,
+        as_rows(small_params, width),
+        as_rows(head_bias, width),
+    ]
     spots = [0]
     for piece in bundle:
         spots.append(spots[-1] + piece.shape[0])
     first = Gather(jnp.concatenate([piece.astype(LOW) for piece in bundle]))
-    first_block = first.along_seq()
-    patches, first_there = hold(patches, first_block)
-    first_plane = first.in_plane()
-    second_shard, _ = hold(
-        jnp.concatenate([up_weight.T.astype(LOW), output_weight.T.astype(LOW)]), first_there
-    )
-    second = Gather(second_shard)
-    second.along_seq()
-    second.block, _ = hold(second.block, first_plane)
-    cells = first.whole()
-    embed_full, qkv_full, small_full, bias_full = (
-        cells[:, here:there] for here, there in zip(spots[:-1], spots[1:])
-    )
-    embed_full, qkv_full = embed_full.reshape(-1, width), qkv_full.reshape(-1, width)
-    gain_bias = from_rows(small_full, small_params.shape).astype(F32)
-    bias_full = lax.dynamic_slice_in_dim(bias_full, pack_place * seq_count, seq_count, 0)
-    bias_full = bias_full[:, 0, : head_bias.shape[0]].reshape(-1)
-    third_shard, _ = hold(down_weight.T.astype(LOW), second.block)
-    third = Gather(third_shard)
-    third_block = third.along_seq()
-    second_plane = second.in_plane()
-    third.block, _ = hold(third.block, second_plane)
-    head_shard, _ = hold(head_weight.astype(LOW), third_block)
-    head_full = lax.all_gather(head_shard, "seq", axis=0, tiled=True)
-    hidden = up_weight.shape[1]
-    own, other = second.halves()
-    up_full = [half[:, :, :hidden].reshape(-1, width) for half in (own, other)]
-    by_chip = by_index([own[k, :, hidden:] for k in range(own.shape[0])], pack_place >> 1)
-    other_chip = by_index([other[k, :, hidden:] for k in range(own.shape[0])], pack_place >> 1)
-    output_full = by_core(by_chip, other_chip, 1).reshape(-1, width)
-    third.in_plane()
-    down_full = [half.reshape(-1, width) for half in third.halves()]
-
+    up_gather, down_gather = Gather(up_weight.T.astype(LOW)), Gather(down_weight.T.astype(LOW))
+    first.along_seq()
+    first.block, patches = hold(first.block, patches)
+    first.in_plane()
     ends = seq_count - 1
     from_left = lax.ppermute(patches[:, shard_len - MAXLEN :], "seq", [(i, i + 1) for i in range(ends)])
     from_right = lax.ppermute(patches[:, :MAXLEN], "seq", [(i + 1, i) for i in range(ends)])
+    from_left, from_right, up_gather.shard = hold(from_left, from_right, up_gather.shard)
+    up_gather.along_seq()
+    *first.parts, up_gather.block, down_gather.shard = hold(*first.parts, up_gather.block, down_gather.shard)
+    embed_full, qkv_full, output_full, small_full, bias_full = first.pieces(spots)
+    embed_full, qkv_full, output_full = (
+        value.reshape(-1, width) for value in (embed_full, qkv_full, output_full)
+    )
+    (gain_bias,) = hold(from_rows(small_full, small_params.shape).astype(F32))
+    bias_full = lax.dynamic_slice_in_dim(bias_full, pack_place * seq_count, seq_count, 0)
+    bias_full = bias_full[:, 0, : head_bias.shape[0]].reshape(-1)
+    up_gather.in_plane()
+    down_gather.along_seq()
+
     window = jnp.concatenate([from_left, patches, from_right], axis=1).reshape(-1, patch_in)
     source, group, live, counts = deal_rows(lengths, keep_mask, shard_len)
     chosen = (source[:, None] == jnp.arange(window.shape[0], dtype=jnp.int32)[None, :]).astype(LOW)
@@ -626,10 +700,18 @@
     ).astype(F32)
 
     embedded = mm("ri,di->rd", tokens, embed_full) + gain_bias[6]
+    embedded, *up_gather.parts, down_gather.block, head_low = hold(
+        embedded, *up_gather.parts, down_gather.block, head_weight.astype(LOW)
+    )
+    down_gather.in_plane()
+    head_full = lax.all_gather(head_low, "seq", axis=0, tiled=True)
+    up_full = [half.reshape(-1, width) for half in up_gather.halves()]
     normed_one = layer_norm(embedded, gain_bias[0], gain_bias[1]).astype(LOW)
     qkv_bias = jnp.concatenate([gain_bias[7], jnp.zeros_like(gain_bias[7]), gain_bias[8]])
     qkv_rows = (mm("rd,ed->re", normed_one, qkv_full) + qkv_bias).astype(LOW)
     attn_low, log_total = attend(qkv_rows, query_id, key_id)
+    attn_low, *down_gather.parts = hold(attn_low, *down_gather.parts)
+    down_full = [half.reshape(-1, width) for half in down_gather.halves()]
     after_attn = embedded + mm("re,de->rd", attn_low, output_full) + gain_bias[9]
     normed_two = layer_norm(after_attn, gain_bias[2], gain_bias[3]).astype(LOW)
     up_bias = jnp.take(
@@ -675,15 +757,12 @@
     traded, pooled_grad = hold(jnp.concatenate([pooled_rows, grad_logits], axis=1), pooled_grad)
     traded = lax.all_gather(traded, "seq", axis=0, tiled=True)
 
-    grad_final = lax.dot_general(
-        member, pooled_grad, (TN, ((), ())), precision=HIGHEST_PREC, preferred_element_type=F32
-    )
-    grad_mlp, grad_gain_f, grad_bias_f = norm_back(after_mlp, gain_bias[4], gain_bias[5], grad_final)
-    grad_mlp_low = grad_mlp.astype(LOW)
+    grad_mlp_low, sums_last, grad_mlp = norm_back(
+        after_mlp, gain_bias[4], pooled_grad, jnp.where(live, group, -1)[:, None]
+    )
     down_sum, up_sum = Scatter(0, width, True), Scatter(1, width, True)
     half = width // 2
     late_sums = [Scatter(0, half), Scatter(1, half)]
-    last_sum = Scatter(0, width)
     down_out = mm("rf,rd->fd", active[1], grad_mlp_low)
     down_keep = mm("rf,rd->fd", active[0], grad_mlp_low)
     grad_mlp_low, down_out, down_keep = hold(grad_mlp_low, down_out, down_keep)
@@ -699,93 +778,93 @@
     grad_normed = mm("rf,fd->rd", grad_upper[0], up_full[0]) + mm("rf,fd->rd", grad_upper[1], up_full[1])
     down_out = down_sum.step(down_out)
     grad_normed, down_out = hold(grad_normed, down_out)
-    grad_two, grad_gain_2, grad_bias_2 = norm_back(after_attn, gain_bias[2], gain_bias[3], grad_normed)
-    grad_attn = grad_mlp + grad_two
-    grad_attn_low = grad_attn.astype(LOW)
+    grad_attn_low, sums_second, grad_attn = norm_back(
+        after_attn, gain_bias[2], grad_normed, grad_mlp
+    )
     grad_mixed = mm("rd,de->re", grad_attn_low, output_full).astype(LOW)
-    output_grad = mm("rd,re->de", grad_attn_low, attn_low)
     up_out = up_sum.step(up_out)
     muon_moments = [m.T for m in (qkv_moment, output_moment, up_moment, down_moment)]
     grad_mixed, up_out, *muon_moments = hold(grad_mixed, up_out, *muon_moments)
     old_columns = to_planes(muon_moments)
     grad_qkv = attend_back(qkv_rows, grad_mixed, log_total, query_id, key_id)
-    grad_qkv, traded, old_columns = hold(grad_qkv, traded, old_columns)
+    output_grad = mm("rd,re->de", grad_attn_low, attn_low)
     late_keep, late_out = late_halves(mm("re,rd->ed", grad_qkv, normed_one), output_grad)
     down_out, up_out = down_sum.step(down_out), up_sum.step(up_out)
     grad_qkv, late_out, down_out, up_out = hold(grad_qkv, late_out, down_out, up_out)
-    qkv_bias_grad = column_sum(grad_qkv)
     grad_normed = mm("re,ed->rd", grad_qkv, qkv_full)
     late = late_keep + swap(late_out, "pack", 1)
     late_outs = [
         each.start_joined(part) for each, part in zip(late_sums, (late[..., :half], late[..., half:]))
     ]
-    grad_normed, *late_outs = hold(grad_normed, *late_outs)
-    grad_one, grad_gain_1, grad_bias_1 = norm_back(embedded, gain_bias[0], gain_bias[1], grad_normed)
-    grad_embed_rows = (grad_attn + grad_one).astype(LOW)
-    small_grad = jnp.concatenate(
-        [
-            jnp.stack(
-                [
-                    grad_gain_1,
-                    grad_bias_1,
-                    grad_gain_2,
-                    grad_bias_2,
-                    grad_gain_f,
-                    grad_bias_f,
-                    column_sum(grad_embed_rows),
-                    qkv_bias_grad[:width],
-                    qkv_bias_grad[2 * width :],
-                    column_sum(grad_attn_low),
-                    column_sum(grad_mlp_low),
-                ]
-            ),
-            jnp.take(
-                jnp.concatenate([column_sum(half) for half in grad_upper]).reshape(pack_count, -1),
-                relative_slots(),
-                axis=0,
-            ).reshape(-1, width),
-        ],
-        axis=0,
-    )
-    devices = pack_count * seq_count
-    small_cells = small_grad.reshape(small_rows, devices, -1).transpose(1, 0, 2).reshape(devices, 1, -1)
-    last_cells = jnp.concatenate(
-        [
-            mm("rd,ri->di", grad_embed_rows, tokens).reshape(devices, -1, width),
-            jnp.pad(small_cells, ((0, 0), (0, 7), (0, width - small_cells.shape[2]))),
-        ],
-        axis=1,
+    grad_normed, late_outs[0], late_outs[1], down_sum.keep, up_sum.keep = hold(
+        grad_normed, *late_outs, down_sum.keep, up_sum.keep
+    )
+    grad_embed_rows, sums_first = norm_back(embedded, gain_bias[0], grad_normed, grad_attn, keep_sum=False)
+    last_keep, last_out = late_halves(mm("rd,ri->di", grad_embed_rows, tokens))
+    down_sum.finish(down_out)
+    up_sum.finish(up_out)
+    early_sum = SeqScatter(jnp.concatenate([down_sum.value, up_sum.value], axis=1))
+    early_out = early_sum.send()
+    last_out, early_out, late_sums[0].keep, late_sums[1].keep, grad_qkv, traded, old_columns = hold(
+        last_out, early_out, late_sums[0].keep, late_sums[1].keep, grad_qkv, traded, old_columns
     )
     all_pooled = pick(traded[:, :width].reshape(-1, seq_count, head_weight.shape[0]), seq_place, 1)
     all_logits = traded[:, width:]
     head_grad = mm("nd,nc->dc", all_pooled, all_logits)
     bias_grad = pick(column_sum(all_logits).reshape(seq_count, -1), seq_place)
-    going = [
-        (down_sum, down_out),
-        (up_sum, up_out),
-        (late_sums[0], late_outs[0]),
-        (late_sums[1], late_outs[1]),
-        (last_sum, last_sum.start(last_cells)),
+    qkv_sum = column_sum(grad_qkv)
+    late_outs = [each.step(sent) for each, sent in zip(late_sums, late_outs)]
+    last = last_keep + swap(last_out, "pack", 1)
+    last = last.reshape((pack_count // 2,) + last.shape[-3:])
+    last_outs = [pick(last, (pack_place ^ k) >> 1) for k in other_chips()]
+    early_out = early_sum.step(early_out)
+    head_grad, bias_grad, qkv_sum, early_out, grad_upper[0], grad_upper[1], *sends = hold(
+        head_grad, bias_grad, qkv_sum, early_out, *grad_upper, *late_outs, *last_outs
+    )
+    small_mine = small_sums(
+        sums_first, sums_second, sums_last, qkv_sum, [column_sum(side) for side in grad_upper]
+    )
+    for each, sent in zip(late_sums, sends[:2]):
+        each.finish(sent)
+    last_parts = [pick(last, pack_place >> 1)] + [
+        swap(sent, "pack", k) for k, sent in zip(other_chips(), sends[2:])
     ]
-    while going:
-        going = [(each, each.step(sent)) for each, sent in going]
-        going = [(each, sent) for each, sent in going if sent is not None]
-    down_share, up_share = down_sum.finish(), up_sum.finish()
-    late_share = jnp.concatenate([each.finish() for each in late_sums], axis=1)
-    qkv_share, output_share = late_share[: qkv_weight.shape[1]], late_share[qkv_weight.shape[1] :]
-    last_share = last_sum.finish()
-    embed_share = last_share[: embed_weight.shape[1]].T
-    small_share = last_share[embed_weight.shape[1], : small_params.size].reshape(small_params.shape)
-
-    shares = (qkv_share, output_share, up_share, down_share, embed_share, small_share, head_grad, bias_grad)
+    late_sum = SeqScatter(
+        jnp.concatenate(
+            [jnp.concatenate([each.value for each in late_sums], axis=2), tree_sum(last_parts)], axis=1
+        )
+    )
+    late_out, small_mine = hold(late_sum.send(), small_mine)
+    small_total = sum_plane(small_mine)
+    while early_out is not None:
+        early_out = early_sum.step(early_out)
+    late_out = late_sum.step(late_out)
+    while late_out is not None:
+        late_out = late_sum.step(late_out)
+    small_total = all_sum(small_total, "seq")
+    down_share, up_share = jnp.split(early_sum.result(), 2)
+    late_share = late_sum.result()
+    widths = [qkv_weight.shape[1], output_weight.shape[1], embed_weight.shape[1]]
+    qkv_share, output_share = late_share[: widths[0]], late_share[widths[0] : widths[0] + widths[1]]
+    embed_share = late_share[widths[0] + widths[1] :].T
+    hidden = down_weight.shape[1] * seq_count
+    small_total = jnp.concatenate(
+        [small_total[:11], small_total[16:, :hidden].reshape(small_rows - 11, width)], axis=0
+    )
+    place = pack_place * seq_count + seq_place
+    small_share = pick(small_total.reshape(small_rows, pack_count * seq_count, -1), place, 1)
+
+    shares = (early_sum.result(), late_share, head_grad, bias_grad)
     square_sum = sum((jnp.sum(piece * piece) for piece in shares))
     sums = jnp.broadcast_to(jnp.stack([loss_part, square_sum])[:, None], (2, BLOCK))
-    sums = sum_all(sums)
-    loss_value, square_total = sums[0, 0], sums[1, 0]
+    sums = sum_plane(sums)
+    muon_shares = (qkv_share, output_share, up_share, down_share)
+    new_columns, sums = hold(to_planes(muon_shares), sums)
+    sums = all_sum(sums, "seq")
+    loss_value, square_total = sums[0, 0], sums[1, 0] + jnp.sum(small_total * small_total)
     grad_norm = jnp.sqrt(square_total)
     factor = jnp.minimum(1.0, CLIP_NORM / (grad_norm + 1e-06))
-    muon_shares = (qkv_share, output_share, up_share, down_share)
-    columns = MUON_MU * old_columns + factor * to_planes(muon_shares)
+    columns = MUON_MU * old_columns + factor * new_columns
     iterates = ortho(columns.reshape(-1, width)).reshape(columns.shape)
     iterates = [iterate.T for iterate in from_planes(iterates, [m.shape[0] for m in muon_moments])]
     moments = [

time: 872 us -> 807 us (0.925)
  other arithmetic: 139 us -> 99.2 us
  matrix products: 209 us -> 184 us
  Pallas kernels: 81.2 us -> 103 us
  local copies, waits for them, and re-layouts: 84.4 us -> 64 us
  starting transfers between devices: 106 us -> 123 us
  waiting for transfers between devices: 219 us -> 203 us
    pallas_call x0 -> x4, Pallas kernels: none -> 34.6 us  [the longest x3 34.1 us: norm_back(): pl.pallas_call(lambda *refs: norm_back_kernel(groups, keep_sum, *refs), g...]
    ppermute x83 -> x85, waiting for transfers between devices: 219 us -> 184 us  [swap(): lax.ppermute(value, axis, [(i, i ^ bit) for i in range(lax.axis_size(axis...]
    dot_general x25, matrix products: 183 us -> 162 us  [mm(): return jnp.einsum(spec, left, right, preferred_element_type=F32)]
    reduce_sum x5 -> x1, other arithmetic: 19.8 us -> 0.62 us  [body(): jnp.sum(small_total * small_total)]
    reduce_sum x7 -> x4, other arithmetic: 25.8 us -> 6.74 us  [column_sum(): return jnp.sum(rows.astype(F32), axis=0)]
    ppermute x83 -> x85, starting transfers between devices: 101 us -> 119 us  [swap(): lax.ppermute(value, axis, [(i, i ^ bit) for i in range(lax.axis_size(axis...]
    ppermute x1, waiting for transfers between devices: 0.01 us -> 13.7 us  [body(): lax.ppermute(patches[:, shard_len - MAXLEN:], 'seq', [(i, i + 1) for i in...]
    pallas_call x1, Pallas kernels: 59.9 us -> 46.9 us  [attend_back(): pl.pallas_call(lambda *refs: attend_back_kernel(width, blocks, *refs), gr...]
  transfers between devices with their start and end apart: 87 -> 89, of which waited for: 46 -> 40; matrix products, arithmetic and copies ran while one was open for 34% -> 29% of each run, Pallas kernels for 9% -> 11%
where the time goes in v3:
time: 807 us; the launch traced here: 801 us
  waiting for transfers between devices  203 us (25%)
  matrix products  184 us (23%)
  starting transfers between devices  123 us (15%)
  Pallas kernels  103 us (13%)
  other arithmetic  99.2 us (12%)
  local copies, waits for them, and re-layouts  64 us (8%)
  between operations  24.5 us (3%)
    ppermute x85, waiting for transfers between devices, swap(): lax.ppermute(value, axis, [(i, i ^ bit) for i in range(lax.axis_size(axis...  184 us
    dot_general x25, matrix products, mm(): return jnp.einsum(spec, left, right, preferred_element_type=F32)  162 us
    ppermute x85, starting transfers between devices, swap(): lax.ppermute(value, axis, [(i, i ^ bit) for i in range(lax.axis_size(axis...  119 us
    pallas_call x1, Pallas kernels, attend_back(): pl.pallas_call(lambda *refs: attend_back_kernel(width, blocks, *refs), gr...  46.9 us
    pallas_call x3, Pallas kernels, norm_back(): pl.pallas_call(lambda *refs: norm_back_kernel(groups, keep_sum, *refs), g...  34.1 us
    pallas_call x1, Pallas kernels, attend(): pl.pallas_call(lambda *refs: attend_kernel(width, blocks, *refs), grid=(b...  21.3 us
    unnamed x297, local copies, waits for them, and re-layouts  17.3 us
  transfers between devices with their start and end apart: 89, of which 40 were waited for; matrix products, arithmetic and copies ran while one was open for 29% of the time, Pallas kernels for 11%

profile of v3, /device:TPU:0, one launch (start us, length us, event | category | flops | bytes accessed | tf_op | source)
XLA Modules:
  0.0 800.6 jit_solution(7349538203790517765)
XLA Ops:
  11.5 5.1 collective-permute-start
  25.0 9.5 %collective-permute-done.1 = bf16[136,768]{1,0:T(8,128)(2,1)} collective-permute-done((bf16[136,768]{1,0:T(8,128)(2,1)S(1)}, bf16[136,768]{1,0:T(8,128)(2,1)}, u32[]{:S(2)}, u32[]{:S(2)}) %collective-permute-start.1) | collective-permute-done | bytes 208928 | tf_op jit(solution)/shard_map/ppermute | solution.py:38
  50.1 13.7 %collective-permute-done.3 = bf16[6,128,768]{2,1,0:T(8,128)(2,1)} collective-permute-done((bf16[6,128,768]{2,1,0:T(8,128)(2,1)}, bf16[6,128,768]{2,1,0:T(8,128)(2,1)}, u32[]{:S(2)}, u32[]{:S(2)}) %collective-permute-start.3) | collective-permute-done | bytes 1179680 | tf_op jit(solution)/shard_map/ppermute | solution.py:675
  63.8 5.1 collective-permute-done.4
  79.3 4.8 collective-permute-done.9
  85.8 10.3 %fusion.23 = bf16[1664,768]{1,0:T(8,128)(2,1)} fusion(bf16[3072,768]{1,0:T(8,128)(2,1)S(1)} %bitcast.446, s32[1664]{0:T(1024)S(1)} %get-tuple-element.362), kind=kOutput, calls=%fused_computation.57 | convolution fusion | flops 7858126848 | bytes 7281152 | tf_op jit(solution)/shard_map/rw,wi->ri/dot_general | solution.py:502
  96.1 5.0 collective-permute-start.15
  107.4 6.2 collective-permute-done.16
  125.9 4.6 convolution_add_fusion.1.refs_0_
  130.4 3.7 collective-permute-done.13
  138.2 3.4 pad_maximum_fusion.3
  145.8 3.1 multiply_reduce_fusion.2
  155.2 11.6 %add_convert_fusion.refs_0_ = bf16[1664,2304]{1,0:T(8,128)(2,1)} fusion(bf16[2304,768]{1,0:T(8,128)(2,1)} %bitcast.451, f32[2304]{0:T(1024)S(1)} %pad_maximum_fusion.17, f32[1664,768]{1,0:T(8,128)} %convolution_add_fusion.1.refs_0_, f32[768]{0:T(1024)S(1)} %copy-done.106, f32[768]{0:T(1024)S(1)} %copy-done.108, f32[1664]{0:T(1024)S(1)} %add_rsqrt_fusion.2, ...), kind=kOutput, calls=%fused_computation.7 | convolution fusion | flops 5902860288 | bytes 16347136 | tf_op jit(solution)/shard_map/rd,ed->re/dot_general | solution.py:502
  166.8 21.3 %shard_map.435 = (bf16[1664,768]{1,0:T(8,128)(2,1)}, f32[13,6,256]{2,1,0:T(8,128)}) custom-call(bf16[1664,2304]{1,0:T(8,128)(2,1)} %add_convert_fusion.refs_0_, s32[13,1,128]{2,1,0:T(1,128)} %select_n.1475.refs_1_.refs_3_, s32[1920,1]{1,0:T(8,128)} %broadcast_in_dim.211.refs_2_.refs_4_), custom_call_target="tpu_custom_call" | custom-call | tf_op jit(solution)/shard_map/pallas_call | solution.py:339
  188.2 4.2 fusion.130
  197.9 8.9 %multiply_convert_fusion.1 = (bf16[1664,1536]{1,0:T(8,128)(2,1)S(1)}, f32[1664,1536]{1,0:T(8,128)}) fusion(f32[1536]{0:T(1024)S(1)} %add.714, bf16[1664,768]{1,0:T(8,128)(2,1)S(1)} %add_convert_fusion.1, bf16[1536,768]{1,0:T(8,128)(2,1)} %bitcast.41), kind=kOutput, calls=%fused_computation.24 | convolution fusion | flops 3941203968 | bytes 20256768 | tf_op jit(solution)/shard_map/rd,fd->rf/dot_general | solution.py:502
  206.7 4.2 fusion.132
  211.0 9.1 %multiply_convert_fusion = (bf16[1664,1536]{1,0:T(8,128)(2,1)S(1)}, f32[1664,1536]{1,0:T(8,128)}) fusion(f32[1536]{0:T(1024)S(1)} %add.718, bf16[1664,768]{1,0:T(8,128)(2,1)S(1)} %add_convert_fusion.1, bf16[1536,768]{1,0:T(8,128)(2,1)} %bitcast.47), kind=kOutput, calls=%fused_computation.22 | convolution fusion | flops 3941203968 | bytes 20256768 | tf_op jit(solution)/shard_map/rd,fd->rf/dot_general | solution.py:502
  220.1 4.8 fusion.131
  230.3 5.0 collective-permute-start.23
  237.8 4.3 collective-permute-done.24
  250.7 5.6 fusion.43
  276.5 11.5 %shard_map.436 = (bf16[1664,768]{1,0:T(8,128)(2,1)}, f32[8,768]{1,0:T(8,128)}, f32[1664,768]{1,0:T(8,128)}) custom-call(f32[1664,768]{1,0:T(8,128)} %copy-done.4, f32[96,768]{1,0:T(8,128)} %maximum_divide_fusion.refs_1_, s32[1664,1]{1,0:T(8,128)} %select_n.1609.refs_2_, f32[1,768]{1,0:T(1,128)} %get-tuple-element.347.refs_3_), custom_call_target="tpu_custom_call" | custom-call | tf_op jit(solution)/shard_map/pallas_call | solution.py:435
  288.0 10.1 %fusion.135 = f32[1536,768]{1,0:T(8,128)} fusion(bf16[1664,1536]{1,0:T(8,128)(2,1)} %copy-done.122, bf16[1664,768]{1,0:T(8,128)(2,1)} %get-tuple-element.129), kind=kOutput, calls=%fused_computation.451 | convolution fusion | flops 3925868544 | bytes 12386304 | tf_op jit(solution)/shard_map/rf,rd->fd/dot_general | solution.py:502
  298.1 6.2 fusion.134
  304.4 7.3 fusion.6
  311.7 6.6 fusion.137
  318.3 9.3 %fusion.12 = bf16[1664,1536]{1,0:T(8,128)(2,1)S(1)} fusion(bf16[1664,768]{1,0:T(8,128)(2,1)S(1)} %copy-done.118, bf16[1536,768]{1,0:T(8,128)(2,1)S(1)} %bitcast.485, f32[1664,1536]{1,0:T(8,128)} %get-tuple-element.377, f32[1536]{0:T(1024)S(1)} %add.718), kind=kOutput, calls=%fused_computation.19 | convolution fusion | flops 3953983488 | bytes 20256768 | tf_op jit(solution)/shard_map/rd,fd->rf/dot_general | solution.py:502
  327.6 4.6 fusion.136
  335.5 6.9 fusion.138
  342.4 7.9 convolution_add_fusion.2.refs_1_
  350.4 3.1 copy_add_fusion
  362.3 12.1 %shard_map.437 = (bf16[1664,768]{1,0:T(8,128)(2,1)}, f32[8,768]{1,0:T(8,128)}, f32[1664,768]{1,0:T(8,128)}) custom-call(f32[1664,768]{1,0:T(8,128)} %copy-done.3, f32[1664,768]{1,0:T(8,128)} %convolution_add_fusion.2.refs_1_, f32[1664,768]{1,0:T(8,128)} %get-tuple-element.135.refs_2_, f32[1,768]{1,0:T(1,128)} %get-tuple-element.348.refs_3_), custom_call_target="tpu_custom_call" | custom-call | tf_op jit(solution)/shard_map/pallas_call | solution.py:435
  374.4 5.5 convolution_convert_fusion.refs_1_
  382.5 46.9 %shard_map.438 = bf16[1664,2304]{1,0:T(8,128)(2,1)} custom-call(bf16[1664,2304]{1,0:T(8,128)(2,1)} %add_convert_fusion.refs_0_, bf16[1664,768]{1,0:T(8,128)(2,1)} %convolution_convert_fusion.refs_1_, f32[13,6,256]{2,1,0:T(8,128)} %get-tuple-element.140.refs_2_, s32[13,1,128]{2,1,0:T(1,128)} %select_n.1475.refs_1_.refs_3_, ...), custom_call_target="tpu_custom_call" | custom-call | tf_op jit(solution)/shard_map/pallas_call | solution.py:364
  429.4 10.5 %fusion.114 = f32[2304,768]{1,0:T(8,128)S(1)} fusion(bf16[1664,2304]{1,0:T(8,128)(2,1)} %shard_map.438, f32[1664,768]{1,0:T(8,128)S(1)} %bitcast.393, f32[768]{0:T(1024)S(1)} %copy-done.107, f32[768]{0:T(1024)S(1)} %copy-done.109, f32[1664]{0:T(1024)S(1)} %copy-done.102, f32[1664]{0:T(1024)S(1)} %copy-done.88), kind=kOutput, calls=%fused_computation.437 | convolution fusion | flops 5895192576 | bytes 19876864 | tf_op jit(solution)/shard_map/re,rd->ed/dot_general | solution.py:502
  459.6 10.6 %collective-permute-done.44 = f32[96,768]{1,0:T(8,128)} collective-permute-done((f32[96,768]{1,0:T(8,128)}, f32[96,768]{1,0:T(8,128)}, u32[]{:S(2)}, u32[]{:S(2)}) %collective-permute-start.44) | collective-permute-done | bytes 294944 | tf_op jit(solution)/shard_map/ppermute | solution.py:38
  470.2 8.7 %collective-permute-done.45 = f32[96,768]{1,0:T(8,128)} collective-permute-done((f32[96,768]{1,0:T(8,128)}, f32[96,768]{1,0:T(8,128)}, u32[]{:S(2)}, u32[]{:S(2)}) %collective-permute-start.45) | collective-permute-done | bytes 294944 | tf_op jit(solution)/shard_map/ppermute | solution.py:38
  483.3 10.9 %fusion.140.refs_1_ = f32[1664,768]{1,0:T(8,128)} fusion(bf16[1664,2304]{1,0:T(8,128)(2,1)} %shard_map.438, bf16[2304,768]{1,0:T(8,128)(2,1)} %bitcast.452), kind=kOutput, calls=%fused_computation.456 | convolution fusion | flops 5888802816 | bytes 16318464 | tf_op jit(solution)/shard_map/re,ed->rd/dot_general | solution.py:502
  494.2 3.1 maximum_add_fusion
  501.2 10.5 %shard_map.439 = (bf16[1664,768]{1,0:T(8,128)(2,1)}, f32[8,768]{1,0:T(8,128)}) custom-call(f32[1664,768]{1,0:T(8,128)} %convolution_add_fusion.1.refs_0_, f32[1664,768]{1,0:T(8,128)} %fusion.140.refs_1_, f32[1664,768]{1,0:T(8,128)} %get-tuple-element.146.refs_2_, f32[1,768]{1,0:T(1,128)} %get-tuple-element.346.refs_3_), custom_call_target="tpu_custom_call" | custom-call | tf_op jit(solution)/shard_map/pallas_call | solution.py:435
  522.8 6.5 collective-permute-start.48
  530.9 4.8 fusion.21
  537.2 4.5 convert_reduce_fusion
  541.6 7.9 collective-permute-done.49
  568.6 15.9 %collective-permute-done.53 = f32[4,24,768]{2,1,0:T(8,128)} collective-permute-done((f32[4,24,768]{2,1,0:T(8,128)}, f32[4,24,768]{2,1,0:T(8,128)}, u32[]{:S(2)}, u32[]{:S(2)}) %collective-permute-start.53) | collective-permute-done | bytes 294944 | tf_op jit(solution)/shard_map/ppermute | solution.py:38
  584.5 5.6 collective-permute-start.58
  595.1 5.8 collective-permute-start.56
  603.4 10.8 %collective-permute-done.58 = f32[1,192,768]{2,1,0:T(8,128)} collective-permute-done((f32[1,192,768]{2,1,0:T(8,128)}, f32[1,192,768]{2,1,0:T(8,128)}, u32[]{:S(2)}, u32[]{:S(2)}) %collective-permute-start.58) | collective-permute-done | bytes 589856 | tf_op jit(solution)/shard_map/ppermute | solution.py:38
  619.6 7.4 collective-permute-done.56
  634.0 14.9 %collective-permute-done.57 = f32[1,120,768]{2,1,0:T(8,128)S(1)} collective-permute-done((f32[1,120,768]{2,1,0:T(8,128)S(1)}, f32[1,120,768]{2,1,0:T(8,128)S(1)}, u32[]{:S(2)}, u32[]{:S(2)}) %collective-permute-start.57) | collective-permute-done | bytes 368672 | tf_op jit(solution)/shard_map/ppermute | solution.py:38
  665.2 4.4 collective-permute-done.59
  669.6 9.4 %collective-permute-done.60 = f32[96,768]{1,0:T(8,128)S(1)} collective-permute-done((f32[96,768]{1,0:T(8,128)S(1)}, f32[96,768]{1,0:T(8,128)S(1)}, u32[]{:S(2)}, u32[]{:S(2)}) %collective-permute-start.60) | collective-permute-done | bytes 294944 | tf_op jit(solution)/shard_map/ppermute | solution.py:38
  680.7 5.9 collective-permute-start.66
  695.8 3.3 fusion.142
  710.6 4.9 collective-permute-done.77
  715.5 6.7 collective-permute-done.78
  726.6 6.6 collective-permute-done.80
  733.2 4.7 collective-permute-done.81
  740.3 3.8 multiply_subtract_fusion
  749.8 3.0 fusion.144
  752.9 3.7 fusion.30
  768.3 5.9 collective-permute-done.84
  774.2 15.7 %collective-permute-done.85 = f32[96,768]{1,0:T(8,128)S(1)} collective-permute-done((f32[96,768]{1,0:T(8,128)S(1)}, f32[96,768]{1,0:T(8,128)S(1)}, u32[]{:S(2)}, u32[]{:S(2)}) %collective-permute-start.85) | collective-permute-done | bytes 294944 | tf_op jit(solution)/shard_map/ppermute | solution.py:38
  (695 shorter events, 268.1 us)
Async XLA Ops:
  7.2 243.5 %all-gather.3.cloned.1.call-start = ((), (), s32[]{:S(2)}) async-start(), calls=%async_computation | async-start | bytes 5406720 | tf_op jit(solution)/shard_map/all_gather | solution.py:707
  11.5 13.5 %collective-permute-start = (bf16[136,768]{1,0:T(8,128)(2,1)S(1)}, bf16[136,768]{1,0:T(8,128)(2,1)}, u32[]{:S(2)}, u32[]{:S(2)}) collective-permute-start(bf16[136,768]{1,0:T(8,128)(2,1)S(1)} %constant_dynamic-update-slice_fusion), channel_id=1, source_target_pairs={{0,3},{1,2},{2,1},{3,0},{4,7},{5,6},{6,5},{7,4},{8,11},{9,10},{10,... | collective-permute-start | bytes 626696 | tf_op jit(solution)/shard_map/ppermute | solution.py:38
  16.6 17.9 %collective-permute-start.1 = (bf16[136,768]{1,0:T(8,128)(2,1)S(1)}, bf16[136,768]{1,0:T(8,128)(2,1)}, u32[]{:S(2)}, u32[]{:S(2)}) collective-permute-start(bf16[136,768]{1,0:T(8,128)(2,1)S(1)} %constant_dynamic-update-slice_fusion), channel_id=1, source_target_pairs={{0,2},{1,3},{2,0},{3,1},{4,6},{5,7},{6,4},{7,5},{8,10},{9,11},{10,... | collective-permute-start | bytes 626696 | tf_op jit(solution)/shard_map/ppermute | solution.py:38
  16.6 17.9 %collective-permute-start.2 = (bf16[136,768]{1,0:T(8,128)(2,1)S(1)}, bf16[136,768]{1,0:T(8,128)(2,1)}, u32[]{:S(2)}, u32[]{:S(2)}) collective-permute-start(bf16[136,768]{1,0:T(8,128)(2,1)S(1)} %constant_dynamic-update-slice_fusion), channel_id=1, source_target_pairs={{0,1},{1,0},{2,3},{3,2},{4,5},{5,4},{6,7},{7,6},{8,9},{9,8},{10,11... | collective-permute-start | bytes 626696 | tf_op jit(solution)/shard_map/ppermute | solution.py:38
  37.4 26.4 %collective-permute-start.3 = (bf16[6,128,768]{2,1,0:T(8,128)(2,1)}, bf16[6,128,768]{2,1,0:T(8,128)(2,1)}, u32[]{:S(2)}, u32[]{:S(2)}) collective-permute-start(bf16[6,128,768]{2,1,0:T(8,128)(2,1)} %get-tuple-element.289), channel_id=1, source_target_pairs={{0,1},{1,2},{2,3},{4,5},{5,6},{6,7},{8,9},{9,10},{10,11},{12,13},{... | collective-permute-start | bytes 3538952 | tf_op jit(solution)/shard_map/ppermute | solution.py:675
  39.9 29.1 %collective-permute-start.4 = (bf16[6,128,768]{2,1,0:T(8,128)(2,1)}, bf16[6,128,768]{2,1,0:T(8,128)(2,1)}, u32[]{:S(2)}, u32[]{:S(2)}) collective-permute-start(bf16[6,128,768]{2,1,0:T(8,128)(2,1)} %get-tuple-element.288), channel_id=1, source_target_pairs={{1,0},{2,1},{3,2},{5,4},{6,5},{7,6},{9,8},{10,9},{11,10},{13,12},{... | collective-permute-start | bytes 3538952 | tf_op jit(solution)/shard_map/ppermute | solution.py:676
  46.6 38.5 %collective-permute-start.5 = (bf16[4,136,768]{2,1,0:T(8,128)(2,1)S(1)}, bf16[4,136,768]{2,1,0:T(8,128)(2,1)S(1)}, u32[]{:S(2)}, u32[]{:S(2)}) collective-permute-start(bf16[4,136,768]{2,1,0:T(8,128)(2,1)S(1)} %pad_maximum_fusion.13), channel_id=1, source_target_pairs={{0,8},{4,12},{8,0},{12,4},{16,24},{20,28},{24,16},{28,20},{1,9},{5... | collective-permute-start | bytes 2506760 | tf_op jit(solution)/shard_map/ppermute | solution.py:38
  48.1 37.1 %collective-permute-start.6 = (bf16[4,136,768]{2,1,0:T(8,128)(2,1)S(1)}, bf16[4,136,768]{2,1,0:T(8,128)(2,1)S(1)}, u32[]{:S(2)}, u32[]{:S(2)}) collective-permute-start(bf16[4,136,768]{2,1,0:T(8,128)(2,1)S(1)} %pad_maximum_fusion.13), channel_id=1, source_target_pairs={{0,16},{4,20},{8,24},{12,28},{16,0},{20,4},{24,8},{28,12},{1,17},{... | collective-permute-start | bytes 2506760 | tf_op jit(solution)/shard_map/ppermute | solution.py:38
  49.6 35.6 %collective-permute-start.7 = (bf16[4,136,768]{2,1,0:T(8,128)(2,1)S(1)}, bf16[4,136,768]{2,1,0:T(8,128)(2,1)S(1)}, u32[]{:S(2)}, u32[]{:S(2)}) collective-permute-start(bf16[4,136,768]{2,1,0:T(8,128)(2,1)S(1)} %pad_maximum_fusion.13), channel_id=1, source_target_pairs={{0,24},{4,28},{8,16},{12,20},{16,8},{20,12},{24,0},{28,4},{1,25},{... | collective-permute-start | bytes 2506760 | tf_op jit(solution)/shard_map/ppermute | solution.py:38
  85.7 30.4 %collective-permute-start.11 = (bf16[4,4,136,768]{3,2,1,0:T(8,128)(2,1)S(1)}, bf16[4,4,136,768]{3,2,1,0:T(8,128)(2,1)S(1)}, u32[]{:S(2)}, u32[]{:S(2)}) collective-permute-start(bf16[4,4,136,768]{3,2,1,0:T(8,128)(2,1)S(1)} %pad_maximum_fusion.2), channel_id=1, source_target_pairs={{0,4},{4,0},{8,12},{12,8},{16,20},{20,16},{24,28},{28,24},{1,5},{5... | collective-permute-start | bytes 10027016 | tf_op jit(solution)/shard_map/ppermute | solution.py:38
  96.1 10.1 %collective-permute-start.15 = (bf16[96,768]{1,0:T(8,128)(2,1)S(1)}, bf16[96,768]{1,0:T(8,128)(2,1)S(1)}, u32[]{:S(2)}, u32[]{:S(2)}) collective-permute-start(bf16[96,768]{1,0:T(8,128)(2,1)S(1)} %convert_bitcast_fusion), channel_id=1, source_target_pairs={{0,3},{1,2},{2,1},{3,0},{4,7},{5,6},{6,5},{7,4},{8,11},{9,10},{10,... | collective-permute-start | bytes 442376 | tf_op jit(solution)/shard_map/ppermute | solution.py:38
  101.1 12.5 %collective-permute-start.16 = (bf16[96,768]{1,0:T(8,128)(2,1)S(1)}, bf16[96,768]{1,0:T(8,128)(2,1)S(1)}, u32[]{:S(2)}, u32[]{:S(2)}) collective-permute-start(bf16[96,768]{1,0:T(8,128)(2,1)S(1)} %convert_bitcast_fusion), channel_id=1, source_target_pairs={{0,2},{1,3},{2,0},{3,1},{4,6},{5,7},{6,4},{7,5},{8,10},{9,11},{10,... | collective-permute-start | bytes 442376 | tf_op jit(solution)/shard_map/ppermute | solution.py:38
  101.1 14.0 %collective-permute-start.17 = (bf16[96,768]{1,0:T(8,128)(2,1)S(1)}, bf16[96,768]{1,0:T(8,128)(2,1)S(1)}, u32[]{:S(2)}, u32[]{:S(2)}) collective-permute-start(bf16[96,768]{1,0:T(8,128)(2,1)S(1)} %convert_bitcast_fusion), channel_id=1, source_target_pairs={{0,1},{1,0},{2,3},{3,2},{4,5},{5,4},{6,7},{7,6},{8,9},{9,8},{10,11... | collective-permute-start | bytes 442376 | tf_op jit(solution)/shard_map/ppermute | solution.py:38
  101.6 28.8 %collective-permute-start.12 = (bf16[4,96,768]{2,1,0:T(8,128)(2,1)}, bf16[4,96,768]{2,1,0:T(8,128)(2,1)}, u32[]{:S(2)}, u32[]{:S(2)}) collective-permute-start(bf16[4,96,768]{2,1,0:T(8,128)(2,1)} %pad_maximum_fusion.14), channel_id=1, source_target_pairs={{0,8},{4,12},{8,0},{12,4},{16,24},{20,28},{24,16},{28,20},{1,9},{5... | collective-permute-start | bytes 1769480 | tf_op jit(solution)/shard_map/ppermute | solution.py:38
  106.2 27.9 %collective-permute-start.13 = (bf16[4,96,768]{2,1,0:T(8,128)(2,1)}, bf16[4,96,768]{2,1,0:T(8,128)(2,1)}, u32[]{:S(2)}, u32[]{:S(2)}) collective-permute-start(bf16[4,96,768]{2,1,0:T(8,128)(2,1)} %pad_maximum_fusion.14), channel_id=1, source_target_pairs={{0,16},{4,20},{8,24},{12,28},{16,0},{20,4},{24,8},{28,12},{1,17},{... | collective-permute-start | bytes 1769480 | tf_op jit(solution)/shard_map/ppermute | solution.py:38
  113.6 20.5 %collective-permute-start.14 = (bf16[4,96,768]{2,1,0:T(8,128)(2,1)}, bf16[4,96,768]{2,1,0:T(8,128)(2,1)}, u32[]{:S(2)}, u32[]{:S(2)}) collective-permute-start(bf16[4,96,768]{2,1,0:T(8,128)(2,1)} %pad_maximum_fusion.14), channel_id=1, source_target_pairs={{0,24},{4,28},{8,16},{12,20},{16,8},{20,12},{24,0},{28,4},{1,25},{... | collective-permute-start | bytes 1769480 | tf_op jit(solution)/shard_map/ppermute | solution.py:38
  134.1 54.0 %collective-permute-start.18 = (bf16[4,96,768]{2,1,0:T(8,128)(2,1)}, bf16[4,96,768]{2,1,0:T(8,128)(2,1)}, u32[]{:S(2)}, u32[]{:S(2)}) collective-permute-start(bf16[4,96,768]{2,1,0:T(8,128)(2,1)} %pad_maximum_fusion.15), channel_id=1, source_target_pairs={{0,8},{4,12},{8,0},{12,4},{16,24},{20,28},{24,16},{28,20},{1,9},{5... | collective-permute-start | bytes 1769480 | tf_op jit(solution)/shard_map/ppermute | solution.py:38
  134.9 53.2 %collective-permute-start.19 = (bf16[4,96,768]{2,1,0:T(8,128)(2,1)}, bf16[4,96,768]{2,1,0:T(8,128)(2,1)}, u32[]{:S(2)}, u32[]{:S(2)}) collective-permute-start(bf16[4,96,768]{2,1,0:T(8,128)(2,1)} %pad_maximum_fusion.15), channel_id=1, source_target_pairs={{0,16},{4,20},{8,24},{12,28},{16,0},{20,4},{24,8},{28,12},{1,17},{... | collective-permute-start | bytes 1769480 | tf_op jit(solution)/shard_map/ppermute | solution.py:38
  136.4 51.7 %collective-permute-start.20 = (bf16[4,96,768]{2,1,0:T(8,128)(2,1)}, bf16[4,96,768]{2,1,0:T(8,128)(2,1)}, u32[]{:S(2)}, u32[]{:S(2)}) collective-permute-start(bf16[4,96,768]{2,1,0:T(8,128)(2,1)} %pad_maximum_fusion.15), channel_id=1, source_target_pairs={{0,24},{4,28},{8,16},{12,20},{16,8},{20,12},{24,0},{28,4},{1,25},{... | collective-permute-start | bytes 1769480 | tf_op jit(solution)/shard_map/ppermute | solution.py:38
  141.6 69.4 %collective-permute-start.21 = (bf16[4,4,96,768]{3,2,1,0:T(8,128)(2,1)}, bf16[4,4,96,768]{3,2,1,0:T(8,128)(2,1)}, u32[]{:S(2)}, u32[]{:S(2)}) collective-permute-start(bf16[4,4,96,768]{3,2,1,0:T(8,128)(2,1)} %pad_maximum_fusion.3), channel_id=1, source_target_pairs={{0,4},{4,0},{8,12},{12,8},{16,20},{20,16},{24,28},{28,24},{1,5},{5... | collective-permute-start | bytes 7077896 | tf_op jit(solution)/shard_map/ppermute | solution.py:38
  155.0 365.8 %all-gather.5.cloned.1.call-start = ((), (), s32[]{:S(2)}) async-start(), calls=%async_computation.1 | async-start | bytes 6881280 | tf_op jit(solution)/shard_map/all_gather | solution.py:758
  196.1 23.9 %collective-permute-start.22 = (bf16[4,4,96,768]{3,2,1,0:T(8,128)(2,1)S(1)}, bf16[4,4,96,768]{3,2,1,0:T(8,128)(2,1)S(1)}, u32[]{:S(2)}, u32[]{:S(2)}) collective-permute-start(bf16[4,4,96,768]{3,2,1,0:T(8,128)(2,1)S(1)} %pad_maximum_fusion.4), channel_id=1, source_target_pairs={{0,4},{4,0},{8,12},{12,8},{16,20},{20,16},{24,28},{28,24},{1,5},{5... | collective-permute-start | bytes 7077896 | tf_op jit(solution)/shard_map/ppermute | solution.py:38
  334.9 15.4 %collective-permute-start.38 = (f32[2,2,4,96,768]{4,3,2,0,1:T(8,128)}, f32[2,2,4,96,768]{4,3,2,0,1:T(8,128)}, u32[]{:S(2)}, u32[]{:S(2)}) collective-permute-start(f32[2,2,4,96,768]{4,3,2,0,1:T(8,128)} %copy.91), channel_id=1, source_target_pairs={{0,4},{4,0},{8,12},{12,8},{16,20},{20,16},{24,28},{28,24},{1,5},{5... | collective-permute-start | bytes 14155784 | tf_op jit(solution)/shard_map/ppermute | solution.py:38
  334.9 20.2 %collective-permute-start.37 = (f32[2,2,4,96,768]{4,3,2,1,0:T(8,128)}, f32[2,2,4,96,768]{4,3,2,1,0:T(8,128)}, u32[]{:S(2)}, u32[]{:S(2)}) collective-permute-start(f32[2,2,4,96,768]{4,3,2,1,0:T(8,128)} %bitcast.70), channel_id=1, source_target_pairs={{0,4},{4,0},{8,12},{12,8},{16,20},{20,16},{24,28},{28,24},{1,5},{5... | collective-permute-start | bytes 14155784 | tf_op jit(solution)/shard_map/ppermute | solution.py:38
  379.9 66.8 %collective-permute-start.40 = (f32[2,4,96,768]{3,2,1,0:T(8,128)}, f32[2,4,96,768]{3,2,1,0:T(8,128)}, u32[]{:S(2)}, u32[]{:S(2)}) collective-permute-start(f32[2,4,96,768]{3,2,1,0:T(8,128)} %slice_bitcast_fusion.2), channel_id=1, source_target_pairs={{0,8},{4,12},{8,0},{12,4},{16,24},{20,28},{24,16},{28,20},{1,9},{5... | collective-permute-start | bytes 7077896 | tf_op jit(solution)/shard_map/ppermute | solution.py:38
  381.3 69.1 %collective-permute-start.39 = (f32[2,4,96,768]{3,2,1,0:T(8,128)}, f32[2,4,96,768]{3,2,1,0:T(8,128)}, u32[]{:S(2)}, u32[]{:S(2)}) collective-permute-start(f32[2,4,96,768]{3,2,1,0:T(8,128)} %slice_bitcast_fusion.3), channel_id=1, source_target_pairs={{0,16},{4,20},{8,24},{12,28},{16,0},{20,4},{24,8},{28,12},{1,17},{... | collective-permute-start | bytes 7077896 | tf_op jit(solution)/shard_map/ppermute | solution.py:38
  454.0 40.3 %collective-permute-start.41 = (f32[2,2,4,96,768]{4,3,2,1,0:T(8,128)}, f32[2,2,4,96,768]{4,3,2,1,0:T(8,128)}, u32[]{:S(2)}, u32[]{:S(2)}) collective-permute-start(f32[2,2,4,96,768]{4,3,2,1,0:T(8,128)} %pad_maximum_fusion.1), channel_id=1, source_target_pairs={{0,4},{4,0},{8,12},{12,8},{16,20},{20,16},{24,28},{28,24},{1,5},{5... | collective-permute-start | bytes 14155784 | tf_op jit(solution)/shard_map/ppermute | solution.py:38
  455.2 15.0 %collective-permute-start.44 = (f32[96,768]{1,0:T(8,128)}, f32[96,768]{1,0:T(8,128)}, u32[]{:S(2)}, u32[]{:S(2)}) collective-permute-start(f32[96,768]{1,0:T(8,128)} %get-tuple-element.317), channel_id=1, source_target_pairs={{0,1},{1,0},{2,3},{3,2},{4,5},{5,4},{6,7},{7,6},{8,9},{9,8},{10,11... | collective-permute-start | bytes 884744 | tf_op jit(solution)/shard_map/ppermute | solution.py:38
  455.2 23.7 %collective-permute-start.45 = (f32[96,768]{1,0:T(8,128)}, f32[96,768]{1,0:T(8,128)}, u32[]{:S(2)}, u32[]{:S(2)}) collective-permute-start(f32[96,768]{1,0:T(8,128)} %get-tuple-element.316), channel_id=1, source_target_pairs={{0,2},{1,3},{2,0},{3,1},{4,6},{5,7},{6,4},{7,5},{8,10},{9,11},{10,... | collective-permute-start | bytes 884744 | tf_op jit(solution)/shard_map/ppermute | solution.py:38
  457.3 21.6 %collective-permute-start.46 = (f32[96,768]{1,0:T(8,128)}, f32[96,768]{1,0:T(8,128)}, u32[]{:S(2)}, u32[]{:S(2)}) collective-permute-start(f32[96,768]{1,0:T(8,128)} %get-tuple-element.315), channel_id=1, source_target_pairs={{0,3},{1,2},{2,1},{3,0},{4,7},{5,6},{6,5},{7,4},{8,11},{9,10},{10,... | collective-permute-start | bytes 884744 | tf_op jit(solution)/shard_map/ppermute | solution.py:38
  481.2 30.4 %collective-permute-start.42 = (f32[4,96,768]{2,1,0:T(8,128)}, f32[4,96,768]{2,1,0:T(8,128)S(1)}, u32[]{:S(2)}, u32[]{:S(2)}) collective-permute-start(f32[4,96,768]{2,1,0:T(8,128)} %get-tuple-element.149), channel_id=1, source_target_pairs={{0,8},{4,12},{8,0},{12,4},{16,24},{20,28},{24,16},{28,20},{1,9},{5... | collective-permute-start | bytes 3538952 | tf_op jit(solution)/shard_map/ppermute | solution.py:38
  482.6 29.2 %collective-permute-start.43 = (f32[4,96,768]{2,1,0:T(8,128)S(1)}, f32[4,96,768]{2,1,0:T(8,128)S(1)}, u32[]{:S(2)}, u32[]{:S(2)}) collective-permute-start(f32[4,96,768]{2,1,0:T(8,128)S(1)} %copy-done.62), channel_id=1, source_target_pairs={{0,16},{4,20},{8,24},{12,28},{16,0},{20,4},{24,8},{28,12},{1,17},{... | collective-permute-start | bytes 3538952 | tf_op jit(solution)/shard_map/ppermute | solution.py:38
  520.9 37.3 %collective-permute-start.50 = (f32[2,2,4,24,768]{4,3,2,1,0:T(8,128)}, f32[2,2,4,24,768]{4,3,2,1,0:T(8,128)}, u32[]{:S(2)}, u32[]{:S(2)}) collective-permute-start(f32[2,2,4,24,768]{4,3,2,1,0:T(8,128)} %dynamic-slice_bitcast_fusion.6), channel_id=1, source_target_pairs={{0,4},{4,0},{8,12},{12,8},{16,20},{20,16},{24,28},{28,24},{1,5},{5... | collective-permute-start | bytes 3538952 | tf_op jit(solution)/shard_map/ppermute | solution.py:38
  520.9 28.7 %collective-permute-start.49 = (f32[2,4,96,384]{3,2,1,0:T(8,128)}, f32[2,4,96,384]{3,2,1,0:T(8,128)}, u32[]{:S(2)}, u32[]{:S(2)}) collective-permute-start(f32[2,4,96,384]{3,2,1,0:T(8,128)} %get-tuple-element.163), channel_id=1, source_target_pairs={{0,8},{4,12},{8,0},{12,4},{16,24},{20,28},{24,16},{28,20},{1,9},{5... | collective-permute-start | bytes 3538952 | tf_op jit(solution)/shard_map/ppermute | solution.py:38
  522.0 29.0 %collective-permute-start.47 = (f32[2,4,96,384]{3,2,1,0:T(8,128)}, f32[2,4,96,384]{3,2,1,0:T(8,128)}, u32[]{:S(2)}, u32[]{:S(2)}) collective-permute-start(f32[2,4,96,384]{3,2,1,0:T(8,128)} %get-tuple-element.158), channel_id=1, source_target_pairs={{0,16},{4,20},{8,24},{12,28},{16,0},{20,4},{24,8},{28,12},{1,17},{... | collective-permute-start | bytes 3538952 | tf_op jit(solution)/shard_map/ppermute | solution.py:38
  522.8 32.9 %collective-permute-start.48 = (f32[2,192,768]{2,1,0:T(8,128)}, f32[2,192,768]{2,1,0:T(8,128)}, u32[]{:S(2)}, u32[]{:S(2)}) collective-permute-start(f32[2,192,768]{2,1,0:T(8,128)} %dynamic-slice_bitcast_fusion.5), channel_id=1, source_target_pairs={{0,1},{1,0},{2,3},{3,2},{4,5},{5,4},{6,7},{7,6},{8,9},{9,8},{10,11... | collective-permute-start | bytes 3538952 | tf_op jit(solution)/shard_map/ppermute | solution.py:38
  561.5 30.1 %collective-permute-start.51 = (f32[4,96,384]{2,1,0:T(8,128)}, f32[4,96,384]{2,1,0:T(8,128)}, u32[]{:S(2)}, u32[]{:S(2)}) collective-permute-start(f32[4,96,384]{2,1,0:T(8,128)} %dynamic-slice_bitcast_fusion.13), channel_id=1, source_target_pairs={{0,8},{4,12},{8,0},{12,4},{16,24},{20,28},{24,16},{28,20},{1,9},{5... | collective-permute-start | bytes 1769480 | tf_op jit(solution)/shard_map/ppermute | solution.py:38
  562.7 21.7 %collective-permute-start.53 = (f32[4,24,768]{2,1,0:T(8,128)}, f32[4,24,768]{2,1,0:T(8,128)}, u32[]{:S(2)}, u32[]{:S(2)}) collective-permute-start(f32[4,24,768]{2,1,0:T(8,128)} %get-tuple-element.167), channel_id=1, source_target_pairs={{0,8},{4,12},{8,0},{12,4},{16,24},{20,28},{24,16},{28,20},{1,9},{5... | collective-permute-start | bytes 884744 | tf_op jit(solution)/shard_map/ppermute | solution.py:38
  563.6 26.5 %collective-permute-start.54 = (f32[4,24,768]{2,1,0:T(8,128)}, f32[4,24,768]{2,1,0:T(8,128)}, u32[]{:S(2)}, u32[]{:S(2)}) collective-permute-start(f32[4,24,768]{2,1,0:T(8,128)} %get-tuple-element.168), channel_id=1, source_target_pairs={{0,16},{4,20},{8,24},{12,28},{16,0},{20,4},{24,8},{28,12},{1,17},{... | collective-permute-start | bytes 884744 | tf_op jit(solution)/shard_map/ppermute | solution.py:38
  565.0 25.4 %collective-permute-start.55 = (f32[4,24,768]{2,1,0:T(8,128)S(1)}, f32[4,24,768]{2,1,0:T(8,128)}, u32[]{:S(2)}, u32[]{:S(2)}) collective-permute-start(f32[4,24,768]{2,1,0:T(8,128)S(1)} %get-tuple-element.169), channel_id=1, source_target_pairs={{0,24},{4,28},{8,16},{12,20},{16,8},{20,12},{24,0},{28,4},{1,25},{... | collective-permute-start | bytes 884744 | tf_op jit(solution)/shard_map/ppermute | solution.py:38
  567.1 25.7 %collective-permute-start.52 = (f32[4,96,384]{2,1,0:T(8,128)S(1)}, f32[4,96,384]{2,1,0:T(8,128)S(1)}, u32[]{:S(2)}, u32[]{:S(2)}) collective-permute-start(f32[4,96,384]{2,1,0:T(8,128)S(1)} %copy-done.74), channel_id=1, source_target_pairs={{0,16},{4,20},{8,24},{12,28},{16,0},{20,4},{24,8},{28,12},{1,17},{... | collective-permute-start | bytes 1769480 | tf_op jit(solution)/shard_map/ppermute | solution.py:38
  584.5 29.7 %collective-permute-start.58 = (f32[1,192,768]{2,1,0:T(8,128)}, f32[1,192,768]{2,1,0:T(8,128)}, u32[]{:S(2)}, u32[]{:S(2)}) collective-permute-start(f32[1,192,768]{2,1,0:T(8,128)} %constant_dynamic-slice_fusion.2), channel_id=1, source_target_pairs={{0,2},{1,3},{2,0},{3,1},{4,6},{5,7},{6,4},{7,5},{8,10},{9,11},{10,... | collective-permute-start | bytes 1769480 | tf_op jit(solution)/shard_map/ppermute | solution.py:38
  595.1 31.9 %collective-permute-start.56 = (f32[2,120,768]{2,1,0:T(8,128)}, f32[2,120,768]{2,1,0:T(8,128)}, u32[]{:S(2)}, u32[]{:S(2)}) collective-permute-start(f32[2,120,768]{2,1,0:T(8,128)} %dynamic-slice_bitcast_fusion.11), channel_id=1, source_target_pairs={{0,1},{1,0},{2,3},{3,2},{4,5},{5,4},{6,7},{7,6},{8,9},{9,8},{10,11... | collective-permute-start | bytes 2211848 | tf_op jit(solution)/shard_map/ppermute | solution.py:38
  603.4 12.7 %collective-permute-start.69 = (f32[24,768]{1,0:T(8,128)S(1)}, f32[24,768]{1,0:T(8,128)S(1)}, u32[]{:S(2)}, u32[]{:S(2)}) collective-permute-start(f32[24,768]{1,0:T(8,128)S(1)} %shard_map.440), channel_id=1, source_target_pairs={{0,4},{4,0},{8,12},{12,8},{16,20},{20,16},{24,28},{28,24},{1,5},{5... | collective-permute-start | bytes 221192 | tf_op jit(solution)/shard_map/ppermute | solution.py:38
  616.0 12.9 %collective-permute-start.70 = (f32[24,768]{1,0:T(8,128)S(1)}, f32[24,768]{1,0:T(8,128)S(1)}, u32[]{:S(2)}, u32[]{:S(2)}) collective-permute-start(f32[24,768]{1,0:T(8,128)S(1)} %add.796), channel_id=1, source_target_pairs={{0,8},{4,12},{8,0},{12,4},{16,24},{20,28},{24,16},{28,20},{1,9},{5... | collective-permute-start | bytes 221192 | tf_op jit(solution)/shard_map/ppermute | solution.py:38
  617.4 11.5 %collective-permute-start.71 = (f32[24,768]{1,0:T(8,128)S(1)}, f32[24,768]{1,0:T(8,128)S(1)}, u32[]{:S(2)}, u32[]{:S(2)}) collective-permute-start(f32[24,768]{1,0:T(8,128)S(1)} %add.796), channel_id=1, source_target_pairs={{0,16},{4,20},{8,24},{12,28},{16,0},{20,4},{24,8},{28,12},{1,17},{... | collective-permute-start | bytes 221192 | tf_op jit(solution)/shard_map/ppermute | solution.py:38
  618.6 10.3 %collective-permute-start.72 = (f32[24,768]{1,0:T(8,128)S(1)}, f32[24,768]{1,0:T(8,128)S(1)}, u32[]{:S(2)}, u32[]{:S(2)}) collective-permute-start(f32[24,768]{1,0:T(8,128)S(1)} %add.796), channel_id=1, source_target_pairs={{0,24},{4,28},{8,16},{12,20},{16,8},{20,12},{24,0},{28,4},{1,25},{... | collective-permute-start | bytes 221192 | tf_op jit(solution)/shard_map/ppermute | solution.py:38
  628.3 20.6 %collective-permute-start.57 = (f32[1,120,768]{2,1,0:T(8,128)S(1)}, f32[1,120,768]{2,1,0:T(8,128)S(1)}, u32[]{:S(2)}, u32[]{:S(2)}) collective-permute-start(f32[1,120,768]{2,1,0:T(8,128)S(1)} %constant_dynamic-slice_fusion.1), channel_id=1, source_target_pairs={{0,2},{1,3},{2,0},{3,1},{4,6},{5,7},{6,4},{7,5},{8,10},{9,11},{10,... | collective-permute-start | bytes 1105928 | tf_op jit(solution)/shard_map/ppermute | solution.py:38
  629.0 26.5 %collective-permute-start.73 = (f32[24,768]{1,0:T(8,128)S(1)}, f32[24,768]{1,0:T(8,128)S(1)}, u32[]{:S(2)}, u32[]{:S(2)}) collective-permute-start(f32[24,768]{1,0:T(8,128)S(1)} %add_add_fusion.3), channel_id=1, source_target_pairs={{0,1},{1,0},{2,3},{3,2},{4,5},{5,4},{6,7},{7,6},{8,9},{9,8},{10,11... | collective-permute-start | bytes 221192 | tf_op jit(solution)/shard_map/ppermute | solution.py:38
  631.6 26.1 %collective-permute-start.74 = (f32[24,768]{1,0:T(8,128)S(1)}, f32[24,768]{1,0:T(8,128)S(1)}, u32[]{:S(2)}, u32[]{:S(2)}) collective-permute-start(f32[24,768]{1,0:T(8,128)S(1)} %add_add_fusion.3), channel_id=1, source_target_pairs={{0,2},{1,3},{2,0},{3,1},{4,6},{5,7},{6,4},{7,5},{8,10},{9,11},{10,... | collective-permute-start | bytes 221192 | tf_op jit(solution)/shard_map/ppermute | solution.py:38
  631.6 28.3 %collective-permute-start.75 = (f32[24,768]{1,0:T(8,128)S(1)}, f32[24,768]{1,0:T(8,128)}, u32[]{:S(2)}, u32[]{:S(2)}) collective-permute-start(f32[24,768]{1,0:T(8,128)S(1)} %add_add_fusion.3), channel_id=1, source_target_pairs={{0,3},{1,2},{2,1},{3,0},{4,7},{5,6},{6,5},{7,4},{8,11},{9,10},{10,... | collective-permute-start | bytes 221192 | tf_op jit(solution)/shard_map/ppermute | solution.py:38
  655.4 14.2 %collective-permute-start.59 = (f32[96,768]{1,0:T(8,128)S(1)}, f32[96,768]{1,0:T(8,128)S(1)}, u32[]{:S(2)}, u32[]{:S(2)}) collective-permute-start(f32[96,768]{1,0:T(8,128)S(1)} %get-tuple-element.310), channel_id=1, source_target_pairs={{0,1},{1,0},{2,3},{3,2},{4,5},{5,4},{6,7},{7,6},{8,9},{9,8},{10,11... | collective-permute-start | bytes 884744 | tf_op jit(solution)/shard_map/ppermute | solution.py:38
  655.5 23.5 %collective-permute-start.60 = (f32[96,768]{1,0:T(8,128)S(1)}, f32[96,768]{1,0:T(8,128)S(1)}, u32[]{:S(2)}, u32[]{:S(2)}) collective-permute-start(f32[96,768]{1,0:T(8,128)S(1)} %get-tuple-element.309), channel_id=1, source_target_pairs={{0,2},{1,3},{2,0},{3,1},{4,6},{5,7},{6,4},{7,5},{8,10},{9,11},{10,... | collective-permute-start | bytes 884744 | tf_op jit(solution)/shard_map/ppermute | solution.py:38
  657.7 21.3 %collective-permute-start.61 = (f32[96,768]{1,0:T(8,128)S(1)}, f32[96,768]{1,0:T(8,128)S(1)}, u32[]{:S(2)}, u32[]{:S(2)}) collective-permute-start(f32[96,768]{1,0:T(8,128)S(1)} %get-tuple-element.308), channel_id=1, source_target_pairs={{0,3},{1,2},{2,1},{3,0},{4,7},{5,6},{6,5},{7,4},{8,11},{9,10},{10,... | collective-permute-start | bytes 884744 | tf_op jit(solution)/shard_map/ppermute | solution.py:38
  680.7 9.0 %collective-permute-start.66 = (f32[2,128]{1,0:T(2,128)S(1)}, f32[2,128]{1,0:T(2,128)S(1)}, u32[]{:S(2)}, u32[]{:S(2)}) collective-permute-start(f32[2,128]{1,0:T(2,128)S(1)} %add_add_fusion.6), channel_id=1, source_target_pairs={{0,1},{1,0},{2,3},{3,2},{4,5},{5,4},{6,7},{7,6},{8,9},{9,8},{10,11... | collective-permute-start | bytes 3080 | tf_op jit(solution)/shard_map/ppermute | solution.py:38
  705.7 9.9 %collective-permute-start.77 = (f32[96,768]{1,0:T(8,128)S(1)}, f32[96,768]{1,0:T(8,128)S(1)}, u32[]{:S(2)}, u32[]{:S(2)}) collective-permute-start(f32[96,768]{1,0:T(8,128)S(1)} %get-tuple-element.306), channel_id=1, source_target_pairs={{0,8},{4,12},{8,0},{12,4},{16,24},{20,28},{24,16},{28,20},{1,9},{5... | collective-permute-start | bytes 884744 | tf_op jit(solution)/shard_map/ppermute | solution.py:38
  706.7 15.5 %collective-permute-start.78 = (f32[96,768]{1,0:T(8,128)S(1)}, f32[96,768]{1,0:T(8,128)S(1)}, u32[]{:S(2)}, u32[]{:S(2)}) collective-permute-start(f32[96,768]{1,0:T(8,128)S(1)} %get-tuple-element.305), channel_id=1, source_target_pairs={{0,16},{4,20},{8,24},{12,28},{16,0},{20,4},{24,8},{28,12},{1,17},{... | collective-permute-start | bytes 884744 | tf_op jit(solution)/shard_map/ppermute | solution.py:38
  707.4 14.7 %collective-permute-start.79 = (f32[96,768]{1,0:T(8,128)S(1)}, f32[96,768]{1,0:T(8,128)S(1)}, u32[]{:S(2)}, u32[]{:S(2)}) collective-permute-start(f32[96,768]{1,0:T(8,128)S(1)} %get-tuple-element.304), channel_id=1, source_target_pairs={{0,24},{4,28},{8,16},{12,20},{16,8},{20,12},{24,0},{28,4},{1,25},{... | collective-permute-start | bytes 884744 | tf_op jit(solution)/shard_map/ppermute | solution.py:38
  722.3 11.0 %collective-permute-start.80 = (f32[96,768]{1,0:T(8,128)S(1)}, f32[96,768]{1,0:T(8,128)S(1)}, u32[]{:S(2)}, u32[]{:S(2)}) collective-permute-start(f32[96,768]{1,0:T(8,128)S(1)} %fusion.69), channel_id=1, source_target_pairs={{0,24},{4,28},{8,16},{12,20},{16,8},{20,12},{24,0},{28,4},{1,25},{... | collective-permute-start | bytes 884744 | tf_op jit(solution)/shard_map/ppermute | solution.py:38
  723.8 14.2 %collective-permute-start.81 = (f32[96,768]{1,0:T(8,128)S(1)}, f32[96,768]{1,0:T(8,128)S(1)}, u32[]{:S(2)}, u32[]{:S(2)}) collective-permute-start(f32[96,768]{1,0:T(8,128)S(1)} %fusion.69), channel_id=1, source_target_pairs={{0,16},{4,20},{8,24},{12,28},{16,0},{20,4},{24,8},{28,12},{1,17},{... | collective-permute-start | bytes 884744 | tf_op jit(solution)/shard_map/ppermute | solution.py:38
  724.8 13.1 %collective-permute-start.82 = (f32[96,768]{1,0:T(8,128)S(1)}, f32[96,768]{1,0:T(8,128)S(1)}, u32[]{:S(2)}, u32[]{:S(2)}) collective-permute-start(f32[96,768]{1,0:T(8,128)S(1)} %fusion.69), channel_id=1, source_target_pairs={{0,8},{4,12},{8,0},{12,4},{16,24},{20,28},{24,16},{28,20},{1,9},{5... | collective-permute-start | bytes 884744 | tf_op jit(solution)/shard_map/ppermute | solution.py:38
  762.3 11.9 %collective-permute-start.84 = (f32[96,768]{1,0:T(8,128)S(1)}, f32[96,768]{1,0:T(8,128)S(1)}, u32[]{:S(2)}, u32[]{:S(2)}) collective-permute-start(f32[96,768]{1,0:T(8,128)S(1)} %get-tuple-element.297), channel_id=1, source_target_pairs={{0,3},{1,2},{2,1},{3,0},{4,7},{5,6},{6,5},{7,4},{8,11},{9,10},{10,... | collective-permute-start | bytes 884744 | tf_op jit(solution)/shard_map/ppermute | solution.py:38
  764.3 25.5 %collective-permute-start.85 = (f32[96,768]{1,0:T(8,128)S(1)}, f32[96,768]{1,0:T(8,128)S(1)}, u32[]{:S(2)}, u32[]{:S(2)}) collective-permute-start(f32[96,768]{1,0:T(8,128)S(1)} %get-tuple-element.296), channel_id=1, source_target_pairs={{0,2},{1,3},{2,0},{3,1},{4,6},{5,7},{6,4},{7,5},{8,10},{9,11},{10,... | collective-permute-start | bytes 884744 | tf_op jit(solution)/shard_map/ppermute | solution.py:38
  764.3 25.5 %collective-permute-start.86 = (f32[96,768]{1,0:T(8,128)S(1)}, f32[96,768]{1,0:T(8,128)S(1)}, u32[]{:S(2)}, u32[]{:S(2)}) collective-permute-start(f32[96,768]{1,0:T(8,128)S(1)} %get-tuple-element.294), channel_id=1, source_target_pairs={{0,1},{1,0},{2,3},{3,2},{4,5},{5,4},{6,7},{7,6},{8,9},{9,8},{10,11... | collective-permute-start | bytes 884744 | tf_op jit(solution)/shard_map/ppermute | solution.py:38
  (172 other events, 1726.4 us)
Sparse Core Ops, SparseCore 0:
  155.2 87.3 all-gather.2
  335.6 101.0 all-gather.4

commit v4 on v3

--- a/solution.py
+++ b/solution.py
@@ -118,20 +118,30 @@
         self.block = by_index(relative(self.shard, "seq"), lax.axis_index("seq"))
         return self.block
 
+    def doubling(self):
+        place, count, bit = lax.axis_index("seq"), lax.axis_size("seq"), 1
+        block = self.shard[None]
+        while bit < count:
+            other = swap(block, "seq", bit)
+            block = jnp.where(
+                (place & bit) == 0,
+                jnp.concatenate([block, other], axis=0),
+                jnp.concatenate([other, block], axis=0),
+            )
+            bit *= 2
+        self.block = block
+        return block
+
     def in_plane(self):
         self.parts = [self.block] + [swap(self.block, "pack", k) for k in other_chips()]
 
     def pieces(self, spots):
-        own = jnp.stack(self.parts)
-        other = swap(own, "pack", 1)
-        chip = lax.axis_index("pack") >> 1
-        found = []
-        for here, there in zip(spots[:-1], spots[1:]):
-            both = [
-                by_index([half[k, :, here:there] for k in range(half.shape[0])], chip) for half in (own, other)
-            ]
-            found.append(by_core(*both, 1).reshape(-1, there - here, own.shape[-1]))
-        return found
+        mine = by_index(self.parts, lax.axis_index("pack") >> 1)
+        other = swap(mine, "pack", 1)
+        return [
+            by_core(mine[:, :, here:there], other[:, :, here:there], 1).reshape(-1, there - here, mine.shape[-1])
+            for here, there in zip(spots[:-1], spots[1:])
+        ]
 
     def halves(self):
         own = jnp.stack(self.parts)
@@ -232,7 +242,10 @@
 
 
 def sum_plane(value):
-    value = value + swap(value, "pack", 1)
+    return sum_chips(value + swap(value, "pack", 1))
+
+
+def sum_chips(value):
     return tree_sum([value] + [swap(value, "pack", k) for k in other_chips()])
 
 
@@ -674,23 +687,20 @@
     ends = seq_count - 1
     from_left = lax.ppermute(patches[:, shard_len - MAXLEN :], "seq", [(i, i + 1) for i in range(ends)])
     from_right = lax.ppermute(patches[:, :MAXLEN], "seq", [(i + 1, i) for i in range(ends)])
-    from_left, from_right, up_gather.shard = hold(from_left, from_right, up_gather.shard)
-    up_gather.along_seq()
-    *first.parts, up_gather.block, down_gather.shard = hold(*first.parts, up_gather.block, down_gather.shard)
-    embed_full, qkv_full, output_full, small_full, bias_full = first.pieces(spots)
-    embed_full, qkv_full, output_full = (
-        value.reshape(-1, width) for value in (embed_full, qkv_full, output_full)
-    )
-    (gain_bias,) = hold(from_rows(small_full, small_params.shape).astype(F32))
-    bias_full = lax.dynamic_slice_in_dim(bias_full, pack_place * seq_count, seq_count, 0)
-    bias_full = bias_full[:, 0, : head_bias.shape[0]].reshape(-1)
-    up_gather.in_plane()
-    down_gather.along_seq()
-
     window = jnp.concatenate([from_left, patches, from_right], axis=1).reshape(-1, patch_in)
     source, group, live, counts = deal_rows(lengths, keep_mask, shard_len)
     chosen = (source[:, None] == jnp.arange(window.shape[0], dtype=jnp.int32)[None, :]).astype(LOW)
     tokens = mm("rw,wi->ri", chosen, window).astype(LOW)
+    tokens, up_gather.shard, *first.parts = hold(tokens, up_gather.shard, *first.parts)
+    up_gather.along_seq()
+    embed_full, qkv_full, output_full, small_full, bias_full = first.pieces(spots)
+    embed_full, qkv_full, output_full = (
+        value.reshape(-1, width) for value in (embed_full, qkv_full, output_full)
+    )
+    (gain_bias,) = hold(from_rows(small_full, small_params.shape).astype(F32))
+    bias_full = lax.dynamic_slice_in_dim(bias_full, pack_place * seq_count, seq_count, 0)
+    bias_full = bias_full[:, 0, : head_bias.shape[0]].reshape(-1)
+
     rows = tokens.shape[0]
     query_id = group.reshape(rows // BLOCK, 1, BLOCK)
     key_id = jnp.pad(jnp.where(live, group, -2), (BLOCK, BLOCK), constant_values=-2)[:, None]
@@ -700,15 +710,18 @@
     ).astype(F32)
 
     embedded = mm("ri,di->rd", tokens, embed_full) + gain_bias[6]
-    embedded, *up_gather.parts, down_gather.block, head_low = hold(
-        embedded, *up_gather.parts, down_gather.block, head_weight.astype(LOW)
-    )
-    down_gather.in_plane()
-    head_full = lax.all_gather(head_low, "seq", axis=0, tiled=True)
-    up_full = [half.reshape(-1, width) for half in up_gather.halves()]
+    embedded, up_gather.block, down_gather.shard = hold(embedded, up_gather.block, down_gather.shard)
+    up_gather.in_plane()
+    down_gather.doubling()
     normed_one = layer_norm(embedded, gain_bias[0], gain_bias[1]).astype(LOW)
     qkv_bias = jnp.concatenate([gain_bias[7], jnp.zeros_like(gain_bias[7]), gain_bias[8]])
     qkv_rows = (mm("rd,ed->re", normed_one, qkv_full) + qkv_bias).astype(LOW)
+    qkv_rows, down_gather.block, head_low, *up_gather.parts = hold(
+        qkv_rows, down_gather.block, head_weight.astype(LOW), *up_gather.parts
+    )
+    head_full = lax.all_gather(head_low, "seq", axis=0, tiled=True)
+    down_gather.in_plane()
+    up_full = [half.reshape(-1, width) for half in up_gather.halves()]
     attn_low, log_total = attend(qkv_rows, query_id, key_id)
     attn_low, *down_gather.parts = hold(attn_low, *down_gather.parts)
     down_full = [half.reshape(-1, width) for half in down_gather.halves()]
@@ -783,65 +796,51 @@
     )
     grad_mixed = mm("rd,de->re", grad_attn_low, output_full).astype(LOW)
     up_out = up_sum.step(up_out)
-    muon_moments = [m.T for m in (qkv_moment, output_moment, up_moment, down_moment)]
-    grad_mixed, up_out, *muon_moments = hold(grad_mixed, up_out, *muon_moments)
-    old_columns = to_planes(muon_moments)
+    grad_mixed, up_out = hold(grad_mixed, up_out)
     grad_qkv = attend_back(qkv_rows, grad_mixed, log_total, query_id, key_id)
+    down_out, up_out = down_sum.step(down_out), up_sum.step(up_out)
+    grad_qkv, down_out, up_out = hold(grad_qkv, down_out, up_out)
+    grad_normed = mm("re,ed->rd", grad_qkv, qkv_full)
+    grad_embed_rows, sums_first = norm_back(embedded, gain_bias[0], grad_normed, grad_attn, keep_sum=False)
     output_grad = mm("rd,re->de", grad_attn_low, attn_low)
-    late_keep, late_out = late_halves(mm("re,rd->ed", grad_qkv, normed_one), output_grad)
-    down_out, up_out = down_sum.step(down_out), up_sum.step(up_out)
-    grad_qkv, late_out, down_out, up_out = hold(grad_qkv, late_out, down_out, up_out)
-    grad_normed = mm("re,ed->rd", grad_qkv, qkv_full)
+    embed_grad = mm("rd,ri->di", grad_embed_rows, tokens)
+    down_sum.finish(down_out)
+    up_sum.finish(up_out)
+    early_sum = SeqScatter(jnp.concatenate([down_sum.value, up_sum.value], axis=1))
+    early_out = early_sum.send()
+    grad_qkv, output_grad, embed_grad, early_out = hold(grad_qkv, output_grad, embed_grad, early_out)
+    late_keep, late_out = late_halves(mm("re,rd->ed", grad_qkv, normed_one), output_grad, embed_grad)
+    late_out, early_sum.keep, grad_qkv, traded = hold(late_out, early_sum.keep, grad_qkv, traded)
+    all_pooled = pick(traded[:, :width].reshape(-1, seq_count, head_weight.shape[0]), seq_place, 1)
+    all_logits = traded[:, width:]
+    head_grad = mm("nd,nc->dc", all_pooled, all_logits)
+    bias_grad = pick(column_sum(all_logits).reshape(seq_count, -1), seq_place)
     late = late_keep + swap(late_out, "pack", 1)
     late_outs = [
         each.start_joined(part) for each, part in zip(late_sums, (late[..., :half], late[..., half:]))
     ]
-    grad_normed, late_outs[0], late_outs[1], down_sum.keep, up_sum.keep = hold(
-        grad_normed, *late_outs, down_sum.keep, up_sum.keep
-    )
-    grad_embed_rows, sums_first = norm_back(embedded, gain_bias[0], grad_normed, grad_attn, keep_sum=False)
-    last_keep, last_out = late_halves(mm("rd,ri->di", grad_embed_rows, tokens))
-    down_sum.finish(down_out)
-    up_sum.finish(up_out)
-    early_sum = SeqScatter(jnp.concatenate([down_sum.value, up_sum.value], axis=1))
-    early_out = early_sum.send()
-    last_out, early_out, late_sums[0].keep, late_sums[1].keep, grad_qkv, traded, old_columns = hold(
-        last_out, early_out, late_sums[0].keep, late_sums[1].keep, grad_qkv, traded, old_columns
-    )
-    all_pooled = pick(traded[:, :width].reshape(-1, seq_count, head_weight.shape[0]), seq_place, 1)
-    all_logits = traded[:, width:]
-    head_grad = mm("nd,nc->dc", all_pooled, all_logits)
-    bias_grad = pick(column_sum(all_logits).reshape(seq_count, -1), seq_place)
-    qkv_sum = column_sum(grad_qkv)
+    head_grad, bias_grad, grad_qkv, early_sum.keep, grad_upper[0], grad_upper[1], *late_outs = hold(
+        head_grad, bias_grad, grad_qkv, early_sum.keep, *grad_upper, *late_outs
+    )
+    small_mine = small_sums(
+        sums_first, sums_second, sums_last, column_sum(grad_qkv), [column_sum(side) for side in grad_upper]
+    )
     late_outs = [each.step(sent) for each, sent in zip(late_sums, late_outs)]
-    last = last_keep + swap(last_out, "pack", 1)
-    last = last.reshape((pack_count // 2,) + last.shape[-3:])
-    last_outs = [pick(last, (pack_place ^ k) >> 1) for k in other_chips()]
     early_out = early_sum.step(early_out)
-    head_grad, bias_grad, qkv_sum, early_out, grad_upper[0], grad_upper[1], *sends = hold(
-        head_grad, bias_grad, qkv_sum, early_out, *grad_upper, *late_outs, *last_outs
-    )
-    small_mine = small_sums(
-        sums_first, sums_second, sums_last, qkv_sum, [column_sum(side) for side in grad_upper]
-    )
-    for each, sent in zip(late_sums, sends[:2]):
+    small_mine, early_out, *late_outs = hold(small_mine, early_out, *late_outs)
+    small_total = small_mine + swap(small_mine, "pack", 1)
+    for each, sent in zip(late_sums, late_outs):
         each.finish(sent)
-    last_parts = [pick(last, pack_place >> 1)] + [
-        swap(sent, "pack", k) for k, sent in zip(other_chips(), sends[2:])
-    ]
-    late_sum = SeqScatter(
-        jnp.concatenate(
-            [jnp.concatenate([each.value for each in late_sums], axis=2), tree_sum(last_parts)], axis=1
-        )
-    )
-    late_out, small_mine = hold(late_sum.send(), small_mine)
-    small_total = sum_plane(small_mine)
+    late_sum = SeqScatter(jnp.concatenate([each.value for each in late_sums], axis=2))
+    late_out, small_total, early_sum.keep = hold(late_sum.send(), small_total, early_sum.keep)
+    small_total = sum_chips(small_total)
     while early_out is not None:
         early_out = early_sum.step(early_out)
     late_out = late_sum.step(late_out)
+    late_out, small_total, early_sum.value = hold(late_out, small_total, early_sum.value)
+    small_total = all_sum(small_total, "seq")
     while late_out is not None:
         late_out = late_sum.step(late_out)
-    small_total = all_sum(small_total, "seq")
     down_share, up_share = jnp.split(early_sum.result(), 2)
     late_share = late_sum.result()
     widths = [qkv_weight.shape[1], output_weight.shape[1], embed_weight.shape[1]]
@@ -857,19 +856,19 @@
     shares = (early_sum.result(), late_share, head_grad, bias_grad)
     square_sum = sum((jnp.sum(piece * piece) for piece in shares))
     sums = jnp.broadcast_to(jnp.stack([loss_part, square_sum])[:, None], (2, BLOCK))
-    sums = sum_plane(sums)
-    muon_shares = (qkv_share, output_share, up_share, down_share)
-    new_columns, sums = hold(to_planes(muon_shares), sums)
-    sums = all_sum(sums, "seq")
+    sums = sum_plane(all_sum(sums, "seq"))
     loss_value, square_total = sums[0, 0], sums[1, 0] + jnp.sum(small_total * small_total)
     grad_norm = jnp.sqrt(square_total)
     factor = jnp.minimum(1.0, CLIP_NORM / (grad_norm + 1e-06))
-    columns = MUON_MU * old_columns + factor * new_columns
+    muon_shares = (qkv_share, output_share, up_share, down_share)
+    moments = [
+        MUON_MU * moment.T + factor * share
+        for moment, share in zip((qkv_moment, output_moment, up_moment, down_moment), muon_shares)
+    ]
+    columns = to_planes(moments)
     iterates = ortho(columns.reshape(-1, width)).reshape(columns.shape)
-    iterates = [iterate.T for iterate in from_planes(iterates, [m.shape[0] for m in muon_moments])]
-    moments = [
-        (MUON_MU * moment + factor * share).T for moment, share in zip(muon_moments, muon_shares)
-    ]
+    iterates = [iterate.T for iterate in from_planes(iterates, [m.shape[0] for m in moments])]
+    moments = [moment.T for moment in moments]
     new_qkv = muon_update(qkv_weight, iterates[0])
     new_output = muon_update(output_weight, iterates[1])
     new_up = muon_update(up_weight, iterates[2])

time: 807 us -> 769 us (0.953)
  starting transfers between devices: 123 us -> 91 us
  local copies, waits for them, and re-layouts: 64 us -> 54.2 us
  waiting for transfers between devices: 203 us -> 212 us
    ppermute x85 -> x77, starting transfers between devices: 119 us -> 88 us  [swap(): lax.ppermute(value, axis, [(i, i ^ bit) for i in range(lax.axis_size(axis...]
    ppermute x85 -> x77, waiting for transfers between devices: 184 us -> 190 us  [swap(): lax.ppermute(value, axis, [(i, i ^ bit) for i in range(lax.axis_size(axis...]
    unnamed x297 -> x213, local copies, waits for them, and re-layouts: 17.3 us -> 13.1 us
  transfers between devices with their start and end apart: 89 -> 81, of which waited for: 40 -> 44; matrix products, arithmetic and copies ran while one was open for 29% -> 27% of each run, Pallas kernels for 11% -> 10%
where the time goes in v4:
time: 769 us; the launch traced here: 763 us
  waiting for transfers between devices  212 us (28%)
  matrix products  183 us (24%)
  Pallas kernels  103 us (13%)
  other arithmetic  96.3 us (13%)
  starting transfers between devices  91 us (12%)
  local copies, waits for them, and re-layouts  54.2 us (7%)
  between operations  23.8 us (3%)
    ppermute x77, waiting for transfers between devices, swap(): lax.ppermute(value, axis, [(i, i ^ bit) for i in range(lax.axis_size(axis...  190 us
    dot_general x25, matrix products, mm(): return jnp.einsum(spec, left, right, preferred_element_type=F32)  161 us
    ppermute x77, starting transfers between devices, swap(): lax.ppermute(value, axis, [(i, i ^ bit) for i in range(lax.axis_size(axis...  88 us
    pallas_call x1, Pallas kernels, attend_back(): pl.pallas_call(lambda *refs: attend_back_kernel(width, blocks, *refs), gr...  46.9 us
    pallas_call x3, Pallas kernels, norm_back(): pl.pallas_call(lambda *refs: norm_back_kernel(groups, keep_sum, *refs), g...  34.3 us
    pallas_call x1, Pallas kernels, attend(): pl.pallas_call(lambda *refs: attend_kernel(width, blocks, *refs), grid=(b...  21.2 us
    ppermute x1, waiting for transfers between devices, body(): lax.ppermute(patches[:, shard_len - MAXLEN:], 'seq', [(i, i + 1) for i in...  16.8 us
  transfers between devices with their start and end apart: 81, of which 44 were waited for; matrix products, arithmetic and copies ran while one was open for 27% of the time, Pallas kernels for 10%

profile of v4, /device:TPU:0, one launch (start us, length us, event | category | flops | bytes accessed | tf_op | source)
XLA Modules:
  0.0 763.4 jit_solution(11389723581642747524)
XLA Ops:
  11.7 5.1 collective-permute-start
  22.9 11.6 %collective-permute-done.1 = bf16[136,768]{1,0:T(8,128)(2,1)S(1)} collective-permute-done((bf16[136,768]{1,0:T(8,128)(2,1)S(1)}, bf16[136,768]{1,0:T(8,128)(2,1)S(1)}, u32[]{:S(2)}, u32[]{:S(2)}) %collective-permute-start.1) | collective-permute-done | bytes 208928 | tf_op jit(solution)/shard_map/ppermute | solution.py:38
  44.2 16.8 %collective-permute-done.3 = bf16[6,128,768]{2,1,0:T(8,128)(2,1)S(1)} collective-permute-done((bf16[6,128,768]{2,1,0:T(8,128)(2,1)S(1)}, bf16[6,128,768]{2,1,0:T(8,128)(2,1)S(1)}, u32[]{:S(2)}, u32[]{:S(2)}) %collective-permute-start.3) | collective-permute-done | bytes 1179680 | tf_op jit(solution)/shard_map/ppermute | solution.py:688
  61.0 4.2 collective-permute-done.4
  65.8 10.3 %fusion.23 = bf16[1664,768]{1,0:T(8,128)(2,1)} fusion(bf16[3072,768]{1,0:T(8,128)(2,1)S(1)} %bitcast.403, s32[1664]{0:T(1024)S(1)} %get-tuple-element.309), kind=kOutput, calls=%fused_computation.57 | convolution fusion | flops 7858126848 | bytes 7281152 | tf_op jit(solution)/shard_map/rw,wi->ri/dot_general | solution.py:515
  76.1 3.1 collective-permute-done.6
  89.4 3.7 collective-permute-start.10
  97.4 3.9 collective-permute-done.10
  101.3 4.3 collective-permute-done.9
  111.9 4.5 convolution_add_fusion.1.refs_0_
  125.2 3.1 multiply_reduce_fusion.2
  134.2 9.3 %add_convert_fusion.refs_0_ = bf16[1664,2304]{1,0:T(8,128)(2,1)} fusion(bf16[2304,768]{1,0:T(8,128)(2,1)S(1)} %bitcast.406, f32[2304]{0:T(1024)S(1)} %pad_maximum_fusion.14, f32[1664,768]{1,0:T(8,128)S(1)} %bitcast.384, f32[768]{0:T(1024)S(1)} %get-tuple-element.297, f32[768]{0:T(1024)S(1)} %get-tuple-element.305, f32[1664]{0:T(1024)S(1)} %add_rsqrt_fusion.2, ...), kind=kOutput, calls=%fused_computation.7 | convolution fusion | flops 5902860288 | bytes 16347136 | tf_op jit(solution)/shard_map/rd,ed->re/dot_general | solution.py:515
  150.3 3.1 pad_maximum_fusion.3
  153.5 21.2 %shard_map.435 = (bf16[1664,768]{1,0:T(8,128)(2,1)}, f32[13,6,256]{2,1,0:T(8,128)}) custom-call(bf16[1664,2304]{1,0:T(8,128)(2,1)} %add_convert_fusion.refs_0_, s32[13,1,128]{2,1,0:T(1,128)} %select_n.787.refs_1_.refs_3_, s32[1920,1]{1,0:T(8,128)} %broadcast_in_dim.215.refs_2_.refs_4_), custom_call_target="tpu_custom_call" | custom-call | tf_op jit(solution)/shard_map/pallas_call | solution.py:352
  174.9 5.7 fusion.135
  185.6 8.9 %multiply_convert_fusion.1 = (bf16[1664,1536]{1,0:T(8,128)(2,1)S(1)}, f32[1664,1536]{1,0:T(8,128)}) fusion(f32[1536]{0:T(1024)S(1)} %add.682, bf16[1664,768]{1,0:T(8,128)(2,1)S(1)} %add_convert_fusion.1, bf16[1536,768]{1,0:T(8,128)(2,1)} %bitcast.38), kind=kOutput, calls=%fused_computation.24 | convolution fusion | flops 3941203968 | bytes 20256768 | tf_op jit(solution)/shard_map/rd,fd->rf/dot_general | solution.py:515
  194.5 4.2 fusion.137
  198.8 9.0 %multiply_convert_fusion = (bf16[1664,1536]{1,0:T(8,128)(2,1)S(1)}, f32[1664,1536]{1,0:T(8,128)}) fusion(f32[1536]{0:T(1024)S(1)} %add.686, bf16[1664,768]{1,0:T(8,128)(2,1)S(1)} %add_convert_fusion.1, bf16[1536,768]{1,0:T(8,128)(2,1)} %bitcast.44), kind=kOutput, calls=%fused_computation.22 | convolution fusion | flops 3941203968 | bytes 20256768 | tf_op jit(solution)/shard_map/rd,fd->rf/dot_general | solution.py:515
  207.8 4.8 fusion.136
  239.8 5.6 fusion.39
  258.2 3.5 collective-permute-start.34
  267.6 11.4 %shard_map.436 = (bf16[1664,768]{1,0:T(8,128)(2,1)}, f32[8,768]{1,0:T(8,128)}, f32[1664,768]{1,0:T(8,128)}) custom-call(f32[1664,768]{1,0:T(8,128)} %copy-done.4, f32[96,768]{1,0:T(8,128)} %maximum_divide_fusion.refs_1_, s32[1664,1]{1,0:T(8,128)} %select_n.869.refs_2_, f32[1,768]{1,0:T(1,128)} %get-tuple-element.294.refs_3_), custom_call_target="tpu_custom_call" | custom-call | tf_op jit(solution)/shard_map/pallas_call | solution.py:448
  279.0 7.5 fusion.140
  286.5 9.3 %fusion.139 = f32[1536,768]{1,0:T(8,128)} fusion(bf16[1664,1536]{1,0:T(8,128)(2,1)} %copy-done.94, bf16[1664,768]{1,0:T(8,128)(2,1)S(1)} %copy-done.91), kind=kOutput, calls=%fused_computation.400 | convolution fusion | flops 3925868544 | bytes 12386304 | tf_op jit(solution)/shard_map/rf,rd->fd/dot_general | solution.py:515
  295.8 9.8 %fusion.6 = bf16[1664,1536]{1,0:T(8,128)(2,1)S(1)} fusion(bf16[1664,768]{1,0:T(8,128)(2,1)S(1)} %copy-done.91, bf16[1536,768]{1,0:T(8,128)(2,1)S(1)} %bitcast.411, f32[1664,1536]{1,0:T(8,128)} %get-tuple-element.322, f32[1536]{0:T(1024)S(1)} %copy-done.74), kind=kOutput, calls=%fused_computation.13 | convolution fusion | flops 3953983488 | bytes 20256768 | tf_op jit(solution)/shard_map/rd,fd->rf/dot_general | solution.py:515
  305.6 4.7 fusion.142
  310.3 9.3 %fusion.12 = bf16[1664,1536]{1,0:T(8,128)(2,1)S(1)} fusion(bf16[1664,768]{1,0:T(8,128)(2,1)S(1)} %copy-done.91, bf16[1536,768]{1,0:T(8,128)(2,1)S(1)} %bitcast.439, f32[1664,1536]{1,0:T(8,128)} %get-tuple-element.324, f32[1536]{0:T(1024)S(1)} %copy-done.72), kind=kOutput, calls=%fused_computation.19 | convolution fusion | flops 3953983488 | bytes 20256768 | tf_op jit(solution)/shard_map/rd,fd->rf/dot_general | solution.py:515
  319.6 4.6 fusion.141
  327.4 7.6 %fusion.143 = f32[1664,768]{1,0:T(8,128)} fusion(bf16[1664,1536]{1,0:T(8,128)(2,1)S(1)} %fusion.6, bf16[1536,768]{1,0:T(8,128)(2,1)} %bitcast.38), kind=kOutput, calls=%fused_computation.404 | convolution fusion | flops 3925868544 | bytes 12582912 | tf_op jit(solution)/shard_map/rf,fd->rd/dot_general | solution.py:515
  335.1 8.3 %convolution_add_fusion.2.refs_1_ = f32[1664,768]{1,0:T(8,128)} fusion(f32[1664,768]{1,0:T(8,128)} %fusion.143, bf16[1664,1536]{1,0:T(8,128)(2,1)S(1)} %fusion.12, bf16[1536,768]{1,0:T(8,128)(2,1)} %bitcast.44), kind=kOutput, calls=%fused_computation.52 | convolution fusion | flops 3927146496 | bytes 17694720 | tf_op jit(solution)/shard_map/rf,fd->rd/dot_general | solution.py:515
  354.9 12.1 %shard_map.437 = (bf16[1664,768]{1,0:T(8,128)(2,1)}, f32[8,768]{1,0:T(8,128)}, f32[1664,768]{1,0:T(8,128)}) custom-call(f32[1664,768]{1,0:T(8,128)} %copy-done.3, f32[1664,768]{1,0:T(8,128)} %convolution_add_fusion.2.refs_1_, f32[1664,768]{1,0:T(8,128)} %get-tuple-element.129.refs_2_, f32[1,768]{1,0:T(1,128)} %get-tuple-element.295.refs_3_), custom_call_target="tpu_custom_call" | custom-call | tf_op jit(solution)/shard_map/pallas_call | solution.py:448
  367.0 5.3 convolution_convert_fusion.refs_1_
  373.5 46.9 %shard_map.438 = bf16[1664,2304]{1,0:T(8,128)(2,1)} custom-call(bf16[1664,2304]{1,0:T(8,128)(2,1)} %add_convert_fusion.refs_0_, bf16[1664,768]{1,0:T(8,128)(2,1)} %convolution_convert_fusion.refs_1_, f32[13,6,256]{2,1,0:T(8,128)} %get-tuple-element.134.refs_2_, s32[13,1,128]{2,1,0:T(1,128)} %select_n.787.refs_1_.refs_3_, ...), custom_call_target="tpu_custom_call" | custom-call | tf_op jit(solution)/shard_map/pallas_call | solution.py:377
  420.5 3.8 fusion.144
  434.1 7.7 %fusion.145.refs_1_ = f32[1664,768]{1,0:T(8,128)} fusion(bf16[1664,2304]{1,0:T(8,128)(2,1)S(1)} %bitcast.388, bf16[2304,768]{1,0:T(8,128)(2,1)S(1)} %bitcast.407), kind=kOutput, calls=%fused_computation.406 | convolution fusion | flops 5888802816 | bytes 16318464 | tf_op jit(solution)/shard_map/re,ed->rd/dot_general | solution.py:515
  441.8 10.8 %shard_map.439 = (bf16[1664,768]{1,0:T(8,128)(2,1)}, f32[8,768]{1,0:T(8,128)}) custom-call(f32[1664,768]{1,0:T(8,128)} %convolution_add_fusion.1.refs_0_, f32[1664,768]{1,0:T(8,128)} %fusion.145.refs_1_, f32[1664,768]{1,0:T(8,128)} %get-tuple-element.138.refs_2_, f32[1,768]{1,0:T(1,128)} %get-tuple-element.293.refs_3_), custom_call_target="tpu_custom_call" | custom-call | tf_op jit(solution)/shard_map/pallas_call | solution.py:448
  452.7 5.0 fusion.146
  467.3 7.6 fusion.120
  487.6 4.8 fusion.21
  492.4 3.3 maximum_add_fusion
  501.0 3.2 convert_reduce_fusion.2
  504.2 3.2 convert_reduce_fusion.1
  507.5 4.4 convert_reduce_fusion
  512.5 15.3 %collective-permute-done.44 = f32[2,192,768]{2,1,0:T(8,128)} collective-permute-done((f32[2,192,768]{2,1,0:T(8,128)}, f32[2,192,768]{2,1,0:T(8,128)}, u32[]{:S(2)}, u32[]{:S(2)}) %collective-permute-start.44) | collective-permute-done | bytes 1179680 | tf_op jit(solution)/shard_map/ppermute | solution.py:38
  530.4 3.3 collective-permute-done.45
  540.9 14.3 %collective-permute-done.46 = f32[4,120,384]{2,1,0:T(8,128)S(1)} collective-permute-done((f32[4,120,384]{2,1,0:T(8,128)S(1)}, f32[4,120,384]{2,1,0:T(8,128)S(1)}, u32[]{:S(2)}, u32[]{:S(2)}) %collective-permute-start.46) | collective-permute-done | bytes 737312 | tf_op jit(solution)/shard_map/ppermute | solution.py:38
  561.3 6.9 collective-permute-done.53
  571.0 12.8 %collective-permute-done.49 = f32[2,120,768]{2,1,0:T(8,128)S(1)} collective-permute-done((f32[2,120,768]{2,1,0:T(8,128)}, f32[2,120,768]{2,1,0:T(8,128)S(1)}, u32[]{:S(2)}, u32[]{:S(2)}) %collective-permute-start.49) | collective-permute-done | bytes 737312 | tf_op jit(solution)/shard_map/ppermute | solution.py:38
  587.8 15.6 %collective-permute-done.54 = f32[1,120,768]{2,1,0:T(8,128)S(1)} collective-permute-done((f32[1,120,768]{2,1,0:T(8,128)S(1)}, f32[1,120,768]{2,1,0:T(8,128)S(1)}, u32[]{:S(2)}, u32[]{:S(2)}) %collective-permute-start.54) | collective-permute-done | bytes 368672 | tf_op jit(solution)/shard_map/ppermute | solution.py:38
  635.5 8.4 %collective-permute-done.65 = f32[96,768]{1,0:T(8,128)S(1)} collective-permute-done((f32[96,768]{1,0:T(8,128)S(1)}, f32[96,768]{1,0:T(8,128)S(1)}, u32[]{:S(2)}, u32[]{:S(2)}) %collective-permute-start.65) | collective-permute-done | bytes 294944 | tf_op jit(solution)/shard_map/ppermute | solution.py:38
  643.9 8.2 %collective-permute-done.66 = f32[96,768]{1,0:T(8,128)S(1)} collective-permute-done((f32[96,768]{1,0:T(8,128)S(1)}, f32[96,768]{1,0:T(8,128)S(1)}, u32[]{:S(2)}, u32[]{:S(2)}) %collective-permute-start.66) | collective-permute-done | bytes 294944 | tf_op jit(solution)/shard_map/ppermute | solution.py:38
  653.6 3.3 fusion.147
  658.0 3.2 collective-permute-done.68
  667.3 6.4 collective-permute-done.69
  673.6 6.2 collective-permute-done.70
  686.0 5.8 collective-permute-done.72
  691.8 4.4 collective-permute-done.73
  698.6 6.1 multiply_subtract_fusion
  707.3 3.0 fusion.148
  710.4 3.0 fusion.149
  713.4 3.7 fusion.30
  725.0 3.6 collective-permute-start.77
  730.9 3.9 collective-permute-done.76
  734.7 17.9 %collective-permute-done.77 = f32[96,768]{1,0:T(8,128)S(1)} collective-permute-done((f32[96,768]{1,0:T(8,128)S(1)}, f32[96,768]{1,0:T(8,128)S(1)}, u32[]{:S(2)}, u32[]{:S(2)}) %collective-permute-start.77) | collective-permute-done | bytes 294944 | tf_op jit(solution)/shard_map/ppermute | solution.py:38
  (566 shorter events, 247.5 us)
Async XLA Ops:
  7.2 232.6 %all-gather.3.cloned.1.call-start = ((), (), s32[]{:S(2)}) async-start(), calls=%async_computation | async-start | bytes 5406720 | tf_op jit(solution)/shard_map/all_gather | solution.py:722
  11.7 11.3 %collective-permute-start = (bf16[136,768]{1,0:T(8,128)(2,1)S(1)}, bf16[136,768]{1,0:T(8,128)(2,1)S(1)}, u32[]{:S(2)}, u32[]{:S(2)}) collective-permute-start(bf16[136,768]{1,0:T(8,128)(2,1)S(1)} %constant_dynamic-update-slice_fusion), channel_id=1, source_target_pairs={{0,3},{1,2},{2,1},{3,0},{4,7},{5,6},{6,5},{7,4},{8,11},{9,10},{10,... | collective-permute-start | bytes 626696 | tf_op jit(solution)/shard_map/ppermute | solution.py:38
  16.8 17.7 %collective-permute-start.1 = (bf16[136,768]{1,0:T(8,128)(2,1)S(1)}, bf16[136,768]{1,0:T(8,128)(2,1)S(1)}, u32[]{:S(2)}, u32[]{:S(2)}) collective-permute-start(bf16[136,768]{1,0:T(8,128)(2,1)S(1)} %constant_dynamic-update-slice_fusion), channel_id=1, source_target_pairs={{0,2},{1,3},{2,0},{3,1},{4,6},{5,7},{6,4},{7,5},{8,10},{9,11},{10,... | collective-permute-start | bytes 626696 | tf_op jit(solution)/shard_map/ppermute | solution.py:38
  16.8 17.7 %collective-permute-start.2 = (bf16[136,768]{1,0:T(8,128)(2,1)S(1)}, bf16[136,768]{1,0:T(8,128)(2,1)S(1)}, u32[]{:S(2)}, u32[]{:S(2)}) collective-permute-start(bf16[136,768]{1,0:T(8,128)(2,1)S(1)} %constant_dynamic-update-slice_fusion), channel_id=1, source_target_pairs={{0,1},{1,0},{2,3},{3,2},{4,5},{5,4},{6,7},{7,6},{8,9},{9,8},{10,11... | collective-permute-start | bytes 626696 | tf_op jit(solution)/shard_map/ppermute | solution.py:38
  34.9 26.1 %collective-permute-start.3 = (bf16[6,128,768]{2,1,0:T(8,128)(2,1)S(1)}, bf16[6,128,768]{2,1,0:T(8,128)(2,1)S(1)}, u32[]{:S(2)}, u32[]{:S(2)}) collective-permute-start(bf16[6,128,768]{2,1,0:T(8,128)(2,1)S(1)} %get-tuple-element.242), channel_id=1, source_target_pairs={{0,1},{1,2},{2,3},{4,5},{5,6},{6,7},{8,9},{9,10},{10,11},{12,13},{... | collective-permute-start | bytes 3538952 | tf_op jit(solution)/shard_map/ppermute | solution.py:688
  36.6 28.6 %collective-permute-start.4 = (bf16[6,128,768]{2,1,0:T(8,128)(2,1)S(1)}, bf16[6,128,768]{2,1,0:T(8,128)(2,1)S(1)}, u32[]{:S(2)}, u32[]{:S(2)}) collective-permute-start(bf16[6,128,768]{2,1,0:T(8,128)(2,1)S(1)} %get-tuple-element.243), channel_id=1, source_target_pairs={{1,0},{2,1},{3,2},{5,4},{6,5},{7,6},{9,8},{10,9},{11,10},{13,12},{... | collective-permute-start | bytes 3538952 | tf_op jit(solution)/shard_map/ppermute | solution.py:689
  40.7 35.4 %collective-permute-start.5 = (bf16[4,136,768]{2,1,0:T(8,128)(2,1)S(1)}, bf16[4,136,768]{2,1,0:T(8,128)(2,1)S(1)}, u32[]{:S(2)}, u32[]{:S(2)}) collective-permute-start(bf16[4,136,768]{2,1,0:T(8,128)(2,1)S(1)} %pad_maximum_fusion.11), channel_id=1, source_target_pairs={{0,8},{4,12},{8,0},{12,4},{16,24},{20,28},{24,16},{28,20},{1,9},{5... | collective-permute-start | bytes 2506760 | tf_op jit(solution)/shard_map/ppermute | solution.py:38
  42.2 37.0 %collective-permute-start.6 = (bf16[4,136,768]{2,1,0:T(8,128)(2,1)S(1)}, bf16[4,136,768]{2,1,0:T(8,128)(2,1)S(1)}, u32[]{:S(2)}, u32[]{:S(2)}) collective-permute-start(bf16[4,136,768]{2,1,0:T(8,128)(2,1)S(1)} %pad_maximum_fusion.11), channel_id=1, source_target_pairs={{0,16},{4,20},{8,24},{12,28},{16,0},{20,4},{24,8},{28,12},{1,17},{... | collective-permute-start | bytes 2506760 | tf_op jit(solution)/shard_map/ppermute | solution.py:38
  43.7 35.5 %collective-permute-start.7 = (bf16[4,136,768]{2,1,0:T(8,128)(2,1)S(1)}, bf16[4,136,768]{2,1,0:T(8,128)(2,1)S(1)}, u32[]{:S(2)}, u32[]{:S(2)}) collective-permute-start(bf16[4,136,768]{2,1,0:T(8,128)(2,1)S(1)} %pad_maximum_fusion.11), channel_id=1, source_target_pairs={{0,24},{4,28},{8,16},{12,20},{16,8},{20,12},{24,0},{28,4},{1,25},{... | collective-permute-start | bytes 2506760 | tf_op jit(solution)/shard_map/ppermute | solution.py:38
  80.1 27.4 %collective-permute-start.8 = (bf16[4,4,136,768]{3,2,1,0:T(8,128)(2,1)S(1)}, bf16[4,4,136,768]{3,2,1,0:T(8,128)(2,1)}, u32[]{:S(2)}, u32[]{:S(2)}) collective-permute-start(bf16[4,4,136,768]{3,2,1,0:T(8,128)(2,1)S(1)} %pad_maximum_fusion.2), channel_id=1, source_target_pairs={{0,4},{4,0},{8,12},{12,8},{16,20},{20,16},{24,28},{28,24},{1,5},{5... | collective-permute-start | bytes 10027016 | tf_op jit(solution)/shard_map/ppermute | solution.py:38
  89.4 11.9 %collective-permute-start.10 = (bf16[96,768]{1,0:T(8,128)(2,1)}, bf16[96,768]{1,0:T(8,128)(2,1)S(1)}, u32[]{:S(2)}, u32[]{:S(2)}) collective-permute-start(bf16[96,768]{1,0:T(8,128)(2,1)} %convert_bitcast_fusion.1), channel_id=1, source_target_pairs={{0,2},{1,3},{2,0},{3,1},{4,6},{5,7},{6,4},{7,5},{8,10},{9,11},{10,... | collective-permute-start | bytes 442376 | tf_op jit(solution)/shard_map/ppermute | solution.py:38
  93.2 8.1 %collective-permute-start.11 = (bf16[96,768]{1,0:T(8,128)(2,1)}, bf16[96,768]{1,0:T(8,128)(2,1)S(1)}, u32[]{:S(2)}, u32[]{:S(2)}) collective-permute-start(bf16[96,768]{1,0:T(8,128)(2,1)} %convert_bitcast_fusion.1), channel_id=1, source_target_pairs={{0,1},{1,0},{2,3},{3,2},{4,5},{5,4},{6,7},{7,6},{8,9},{9,8},{10,11... | collective-permute-start | bytes 442376 | tf_op jit(solution)/shard_map/ppermute | solution.py:38
  95.0 10.6 %collective-permute-start.9 = (bf16[96,768]{1,0:T(8,128)(2,1)}, bf16[96,768]{1,0:T(8,128)(2,1)S(1)}, u32[]{:S(2)}, u32[]{:S(2)}) collective-permute-start(bf16[96,768]{1,0:T(8,128)(2,1)} %convert_bitcast_fusion.1), channel_id=1, source_target_pairs={{0,3},{1,2},{2,1},{3,0},{4,7},{5,6},{6,5},{7,4},{8,11},{9,10},{10,... | collective-permute-start | bytes 442376 | tf_op jit(solution)/shard_map/ppermute | solution.py:38
  116.4 30.2 %collective-permute-start.14 = (bf16[4,96,768]{2,1,0:T(8,128)(2,1)S(1)}, bf16[4,96,768]{2,1,0:T(8,128)(2,1)}, u32[]{:S(2)}, u32[]{:S(2)}) collective-permute-start(bf16[4,96,768]{2,1,0:T(8,128)(2,1)S(1)} %copy-done.32), channel_id=1, source_target_pairs={{0,8},{4,12},{8,0},{12,4},{16,24},{20,28},{24,16},{28,20},{1,9},{5... | collective-permute-start | bytes 1769480 | tf_op jit(solution)/shard_map/ppermute | solution.py:38
  117.6 29.0 %collective-permute-start.15 = (bf16[4,96,768]{2,1,0:T(8,128)(2,1)S(1)}, bf16[4,96,768]{2,1,0:T(8,128)(2,1)}, u32[]{:S(2)}, u32[]{:S(2)}) collective-permute-start(bf16[4,96,768]{2,1,0:T(8,128)(2,1)S(1)} %copy-done.32), channel_id=1, source_target_pairs={{0,16},{4,20},{8,24},{12,28},{16,0},{20,4},{24,8},{28,12},{1,17},{... | collective-permute-start | bytes 1769480 | tf_op jit(solution)/shard_map/ppermute | solution.py:38
  118.4 28.2 %collective-permute-start.16 = (bf16[4,96,768]{2,1,0:T(8,128)(2,1)S(1)}, bf16[4,96,768]{2,1,0:T(8,128)(2,1)}, u32[]{:S(2)}, u32[]{:S(2)}) collective-permute-start(bf16[4,96,768]{2,1,0:T(8,128)(2,1)S(1)} %copy-done.32), channel_id=1, source_target_pairs={{0,24},{4,28},{8,16},{12,20},{16,8},{20,12},{24,0},{28,4},{1,25},{... | collective-permute-start | bytes 1769480 | tf_op jit(solution)/shard_map/ppermute | solution.py:38
  119.9 11.4 %collective-permute-start.12 = (bf16[1,96,768]{2,1,0:T(8,128)(2,1)S(1)}, bf16[1,96,768]{2,1,0:T(8,128)(2,1)S(1)}, u32[]{:S(2)}, u32[]{:S(2)}) collective-permute-start(bf16[1,96,768]{2,1,0:T(8,128)(2,1)S(1)} %bitcast.419), channel_id=1, source_target_pairs={{0,1},{1,0},{2,3},{3,2},{4,5},{5,4},{6,7},{7,6},{8,9},{9,8},{10,11... | collective-permute-start | bytes 442376 | tf_op jit(solution)/shard_map/ppermute | solution.py:38
  131.3 15.1 %collective-permute-start.13 = (bf16[2,96,768]{2,1,0:T(8,128)(2,1)S(1)}, bf16[2,96,768]{2,1,0:T(8,128)(2,1)S(1)}, u32[]{:S(2)}, u32[]{:S(2)}) collective-permute-start(bf16[2,96,768]{2,1,0:T(8,128)(2,1)S(1)} %maximum_select_fusion.7), channel_id=1, source_target_pairs={{0,2},{1,3},{2,0},{3,1},{4,6},{5,7},{6,4},{7,5},{8,10},{9,11},{10,... | collective-permute-start | bytes 884744 | tf_op jit(solution)/shard_map/ppermute | solution.py:38
  146.6 28.0 %collective-permute-start.17 = (bf16[4,96,768]{2,1,0:T(8,128)(2,1)S(1)}, bf16[4,96,768]{2,1,0:T(8,128)(2,1)}, u32[]{:S(2)}, u32[]{:S(2)}) collective-permute-start(bf16[4,96,768]{2,1,0:T(8,128)(2,1)S(1)} %maximum_select_fusion.4), channel_id=1, source_target_pairs={{0,8},{4,12},{8,0},{12,4},{16,24},{20,28},{24,16},{28,20},{1,9},{5... | collective-permute-start | bytes 1769480 | tf_op jit(solution)/shard_map/ppermute | solution.py:38
  147.9 26.8 %collective-permute-start.18 = (bf16[4,96,768]{2,1,0:T(8,128)(2,1)S(1)}, bf16[4,96,768]{2,1,0:T(8,128)(2,1)}, u32[]{:S(2)}, u32[]{:S(2)}) collective-permute-start(bf16[4,96,768]{2,1,0:T(8,128)(2,1)S(1)} %maximum_select_fusion.4), channel_id=1, source_target_pairs={{0,16},{4,20},{8,24},{12,28},{16,0},{20,4},{24,8},{28,12},{1,17},{... | collective-permute-start | bytes 1769480 | tf_op jit(solution)/shard_map/ppermute | solution.py:38
  148.7 26.2 %collective-permute-start.19 = (bf16[4,96,768]{2,1,0:T(8,128)(2,1)S(1)}, bf16[4,96,768]{2,1,0:T(8,128)(2,1)}, u32[]{:S(2)}, u32[]{:S(2)}) collective-permute-start(bf16[4,96,768]{2,1,0:T(8,128)(2,1)S(1)} %maximum_select_fusion.4), channel_id=1, source_target_pairs={{0,24},{4,28},{8,16},{12,20},{16,8},{20,12},{24,0},{28,4},{1,25},{... | collective-permute-start | bytes 1769480 | tf_op jit(solution)/shard_map/ppermute | solution.py:38
  153.4 45.4 %collective-permute-start.20 = (bf16[4,4,96,768]{3,2,1,0:T(8,128)(2,1)}, bf16[4,4,96,768]{3,2,1,0:T(8,128)(2,1)}, u32[]{:S(2)}, u32[]{:S(2)}) collective-permute-start(bf16[4,4,96,768]{3,2,1,0:T(8,128)(2,1)} %pad_maximum_fusion.3), channel_id=1, source_target_pairs={{0,4},{4,0},{8,12},{12,8},{16,20},{20,16},{24,28},{28,24},{1,5},{5... | collective-permute-start | bytes 7077896 | tf_op jit(solution)/shard_map/ppermute | solution.py:38
  153.4 325.1 %all-gather.5.cloned.1.call-start = ((), (), s32[]{:S(2)}) async-start(), calls=%async_computation.1 | async-start | bytes 6881280 | tf_op jit(solution)/shard_map/all_gather | solution.py:771
  184.2 23.6 %collective-permute-start.21 = (bf16[4,4,96,768]{3,2,1,0:T(8,128)(2,1)S(1)}, bf16[4,4,96,768]{3,2,1,0:T(8,128)(2,1)S(1)}, u32[]{:S(2)}, u32[]{:S(2)}) collective-permute-start(bf16[4,4,96,768]{3,2,1,0:T(8,128)(2,1)S(1)} %pad_maximum_fusion.4), channel_id=1, source_target_pairs={{0,4},{4,0},{8,12},{12,8},{16,20},{20,16},{24,28},{28,24},{1,5},{5... | collective-permute-start | bytes 7077896 | tf_op jit(solution)/shard_map/ppermute | solution.py:38
  218.0 8.1 %collective-permute-start.22 = (bf16[24,768]{1,0:T(8,128)(2,1)S(1)}, bf16[24,768]{1,0:T(8,128)(2,1)S(1)}, u32[]{:S(2)}, u32[]{:S(2)}) collective-permute-start(bf16[24,768]{1,0:T(8,128)(2,1)S(1)} %get-tuple-element.290), channel_id=1, source_target_pairs={{0,1},{1,0},{2,3},{3,2},{4,5},{5,4},{6,7},{7,6},{8,9},{9,8},{10,11... | collective-permute-start | bytes 110600 | tf_op jit(solution)/shard_map/ppermute | solution.py:38
  219.5 6.6 collective-permute-start.23
  222.2 6.7 collective-permute-start.24
  257.3 6.6 collective-permute-start.33
  258.2 7.7 %collective-permute-start.34 = (f32[24,768]{1,0:T(8,128)S(1)}, f32[24,768]{1,0:T(8,128)S(1)}, u32[]{:S(2)}, u32[]{:S(2)}) collective-permute-start(f32[24,768]{1,0:T(8,128)S(1)} %fusion.88), channel_id=1, source_target_pairs={{0,2},{1,3},{2,0},{3,1},{4,6},{5,7},{6,4},{7,5},{8,10},{9,11},{10,... | collective-permute-start | bytes 221192 | tf_op jit(solution)/shard_map/ppermute | solution.py:38
  326.9 16.4 %collective-permute-start.37 = (f32[2,2,4,96,768]{4,3,2,0,1:T(8,128)}, f32[2,2,4,96,768]{4,3,2,0,1:T(8,128)S(1)}, u32[]{:S(2)}, u32[]{:S(2)}) collective-permute-start(f32[2,2,4,96,768]{4,3,2,0,1:T(8,128)} %copy.91), channel_id=1, source_target_pairs={{0,4},{4,0},{8,12},{12,8},{16,20},{20,16},{24,28},{28,24},{1,5},{5... | collective-permute-start | bytes 14155784 | tf_op jit(solution)/shard_map/ppermute | solution.py:38
  326.9 23.3 %collective-permute-start.36 = (f32[2,2,4,96,768]{4,3,2,1,0:T(8,128)}, f32[2,2,4,96,768]{4,3,2,1,0:T(8,128)S(1)}, u32[]{:S(2)}, u32[]{:S(2)}) collective-permute-start(f32[2,2,4,96,768]{4,3,2,1,0:T(8,128)} %bitcast.437), channel_id=1, source_target_pairs={{0,4},{4,0},{8,12},{12,8},{16,20},{20,16},{24,28},{28,24},{1,5},{5... | collective-permute-start | bytes 14155784 | tf_op jit(solution)/shard_map/ppermute | solution.py:38
  372.3 53.4 %collective-permute-start.39 = (f32[2,4,96,768]{3,2,1,0:T(8,128)}, f32[2,4,96,768]{3,2,1,0:T(8,128)S(1)}, u32[]{:S(2)}, u32[]{:S(2)}) collective-permute-start(f32[2,4,96,768]{3,2,1,0:T(8,128)} %slice_bitcast_fusion.2), channel_id=1, source_target_pairs={{0,8},{4,12},{8,0},{12,4},{16,24},{20,28},{24,16},{28,20},{1,9},{5... | collective-permute-start | bytes 7077896 | tf_op jit(solution)/shard_map/ppermute | solution.py:38
  373.1 56.0 %collective-permute-start.38 = (f32[2,4,96,768]{3,2,1,0:T(8,128)}, f32[2,4,96,768]{3,2,1,0:T(8,128)}, u32[]{:S(2)}, u32[]{:S(2)}) collective-permute-start(f32[2,4,96,768]{3,2,1,0:T(8,128)} %slice_bitcast_fusion.3), channel_id=1, source_target_pairs={{0,16},{4,20},{8,24},{12,28},{16,0},{20,4},{24,8},{28,12},{1,17},{... | collective-permute-start | bytes 7077896 | tf_op jit(solution)/shard_map/ppermute | solution.py:38
  432.3 27.4 %collective-permute-start.40 = (f32[4,96,768]{2,1,0:T(8,128)}, f32[4,96,768]{2,1,0:T(8,128)}, u32[]{:S(2)}, u32[]{:S(2)}) collective-permute-start(f32[4,96,768]{2,1,0:T(8,128)} %slice_bitcast_fusion.9), channel_id=1, source_target_pairs={{0,8},{4,12},{8,0},{12,4},{16,24},{20,28},{24,16},{28,20},{1,9},{5... | collective-permute-start | bytes 3538952 | tf_op jit(solution)/shard_map/ppermute | solution.py:38
  433.1 28.1 %collective-permute-start.41 = (f32[4,96,768]{2,1,0:T(8,128)}, f32[4,96,768]{2,1,0:T(8,128)}, u32[]{:S(2)}, u32[]{:S(2)}) collective-permute-start(f32[4,96,768]{2,1,0:T(8,128)} %slice_bitcast_fusion.8), channel_id=1, source_target_pairs={{0,16},{4,20},{8,24},{12,28},{16,0},{20,4},{24,8},{28,12},{1,17},{... | collective-permute-start | bytes 3538952 | tf_op jit(solution)/shard_map/ppermute | solution.py:38
  478.5 13.9 %collective-permute-start.42 = (f32[2,2,4,120,768]{4,3,2,1,0:T(8,128)}, f32[2,2,4,120,768]{4,3,2,1,0:T(8,128)}, u32[]{:S(2)}, u32[]{:S(2)}) collective-permute-start(f32[2,2,4,120,768]{4,3,2,1,0:T(8,128)} %pad_maximum_fusion), channel_id=1, source_target_pairs={{0,4},{4,0},{8,12},{12,8},{16,20},{20,16},{24,28},{28,24},{1,5},{5... | collective-permute-start | bytes 17694728 | tf_op jit(solution)/shard_map/ppermute | solution.py:38
  498.7 35.0 %collective-permute-start.45 = (f32[2,4,120,384]{3,2,1,0:T(8,128)}, f32[2,4,120,384]{3,2,1,0:T(8,128)}, u32[]{:S(2)}, u32[]{:S(2)}) collective-permute-start(f32[2,4,120,384]{3,2,1,0:T(8,128)} %dynamic-slice_bitcast_fusion.2), channel_id=1, source_target_pairs={{0,8},{4,12},{8,0},{12,4},{16,24},{20,28},{24,16},{28,20},{1,9},{5... | collective-permute-start | bytes 4423688 | tf_op jit(solution)/shard_map/ppermute | solution.py:38
  499.5 28.4 %collective-permute-start.44 = (f32[2,192,768]{2,1,0:T(8,128)}, f32[2,192,768]{2,1,0:T(8,128)}, u32[]{:S(2)}, u32[]{:S(2)}) collective-permute-start(f32[2,192,768]{2,1,0:T(8,128)} %get-tuple-element.158), channel_id=1, source_target_pairs={{0,1},{1,0},{2,3},{3,2},{4,5},{5,4},{6,7},{7,6},{8,9},{9,8},{10,11... | collective-permute-start | bytes 3538952 | tf_op jit(solution)/shard_map/ppermute | solution.py:38
  499.8 35.6 %collective-permute-start.43 = (f32[2,4,120,384]{3,2,1,0:T(8,128)}, f32[2,4,120,384]{3,2,1,0:T(8,128)}, u32[]{:S(2)}, u32[]{:S(2)}) collective-permute-start(f32[2,4,120,384]{3,2,1,0:T(8,128)} %dynamic-slice_bitcast_fusion.3), channel_id=1, source_target_pairs={{0,16},{4,20},{8,24},{12,28},{16,0},{20,4},{24,8},{28,12},{1,17},{... | collective-permute-start | bytes 4423688 | tf_op jit(solution)/shard_map/ppermute | solution.py:38
  537.0 18.2 %collective-permute-start.46 = (f32[4,120,384]{2,1,0:T(8,128)S(1)}, f32[4,120,384]{2,1,0:T(8,128)S(1)}, u32[]{:S(2)}, u32[]{:S(2)}) collective-permute-start(f32[4,120,384]{2,1,0:T(8,128)S(1)} %dynamic-slice_bitcast_fusion.13), channel_id=1, source_target_pairs={{0,8},{4,12},{8,0},{12,4},{16,24},{20,28},{24,16},{28,20},{1,9},{5... | collective-permute-start | bytes 2211848 | tf_op jit(solution)/shard_map/ppermute | solution.py:38
  537.8 17.8 %collective-permute-start.47 = (f32[4,120,384]{2,1,0:T(8,128)S(1)}, f32[4,120,384]{2,1,0:T(8,128)S(1)}, u32[]{:S(2)}, u32[]{:S(2)}) collective-permute-start(f32[4,120,384]{2,1,0:T(8,128)S(1)} %dynamic-slice_bitcast_fusion.12), channel_id=1, source_target_pairs={{0,16},{4,20},{8,24},{12,28},{16,0},{20,4},{24,8},{28,12},{1,17},{... | collective-permute-start | bytes 2211848 | tf_op jit(solution)/shard_map/ppermute | solution.py:38
  538.6 29.7 %collective-permute-start.53 = (f32[1,192,768]{2,1,0:T(8,128)}, f32[1,192,768]{2,1,0:T(8,128)}, u32[]{:S(2)}, u32[]{:S(2)}) collective-permute-start(f32[1,192,768]{2,1,0:T(8,128)} %get-tuple-element.166), channel_id=1, source_target_pairs={{0,2},{1,3},{2,0},{3,1},{4,6},{5,7},{6,4},{7,5},{8,10},{9,11},{10,... | collective-permute-start | bytes 1769480 | tf_op jit(solution)/shard_map/ppermute | solution.py:38
  556.8 27.0 %collective-permute-start.49 = (f32[2,120,768]{2,1,0:T(8,128)}, f32[2,120,768]{2,1,0:T(8,128)S(1)}, u32[]{:S(2)}, u32[]{:S(2)}) collective-permute-start(f32[2,120,768]{2,1,0:T(8,128)} %dynamic-slice_bitcast_fusion.11), channel_id=1, source_target_pairs={{0,1},{1,0},{2,3},{3,2},{4,5},{5,4},{6,7},{7,6},{8,9},{9,8},{10,11... | collective-permute-start | bytes 2211848 | tf_op jit(solution)/shard_map/ppermute | solution.py:38
  557.2 12.2 %collective-permute-start.50 = (f32[24,768]{1,0:T(8,128)S(1)}, f32[24,768]{1,0:T(8,128)S(1)}, u32[]{:S(2)}, u32[]{:S(2)}) collective-permute-start(f32[24,768]{1,0:T(8,128)S(1)} %add.740), channel_id=1, source_target_pairs={{0,8},{4,12},{8,0},{12,4},{16,24},{20,28},{24,16},{28,20},{1,9},{5... | collective-permute-start | bytes 221192 | tf_op jit(solution)/shard_map/ppermute | solution.py:38
  558.8 10.6 %collective-permute-start.51 = (f32[24,768]{1,0:T(8,128)S(1)}, f32[24,768]{1,0:T(8,128)}, u32[]{:S(2)}, u32[]{:S(2)}) collective-permute-start(f32[24,768]{1,0:T(8,128)S(1)} %add.740), channel_id=1, source_target_pairs={{0,16},{4,20},{8,24},{12,28},{16,0},{20,4},{24,8},{28,12},{1,17},{... | collective-permute-start | bytes 221192 | tf_op jit(solution)/shard_map/ppermute | solution.py:38
  559.3 10.8 %collective-permute-start.52 = (f32[24,768]{1,0:T(8,128)S(1)}, f32[24,768]{1,0:T(8,128)}, u32[]{:S(2)}, u32[]{:S(2)}) collective-permute-start(f32[24,768]{1,0:T(8,128)S(1)} %add.740), channel_id=1, source_target_pairs={{0,24},{4,28},{8,16},{12,20},{16,8},{20,12},{24,0},{28,4},{1,25},{... | collective-permute-start | bytes 221192 | tf_op jit(solution)/shard_map/ppermute | solution.py:38
  584.0 19.4 %collective-permute-start.54 = (f32[1,120,768]{2,1,0:T(8,128)S(1)}, f32[1,120,768]{2,1,0:T(8,128)S(1)}, u32[]{:S(2)}, u32[]{:S(2)}) collective-permute-start(f32[1,120,768]{2,1,0:T(8,128)S(1)} %constant_dynamic-slice_fusion.1), channel_id=1, source_target_pairs={{0,2},{1,3},{2,0},{3,1},{4,6},{5,7},{6,4},{7,5},{8,10},{9,11},{10,... | collective-permute-start | bytes 1105928 | tf_op jit(solution)/shard_map/ppermute | solution.py:38
  606.8 7.1 collective-permute-start.55
  606.8 8.8 %collective-permute-start.56 = (f32[2,128]{1,0:T(2,128)S(1)}, f32[2,128]{1,0:T(2,128)S(1)}, u32[]{:S(2)}, u32[]{:S(2)}) collective-permute-start(f32[2,128]{1,0:T(2,128)S(1)} %broadcast_in_dim.213), channel_id=1, source_target_pairs={{0,2},{1,3},{2,0},{3,1},{4,6},{5,7},{6,4},{7,5},{8,10},{9,11},{10,... | collective-permute-start | bytes 3080 | tf_op jit(solution)/shard_map/ppermute | solution.py:38
  611.2 7.4 collective-permute-start.63
  613.9 6.3 collective-permute-start.64
  631.0 12.9 %collective-permute-start.65 = (f32[96,768]{1,0:T(8,128)S(1)}, f32[96,768]{1,0:T(8,128)S(1)}, u32[]{:S(2)}, u32[]{:S(2)}) collective-permute-start(f32[96,768]{1,0:T(8,128)S(1)} %get-tuple-element.264), channel_id=1, source_target_pairs={{0,1},{1,0},{2,3},{3,2},{4,5},{5,4},{6,7},{7,6},{8,9},{9,8},{10,11... | collective-permute-start | bytes 884744 | tf_op jit(solution)/shard_map/ppermute | solution.py:38
  631.9 20.3 %collective-permute-start.66 = (f32[96,768]{1,0:T(8,128)S(1)}, f32[96,768]{1,0:T(8,128)S(1)}, u32[]{:S(2)}, u32[]{:S(2)}) collective-permute-start(f32[96,768]{1,0:T(8,128)S(1)} %get-tuple-element.263), channel_id=1, source_target_pairs={{0,2},{1,3},{2,0},{3,1},{4,6},{5,7},{6,4},{7,5},{8,10},{9,11},{10,... | collective-permute-start | bytes 884744 | tf_op jit(solution)/shard_map/ppermute | solution.py:38
  633.5 18.7 %collective-permute-start.67 = (f32[96,768]{1,0:T(8,128)S(1)}, f32[96,768]{1,0:T(8,128)S(1)}, u32[]{:S(2)}, u32[]{:S(2)}) collective-permute-start(f32[96,768]{1,0:T(8,128)S(1)} %get-tuple-element.262), channel_id=1, source_target_pairs={{0,3},{1,2},{2,1},{3,0},{4,7},{5,6},{6,5},{7,4},{8,11},{9,10},{10,... | collective-permute-start | bytes 884744 | tf_op jit(solution)/shard_map/ppermute | solution.py:38
  663.7 9.9 %collective-permute-start.69 = (f32[96,768]{1,0:T(8,128)S(1)}, f32[96,768]{1,0:T(8,128)S(1)}, u32[]{:S(2)}, u32[]{:S(2)}) collective-permute-start(f32[96,768]{1,0:T(8,128)S(1)} %get-tuple-element.260), channel_id=1, source_target_pairs={{0,8},{4,12},{8,0},{12,4},{16,24},{20,28},{24,16},{28,20},{1,9},{5... | collective-permute-start | bytes 884744 | tf_op jit(solution)/shard_map/ppermute | solution.py:38
  664.7 15.1 %collective-permute-start.70 = (f32[96,768]{1,0:T(8,128)S(1)}, f32[96,768]{1,0:T(8,128)S(1)}, u32[]{:S(2)}, u32[]{:S(2)}) collective-permute-start(f32[96,768]{1,0:T(8,128)S(1)} %get-tuple-element.259), channel_id=1, source_target_pairs={{0,16},{4,20},{8,24},{12,28},{16,0},{20,4},{24,8},{28,12},{1,17},{... | collective-permute-start | bytes 884744 | tf_op jit(solution)/shard_map/ppermute | solution.py:38
  666.4 13.5 %collective-permute-start.71 = (f32[96,768]{1,0:T(8,128)S(1)}, f32[96,768]{1,0:T(8,128)S(1)}, u32[]{:S(2)}, u32[]{:S(2)}) collective-permute-start(f32[96,768]{1,0:T(8,128)S(1)} %get-tuple-element.258), channel_id=1, source_target_pairs={{0,24},{4,28},{8,16},{12,20},{16,8},{20,12},{24,0},{28,4},{1,25},{... | collective-permute-start | bytes 884744 | tf_op jit(solution)/shard_map/ppermute | solution.py:38
  680.9 10.9 %collective-permute-start.72 = (f32[96,768]{1,0:T(8,128)S(1)}, f32[96,768]{1,0:T(8,128)S(1)}, u32[]{:S(2)}, u32[]{:S(2)}) collective-permute-start(f32[96,768]{1,0:T(8,128)S(1)} %fusion.69), channel_id=1, source_target_pairs={{0,24},{4,28},{8,16},{12,20},{16,8},{20,12},{24,0},{28,4},{1,25},{... | collective-permute-start | bytes 884744 | tf_op jit(solution)/shard_map/ppermute | solution.py:38
  682.5 13.7 %collective-permute-start.73 = (f32[96,768]{1,0:T(8,128)S(1)}, f32[96,768]{1,0:T(8,128)S(1)}, u32[]{:S(2)}, u32[]{:S(2)}) collective-permute-start(f32[96,768]{1,0:T(8,128)S(1)} %fusion.69), channel_id=1, source_target_pairs={{0,16},{4,20},{8,24},{12,28},{16,0},{20,4},{24,8},{28,12},{1,17},{... | collective-permute-start | bytes 884744 | tf_op jit(solution)/shard_map/ppermute | solution.py:38
  683.7 12.5 %collective-permute-start.74 = (f32[96,768]{1,0:T(8,128)S(1)}, f32[96,768]{1,0:T(8,128)S(1)}, u32[]{:S(2)}, u32[]{:S(2)}) collective-permute-start(f32[96,768]{1,0:T(8,128)S(1)} %fusion.69), channel_id=1, source_target_pairs={{0,8},{4,12},{8,0},{12,4},{16,24},{20,28},{24,16},{28,20},{1,9},{5... | collective-permute-start | bytes 884744 | tf_op jit(solution)/shard_map/ppermute | solution.py:38
  696.6 8.0 %collective-permute-start.75 = (f32[4,96,768]{2,1,0:T(8,128)S(1)}, f32[4,96,768]{2,1,0:T(8,128)S(1)}, u32[]{:S(2)}, u32[]{:S(2)}) collective-permute-start(f32[4,96,768]{2,1,0:T(8,128)S(1)} %get-tuple-element.252), channel_id=1, source_target_pairs={{0,4},{4,0},{8,12},{12,8},{16,20},{20,16},{24,28},{28,24},{1,5},{5... | collective-permute-start | bytes 3538952 | tf_op jit(solution)/shard_map/ppermute | solution.py:38
  722.8 11.9 %collective-permute-start.76 = (f32[96,768]{1,0:T(8,128)S(1)}, f32[96,768]{1,0:T(8,128)S(1)}, u32[]{:S(2)}, u32[]{:S(2)}) collective-permute-start(f32[96,768]{1,0:T(8,128)S(1)} %get-tuple-element.251), channel_id=1, source_target_pairs={{0,3},{1,2},{2,1},{3,0},{4,7},{5,6},{6,5},{7,4},{8,11},{9,10},{10,... | collective-permute-start | bytes 884744 | tf_op jit(solution)/shard_map/ppermute | solution.py:38
  725.0 27.6 %collective-permute-start.77 = (f32[96,768]{1,0:T(8,128)S(1)}, f32[96,768]{1,0:T(8,128)S(1)}, u32[]{:S(2)}, u32[]{:S(2)}) collective-permute-start(f32[96,768]{1,0:T(8,128)S(1)} %get-tuple-element.250), channel_id=1, source_target_pairs={{0,2},{1,3},{2,0},{3,1},{4,6},{5,7},{6,4},{7,5},{8,10},{9,11},{10,... | collective-permute-start | bytes 884744 | tf_op jit(solution)/shard_map/ppermute | solution.py:38
  728.6 24.0 %collective-permute-start.78 = (f32[96,768]{1,0:T(8,128)S(1)}, f32[96,768]{1,0:T(8,128)S(1)}, u32[]{:S(2)}, u32[]{:S(2)}) collective-permute-start(f32[96,768]{1,0:T(8,128)S(1)} %get-tuple-element.248), channel_id=1, source_target_pairs={{0,1},{1,0},{2,3},{3,2},{4,5},{5,4},{6,7},{7,6},{8,9},{9,8},{10,11... | collective-permute-start | bytes 884744 | tf_op jit(solution)/shard_map/ppermute | solution.py:38
  (121 other events, 1283.9 us)
Sparse Core Ops, SparseCore 0:
  153.5 86.2 all-gather.2
  373.6 102.8 all-gather.4

commit v5 on v4

--- a/solution.py
+++ b/solution.py
@@ -116,7 +116,12 @@
 
     def along_seq(self):
         self.block = by_index(relative(self.shard, "seq"), lax.axis_index("seq"))
-        return self.block
+
+    def send_seq(self):
+        self.parts = relative(self.shard, "seq")
+
+    def join_seq(self):
+        self.block = by_index(self.parts, lax.axis_index("seq"))
 
     def doubling(self):
         place, count, bit = lax.axis_index("seq"), lax.axis_size("seq"), 1
@@ -692,7 +697,7 @@
     chosen = (source[:, None] == jnp.arange(window.shape[0], dtype=jnp.int32)[None, :]).astype(LOW)
     tokens = mm("rw,wi->ri", chosen, window).astype(LOW)
     tokens, up_gather.shard, *first.parts = hold(tokens, up_gather.shard, *first.parts)
-    up_gather.along_seq()
+    up_gather.send_seq()
     embed_full, qkv_full, output_full, small_full, bias_full = first.pieces(spots)
     embed_full, qkv_full, output_full = (
         value.reshape(-1, width) for value in (embed_full, qkv_full, output_full)
@@ -710,7 +715,8 @@
     ).astype(F32)
 
     embedded = mm("ri,di->rd", tokens, embed_full) + gain_bias[6]
-    embedded, up_gather.block, down_gather.shard = hold(embedded, up_gather.block, down_gather.shard)
+    embedded, up_gather.parts[0], down_gather.shard = hold(embedded, up_gather.parts[0], down_gather.shard)
+    up_gather.join_seq()
     up_gather.in_plane()
     down_gather.doubling()
     normed_one = layer_norm(embedded, gain_bias[0], gain_bias[1]).astype(LOW)
@@ -776,6 +782,7 @@
     down_sum, up_sum = Scatter(0, width, True), Scatter(1, width, True)
     half = width // 2
     late_sums = [Scatter(0, half), Scatter(1, half)]
+    pair_sums = [Scatter(0, half), Scatter(1, half)]
     down_out = mm("rf,rd->fd", active[1], grad_mlp_low)
     down_keep = mm("rf,rd->fd", active[0], grad_mlp_low)
     grad_mlp_low, down_out, down_keep = hold(grad_mlp_low, down_out, down_keep)
@@ -806,42 +813,52 @@
     embed_grad = mm("rd,ri->di", grad_embed_rows, tokens)
     down_sum.finish(down_out)
     up_sum.finish(up_out)
-    early_sum = SeqScatter(jnp.concatenate([down_sum.value, up_sum.value], axis=1))
-    early_out = early_sum.send()
-    grad_qkv, output_grad, embed_grad, early_out = hold(grad_qkv, output_grad, embed_grad, early_out)
-    late_keep, late_out = late_halves(mm("re,rd->ed", grad_qkv, normed_one), output_grad, embed_grad)
-    late_out, early_sum.keep, grad_qkv, traded = hold(late_out, early_sum.keep, grad_qkv, traded)
-    all_pooled = pick(traded[:, :width].reshape(-1, seq_count, head_weight.shape[0]), seq_place, 1)
+    early = jnp.concatenate([down_sum.value, up_sum.value], axis=1)
+    pair_keep, pair_out = late_halves(output_grad, embed_grad)
+    grad_qkv, pair_out, early = hold(grad_qkv, pair_out, early)
+    early = lax.psum_scatter(early, "seq", scatter_dimension=0)
+    late_keep, late_out = late_halves(mm("re,rd->ed", grad_qkv, normed_one))
+    pair = pair_keep + swap(pair_out, "pack", 1)
+    pair_outs = [
+        each.start_joined(part) for each, part in zip(pair_sums, (pair[..., :half], pair[..., half:]))
+    ]
+    late_out, grad_qkv, traded, *pair_outs = hold(late_out, grad_qkv, traded, *pair_outs)
     all_logits = traded[:, width:]
-    head_grad = mm("nd,nc->dc", all_pooled, all_logits)
     bias_grad = pick(column_sum(all_logits).reshape(seq_count, -1), seq_place)
     late = late_keep + swap(late_out, "pack", 1)
     late_outs = [
         each.start_joined(part) for each, part in zip(late_sums, (late[..., :half], late[..., half:]))
     ]
-    head_grad, bias_grad, grad_qkv, early_sum.keep, grad_upper[0], grad_upper[1], *late_outs = hold(
-        head_grad, bias_grad, grad_qkv, early_sum.keep, *grad_upper, *late_outs
-    )
+    bias_grad, grad_qkv, traded, grad_upper[0], grad_upper[1], *held = hold(
+        bias_grad, grad_qkv, traded, *grad_upper, *late_outs, *[each.keep for each in pair_sums]
+    )
+    late_outs = held[:2]
+    pair_sums[0].keep, pair_sums[1].keep = held[2:]
+    all_pooled = pick(traded[:, :width].reshape(-1, seq_count, head_weight.shape[0]), seq_place, 1)
+    head_grad = mm("nd,nc->dc", all_pooled, traded[:, width:])
     small_mine = small_sums(
         sums_first, sums_second, sums_last, column_sum(grad_qkv), [column_sum(side) for side in grad_upper]
     )
+    for each, sent in zip(pair_sums, pair_outs):
+        each.finish(sent)
+    pair = jnp.concatenate([each.value for each in pair_sums], axis=2)
     late_outs = [each.step(sent) for each, sent in zip(late_sums, late_outs)]
-    early_out = early_sum.step(early_out)
-    small_mine, early_out, *late_outs = hold(small_mine, early_out, *late_outs)
+    small_mine, head_grad, pair, *late_outs = hold(small_mine, head_grad, pair, *late_outs)
     small_total = small_mine + swap(small_mine, "pack", 1)
     for each, sent in zip(late_sums, late_outs):
         each.finish(sent)
-    late_sum = SeqScatter(jnp.concatenate([each.value for each in late_sums], axis=2))
-    late_out, small_total, early_sum.keep = hold(late_sum.send(), small_total, early_sum.keep)
+    late_sum = SeqScatter(
+        jnp.concatenate([jnp.concatenate([each.value for each in late_sums], axis=2), pair], axis=1)
+    )
+    late_out, small_total, early = hold(late_sum.send(), small_total, early)
     small_total = sum_chips(small_total)
-    while early_out is not None:
-        early_out = early_sum.step(early_out)
     late_out = late_sum.step(late_out)
-    late_out, small_total, early_sum.value = hold(late_out, small_total, early_sum.value)
+    late_out, small_total = hold(late_out, small_total)
     small_total = all_sum(small_total, "seq")
     while late_out is not None:
         late_out = late_sum.step(late_out)
-    down_share, up_share = jnp.split(early_sum.result(), 2)
+    late_sum.value, small_total = hold(late_sum.value, small_total)
+    down_share, up_share = jnp.split(early, 2)
     late_share = late_sum.result()
     widths = [qkv_weight.shape[1], output_weight.shape[1], embed_weight.shape[1]]
     qkv_share, output_share = late_share[: widths[0]], late_share[widths[0] : widths[0] + widths[1]]
@@ -853,7 +870,7 @@
     place = pack_place * seq_count + seq_place
     small_share = pick(small_total.reshape(small_rows, pack_count * seq_count, -1), place, 1)
 
-    shares = (early_sum.result(), late_share, head_grad, bias_grad)
+    shares = (early, late_share, head_grad, bias_grad)
     square_sum = sum((jnp.sum(piece * piece) for piece in shares))
     sums = jnp.broadcast_to(jnp.stack([loss_part, square_sum])[:, None], (2, BLOCK))
     sums = sum_plane(all_sum(sums, "seq"))

time: 769 us -> 743 us (0.966)
  waiting for transfers between devices: 212 us -> 180 us
    ppermute x77 -> x80, waiting for transfers between devices: 190 us -> 157 us  [swap(): lax.ppermute(value, axis, [(i, i ^ bit) for i in range(lax.axis_size(axis...]
    add x10 -> x14, other arithmetic: 14 us -> 17.9 us  [step(): self.value = self.keep + swap(sent, 'pack', self.bit)]
    ppermute x77 -> x80, starting transfers between devices: 88 us -> 90.4 us  [swap(): lax.ppermute(value, axis, [(i, i ^ bit) for i in range(lax.axis_size(axis...]
  transfers between devices with their start and end apart: 81 -> 85, of which waited for: 44 -> 48; matrix products, arithmetic and copies ran while one was open for 27% -> 30% of each run, Pallas kernels for 10% -> 11%
where the time goes in v5:
time: 743 us; the launch traced here: 737 us
  matrix products  186 us (25%)
  waiting for transfers between devices  180 us (24%)
  Pallas kernels  103 us (14%)
  other arithmetic  98 us (13%)
  starting transfers between devices  93.5 us (13%)
  local copies, waits for them, and re-layouts  53.8 us (7%)
  between operations  23.6 us (3%)
    dot_general x25, matrix products, mm(): return jnp.einsum(spec, left, right, preferred_element_type=F32)  164 us
    ppermute x80, waiting for transfers between devices, swap(): lax.ppermute(value, axis, [(i, i ^ bit) for i in range(lax.axis_size(axis...  157 us
    ppermute x80, starting transfers between devices, swap(): lax.ppermute(value, axis, [(i, i ^ bit) for i in range(lax.axis_size(axis...  90.4 us
    pallas_call x1, Pallas kernels, attend_back(): pl.pallas_call(lambda *refs: attend_back_kernel(width, blocks, *refs), gr...  47 us
    pallas_call x3, Pallas kernels, norm_back(): pl.pallas_call(lambda *refs: norm_back_kernel(groups, keep_sum, *refs), g...  34.3 us
    pallas_call x1, Pallas kernels, attend(): pl.pallas_call(lambda *refs: attend_kernel(width, blocks, *refs), grid=(b...  21.1 us
    add x14, other arithmetic, step(): self.value = self.keep + swap(sent, 'pack', self.bit)  17.9 us
    ppermute x1, waiting for transfers between devices, body(): lax.ppermute(patches[:, shard_len - MAXLEN:], 'seq', [(i, i + 1) for i in...  16.8 us
  transfers between devices with their start and end apart: 85, of which 48 were waited for; matrix products, arithmetic and copies ran while one was open for 30% of the time, Pallas kernels for 11%

profile of v5, /device:TPU:0, one launch (start us, length us, event | category | flops | bytes accessed | tf_op | source)
XLA Modules:
  0.0 737.3 jit_solution(16512872008610895391)
XLA Ops:
  11.7 5.1 collective-permute-start
  22.9 11.6 %collective-permute-done.1 = bf16[136,768]{1,0:T(8,128)(2,1)S(1)} collective-permute-done((bf16[136,768]{1,0:T(8,128)(2,1)S(1)}, bf16[136,768]{1,0:T(8,128)(2,1)S(1)}, u32[]{:S(2)}, u32[]{:S(2)}) %collective-permute-start.1) | collective-permute-done | bytes 208928 | tf_op jit(solution)/shard_map/ppermute | solution.py:38
  44.2 16.8 %collective-permute-done.3 = bf16[6,128,768]{2,1,0:T(8,128)(2,1)S(1)} collective-permute-done((bf16[6,128,768]{2,1,0:T(8,128)(2,1)S(1)}, bf16[6,128,768]{2,1,0:T(8,128)(2,1)S(1)}, u32[]{:S(2)}, u32[]{:S(2)}) %collective-permute-start.3) | collective-permute-done | bytes 1179680 | tf_op jit(solution)/shard_map/ppermute | solution.py:693
  61.0 4.2 collective-permute-done.4
  65.7 10.3 %fusion.23 = bf16[1664,768]{1,0:T(8,128)(2,1)} fusion(bf16[3072,768]{1,0:T(8,128)(2,1)S(1)} %bitcast.396, s32[1664]{0:T(1024)S(1)} %get-tuple-element.313), kind=kOutput, calls=%fused_computation.55 | convolution fusion | flops 7858126848 | bytes 7281152 | tf_op jit(solution)/shard_map/rw,wi->ri/dot_general | solution.py:520
  76.0 3.2 collective-permute-done.6
  89.4 5.0 collective-permute-start.11
  102.5 4.5 convolution_add_fusion.1.refs_0_
  116.2 3.1 multiply_reduce_fusion.2
  122.3 2.9 collective-permute-start.10
  125.3 9.3 %add_convert_fusion.refs_0_ = bf16[1664,2304]{1,0:T(8,128)(2,1)} fusion(bf16[2304,768]{1,0:T(8,128)(2,1)S(1)} %bitcast.399, f32[2304]{0:T(1024)S(1)} %pad_maximum_fusion.15, f32[1664,768]{1,0:T(8,128)S(1)} %bitcast.375, f32[768]{0:T(1024)S(1)} %get-tuple-element.301, f32[768]{0:T(1024)S(1)} %get-tuple-element.309, f32[1664]{0:T(1024)S(1)} %add_rsqrt_fusion.2, ...), kind=kOutput, calls=%fused_computation.7 | convolution fusion | flops 5902860288 | bytes 16347136 | tf_op jit(solution)/shard_map/rd,ed->re/dot_general | solution.py:520
  141.1 3.2 pad_maximum_fusion.2
  144.4 21.1 %shard_map.435 = (bf16[1664,768]{1,0:T(8,128)(2,1)}, f32[13,6,256]{2,1,0:T(8,128)}) custom-call(bf16[1664,2304]{1,0:T(8,128)(2,1)} %add_convert_fusion.refs_0_, s32[13,1,128]{2,1,0:T(1,128)} %select_n.794.refs_1_.refs_3_, s32[1920,1]{1,0:T(8,128)} %broadcast_in_dim.215.refs_2_.refs_4_), custom_call_target="tpu_custom_call" | custom-call | tf_op jit(solution)/shard_map/pallas_call | solution.py:357
  166.3 5.7 fusion.133
  176.8 8.8 %multiply_convert_fusion.1 = (bf16[1664,1536]{1,0:T(8,128)(2,1)S(1)}, f32[1664,1536]{1,0:T(8,128)}) fusion(f32[1536]{0:T(1024)S(1)} %add.698, bf16[1664,768]{1,0:T(8,128)(2,1)S(1)} %add_convert_fusion.1, bf16[1536,768]{1,0:T(8,128)(2,1)} %bitcast.38), kind=kOutput, calls=%fused_computation.24 | convolution fusion | flops 3941203968 | bytes 20256768 | tf_op jit(solution)/shard_map/rd,fd->rf/dot_general | solution.py:520
  185.6 4.2 fusion.135
  189.9 9.0 %multiply_convert_fusion = (bf16[1664,1536]{1,0:T(8,128)(2,1)S(1)}, f32[1664,1536]{1,0:T(8,128)}) fusion(f32[1536]{0:T(1024)S(1)} %add.702, bf16[1664,768]{1,0:T(8,128)(2,1)S(1)} %add_convert_fusion.1, bf16[1536,768]{1,0:T(8,128)(2,1)} %bitcast.44), kind=kOutput, calls=%fused_computation.22 | convolution fusion | flops 3941203968 | bytes 20256768 | tf_op jit(solution)/shard_map/rd,fd->rf/dot_general | solution.py:520
  199.0 4.8 fusion.134
  206.2 3.0 fusion.59
  230.9 5.6 fusion.39
  257.3 11.4 %shard_map.436 = (bf16[1664,768]{1,0:T(8,128)(2,1)}, f32[8,768]{1,0:T(8,128)}, f32[1664,768]{1,0:T(8,128)}) custom-call(f32[1664,768]{1,0:T(8,128)} %copy-done.4, f32[96,768]{1,0:T(8,128)} %maximum_divide_fusion.refs_1_, s32[1664,1]{1,0:T(8,128)} %select_n.876.refs_2_, f32[1,768]{1,0:T(1,128)} %get-tuple-element.298.refs_3_), custom_call_target="tpu_custom_call" | custom-call | tf_op jit(solution)/shard_map/pallas_call | solution.py:453
  268.7 7.5 %fusion.138 = f32[1536,768]{1,0:T(8,128)S(1)} fusion(bf16[1664,1536]{1,0:T(8,128)(2,1)} %copy-done.103, bf16[1664,768]{1,0:T(8,128)(2,1)} %get-tuple-element.126), kind=kOutput, calls=%fused_computation.403 | convolution fusion | flops 3925868544 | bytes 12386304 | tf_op jit(solution)/shard_map/rf,rd->fd/dot_general | solution.py:520
  276.2 9.3 %fusion.137 = f32[1536,768]{1,0:T(8,128)} fusion(bf16[1664,1536]{1,0:T(8,128)(2,1)} %copy-done.102, bf16[1664,768]{1,0:T(8,128)(2,1)S(1)} %copy-done.99), kind=kOutput, calls=%fused_computation.402 | convolution fusion | flops 3925868544 | bytes 12386304 | tf_op jit(solution)/shard_map/rf,rd->fd/dot_general | solution.py:520
  285.4 9.7 %fusion.6 = bf16[1664,1536]{1,0:T(8,128)(2,1)S(1)} fusion(bf16[1664,768]{1,0:T(8,128)(2,1)S(1)} %copy-done.99, bf16[1536,768]{1,0:T(8,128)(2,1)S(1)} %bitcast.406, f32[1664,1536]{1,0:T(8,128)} %get-tuple-element.326, f32[1536]{0:T(1024)S(1)} %copy-done.78), kind=kOutput, calls=%fused_computation.13 | convolution fusion | flops 3953983488 | bytes 20256768 | tf_op jit(solution)/shard_map/rd,fd->rf/dot_general | solution.py:520
  295.2 4.7 fusion.140
  299.9 9.3 %fusion.12 = bf16[1664,1536]{1,0:T(8,128)(2,1)S(1)} fusion(bf16[1664,768]{1,0:T(8,128)(2,1)S(1)} %copy-done.99, bf16[1536,768]{1,0:T(8,128)(2,1)S(1)} %bitcast.434, f32[1664,1536]{1,0:T(8,128)} %get-tuple-element.328, f32[1536]{0:T(1024)S(1)} %copy-done.76), kind=kOutput, calls=%fused_computation.19 | convolution fusion | flops 3953983488 | bytes 20256768 | tf_op jit(solution)/shard_map/rd,fd->rf/dot_general | solution.py:520
  309.2 4.6 fusion.139
  317.0 7.6 %fusion.141 = f32[1664,768]{1,0:T(8,128)} fusion(bf16[1664,1536]{1,0:T(8,128)(2,1)S(1)} %fusion.6, bf16[1536,768]{1,0:T(8,128)(2,1)} %bitcast.38), kind=kOutput, calls=%fused_computation.406 | convolution fusion | flops 3925868544 | bytes 12582912 | tf_op jit(solution)/shard_map/rf,fd->rd/dot_general | solution.py:520
  324.6 8.3 %convolution_add_fusion.2.refs_1_ = f32[1664,768]{1,0:T(8,128)} fusion(f32[1664,768]{1,0:T(8,128)} %fusion.141, bf16[1664,1536]{1,0:T(8,128)(2,1)S(1)} %fusion.12, bf16[1536,768]{1,0:T(8,128)(2,1)} %bitcast.44), kind=kOutput, calls=%fused_computation.50 | convolution fusion | flops 3927146496 | bytes 17694720 | tf_op jit(solution)/shard_map/rf,fd->rd/dot_general | solution.py:520
  335.1 2.9 copy_add_fusion
  344.5 12.1 %shard_map.437 = (bf16[1664,768]{1,0:T(8,128)(2,1)}, f32[8,768]{1,0:T(8,128)}, f32[1664,768]{1,0:T(8,128)}) custom-call(f32[1664,768]{1,0:T(8,128)} %copy-done.3, f32[1664,768]{1,0:T(8,128)} %convolution_add_fusion.2.refs_1_, f32[1664,768]{1,0:T(8,128)} %get-tuple-element.132.refs_2_, f32[1,768]{1,0:T(1,128)} %get-tuple-element.299.refs_3_), custom_call_target="tpu_custom_call" | custom-call | tf_op jit(solution)/shard_map/pallas_call | solution.py:453
  356.6 5.3 convolution_convert_fusion.refs_1_
  363.7 47.0 %shard_map.438 = bf16[1664,2304]{1,0:T(8,128)(2,1)} custom-call(bf16[1664,2304]{1,0:T(8,128)(2,1)} %add_convert_fusion.refs_0_, bf16[1664,768]{1,0:T(8,128)(2,1)} %convolution_convert_fusion.refs_1_, f32[13,6,256]{2,1,0:T(8,128)} %get-tuple-element.137.refs_2_, s32[13,1,128]{2,1,0:T(1,128)} %select_n.794.refs_1_.refs_3_, ...), custom_call_target="tpu_custom_call" | custom-call | tf_op jit(solution)/shard_map/pallas_call | solution.py:382
  410.8 5.0 fusion.142
  426.2 7.8 %fusion.143.refs_1_ = f32[1664,768]{1,0:T(8,128)} fusion(bf16[1664,2304]{1,0:T(8,128)(2,1)S(1)} %bitcast.377, bf16[2304,768]{1,0:T(8,128)(2,1)S(1)} %bitcast.400), kind=kOutput, calls=%fused_computation.408 | convolution fusion | flops 5888802816 | bytes 16318464 | tf_op jit(solution)/shard_map/re,ed->rd/dot_general | solution.py:520
  434.0 10.9 %shard_map.439 = (bf16[1664,768]{1,0:T(8,128)(2,1)}, f32[8,768]{1,0:T(8,128)}) custom-call(f32[1664,768]{1,0:T(8,128)} %convolution_add_fusion.1.refs_0_, f32[1664,768]{1,0:T(8,128)} %fusion.143.refs_1_, f32[1664,768]{1,0:T(8,128)} %get-tuple-element.141.refs_2_, f32[1,768]{1,0:T(1,128)} %get-tuple-element.297.refs_3_), custom_call_target="tpu_custom_call" | custom-call | tf_op jit(solution)/shard_map/pallas_call | solution.py:453
  444.9 4.1 fusion.144
  456.1 11.5 %fusion.116 = f32[2304,768]{1,0:T(8,128)S(1)} fusion(bf16[1664,2304]{1,0:T(8,128)(2,1)} %shard_map.438, f32[1664,768]{1,0:T(8,128)} %convolution_add_fusion.1.refs_0_, f32[768]{0:T(1024)S(1)} %copy-done.86, f32[768]{0:T(1024)S(1)} %copy-done.88, f32[1664]{0:T(1024)S(1)} %copy-done.80, f32[1664]{0:T(1024)S(1)} %copy-done.62), kind=kOutput, calls=%fused_computation.389 | convolution fusion | flops 5895192576 | bytes 19876864 | tf_op jit(solution)/shard_map/re,rd->ed/dot_general | solution.py:520
  473.9 2.9 convert_reduce_fusion.3
  480.1 3.5 bitcast_add_fusion
  488.4 4.8 collective-permute-done.45
  499.6 3.3 convert_reduce_fusion.2
  502.8 3.5 fusion.21
  506.4 5.1 convert_reduce_fusion
  513.0 5.4 collective-permute-done.46
  529.6 7.3 collective-permute-done.50
  550.1 7.8 %collective-permute-done.53 = f32[2,120,768]{2,1,0:T(8,128)S(1)} collective-permute-done((f32[2,120,768]{2,1,0:T(8,128)}, f32[2,120,768]{2,1,0:T(8,128)S(1)}, u32[]{:S(2)}, u32[]{:S(2)}) %collective-permute-start.53) | collective-permute-done | bytes 737312 | tf_op jit(solution)/shard_map/ppermute | solution.py:38
  567.7 12.8 %collective-permute-done.59 = f32[24,768]{1,0:T(8,128)S(1)} collective-permute-done((f32[24,768]{1,0:T(8,128)S(1)}, f32[24,768]{1,0:T(8,128)S(1)}, u32[]{:S(2)}, u32[]{:S(2)}) %collective-permute-start.59) | collective-permute-done | bytes 73760 | tf_op jit(solution)/shard_map/ppermute | solution.py:38
  602.4 2.9 collective-permute-start.69
  606.8 8.3 %collective-permute-done.68 = f32[96,768]{1,0:T(8,128)S(1)} collective-permute-done((f32[96,768]{1,0:T(8,128)S(1)}, f32[96,768]{1,0:T(8,128)S(1)}, u32[]{:S(2)}, u32[]{:S(2)}) %collective-permute-start.68) | collective-permute-done | bytes 294944 | tf_op jit(solution)/shard_map/ppermute | solution.py:38
  615.1 10.9 %collective-permute-done.69 = f32[96,768]{1,0:T(8,128)S(1)} collective-permute-done((f32[96,768]{1,0:T(8,128)S(1)}, f32[96,768]{1,0:T(8,128)S(1)}, u32[]{:S(2)}, u32[]{:S(2)}) %collective-permute-start.69) | collective-permute-done | bytes 294944 | tf_op jit(solution)/shard_map/ppermute | solution.py:38
  627.5 3.3 fusion.145
  631.9 3.2 collective-permute-done.71
  641.1 6.4 collective-permute-done.72
  647.5 6.4 collective-permute-done.73
  660.1 5.8 collective-permute-done.75
  665.9 4.5 collective-permute-done.76
  672.7 6.3 multiply_subtract_fusion
  681.7 3.0 fusion.146
  684.8 3.0 fusion.147
  687.8 3.7 fusion.30
  699.7 3.4 collective-permute-start.80
  705.4 3.7 collective-permute-done.79
  709.1 17.9 %collective-permute-done.80 = f32[96,768]{1,0:T(8,128)S(1)} collective-permute-done((f32[96,768]{1,0:T(8,128)S(1)}, f32[96,768]{1,0:T(8,128)S(1)}, u32[]{:S(2)}, u32[]{:S(2)}) %collective-permute-start.80) | collective-permute-done | bytes 294944 | tf_op jit(solution)/shard_map/ppermute | solution.py:38
  (605 shorter events, 244.1 us)
Async XLA Ops:
  7.2 223.7 %all-gather.3.cloned.1.call-start = ((), (), s32[]{:S(2)}) async-start(), calls=%async_computation.1 | async-start | bytes 5406720 | tf_op jit(solution)/shard_map/all_gather | solution.py:728
  11.7 11.3 %collective-permute-start = (bf16[136,768]{1,0:T(8,128)(2,1)S(1)}, bf16[136,768]{1,0:T(8,128)(2,1)S(1)}, u32[]{:S(2)}, u32[]{:S(2)}) collective-permute-start(bf16[136,768]{1,0:T(8,128)(2,1)S(1)} %constant_dynamic-update-slice_fusion), channel_id=1, source_target_pairs={{0,3},{1,2},{2,1},{3,0},{4,7},{5,6},{6,5},{7,4},{8,11},{9,10},{10,... | collective-permute-start | bytes 626696 | tf_op jit(solution)/shard_map/ppermute | solution.py:38
  16.8 17.7 %collective-permute-start.1 = (bf16[136,768]{1,0:T(8,128)(2,1)S(1)}, bf16[136,768]{1,0:T(8,128)(2,1)S(1)}, u32[]{:S(2)}, u32[]{:S(2)}) collective-permute-start(bf16[136,768]{1,0:T(8,128)(2,1)S(1)} %constant_dynamic-update-slice_fusion), channel_id=1, source_target_pairs={{0,2},{1,3},{2,0},{3,1},{4,6},{5,7},{6,4},{7,5},{8,10},{9,11},{10,... | collective-permute-start | bytes 626696 | tf_op jit(solution)/shard_map/ppermute | solution.py:38
  16.8 17.7 %collective-permute-start.2 = (bf16[136,768]{1,0:T(8,128)(2,1)S(1)}, bf16[136,768]{1,0:T(8,128)(2,1)S(1)}, u32[]{:S(2)}, u32[]{:S(2)}) collective-permute-start(bf16[136,768]{1,0:T(8,128)(2,1)S(1)} %constant_dynamic-update-slice_fusion), channel_id=1, source_target_pairs={{0,1},{1,0},{2,3},{3,2},{4,5},{5,4},{6,7},{7,6},{8,9},{9,8},{10,11... | collective-permute-start | bytes 626696 | tf_op jit(solution)/shard_map/ppermute | solution.py:38
  34.9 26.1 %collective-permute-start.3 = (bf16[6,128,768]{2,1,0:T(8,128)(2,1)S(1)}, bf16[6,128,768]{2,1,0:T(8,128)(2,1)S(1)}, u32[]{:S(2)}, u32[]{:S(2)}) collective-permute-start(bf16[6,128,768]{2,1,0:T(8,128)(2,1)S(1)} %get-tuple-element.244), channel_id=1, source_target_pairs={{0,1},{1,2},{2,3},{4,5},{5,6},{6,7},{8,9},{9,10},{10,11},{12,13},{... | collective-permute-start | bytes 3538952 | tf_op jit(solution)/shard_map/ppermute | solution.py:693
  36.6 28.6 %collective-permute-start.4 = (bf16[6,128,768]{2,1,0:T(8,128)(2,1)S(1)}, bf16[6,128,768]{2,1,0:T(8,128)(2,1)S(1)}, u32[]{:S(2)}, u32[]{:S(2)}) collective-permute-start(bf16[6,128,768]{2,1,0:T(8,128)(2,1)S(1)} %get-tuple-element.245), channel_id=1, source_target_pairs={{1,0},{2,1},{3,2},{5,4},{6,5},{7,6},{9,8},{10,9},{11,10},{13,12},{... | collective-permute-start | bytes 3538952 | tf_op jit(solution)/shard_map/ppermute | solution.py:694
  40.7 35.3 %collective-permute-start.5 = (bf16[4,136,768]{2,1,0:T(8,128)(2,1)S(1)}, bf16[4,136,768]{2,1,0:T(8,128)(2,1)S(1)}, u32[]{:S(2)}, u32[]{:S(2)}) collective-permute-start(bf16[4,136,768]{2,1,0:T(8,128)(2,1)S(1)} %pad_maximum_fusion.11), channel_id=1, source_target_pairs={{0,8},{4,12},{8,0},{12,4},{16,24},{20,28},{24,16},{28,20},{1,9},{5... | collective-permute-start | bytes 2506760 | tf_op jit(solution)/shard_map/ppermute | solution.py:38
  42.2 37.0 %collective-permute-start.6 = (bf16[4,136,768]{2,1,0:T(8,128)(2,1)S(1)}, bf16[4,136,768]{2,1,0:T(8,128)(2,1)S(1)}, u32[]{:S(2)}, u32[]{:S(2)}) collective-permute-start(bf16[4,136,768]{2,1,0:T(8,128)(2,1)S(1)} %pad_maximum_fusion.11), channel_id=1, source_target_pairs={{0,16},{4,20},{8,24},{12,28},{16,0},{20,4},{24,8},{28,12},{1,17},{... | collective-permute-start | bytes 2506760 | tf_op jit(solution)/shard_map/ppermute | solution.py:38
  43.7 35.5 %collective-permute-start.7 = (bf16[4,136,768]{2,1,0:T(8,128)(2,1)S(1)}, bf16[4,136,768]{2,1,0:T(8,128)(2,1)S(1)}, u32[]{:S(2)}, u32[]{:S(2)}) collective-permute-start(bf16[4,136,768]{2,1,0:T(8,128)(2,1)S(1)} %pad_maximum_fusion.11), channel_id=1, source_target_pairs={{0,24},{4,28},{8,16},{12,20},{16,8},{20,12},{24,0},{28,4},{1,25},{... | collective-permute-start | bytes 2506760 | tf_op jit(solution)/shard_map/ppermute | solution.py:38
  80.1 17.4 %collective-permute-start.8 = (bf16[4,4,136,768]{3,2,1,0:T(8,128)(2,1)S(1)}, bf16[4,4,136,768]{3,2,1,0:T(8,128)(2,1)}, u32[]{:S(2)}, u32[]{:S(2)}) collective-permute-start(bf16[4,4,136,768]{3,2,1,0:T(8,128)(2,1)S(1)} %pad_maximum_fusion.1), channel_id=1, source_target_pairs={{0,4},{4,0},{8,12},{12,8},{16,20},{20,16},{24,28},{28,24},{1,5},{5... | collective-permute-start | bytes 10027016 | tf_op jit(solution)/shard_map/ppermute | solution.py:38
  89.4 17.6 %collective-permute-start.11 = (bf16[96,768]{1,0:T(8,128)(2,1)}, bf16[96,768]{1,0:T(8,128)(2,1)}, u32[]{:S(2)}, u32[]{:S(2)}) collective-permute-start(bf16[96,768]{1,0:T(8,128)(2,1)} %convert_bitcast_fusion.1), channel_id=1, source_target_pairs={{0,3},{1,2},{2,1},{3,0},{4,7},{5,6},{6,5},{7,4},{8,11},{9,10},{10,... | collective-permute-start | bytes 442376 | tf_op jit(solution)/shard_map/ppermute | solution.py:38
  94.4 13.0 %collective-permute-start.12 = (bf16[96,768]{1,0:T(8,128)(2,1)}, bf16[96,768]{1,0:T(8,128)(2,1)}, u32[]{:S(2)}, u32[]{:S(2)}) collective-permute-start(bf16[96,768]{1,0:T(8,128)(2,1)} %convert_bitcast_fusion.1), channel_id=1, source_target_pairs={{0,2},{1,3},{2,0},{3,1},{4,6},{5,7},{6,4},{7,5},{8,10},{9,11},{10,... | collective-permute-start | bytes 442376 | tf_op jit(solution)/shard_map/ppermute | solution.py:38
  94.4 13.0 %collective-permute-start.13 = (bf16[96,768]{1,0:T(8,128)(2,1)}, bf16[96,768]{1,0:T(8,128)(2,1)}, u32[]{:S(2)}, u32[]{:S(2)}) collective-permute-start(bf16[96,768]{1,0:T(8,128)(2,1)} %convert_bitcast_fusion.1), channel_id=1, source_target_pairs={{0,1},{1,0},{2,3},{3,2},{4,5},{5,4},{6,7},{7,6},{8,9},{9,8},{10,11... | collective-permute-start | bytes 442376 | tf_op jit(solution)/shard_map/ppermute | solution.py:38
  108.7 28.7 %collective-permute-start.14 = (bf16[4,96,768]{2,1,0:T(8,128)(2,1)S(1)}, bf16[4,96,768]{2,1,0:T(8,128)(2,1)}, u32[]{:S(2)}, u32[]{:S(2)}) collective-permute-start(bf16[4,96,768]{2,1,0:T(8,128)(2,1)S(1)} %pad_maximum_fusion.12), channel_id=1, source_target_pairs={{0,8},{4,12},{8,0},{12,4},{16,24},{20,28},{24,16},{28,20},{1,9},{5... | collective-permute-start | bytes 1769480 | tf_op jit(solution)/shard_map/ppermute | solution.py:38
  110.0 27.4 %collective-permute-start.15 = (bf16[4,96,768]{2,1,0:T(8,128)(2,1)S(1)}, bf16[4,96,768]{2,1,0:T(8,128)(2,1)}, u32[]{:S(2)}, u32[]{:S(2)}) collective-permute-start(bf16[4,96,768]{2,1,0:T(8,128)(2,1)S(1)} %pad_maximum_fusion.12), channel_id=1, source_target_pairs={{0,16},{4,20},{8,24},{12,28},{16,0},{20,4},{24,8},{28,12},{1,17},{... | collective-permute-start | bytes 1769480 | tf_op jit(solution)/shard_map/ppermute | solution.py:38
  110.8 26.7 %collective-permute-start.16 = (bf16[4,96,768]{2,1,0:T(8,128)(2,1)S(1)}, bf16[4,96,768]{2,1,0:T(8,128)(2,1)}, u32[]{:S(2)}, u32[]{:S(2)}) collective-permute-start(bf16[4,96,768]{2,1,0:T(8,128)(2,1)S(1)} %pad_maximum_fusion.12), channel_id=1, source_target_pairs={{0,24},{4,28},{8,16},{12,20},{16,8},{20,12},{24,0},{28,4},{1,25},{... | collective-permute-start | bytes 1769480 | tf_op jit(solution)/shard_map/ppermute | solution.py:38
  112.3 10.0 %collective-permute-start.9 = (bf16[1,96,768]{2,1,0:T(8,128)(2,1)S(1)}, bf16[1,96,768]{2,1,0:T(8,128)(2,1)S(1)}, u32[]{:S(2)}, u32[]{:S(2)}) collective-permute-start(bf16[1,96,768]{2,1,0:T(8,128)(2,1)S(1)} %bitcast.414), channel_id=1, source_target_pairs={{0,1},{1,0},{2,3},{3,2},{4,5},{5,4},{6,7},{7,6},{8,9},{9,8},{10,11... | collective-permute-start | bytes 442376 | tf_op jit(solution)/shard_map/ppermute | solution.py:38
  122.3 15.0 %collective-permute-start.10 = (bf16[2,96,768]{2,1,0:T(8,128)(2,1)S(1)}, bf16[2,96,768]{2,1,0:T(8,128)(2,1)S(1)}, u32[]{:S(2)}, u32[]{:S(2)}) collective-permute-start(bf16[2,96,768]{2,1,0:T(8,128)(2,1)S(1)} %maximum_select_fusion.7), channel_id=1, source_target_pairs={{0,2},{1,3},{2,0},{3,1},{4,6},{5,7},{6,4},{7,5},{8,10},{9,11},{10,... | collective-permute-start | bytes 884744 | tf_op jit(solution)/shard_map/ppermute | solution.py:38
  137.5 28.0 %collective-permute-start.17 = (bf16[4,96,768]{2,1,0:T(8,128)(2,1)S(1)}, bf16[4,96,768]{2,1,0:T(8,128)(2,1)}, u32[]{:S(2)}, u32[]{:S(2)}) collective-permute-start(bf16[4,96,768]{2,1,0:T(8,128)(2,1)S(1)} %maximum_select_fusion.4), channel_id=1, source_target_pairs={{0,8},{4,12},{8,0},{12,4},{16,24},{20,28},{24,16},{28,20},{1,9},{5... | collective-permute-start | bytes 1769480 | tf_op jit(solution)/shard_map/ppermute | solution.py:38
  138.7 26.8 %collective-permute-start.18 = (bf16[4,96,768]{2,1,0:T(8,128)(2,1)S(1)}, bf16[4,96,768]{2,1,0:T(8,128)(2,1)}, u32[]{:S(2)}, u32[]{:S(2)}) collective-permute-start(bf16[4,96,768]{2,1,0:T(8,128)(2,1)S(1)} %maximum_select_fusion.4), channel_id=1, source_target_pairs={{0,16},{4,20},{8,24},{12,28},{16,0},{20,4},{24,8},{28,12},{1,17},{... | collective-permute-start | bytes 1769480 | tf_op jit(solution)/shard_map/ppermute | solution.py:38
  139.8 26.4 %collective-permute-start.19 = (bf16[4,96,768]{2,1,0:T(8,128)(2,1)S(1)}, bf16[4,96,768]{2,1,0:T(8,128)(2,1)}, u32[]{:S(2)}, u32[]{:S(2)}) collective-permute-start(bf16[4,96,768]{2,1,0:T(8,128)(2,1)S(1)} %maximum_select_fusion.4), channel_id=1, source_target_pairs={{0,24},{4,28},{8,16},{12,20},{16,8},{20,12},{24,0},{28,4},{1,25},{... | collective-permute-start | bytes 1769480 | tf_op jit(solution)/shard_map/ppermute | solution.py:38
  144.3 45.6 %collective-permute-start.20 = (bf16[4,4,96,768]{3,2,1,0:T(8,128)(2,1)}, bf16[4,4,96,768]{3,2,1,0:T(8,128)(2,1)}, u32[]{:S(2)}, u32[]{:S(2)}) collective-permute-start(bf16[4,4,96,768]{3,2,1,0:T(8,128)(2,1)} %pad_maximum_fusion.2), channel_id=1, source_target_pairs={{0,4},{4,0},{8,12},{12,8},{16,20},{20,16},{24,28},{28,24},{1,5},{5... | collective-permute-start | bytes 7077896 | tf_op jit(solution)/shard_map/ppermute | solution.py:38
  144.3 329.0 %all-gather.5.cloned.1.call-start = ((), (), s32[]{:S(2)}) async-start(), calls=%async_computation.2 | async-start | bytes 6881280 | tf_op jit(solution)/shard_map/all_gather | solution.py:777
  175.6 23.4 %collective-permute-start.21 = (bf16[4,4,96,768]{3,2,1,0:T(8,128)(2,1)S(1)}, bf16[4,4,96,768]{3,2,1,0:T(8,128)(2,1)S(1)}, u32[]{:S(2)}, u32[]{:S(2)}) collective-permute-start(bf16[4,4,96,768]{3,2,1,0:T(8,128)(2,1)S(1)} %pad_maximum_fusion.3), channel_id=1, source_target_pairs={{0,4},{4,0},{8,12},{12,8},{16,20},{20,16},{24,28},{28,24},{1,5},{5... | collective-permute-start | bytes 7077896 | tf_op jit(solution)/shard_map/ppermute | solution.py:38
  209.2 7.4 %collective-permute-start.22 = (bf16[24,768]{1,0:T(8,128)(2,1)S(1)}, bf16[24,768]{1,0:T(8,128)(2,1)S(1)}, u32[]{:S(2)}, u32[]{:S(2)}) collective-permute-start(bf16[24,768]{1,0:T(8,128)(2,1)S(1)} %get-tuple-element.294), channel_id=1, source_target_pairs={{0,1},{1,0},{2,3},{3,2},{4,5},{5,4},{6,7},{7,6},{8,9},{9,8},{10,11... | collective-permute-start | bytes 110600 | tf_op jit(solution)/shard_map/ppermute | solution.py:38
  210.4 6.8 collective-permute-start.23
  212.9 6.6 collective-permute-start.24
  249.3 7.2 collective-permute-start.34
  250.0 6.4 collective-permute-start.35
  316.5 16.4 %collective-permute-start.37 = (f32[2,2,4,96,768]{4,3,2,0,1:T(8,128)}, f32[2,2,4,96,768]{4,3,2,0,1:T(8,128)S(1)}, u32[]{:S(2)}, u32[]{:S(2)}) collective-permute-start(f32[2,2,4,96,768]{4,3,2,0,1:T(8,128)} %copy.87), channel_id=1, source_target_pairs={{0,4},{4,0},{8,12},{12,8},{16,20},{20,16},{24,28},{28,24},{1,5},{5... | collective-permute-start | bytes 14155784 | tf_op jit(solution)/shard_map/ppermute | solution.py:38
  316.5 23.2 %collective-permute-start.36 = (f32[2,2,4,96,768]{4,3,2,1,0:T(8,128)}, f32[2,2,4,96,768]{4,3,2,1,0:T(8,128)S(1)}, u32[]{:S(2)}, u32[]{:S(2)}) collective-permute-start(f32[2,2,4,96,768]{4,3,2,1,0:T(8,128)} %bitcast.432), channel_id=1, source_target_pairs={{0,4},{4,0},{8,12},{12,8},{16,20},{20,16},{24,28},{28,24},{1,5},{5... | collective-permute-start | bytes 14155784 | tf_op jit(solution)/shard_map/ppermute | solution.py:38
  361.9 53.9 %collective-permute-start.39 = (f32[2,4,96,768]{3,2,1,0:T(8,128)}, f32[2,4,96,768]{3,2,1,0:T(8,128)}, u32[]{:S(2)}, u32[]{:S(2)}) collective-permute-start(f32[2,4,96,768]{3,2,1,0:T(8,128)} %slice_bitcast_fusion.2), channel_id=1, source_target_pairs={{0,8},{4,12},{8,0},{12,4},{16,24},{20,28},{24,16},{28,20},{1,9},{5... | collective-permute-start | bytes 7077896 | tf_op jit(solution)/shard_map/ppermute | solution.py:38
  362.7 57.8 %collective-permute-start.38 = (f32[2,4,96,768]{3,2,1,0:T(8,128)}, f32[2,4,96,768]{3,2,1,0:T(8,128)}, u32[]{:S(2)}, u32[]{:S(2)}) collective-permute-start(f32[2,4,96,768]{3,2,1,0:T(8,128)} %slice_bitcast_fusion.3), channel_id=1, source_target_pairs={{0,16},{4,20},{8,24},{12,28},{16,0},{20,4},{24,8},{28,12},{1,17},{... | collective-permute-start | bytes 7077896 | tf_op jit(solution)/shard_map/ppermute | solution.py:38
  363.7 177.7 %reduce-scatter.2.cloned.1.call-start = ((), (), s32[]{:S(2)}) async-start(), calls=%async_computation.3 | async-start | bytes 2949120 | tf_op jit(solution)/shard_map/reduce_scatter | solution.py:819
  423.8 27.6 %collective-permute-start.40 = (f32[4,96,768]{2,1,0:T(8,128)}, f32[4,96,768]{2,1,0:T(8,128)}, u32[]{:S(2)}, u32[]{:S(2)}) collective-permute-start(f32[4,96,768]{2,1,0:T(8,128)} %slice_bitcast_fusion.9), channel_id=1, source_target_pairs={{0,8},{4,12},{8,0},{12,4},{16,24},{20,28},{24,16},{28,20},{1,9},{5... | collective-permute-start | bytes 3538952 | tf_op jit(solution)/shard_map/ppermute | solution.py:38
  424.9 28.2 %collective-permute-start.41 = (f32[4,96,768]{2,1,0:T(8,128)}, f32[4,96,768]{2,1,0:T(8,128)}, u32[]{:S(2)}, u32[]{:S(2)}) collective-permute-start(f32[4,96,768]{2,1,0:T(8,128)} %slice_bitcast_fusion.8), channel_id=1, source_target_pairs={{0,16},{4,20},{8,24},{12,28},{16,0},{20,4},{24,8},{28,12},{1,17},{... | collective-permute-start | bytes 3538952 | tf_op jit(solution)/shard_map/ppermute | solution.py:38
  456.1 15.5 %collective-permute-start.42 = (f32[2,2,4,48,768]{4,3,2,1,0:T(8,128)}, f32[2,2,4,48,768]{4,3,2,1,0:T(8,128)S(1)}, u32[]{:S(2)}, u32[]{:S(2)}) collective-permute-start(f32[2,2,4,48,768]{4,3,2,1,0:T(8,128)} %pad_maximum_fusion.4), channel_id=1, source_target_pairs={{0,4},{4,0},{8,12},{12,8},{16,20},{20,16},{24,28},{28,24},{1,5},{5... | collective-permute-start | bytes 7077896 | tf_op jit(solution)/shard_map/ppermute | solution.py:38
  473.3 6.7 collective-permute-start.43
  476.9 16.2 %collective-permute-start.45 = (f32[2,4,48,384]{3,2,1,0:T(8,128)S(1)}, f32[2,4,48,384]{3,2,1,0:T(8,128)S(1)}, u32[]{:S(2)}, u32[]{:S(2)}) collective-permute-start(f32[2,4,48,384]{3,2,1,0:T(8,128)S(1)} %get-tuple-element.160), channel_id=1, source_target_pairs={{0,16},{4,20},{8,24},{12,28},{16,0},{20,4},{24,8},{28,12},{1,17},{... | collective-permute-start | bytes 1769480 | tf_op jit(solution)/shard_map/ppermute | solution.py:38
  477.8 17.2 %collective-permute-start.47 = (f32[2,4,48,384]{3,2,1,0:T(8,128)}, f32[2,4,48,384]{3,2,1,0:T(8,128)S(1)}, u32[]{:S(2)}, u32[]{:S(2)}) collective-permute-start(f32[2,4,48,384]{3,2,1,0:T(8,128)} %get-tuple-element.162), channel_id=1, source_target_pairs={{0,8},{4,12},{8,0},{12,4},{16,24},{20,28},{24,16},{28,20},{1,9},{5... | collective-permute-start | bytes 1769480 | tf_op jit(solution)/shard_map/ppermute | solution.py:38
  486.3 35.1 %collective-permute-start.49 = (f32[2,4,72,384]{3,2,1,0:T(8,128)}, f32[2,4,72,384]{3,2,1,0:T(8,128)}, u32[]{:S(2)}, u32[]{:S(2)}) collective-permute-start(f32[2,4,72,384]{3,2,1,0:T(8,128)} %dynamic-slice_bitcast_fusion.6), channel_id=1, source_target_pairs={{0,8},{4,12},{8,0},{12,4},{16,24},{20,28},{24,16},{28,20},{1,9},{5... | collective-permute-start | bytes 2654216 | tf_op jit(solution)/shard_map/ppermute | solution.py:38
  487.2 36.3 %collective-permute-start.44 = (f32[2,4,72,384]{3,2,1,0:T(8,128)}, f32[2,4,72,384]{3,2,1,0:T(8,128)}, u32[]{:S(2)}, u32[]{:S(2)}) collective-permute-start(f32[2,4,72,384]{3,2,1,0:T(8,128)} %dynamic-slice_bitcast_fusion.7), channel_id=1, source_target_pairs={{0,16},{4,20},{8,24},{12,28},{16,0},{20,4},{24,8},{28,12},{1,17},{... | collective-permute-start | bytes 2654216 | tf_op jit(solution)/shard_map/ppermute | solution.py:38
  494.2 24.2 %collective-permute-start.46 = (f32[4,48,384]{2,1,0:T(8,128)}, f32[4,48,384]{2,1,0:T(8,128)}, u32[]{:S(2)}, u32[]{:S(2)}) collective-permute-start(f32[4,48,384]{2,1,0:T(8,128)} %dynamic-slice_bitcast_fusion.22), channel_id=1, source_target_pairs={{0,8},{4,12},{8,0},{12,4},{16,24},{20,28},{24,16},{28,20},{1,9},{5... | collective-permute-start | bytes 884744 | tf_op jit(solution)/shard_map/ppermute | solution.py:38
  496.8 22.7 %collective-permute-start.48 = (f32[4,48,384]{2,1,0:T(8,128)}, f32[4,48,384]{2,1,0:T(8,128)}, u32[]{:S(2)}, u32[]{:S(2)}) collective-permute-start(f32[4,48,384]{2,1,0:T(8,128)} %dynamic-slice_bitcast_fusion.21), channel_id=1, source_target_pairs={{0,16},{4,20},{8,24},{12,28},{16,0},{20,4},{24,8},{28,12},{1,17},{... | collective-permute-start | bytes 884744 | tf_op jit(solution)/shard_map/ppermute | solution.py:38
  525.7 11.2 %collective-permute-start.50 = (f32[4,72,384]{2,1,0:T(8,128)}, f32[4,72,384]{2,1,0:T(8,128)}, u32[]{:S(2)}, u32[]{:S(2)}) collective-permute-start(f32[4,72,384]{2,1,0:T(8,128)} %dynamic-slice_bitcast_fusion.14), channel_id=1, source_target_pairs={{0,8},{4,12},{8,0},{12,4},{16,24},{20,28},{24,16},{28,20},{1,9},{5... | collective-permute-start | bytes 1327112 | tf_op jit(solution)/shard_map/ppermute | solution.py:38
  526.9 11.2 %collective-permute-start.51 = (f32[4,72,384]{2,1,0:T(8,128)}, f32[4,72,384]{2,1,0:T(8,128)}, u32[]{:S(2)}, u32[]{:S(2)}) collective-permute-start(f32[4,72,384]{2,1,0:T(8,128)} %dynamic-slice_bitcast_fusion.13), channel_id=1, source_target_pairs={{0,16},{4,20},{8,24},{12,28},{16,0},{20,4},{24,8},{28,12},{1,17},{... | collective-permute-start | bytes 1327112 | tf_op jit(solution)/shard_map/ppermute | solution.py:38
  541.3 16.5 %collective-permute-start.53 = (f32[2,120,768]{2,1,0:T(8,128)}, f32[2,120,768]{2,1,0:T(8,128)S(1)}, u32[]{:S(2)}, u32[]{:S(2)}) collective-permute-start(f32[2,120,768]{2,1,0:T(8,128)} %dynamic-slice_bitcast_fusion.8), channel_id=1, source_target_pairs={{0,1},{1,0},{2,3},{3,2},{4,5},{5,4},{6,7},{7,6},{8,9},{9,8},{10,11... | collective-permute-start | bytes 2211848 | tf_op jit(solution)/shard_map/ppermute | solution.py:38
  559.1 21.4 %collective-permute-start.57 = (f32[1,120,768]{2,1,0:T(8,128)S(1)}, f32[1,120,768]{2,1,0:T(8,128)S(1)}, u32[]{:S(2)}, u32[]{:S(2)}) collective-permute-start(f32[1,120,768]{2,1,0:T(8,128)S(1)} %constant_dynamic-slice_fusion.1), channel_id=1, source_target_pairs={{0,2},{1,3},{2,0},{3,1},{4,6},{5,7},{6,4},{7,5},{8,10},{9,11},{10,... | collective-permute-start | bytes 1105928 | tf_op jit(solution)/shard_map/ppermute | solution.py:38
  560.6 7.1 collective-permute-start.58
  562.4 18.1 %collective-permute-start.59 = (f32[24,768]{1,0:T(8,128)S(1)}, f32[24,768]{1,0:T(8,128)S(1)}, u32[]{:S(2)}, u32[]{:S(2)}) collective-permute-start(f32[24,768]{1,0:T(8,128)S(1)} %add_add_fusion.3), channel_id=1, source_target_pairs={{0,2},{1,3},{2,0},{3,1},{4,6},{5,7},{6,4},{7,5},{8,10},{9,11},{10,... | collective-permute-start | bytes 221192 | tf_op jit(solution)/shard_map/ppermute | solution.py:38
  564.0 16.5 %collective-permute-start.60 = (f32[24,768]{1,0:T(8,128)S(1)}, f32[24,768]{1,0:T(8,128)S(1)}, u32[]{:S(2)}, u32[]{:S(2)}) collective-permute-start(f32[24,768]{1,0:T(8,128)S(1)} %add_add_fusion.3), channel_id=1, source_target_pairs={{0,3},{1,2},{2,1},{3,0},{4,7},{5,6},{6,5},{7,4},{8,11},{9,10},{10,... | collective-permute-start | bytes 221192 | tf_op jit(solution)/shard_map/ppermute | solution.py:38
  602.4 12.7 %collective-permute-start.68 = (f32[96,768]{1,0:T(8,128)S(1)}, f32[96,768]{1,0:T(8,128)S(1)}, u32[]{:S(2)}, u32[]{:S(2)}) collective-permute-start(f32[96,768]{1,0:T(8,128)S(1)} %get-tuple-element.266), channel_id=1, source_target_pairs={{0,1},{1,0},{2,3},{3,2},{4,5},{5,4},{6,7},{7,6},{8,9},{9,8},{10,11... | collective-permute-start | bytes 884744 | tf_op jit(solution)/shard_map/ppermute | solution.py:38
  602.4 23.6 %collective-permute-start.69 = (f32[96,768]{1,0:T(8,128)S(1)}, f32[96,768]{1,0:T(8,128)S(1)}, u32[]{:S(2)}, u32[]{:S(2)}) collective-permute-start(f32[96,768]{1,0:T(8,128)S(1)} %get-tuple-element.265), channel_id=1, source_target_pairs={{0,2},{1,3},{2,0},{3,1},{4,6},{5,7},{6,4},{7,5},{8,10},{9,11},{10,... | collective-permute-start | bytes 884744 | tf_op jit(solution)/shard_map/ppermute | solution.py:38
  605.4 20.6 %collective-permute-start.70 = (f32[96,768]{1,0:T(8,128)S(1)}, f32[96,768]{1,0:T(8,128)S(1)}, u32[]{:S(2)}, u32[]{:S(2)}) collective-permute-start(f32[96,768]{1,0:T(8,128)S(1)} %get-tuple-element.264), channel_id=1, source_target_pairs={{0,3},{1,2},{2,1},{3,0},{4,7},{5,6},{6,5},{7,4},{8,11},{9,10},{10,... | collective-permute-start | bytes 884744 | tf_op jit(solution)/shard_map/ppermute | solution.py:38
  637.6 9.9 %collective-permute-start.72 = (f32[96,768]{1,0:T(8,128)S(1)}, f32[96,768]{1,0:T(8,128)S(1)}, u32[]{:S(2)}, u32[]{:S(2)}) collective-permute-start(f32[96,768]{1,0:T(8,128)S(1)} %get-tuple-element.262), channel_id=1, source_target_pairs={{0,8},{4,12},{8,0},{12,4},{16,24},{20,28},{24,16},{28,20},{1,9},{5... | collective-permute-start | bytes 884744 | tf_op jit(solution)/shard_map/ppermute | solution.py:38
  638.8 15.1 %collective-permute-start.73 = (f32[96,768]{1,0:T(8,128)S(1)}, f32[96,768]{1,0:T(8,128)S(1)}, u32[]{:S(2)}, u32[]{:S(2)}) collective-permute-start(f32[96,768]{1,0:T(8,128)S(1)} %get-tuple-element.261), channel_id=1, source_target_pairs={{0,16},{4,20},{8,24},{12,28},{16,0},{20,4},{24,8},{28,12},{1,17},{... | collective-permute-start | bytes 884744 | tf_op jit(solution)/shard_map/ppermute | solution.py:38
  639.6 14.3 %collective-permute-start.74 = (f32[96,768]{1,0:T(8,128)S(1)}, f32[96,768]{1,0:T(8,128)S(1)}, u32[]{:S(2)}, u32[]{:S(2)}) collective-permute-start(f32[96,768]{1,0:T(8,128)S(1)} %get-tuple-element.260), channel_id=1, source_target_pairs={{0,24},{4,28},{8,16},{12,20},{16,8},{20,12},{24,0},{28,4},{1,25},{... | collective-permute-start | bytes 884744 | tf_op jit(solution)/shard_map/ppermute | solution.py:38
  654.9 10.9 %collective-permute-start.75 = (f32[96,768]{1,0:T(8,128)S(1)}, f32[96,768]{1,0:T(8,128)S(1)}, u32[]{:S(2)}, u32[]{:S(2)}) collective-permute-start(f32[96,768]{1,0:T(8,128)S(1)} %fusion.69), channel_id=1, source_target_pairs={{0,24},{4,28},{8,16},{12,20},{16,8},{20,12},{24,0},{28,4},{1,25},{... | collective-permute-start | bytes 884744 | tf_op jit(solution)/shard_map/ppermute | solution.py:38
  656.6 13.7 %collective-permute-start.76 = (f32[96,768]{1,0:T(8,128)S(1)}, f32[96,768]{1,0:T(8,128)S(1)}, u32[]{:S(2)}, u32[]{:S(2)}) collective-permute-start(f32[96,768]{1,0:T(8,128)S(1)} %fusion.69), channel_id=1, source_target_pairs={{0,16},{4,20},{8,24},{12,28},{16,0},{20,4},{24,8},{28,12},{1,17},{... | collective-permute-start | bytes 884744 | tf_op jit(solution)/shard_map/ppermute | solution.py:38
  657.3 13.1 %collective-permute-start.77 = (f32[96,768]{1,0:T(8,128)S(1)}, f32[96,768]{1,0:T(8,128)S(1)}, u32[]{:S(2)}, u32[]{:S(2)}) collective-permute-start(f32[96,768]{1,0:T(8,128)S(1)} %fusion.69), channel_id=1, source_target_pairs={{0,8},{4,12},{8,0},{12,4},{16,24},{20,28},{24,16},{28,20},{1,9},{5... | collective-permute-start | bytes 884744 | tf_op jit(solution)/shard_map/ppermute | solution.py:38
  670.8 8.2 %collective-permute-start.78 = (f32[4,96,768]{2,1,0:T(8,128)S(1)}, f32[4,96,768]{2,1,0:T(8,128)S(1)}, u32[]{:S(2)}, u32[]{:S(2)}) collective-permute-start(f32[4,96,768]{2,1,0:T(8,128)S(1)} %get-tuple-element.254), channel_id=1, source_target_pairs={{0,4},{4,0},{8,12},{12,8},{16,20},{20,16},{24,28},{28,24},{1,5},{5... | collective-permute-start | bytes 3538952 | tf_op jit(solution)/shard_map/ppermute | solution.py:38
  697.2 11.9 %collective-permute-start.79 = (f32[96,768]{1,0:T(8,128)S(1)}, f32[96,768]{1,0:T(8,128)S(1)}, u32[]{:S(2)}, u32[]{:S(2)}) collective-permute-start(f32[96,768]{1,0:T(8,128)S(1)} %get-tuple-element.253), channel_id=1, source_target_pairs={{0,3},{1,2},{2,1},{3,0},{4,7},{5,6},{6,5},{7,4},{8,11},{9,10},{10,... | collective-permute-start | bytes 884744 | tf_op jit(solution)/shard_map/ppermute | solution.py:38
  699.7 27.3 %collective-permute-start.80 = (f32[96,768]{1,0:T(8,128)S(1)}, f32[96,768]{1,0:T(8,128)S(1)}, u32[]{:S(2)}, u32[]{:S(2)}) collective-permute-start(f32[96,768]{1,0:T(8,128)S(1)} %get-tuple-element.252), channel_id=1, source_target_pairs={{0,2},{1,3},{2,0},{3,1},{4,6},{5,7},{6,4},{7,5},{8,10},{9,11},{10,... | collective-permute-start | bytes 884744 | tf_op jit(solution)/shard_map/ppermute | solution.py:38
  703.1 23.9 %collective-permute-start.81 = (f32[96,768]{1,0:T(8,128)S(1)}, f32[96,768]{1,0:T(8,128)S(1)}, u32[]{:S(2)}, u32[]{:S(2)}) collective-permute-start(f32[96,768]{1,0:T(8,128)S(1)} %get-tuple-element.250), channel_id=1, source_target_pairs={{0,1},{1,0},{2,3},{3,2},{4,5},{5,4},{6,7},{7,6},{8,9},{9,8},{10,11... | collective-permute-start | bytes 884744 | tf_op jit(solution)/shard_map/ppermute | solution.py:38
  (136 other events, 1367.0 us)
Sparse Core Ops, SparseCore 0:
  144.4 86.3 all-gather.2
  363.8 100.6 all-gather.4
  474.0 46.2 reduce-scatter.1

commit v6 on v5

--- a/solution.py
+++ b/solution.py
@@ -234,16 +234,63 @@
     return tree_sum(parts)
 
 
-def pack_sum(value):
-    pack_place, count = lax.axis_index("pack"), lax.axis_size("pack")
-    core = pack_place & 1
-    split = value.reshape(count // 2, 2, -1, value.shape[1])
-    mine = pick(split, core, 1) + swap(pick(split, 1 - core, 1), "pack", 1)
-    chip = pack_place >> 1
-    parts = [pick(mine, chip)] + [swap(pick(mine, chip ^ (k // 2)), "pack", k) for k in other_chips()]
-    total = tree_sum(parts)
-    mine = by_index([total] + [swap(total, "pack", k) for k in other_chips()], chip)
-    return by_core(mine, swap(mine, "pack", 1), 1).reshape(value.shape)
+def column_all_sum(value):
+    seq_place, count = lax.axis_index("seq"), lax.axis_size("seq")
+    core = lax.axis_index("pack") & 1
+    split = value.reshape(2, count, -1, value.shape[1])
+    mine = pick(split, core) + swap(pick(split, 1 - core), "pack", 1)
+    parts = [pick(mine, seq_place)] + [swap(pick(mine, seq_place ^ k), "seq", k) for k in range(1, count)]
+    mine = by_index(relative(tree_sum(parts), "seq"), seq_place)
+    return by_core(mine, swap(mine, "pack", 1), 0).reshape(value.shape)
+
+
+def fold(matrix):
+    count, width = matrix.shape[0] // BLOCK, matrix.shape[0]
+
+    def row(i):
+        return matrix[i * BLOCK : (i + 1) * BLOCK, i * BLOCK :]
+
+    return jnp.concatenate(
+        [jnp.concatenate([row(i), row(count - 1 - i)], axis=1) for i in range(count // 2)], axis=0
+    )
+
+
+def unfold_kernel(folded_ref, out_ref, scale_ref):
+    width = out_ref.shape[0]
+    count = width // BLOCK
+
+    def block(i, j):
+        line = min(i, count - 1 - i)
+        column = (j - i) * BLOCK + (0 if line == i else width - line * BLOCK)
+        return folded_ref[line * BLOCK : (line + 1) * BLOCK, column : column + BLOCK]
+
+    row = lax.broadcasted_iota(jnp.int32, (BLOCK, BLOCK), 0)
+    column = lax.broadcasted_iota(jnp.int32, (BLOCK, BLOCK), 1)
+    diagonal = jnp.zeros((BLOCK, BLOCK), F32)
+    for i in range(count):
+        diagonal += jnp.where(row == column, block(i, i), 0.0)
+    trace = jnp.sum(jnp.sum(diagonal, axis=0, keepdims=True), axis=1, keepdims=True)
+    scale = 1.0 / (jnp.sqrt(trace) + 1e-07)
+    for i in range(count):
+        for j in range(i, count):
+            value = block(i, j) * scale * scale
+            out_ref[i * BLOCK : (i + 1) * BLOCK, j * BLOCK : (j + 1) * BLOCK] = value
+            if j > i:
+                out_ref[j * BLOCK : (j + 1) * BLOCK, i * BLOCK : (i + 1) * BLOCK] = value.T
+    scale_ref[...] = jnp.broadcast_to(scale, scale_ref.shape)
+
+
+def unfold(folded, width):
+    whole = pl.BlockSpec(memory_space=pltpu.VMEM)
+    matrix, scale = pl.pallas_call(
+        unfold_kernel,
+        in_specs=[whole],
+        out_specs=[whole, whole],
+        out_shape=[jax.ShapeDtypeStruct((width, width), F32), jax.ShapeDtypeStruct((8, BLOCK), F32)],
+        compiler_params=pltpu.CompilerParams(vmem_limit_bytes=32 << 20),
+        cost_estimate=NO_COST,
+    )(folded)
+    return matrix, scale[0, 0]
 
 
 def sum_plane(value):
@@ -529,12 +576,9 @@
 
 
 def ortho(columns):
-    gram_mat = pack_sum(
-        lax.dot_general(columns, columns, (TN, ((), ())), precision=NS_PREC, preferred_element_type=F32)
-    )
-    scale = 1.0 / (jnp.sqrt(jnp.trace(gram_mat)) + 1e-07)
+    gram_part = lax.dot_general(columns, columns, (TN, ((), ())), precision=NS_PREC, preferred_element_type=F32)
+    gram_mat, scale = unfold(column_all_sum(fold(gram_part)), columns.shape[1])
     iterate = columns * scale
-    gram_mat = gram_mat * scale * scale
     eye = jnp.eye(gram_mat.shape[0], dtype=F32)
     for step in range(NS_STEPS):
         if step < NS_STEPS - 1:
@@ -549,20 +593,20 @@
     return iterate
 
 
-def to_planes(shards):
-    seq_count, seq_place = lax.axis_size("seq"), lax.axis_index("seq")
+def to_columns(shards):
+    chip = lax.axis_index("pack") >> 1
     most = max(m.shape[0] for m in shards)
     filled = [jnp.pad(m, ((0, most - m.shape[0]), (0, 0))) for m in shards]
-    filled += [jnp.zeros_like(filled[0])] * (seq_count - len(shards))
+    filled += [jnp.zeros_like(filled[0])] * (lax.axis_size("pack") // 2 - len(shards))
     stacked = jnp.stack(filled)
-    parts = [pick(stacked, seq_place)]
-    parts += [swap(pick(stacked, seq_place ^ k), "seq", k) for k in range(1, seq_count)]
+    parts = [pick(stacked, chip)]
+    parts += [swap(pick(stacked, chip ^ (k // 2)), "pack", k) for k in other_chips()]
     return jnp.stack(parts)
 
 
-def from_planes(value, counts):
-    back = [value[0]] + [swap(value[k], "seq", k) for k in range(1, lax.axis_size("seq"))]
-    return [_choose(back, lax.axis_index("seq"), m)[:count] for m, count in enumerate(counts)]
+def from_columns(value, counts):
+    back = [value[0]] + [swap(value[k // 2], "pack", k) for k in other_chips()]
+    return [_choose(back, lax.axis_index("pack") >> 1, m)[:count] for m, count in enumerate(counts)]
 
 
 def muon_update(weight, iterate):
@@ -882,9 +926,9 @@
         MUON_MU * moment.T + factor * share
         for moment, share in zip((qkv_moment, output_moment, up_moment, down_moment), muon_shares)
     ]
-    columns = to_planes(moments)
+    columns = to_columns(moments)
     iterates = ortho(columns.reshape(-1, width)).reshape(columns.shape)
-    iterates = [iterate.T for iterate in from_planes(iterates, [m.shape[0] for m in moments])]
+    iterates = [iterate.T for iterate in from_columns(iterates, [m.shape[0] for m in moments])]
     moments = [moment.T for moment in moments]
     new_qkv = muon_update(qkv_weight, iterates[0])
     new_output = muon_update(output_weight, iterates[1])

time: 743 us -> 717 us (0.965)
  waiting for transfers between devices: 180 us -> 161 us
    ppermute x80, waiting for transfers between devices: 157 us -> 138 us  [swap(): lax.ppermute(value, axis, [(i, i ^ bit) for i in range(lax.axis_size(axis...]
    unnamed x233 -> x235, local copies, waits for them, and re-layouts: 15.1 us -> 14.2 us
  transfers between devices with their start and end apart: 85 -> 85, of which waited for: 48 -> 48; matrix products, arithmetic and copies ran while one was open for 30% -> 31% of each run, Pallas kernels for 11% -> 11%
where the time goes in v6:
time: 717 us; the launch traced here: 711 us
  matrix products  184 us (26%)
  waiting for transfers between devices  161 us (22%)
  Pallas kernels  104 us (15%)
  other arithmetic  94.9 us (13%)
  starting transfers between devices  92.4 us (13%)
  local copies, waits for them, and re-layouts  52.4 us (7%)
  between operations  22.9 us (3%)
    dot_general x25, matrix products, mm(): return jnp.einsum(spec, left, right, preferred_element_type=F32)  164 us
    ppermute x80, waiting for transfers between devices, swap(): lax.ppermute(value, axis, [(i, i ^ bit) for i in range(lax.axis_size(axis...  138 us
    ppermute x80, starting transfers between devices, swap(): lax.ppermute(value, axis, [(i, i ^ bit) for i in range(lax.axis_size(axis...  89.3 us
    pallas_call x1, Pallas kernels, attend_back(): pl.pallas_call(lambda *refs: attend_back_kernel(width, blocks, *refs), gr...  47.1 us
    pallas_call x3, Pallas kernels, norm_back(): pl.pallas_call(lambda *refs: norm_back_kernel(groups, keep_sum, *refs), g...  34.3 us
    pallas_call x1, Pallas kernels, attend(): pl.pallas_call(lambda *refs: attend_kernel(width, blocks, *refs), grid=(b...  21.2 us
    add x14, other arithmetic, step(): self.value = self.keep + swap(sent, 'pack', self.bit)  17.9 us
    ppermute x1, waiting for transfers between devices, body(): lax.ppermute(patches[:, shard_len - MAXLEN:], 'seq', [(i, i + 1) for i in...  16.8 us
  transfers between devices with their start and end apart: 85, of which 48 were waited for; matrix products, arithmetic and copies ran while one was open for 31% of the time, Pallas kernels for 11%

profile of v6, /device:TPU:0, one launch (start us, length us, event | category | flops | bytes accessed | tf_op | source)
XLA Modules:
  0.0 711.3 jit_solution(15626486409557735375)
XLA Ops:
  11.7 5.1 collective-permute-start
  22.9 11.6 %collective-permute-done.1 = bf16[136,768]{1,0:T(8,128)(2,1)S(1)} collective-permute-done((bf16[136,768]{1,0:T(8,128)(2,1)S(1)}, bf16[136,768]{1,0:T(8,128)(2,1)S(1)}, u32[]{:S(2)}, u32[]{:S(2)}) %collective-permute-start.1) | collective-permute-done | bytes 208928 | tf_op jit(solution)/shard_map/ppermute | solution.py:38
  44.2 16.8 %collective-permute-done.3 = bf16[6,128,768]{2,1,0:T(8,128)(2,1)S(1)} collective-permute-done((bf16[6,128,768]{2,1,0:T(8,128)(2,1)S(1)}, bf16[6,128,768]{2,1,0:T(8,128)(2,1)S(1)}, u32[]{:S(2)}, u32[]{:S(2)}) %collective-permute-start.3) | collective-permute-done | bytes 1179680 | tf_op jit(solution)/shard_map/ppermute | solution.py:737
  61.0 4.2 collective-permute-done.4
  65.7 10.3 %fusion.23 = bf16[1664,768]{1,0:T(8,128)(2,1)} fusion(bf16[3072,768]{1,0:T(8,128)(2,1)S(1)} %bitcast.386, s32[1664]{0:T(1024)S(1)} %get-tuple-element.317), kind=kOutput, calls=%fused_computation.55 | convolution fusion | flops 7858126848 | bytes 7281152 | tf_op jit(solution)/shard_map/rw,wi->ri/dot_general | solution.py:567
  76.0 3.1 collective-permute-done.6
  80.2 2.7 convert_element_type.174
  89.4 5.0 collective-permute-start.11
  102.5 4.5 convolution_add_fusion.1.refs_0_
  113.5 2.8 reduce_sum.243
  116.2 3.1 multiply_reduce_fusion.2
  122.3 2.9 collective-permute-start.10
  125.3 9.3 %add_convert_fusion.refs_0_ = bf16[1664,2304]{1,0:T(8,128)(2,1)} fusion(bf16[2304,768]{1,0:T(8,128)(2,1)S(1)} %bitcast.388, f32[2304]{0:T(1024)S(1)} %pad_maximum_fusion.16, f32[1664,768]{1,0:T(8,128)S(1)} %bitcast.366, f32[768]{0:T(1024)S(1)} %get-tuple-element.305, f32[768]{0:T(1024)S(1)} %get-tuple-element.313, f32[1664]{0:T(1024)S(1)} %add_rsqrt_fusion.2, ...), kind=kOutput, calls=%fused_computation.7 | convolution fusion | flops 5902860288 | bytes 16347136 | tf_op jit(solution)/shard_map/rd,ed->re/dot_general | solution.py:567
  141.2 3.2 pad_maximum_fusion.2
  144.4 21.2 %shard_map.435 = (bf16[1664,768]{1,0:T(8,128)(2,1)}, f32[13,6,256]{2,1,0:T(8,128)}) custom-call(bf16[1664,2304]{1,0:T(8,128)(2,1)} %add_convert_fusion.refs_0_, s32[13,1,128]{2,1,0:T(1,128)} %select_n.787.refs_1_.refs_3_, s32[1920,1]{1,0:T(8,128)} %broadcast_in_dim.210.refs_2_.refs_4_), custom_call_target="tpu_custom_call" | custom-call | tf_op jit(solution)/shard_map/pallas_call | solution.py:404
  166.2 5.7 fusion.135
  172.7 2.8 pad_maximum_fusion.3
  176.8 8.7 %multiply_convert_fusion.1 = (bf16[1664,1536]{1,0:T(8,128)(2,1)S(1)}, f32[1664,1536]{1,0:T(8,128)}) fusion(f32[1536]{0:T(1024)S(1)} %add.688, bf16[1664,768]{1,0:T(8,128)(2,1)S(1)} %add_convert_fusion.1, bf16[1536,768]{1,0:T(8,128)(2,1)} %bitcast.38), kind=kOutput, calls=%fused_computation.24 | convolution fusion | flops 3941203968 | bytes 20256768 | tf_op jit(solution)/shard_map/rd,fd->rf/dot_general | solution.py:567
  185.5 4.2 fusion.137
  189.8 9.0 %multiply_convert_fusion = (bf16[1664,1536]{1,0:T(8,128)(2,1)S(1)}, f32[1664,1536]{1,0:T(8,128)}) fusion(f32[1536]{0:T(1024)S(1)} %add.692, bf16[1664,768]{1,0:T(8,128)(2,1)S(1)} %add_convert_fusion.1, bf16[1536,768]{1,0:T(8,128)(2,1)} %bitcast.44), kind=kOutput, calls=%fused_computation.22 | convolution fusion | flops 3941203968 | bytes 20256768 | tf_op jit(solution)/shard_map/rd,fd->rf/dot_general | solution.py:567
  198.9 4.8 fusion.136
  206.1 3.0 fusion.59
  230.9 5.6 fusion.39
  250.0 2.9 collective-permute-start.35
  257.3 11.4 %shard_map.436 = (bf16[1664,768]{1,0:T(8,128)(2,1)}, f32[8,768]{1,0:T(8,128)}, f32[1664,768]{1,0:T(8,128)}) custom-call(f32[1664,768]{1,0:T(8,128)} %copy-done.4, f32[96,768]{1,0:T(8,128)} %maximum_divide_fusion.refs_1_, s32[1664,1]{1,0:T(8,128)} %select_n.872.refs_2_, f32[1,768]{1,0:T(1,128)} %get-tuple-element.302.refs_3_), custom_call_target="tpu_custom_call" | custom-call | tf_op jit(solution)/shard_map/pallas_call | solution.py:500
  268.7 7.5 %fusion.140 = f32[1536,768]{1,0:T(8,128)S(1)} fusion(bf16[1664,1536]{1,0:T(8,128)(2,1)} %copy-done.104, bf16[1664,768]{1,0:T(8,128)(2,1)} %get-tuple-element.128), kind=kOutput, calls=%fused_computation.402 | convolution fusion | flops 3925868544 | bytes 12386304 | tf_op jit(solution)/shard_map/rf,rd->fd/dot_general | solution.py:567
  276.2 9.3 %fusion.139 = f32[1536,768]{1,0:T(8,128)} fusion(bf16[1664,1536]{1,0:T(8,128)(2,1)} %copy-done.103, bf16[1664,768]{1,0:T(8,128)(2,1)S(1)} %copy-done.100), kind=kOutput, calls=%fused_computation.401 | convolution fusion | flops 3925868544 | bytes 12386304 | tf_op jit(solution)/shard_map/rf,rd->fd/dot_general | solution.py:567
  285.4 9.7 %fusion.6 = bf16[1664,1536]{1,0:T(8,128)(2,1)S(1)} fusion(bf16[1664,768]{1,0:T(8,128)(2,1)S(1)} %copy-done.100, bf16[1536,768]{1,0:T(8,128)(2,1)S(1)} %bitcast.395, f32[1664,1536]{1,0:T(8,128)} %get-tuple-element.330, f32[1536]{0:T(1024)S(1)} %copy-done.79), kind=kOutput, calls=%fused_computation.13 | convolution fusion | flops 3953983488 | bytes 20256768 | tf_op jit(solution)/shard_map/rd,fd->rf/dot_general | solution.py:567
  295.2 4.7 fusion.142
  299.9 9.3 %fusion.12 = bf16[1664,1536]{1,0:T(8,128)(2,1)S(1)} fusion(bf16[1664,768]{1,0:T(8,128)(2,1)S(1)} %copy-done.100, bf16[1536,768]{1,0:T(8,128)(2,1)S(1)} %bitcast.427, f32[1664,1536]{1,0:T(8,128)} %get-tuple-element.332, f32[1536]{0:T(1024)S(1)} %copy-done.77), kind=kOutput, calls=%fused_computation.19 | convolution fusion | flops 3953983488 | bytes 20256768 | tf_op jit(solution)/shard_map/rd,fd->rf/dot_general | solution.py:567
  309.2 4.6 fusion.141
  317.0 7.6 %fusion.143 = f32[1664,768]{1,0:T(8,128)} fusion(bf16[1664,1536]{1,0:T(8,128)(2,1)S(1)} %fusion.6, bf16[1536,768]{1,0:T(8,128)(2,1)} %bitcast.38), kind=kOutput, calls=%fused_computation.405 | convolution fusion | flops 3925868544 | bytes 12582912 | tf_op jit(solution)/shard_map/rf,fd->rd/dot_general | solution.py:567
  324.6 8.3 %convolution_add_fusion.2.refs_1_ = f32[1664,768]{1,0:T(8,128)} fusion(f32[1664,768]{1,0:T(8,128)} %fusion.143, bf16[1664,1536]{1,0:T(8,128)(2,1)S(1)} %fusion.12, bf16[1536,768]{1,0:T(8,128)(2,1)} %bitcast.44), kind=kOutput, calls=%fused_computation.50 | convolution fusion | flops 3927146496 | bytes 17694720 | tf_op jit(solution)/shard_map/rf,fd->rd/dot_general | solution.py:567
  335.1 2.9 copy_add_fusion
  344.5 12.0 %shard_map.437 = (bf16[1664,768]{1,0:T(8,128)(2,1)}, f32[8,768]{1,0:T(8,128)}, f32[1664,768]{1,0:T(8,128)}) custom-call(f32[1664,768]{1,0:T(8,128)} %copy-done.3, f32[1664,768]{1,0:T(8,128)} %convolution_add_fusion.2.refs_1_, f32[1664,768]{1,0:T(8,128)} %get-tuple-element.134.refs_2_, f32[1,768]{1,0:T(1,128)} %get-tuple-element.303.refs_3_), custom_call_target="tpu_custom_call" | custom-call | tf_op jit(solution)/shard_map/pallas_call | solution.py:500
  356.6 5.3 convolution_convert_fusion.refs_1_
  363.7 47.1 %shard_map.438 = bf16[1664,2304]{1,0:T(8,128)(2,1)} custom-call(bf16[1664,2304]{1,0:T(8,128)(2,1)} %add_convert_fusion.refs_0_, bf16[1664,768]{1,0:T(8,128)(2,1)} %convolution_convert_fusion.refs_1_, f32[13,6,256]{2,1,0:T(8,128)} %get-tuple-element.139.refs_2_, s32[13,1,128]{2,1,0:T(1,128)} %select_n.787.refs_1_.refs_3_, ...), custom_call_target="tpu_custom_call" | custom-call | tf_op jit(solution)/shard_map/pallas_call | solution.py:429
  410.8 5.0 fusion.144
  426.1 7.8 %fusion.145.refs_1_ = f32[1664,768]{1,0:T(8,128)} fusion(bf16[1664,2304]{1,0:T(8,128)(2,1)S(1)} %bitcast.368, bf16[2304,768]{1,0:T(8,128)(2,1)S(1)} %bitcast.389), kind=kOutput, calls=%fused_computation.407 | convolution fusion | flops 5888802816 | bytes 16318464 | tf_op jit(solution)/shard_map/re,ed->rd/dot_general | solution.py:567
  433.9 10.9 %shard_map.439 = (bf16[1664,768]{1,0:T(8,128)(2,1)}, f32[8,768]{1,0:T(8,128)}) custom-call(f32[1664,768]{1,0:T(8,128)} %convolution_add_fusion.1.refs_0_, f32[1664,768]{1,0:T(8,128)} %fusion.145.refs_1_, f32[1664,768]{1,0:T(8,128)} %get-tuple-element.143.refs_2_, f32[1,768]{1,0:T(1,128)} %get-tuple-element.301.refs_3_), custom_call_target="tpu_custom_call" | custom-call | tf_op jit(solution)/shard_map/pallas_call | solution.py:500
  444.8 4.1 fusion.146
  456.1 11.5 %fusion.118 = f32[2304,768]{1,0:T(8,128)S(1)} fusion(bf16[1664,2304]{1,0:T(8,128)(2,1)} %shard_map.438, f32[1664,768]{1,0:T(8,128)} %convolution_add_fusion.1.refs_0_, f32[768]{0:T(1024)S(1)} %copy-done.87, f32[768]{0:T(1024)S(1)} %copy-done.89, f32[1664]{0:T(1024)S(1)} %copy-done.81, f32[1664]{0:T(1024)S(1)} %copy-done.64), kind=kOutput, calls=%fused_computation.388 | convolution fusion | flops 5895192576 | bytes 19876864 | tf_op jit(solution)/shard_map/re,rd->ed/dot_general | solution.py:567
  473.9 2.9 convert_reduce_fusion.3
  480.1 3.5 bitcast_add_fusion
  488.4 4.8 collective-permute-done.45
  499.6 3.3 convert_reduce_fusion.2
  502.8 3.5 fusion.21
  506.4 5.1 convert_reduce_fusion
  513.0 5.4 collective-permute-done.46
  529.6 7.3 %collective-permute-done.50 = f32[4,72,384]{2,1,0:T(8,128)} collective-permute-done((f32[4,72,384]{2,1,0:T(8,128)}, f32[4,72,384]{2,1,0:T(8,128)}, u32[]{:S(2)}, u32[]{:S(2)}) %collective-permute-start.50) | collective-permute-done | bytes 442400 | tf_op jit(solution)/shard_map/ppermute | solution.py:38
  550.1 7.8 %collective-permute-done.53 = f32[2,120,768]{2,1,0:T(8,128)S(1)} collective-permute-done((f32[2,120,768]{2,1,0:T(8,128)}, f32[2,120,768]{2,1,0:T(8,128)S(1)}, u32[]{:S(2)}, u32[]{:S(2)}) %collective-permute-start.53) | collective-permute-done | bytes 737312 | tf_op jit(solution)/shard_map/ppermute | solution.py:38
  567.7 12.8 %collective-permute-done.59 = f32[24,768]{1,0:T(8,128)S(1)} collective-permute-done((f32[24,768]{1,0:T(8,128)S(1)}, f32[24,768]{1,0:T(8,128)S(1)}, u32[]{:S(2)}, u32[]{:S(2)}) %collective-permute-start.59) | collective-permute-done | bytes 73760 | tf_op jit(solution)/shard_map/ppermute | solution.py:38
  607.5 6.5 collective-permute-done.68
  613.9 4.5 collective-permute-done.69
  625.5 3.0 collective-permute-start.73
  630.9 4.4 collective-permute-done.72
  635.2 6.1 collective-permute-done.73
  650.1 10.2 %collective-permute-done.76 = f32[48,896]{1,0:T(8,128)S(1)} collective-permute-done((f32[48,896]{1,0:T(8,128)S(1)}, f32[48,896]{1,0:T(8,128)S(1)}, u32[]{:S(2)}, u32[]{:S(2)}) %collective-permute-start.76) | collective-permute-done | bytes 172064 | tf_op jit(solution)/shard_map/ppermute | solution.py:38
  660.5 6.3 multiply_subtract_fusion
  667.4 3.0 fusion.147
  670.4 3.1 fusion.148
  673.5 3.5 fusion.30
  689.2 5.9 collective-permute-done.79
  695.1 5.9 collective-permute-done.80
  (613 shorter events, 238.0 us)
Async XLA Ops:
  7.2 223.7 %all-gather.3.cloned.1.call-start = ((), (), s32[]{:S(2)}) async-start(), calls=%async_computation.1 | async-start | bytes 5406720 | tf_op jit(solution)/shard_map/all_gather | solution.py:772
  11.7 11.3 %collective-permute-start = (bf16[136,768]{1,0:T(8,128)(2,1)S(1)}, bf16[136,768]{1,0:T(8,128)(2,1)S(1)}, u32[]{:S(2)}, u32[]{:S(2)}) collective-permute-start(bf16[136,768]{1,0:T(8,128)(2,1)S(1)} %constant_dynamic-update-slice_fusion), channel_id=1, source_target_pairs={{0,3},{1,2},{2,1},{3,0},{4,7},{5,6},{6,5},{7,4},{8,11},{9,10},{10,... | collective-permute-start | bytes 626696 | tf_op jit(solution)/shard_map/ppermute | solution.py:38
  16.8 17.7 %collective-permute-start.1 = (bf16[136,768]{1,0:T(8,128)(2,1)S(1)}, bf16[136,768]{1,0:T(8,128)(2,1)S(1)}, u32[]{:S(2)}, u32[]{:S(2)}) collective-permute-start(bf16[136,768]{1,0:T(8,128)(2,1)S(1)} %constant_dynamic-update-slice_fusion), channel_id=1, source_target_pairs={{0,2},{1,3},{2,0},{3,1},{4,6},{5,7},{6,4},{7,5},{8,10},{9,11},{10,... | collective-permute-start | bytes 626696 | tf_op jit(solution)/shard_map/ppermute | solution.py:38
  16.8 17.7 %collective-permute-start.2 = (bf16[136,768]{1,0:T(8,128)(2,1)S(1)}, bf16[136,768]{1,0:T(8,128)(2,1)S(1)}, u32[]{:S(2)}, u32[]{:S(2)}) collective-permute-start(bf16[136,768]{1,0:T(8,128)(2,1)S(1)} %constant_dynamic-update-slice_fusion), channel_id=1, source_target_pairs={{0,1},{1,0},{2,3},{3,2},{4,5},{5,4},{6,7},{7,6},{8,9},{9,8},{10,11... | collective-permute-start | bytes 626696 | tf_op jit(solution)/shard_map/ppermute | solution.py:38
  34.9 26.1 %collective-permute-start.3 = (bf16[6,128,768]{2,1,0:T(8,128)(2,1)S(1)}, bf16[6,128,768]{2,1,0:T(8,128)(2,1)S(1)}, u32[]{:S(2)}, u32[]{:S(2)}) collective-permute-start(bf16[6,128,768]{2,1,0:T(8,128)(2,1)S(1)} %get-tuple-element.248), channel_id=1, source_target_pairs={{0,1},{1,2},{2,3},{4,5},{5,6},{6,7},{8,9},{9,10},{10,11},{12,13},{... | collective-permute-start | bytes 3538952 | tf_op jit(solution)/shard_map/ppermute | solution.py:737
  36.6 28.6 %collective-permute-start.4 = (bf16[6,128,768]{2,1,0:T(8,128)(2,1)S(1)}, bf16[6,128,768]{2,1,0:T(8,128)(2,1)S(1)}, u32[]{:S(2)}, u32[]{:S(2)}) collective-permute-start(bf16[6,128,768]{2,1,0:T(8,128)(2,1)S(1)} %get-tuple-element.249), channel_id=1, source_target_pairs={{1,0},{2,1},{3,2},{5,4},{6,5},{7,6},{9,8},{10,9},{11,10},{13,12},{... | collective-permute-start | bytes 3538952 | tf_op jit(solution)/shard_map/ppermute | solution.py:738
  40.7 35.3 %collective-permute-start.5 = (bf16[4,136,768]{2,1,0:T(8,128)(2,1)S(1)}, bf16[4,136,768]{2,1,0:T(8,128)(2,1)S(1)}, u32[]{:S(2)}, u32[]{:S(2)}) collective-permute-start(bf16[4,136,768]{2,1,0:T(8,128)(2,1)S(1)} %pad_maximum_fusion.10), channel_id=1, source_target_pairs={{0,8},{4,12},{8,0},{12,4},{16,24},{20,28},{24,16},{28,20},{1,9},{5... | collective-permute-start | bytes 2506760 | tf_op jit(solution)/shard_map/ppermute | solution.py:38
  42.2 37.0 %collective-permute-start.6 = (bf16[4,136,768]{2,1,0:T(8,128)(2,1)S(1)}, bf16[4,136,768]{2,1,0:T(8,128)(2,1)S(1)}, u32[]{:S(2)}, u32[]{:S(2)}) collective-permute-start(bf16[4,136,768]{2,1,0:T(8,128)(2,1)S(1)} %pad_maximum_fusion.10), channel_id=1, source_target_pairs={{0,16},{4,20},{8,24},{12,28},{16,0},{20,4},{24,8},{28,12},{1,17},{... | collective-permute-start | bytes 2506760 | tf_op jit(solution)/shard_map/ppermute | solution.py:38
  43.7 35.5 %collective-permute-start.7 = (bf16[4,136,768]{2,1,0:T(8,128)(2,1)S(1)}, bf16[4,136,768]{2,1,0:T(8,128)(2,1)S(1)}, u32[]{:S(2)}, u32[]{:S(2)}) collective-permute-start(bf16[4,136,768]{2,1,0:T(8,128)(2,1)S(1)} %pad_maximum_fusion.10), channel_id=1, source_target_pairs={{0,24},{4,28},{8,16},{12,20},{16,8},{20,12},{24,0},{28,4},{1,25},{... | collective-permute-start | bytes 2506760 | tf_op jit(solution)/shard_map/ppermute | solution.py:38
  80.1 17.4 %collective-permute-start.8 = (bf16[4,4,136,768]{3,2,1,0:T(8,128)(2,1)S(1)}, bf16[4,4,136,768]{3,2,1,0:T(8,128)(2,1)}, u32[]{:S(2)}, u32[]{:S(2)}) collective-permute-start(bf16[4,4,136,768]{3,2,1,0:T(8,128)(2,1)S(1)} %pad_maximum_fusion.1), channel_id=1, source_target_pairs={{0,4},{4,0},{8,12},{12,8},{16,20},{20,16},{24,28},{28,24},{1,5},{5... | collective-permute-start | bytes 10027016 | tf_op jit(solution)/shard_map/ppermute | solution.py:38
  89.4 17.6 %collective-permute-start.11 = (bf16[96,768]{1,0:T(8,128)(2,1)}, bf16[96,768]{1,0:T(8,128)(2,1)}, u32[]{:S(2)}, u32[]{:S(2)}) collective-permute-start(bf16[96,768]{1,0:T(8,128)(2,1)} %convert_bitcast_fusion.1), channel_id=1, source_target_pairs={{0,3},{1,2},{2,1},{3,0},{4,7},{5,6},{6,5},{7,4},{8,11},{9,10},{10,... | collective-permute-start | bytes 442376 | tf_op jit(solution)/shard_map/ppermute | solution.py:38
  94.4 13.0 %collective-permute-start.12 = (bf16[96,768]{1,0:T(8,128)(2,1)}, bf16[96,768]{1,0:T(8,128)(2,1)}, u32[]{:S(2)}, u32[]{:S(2)}) collective-permute-start(bf16[96,768]{1,0:T(8,128)(2,1)} %convert_bitcast_fusion.1), channel_id=1, source_target_pairs={{0,2},{1,3},{2,0},{3,1},{4,6},{5,7},{6,4},{7,5},{8,10},{9,11},{10,... | collective-permute-start | bytes 442376 | tf_op jit(solution)/shard_map/ppermute | solution.py:38
  94.4 13.0 %collective-permute-start.13 = (bf16[96,768]{1,0:T(8,128)(2,1)}, bf16[96,768]{1,0:T(8,128)(2,1)}, u32[]{:S(2)}, u32[]{:S(2)}) collective-permute-start(bf16[96,768]{1,0:T(8,128)(2,1)} %convert_bitcast_fusion.1), channel_id=1, source_target_pairs={{0,1},{1,0},{2,3},{3,2},{4,5},{5,4},{6,7},{7,6},{8,9},{9,8},{10,11... | collective-permute-start | bytes 442376 | tf_op jit(solution)/shard_map/ppermute | solution.py:38
  108.7 28.7 %collective-permute-start.14 = (bf16[4,96,768]{2,1,0:T(8,128)(2,1)S(1)}, bf16[4,96,768]{2,1,0:T(8,128)(2,1)}, u32[]{:S(2)}, u32[]{:S(2)}) collective-permute-start(bf16[4,96,768]{2,1,0:T(8,128)(2,1)S(1)} %pad_maximum_fusion.13), channel_id=1, source_target_pairs={{0,8},{4,12},{8,0},{12,4},{16,24},{20,28},{24,16},{28,20},{1,9},{5... | collective-permute-start | bytes 1769480 | tf_op jit(solution)/shard_map/ppermute | solution.py:38
  110.0 27.4 %collective-permute-start.15 = (bf16[4,96,768]{2,1,0:T(8,128)(2,1)S(1)}, bf16[4,96,768]{2,1,0:T(8,128)(2,1)}, u32[]{:S(2)}, u32[]{:S(2)}) collective-permute-start(bf16[4,96,768]{2,1,0:T(8,128)(2,1)S(1)} %pad_maximum_fusion.13), channel_id=1, source_target_pairs={{0,16},{4,20},{8,24},{12,28},{16,0},{20,4},{24,8},{28,12},{1,17},{... | collective-permute-start | bytes 1769480 | tf_op jit(solution)/shard_map/ppermute | solution.py:38
  110.9 26.7 %collective-permute-start.16 = (bf16[4,96,768]{2,1,0:T(8,128)(2,1)S(1)}, bf16[4,96,768]{2,1,0:T(8,128)(2,1)}, u32[]{:S(2)}, u32[]{:S(2)}) collective-permute-start(bf16[4,96,768]{2,1,0:T(8,128)(2,1)S(1)} %pad_maximum_fusion.13), channel_id=1, source_target_pairs={{0,24},{4,28},{8,16},{12,20},{16,8},{20,12},{24,0},{28,4},{1,25},{... | collective-permute-start | bytes 1769480 | tf_op jit(solution)/shard_map/ppermute | solution.py:38
  112.3 10.0 %collective-permute-start.9 = (bf16[1,96,768]{2,1,0:T(8,128)(2,1)S(1)}, bf16[1,96,768]{2,1,0:T(8,128)(2,1)S(1)}, u32[]{:S(2)}, u32[]{:S(2)}) collective-permute-start(bf16[1,96,768]{2,1,0:T(8,128)(2,1)S(1)} %bitcast.404), channel_id=1, source_target_pairs={{0,1},{1,0},{2,3},{3,2},{4,5},{5,4},{6,7},{7,6},{8,9},{9,8},{10,11... | collective-permute-start | bytes 442376 | tf_op jit(solution)/shard_map/ppermute | solution.py:38
  122.3 15.0 %collective-permute-start.10 = (bf16[2,96,768]{2,1,0:T(8,128)(2,1)S(1)}, bf16[2,96,768]{2,1,0:T(8,128)(2,1)S(1)}, u32[]{:S(2)}, u32[]{:S(2)}) collective-permute-start(bf16[2,96,768]{2,1,0:T(8,128)(2,1)S(1)} %maximum_select_fusion.7), channel_id=1, source_target_pairs={{0,2},{1,3},{2,0},{3,1},{4,6},{5,7},{6,4},{7,5},{8,10},{9,11},{10,... | collective-permute-start | bytes 884744 | tf_op jit(solution)/shard_map/ppermute | solution.py:38
  137.5 28.0 %collective-permute-start.17 = (bf16[4,96,768]{2,1,0:T(8,128)(2,1)S(1)}, bf16[4,96,768]{2,1,0:T(8,128)(2,1)}, u32[]{:S(2)}, u32[]{:S(2)}) collective-permute-start(bf16[4,96,768]{2,1,0:T(8,128)(2,1)S(1)} %maximum_select_fusion.4), channel_id=1, source_target_pairs={{0,8},{4,12},{8,0},{12,4},{16,24},{20,28},{24,16},{28,20},{1,9},{5... | collective-permute-start | bytes 1769480 | tf_op jit(solution)/shard_map/ppermute | solution.py:38
  138.7 26.9 %collective-permute-start.18 = (bf16[4,96,768]{2,1,0:T(8,128)(2,1)S(1)}, bf16[4,96,768]{2,1,0:T(8,128)(2,1)}, u32[]{:S(2)}, u32[]{:S(2)}) collective-permute-start(bf16[4,96,768]{2,1,0:T(8,128)(2,1)S(1)} %maximum_select_fusion.4), channel_id=1, source_target_pairs={{0,16},{4,20},{8,24},{12,28},{16,0},{20,4},{24,8},{28,12},{1,17},{... | collective-permute-start | bytes 1769480 | tf_op jit(solution)/shard_map/ppermute | solution.py:38
  139.9 26.4 %collective-permute-start.19 = (bf16[4,96,768]{2,1,0:T(8,128)(2,1)S(1)}, bf16[4,96,768]{2,1,0:T(8,128)(2,1)}, u32[]{:S(2)}, u32[]{:S(2)}) collective-permute-start(bf16[4,96,768]{2,1,0:T(8,128)(2,1)S(1)} %maximum_select_fusion.4), channel_id=1, source_target_pairs={{0,24},{4,28},{8,16},{12,20},{16,8},{20,12},{24,0},{28,4},{1,25},{... | collective-permute-start | bytes 1769480 | tf_op jit(solution)/shard_map/ppermute | solution.py:38
  144.3 45.5 %collective-permute-start.20 = (bf16[4,4,96,768]{3,2,1,0:T(8,128)(2,1)}, bf16[4,4,96,768]{3,2,1,0:T(8,128)(2,1)}, u32[]{:S(2)}, u32[]{:S(2)}) collective-permute-start(bf16[4,4,96,768]{3,2,1,0:T(8,128)(2,1)} %pad_maximum_fusion.2), channel_id=1, source_target_pairs={{0,4},{4,0},{8,12},{12,8},{16,20},{20,16},{24,28},{28,24},{1,5},{5... | collective-permute-start | bytes 7077896 | tf_op jit(solution)/shard_map/ppermute | solution.py:38
  144.4 329.0 %all-gather.5.cloned.1.call-start = ((), (), s32[]{:S(2)}) async-start(), calls=%async_computation.2 | async-start | bytes 6881280 | tf_op jit(solution)/shard_map/all_gather | solution.py:821
  175.5 23.3 %collective-permute-start.21 = (bf16[4,4,96,768]{3,2,1,0:T(8,128)(2,1)S(1)}, bf16[4,4,96,768]{3,2,1,0:T(8,128)(2,1)S(1)}, u32[]{:S(2)}, u32[]{:S(2)}) collective-permute-start(bf16[4,4,96,768]{3,2,1,0:T(8,128)(2,1)S(1)} %pad_maximum_fusion.3), channel_id=1, source_target_pairs={{0,4},{4,0},{8,12},{12,8},{16,20},{20,16},{24,28},{28,24},{1,5},{5... | collective-permute-start | bytes 7077896 | tf_op jit(solution)/shard_map/ppermute | solution.py:38
  209.2 7.3 %collective-permute-start.22 = (bf16[24,768]{1,0:T(8,128)(2,1)S(1)}, bf16[24,768]{1,0:T(8,128)(2,1)S(1)}, u32[]{:S(2)}, u32[]{:S(2)}) collective-permute-start(bf16[24,768]{1,0:T(8,128)(2,1)S(1)} %get-tuple-element.298), channel_id=1, source_target_pairs={{0,1},{1,0},{2,3},{3,2},{4,5},{5,4},{6,7},{7,6},{8,9},{9,8},{10,11... | collective-permute-start | bytes 110600 | tf_op jit(solution)/shard_map/ppermute | solution.py:38
  210.4 6.8 collective-permute-start.23
  212.9 6.6 collective-permute-start.24
  249.3 7.2 %collective-permute-start.34 = (f32[24,768]{1,0:T(8,128)S(1)}, f32[24,768]{1,0:T(8,128)S(1)}, u32[]{:S(2)}, u32[]{:S(2)}) collective-permute-start(f32[24,768]{1,0:T(8,128)S(1)} %fusion.84), channel_id=1, source_target_pairs={{0,2},{1,3},{2,0},{3,1},{4,6},{5,7},{6,4},{7,5},{8,10},{9,11},{10,... | collective-permute-start | bytes 221192 | tf_op jit(solution)/shard_map/ppermute | solution.py:38
  250.0 6.5 collective-permute-start.35
  316.5 16.4 %collective-permute-start.37 = (f32[2,2,4,96,768]{4,3,2,0,1:T(8,128)}, f32[2,2,4,96,768]{4,3,2,0,1:T(8,128)S(1)}, u32[]{:S(2)}, u32[]{:S(2)}) collective-permute-start(f32[2,2,4,96,768]{4,3,2,0,1:T(8,128)} %copy.86), channel_id=1, source_target_pairs={{0,4},{4,0},{8,12},{12,8},{16,20},{20,16},{24,28},{28,24},{1,5},{5... | collective-permute-start | bytes 14155784 | tf_op jit(solution)/shard_map/ppermute | solution.py:38
  316.5 23.2 %collective-permute-start.36 = (f32[2,2,4,96,768]{4,3,2,1,0:T(8,128)}, f32[2,2,4,96,768]{4,3,2,1,0:T(8,128)S(1)}, u32[]{:S(2)}, u32[]{:S(2)}) collective-permute-start(f32[2,2,4,96,768]{4,3,2,1,0:T(8,128)} %bitcast.425), channel_id=1, source_target_pairs={{0,4},{4,0},{8,12},{12,8},{16,20},{20,16},{24,28},{28,24},{1,5},{5... | collective-permute-start | bytes 14155784 | tf_op jit(solution)/shard_map/ppermute | solution.py:38
  361.9 54.0 %collective-permute-start.39 = (f32[2,4,96,768]{3,2,1,0:T(8,128)}, f32[2,4,96,768]{3,2,1,0:T(8,128)}, u32[]{:S(2)}, u32[]{:S(2)}) collective-permute-start(f32[2,4,96,768]{3,2,1,0:T(8,128)} %slice_bitcast_fusion.2), channel_id=1, source_target_pairs={{0,8},{4,12},{8,0},{12,4},{16,24},{20,28},{24,16},{28,20},{1,9},{5... | collective-permute-start | bytes 7077896 | tf_op jit(solution)/shard_map/ppermute | solution.py:38
  362.7 57.9 %collective-permute-start.38 = (f32[2,4,96,768]{3,2,1,0:T(8,128)}, f32[2,4,96,768]{3,2,1,0:T(8,128)}, u32[]{:S(2)}, u32[]{:S(2)}) collective-permute-start(f32[2,4,96,768]{3,2,1,0:T(8,128)} %slice_bitcast_fusion.3), channel_id=1, source_target_pairs={{0,16},{4,20},{8,24},{12,28},{16,0},{20,4},{24,8},{28,12},{1,17},{... | collective-permute-start | bytes 7077896 | tf_op jit(solution)/shard_map/ppermute | solution.py:38
  363.6 177.7 %reduce-scatter.2.cloned.1.call-start = ((), (), s32[]{:S(2)}) async-start(), calls=%async_computation.3 | async-start | bytes 2949120 | tf_op jit(solution)/shard_map/reduce_scatter | solution.py:863
  423.8 27.6 %collective-permute-start.40 = (f32[4,96,768]{2,1,0:T(8,128)}, f32[4,96,768]{2,1,0:T(8,128)}, u32[]{:S(2)}, u32[]{:S(2)}) collective-permute-start(f32[4,96,768]{2,1,0:T(8,128)} %slice_bitcast_fusion.9), channel_id=1, source_target_pairs={{0,8},{4,12},{8,0},{12,4},{16,24},{20,28},{24,16},{28,20},{1,9},{5... | collective-permute-start | bytes 3538952 | tf_op jit(solution)/shard_map/ppermute | solution.py:38
  424.9 28.2 %collective-permute-start.41 = (f32[4,96,768]{2,1,0:T(8,128)}, f32[4,96,768]{2,1,0:T(8,128)}, u32[]{:S(2)}, u32[]{:S(2)}) collective-permute-start(f32[4,96,768]{2,1,0:T(8,128)} %slice_bitcast_fusion.8), channel_id=1, source_target_pairs={{0,16},{4,20},{8,24},{12,28},{16,0},{20,4},{24,8},{28,12},{1,17},{... | collective-permute-start | bytes 3538952 | tf_op jit(solution)/shard_map/ppermute | solution.py:38
  456.1 15.5 %collective-permute-start.42 = (f32[2,2,4,48,768]{4,3,2,1,0:T(8,128)}, f32[2,2,4,48,768]{4,3,2,1,0:T(8,128)S(1)}, u32[]{:S(2)}, u32[]{:S(2)}) collective-permute-start(f32[2,2,4,48,768]{4,3,2,1,0:T(8,128)} %pad_maximum_fusion.4), channel_id=1, source_target_pairs={{0,4},{4,0},{8,12},{12,8},{16,20},{20,16},{24,28},{28,24},{1,5},{5... | collective-permute-start | bytes 7077896 | tf_op jit(solution)/shard_map/ppermute | solution.py:38
  473.3 6.7 collective-permute-start.43
  476.9 16.2 %collective-permute-start.45 = (f32[2,4,48,384]{3,2,1,0:T(8,128)S(1)}, f32[2,4,48,384]{3,2,1,0:T(8,128)S(1)}, u32[]{:S(2)}, u32[]{:S(2)}) collective-permute-start(f32[2,4,48,384]{3,2,1,0:T(8,128)S(1)} %get-tuple-element.162), channel_id=1, source_target_pairs={{0,16},{4,20},{8,24},{12,28},{16,0},{20,4},{24,8},{28,12},{1,17},{... | collective-permute-start | bytes 1769480 | tf_op jit(solution)/shard_map/ppermute | solution.py:38
  477.9 17.2 %collective-permute-start.47 = (f32[2,4,48,384]{3,2,1,0:T(8,128)}, f32[2,4,48,384]{3,2,1,0:T(8,128)S(1)}, u32[]{:S(2)}, u32[]{:S(2)}) collective-permute-start(f32[2,4,48,384]{3,2,1,0:T(8,128)} %get-tuple-element.164), channel_id=1, source_target_pairs={{0,8},{4,12},{8,0},{12,4},{16,24},{20,28},{24,16},{28,20},{1,9},{5... | collective-permute-start | bytes 1769480 | tf_op jit(solution)/shard_map/ppermute | solution.py:38
  486.3 35.1 %collective-permute-start.49 = (f32[2,4,72,384]{3,2,1,0:T(8,128)}, f32[2,4,72,384]{3,2,1,0:T(8,128)}, u32[]{:S(2)}, u32[]{:S(2)}) collective-permute-start(f32[2,4,72,384]{3,2,1,0:T(8,128)} %dynamic-slice_bitcast_fusion.5), channel_id=1, source_target_pairs={{0,8},{4,12},{8,0},{12,4},{16,24},{20,28},{24,16},{28,20},{1,9},{5... | collective-permute-start | bytes 2654216 | tf_op jit(solution)/shard_map/ppermute | solution.py:38
  487.2 36.3 %collective-permute-start.44 = (f32[2,4,72,384]{3,2,1,0:T(8,128)}, f32[2,4,72,384]{3,2,1,0:T(8,128)}, u32[]{:S(2)}, u32[]{:S(2)}) collective-permute-start(f32[2,4,72,384]{3,2,1,0:T(8,128)} %dynamic-slice_bitcast_fusion.6), channel_id=1, source_target_pairs={{0,16},{4,20},{8,24},{12,28},{16,0},{20,4},{24,8},{28,12},{1,17},{... | collective-permute-start | bytes 2654216 | tf_op jit(solution)/shard_map/ppermute | solution.py:38
  494.2 24.2 %collective-permute-start.46 = (f32[4,48,384]{2,1,0:T(8,128)}, f32[4,48,384]{2,1,0:T(8,128)}, u32[]{:S(2)}, u32[]{:S(2)}) collective-permute-start(f32[4,48,384]{2,1,0:T(8,128)} %dynamic-slice_bitcast_fusion.19), channel_id=1, source_target_pairs={{0,8},{4,12},{8,0},{12,4},{16,24},{20,28},{24,16},{28,20},{1,9},{5... | collective-permute-start | bytes 884744 | tf_op jit(solution)/shard_map/ppermute | solution.py:38
  496.8 22.7 %collective-permute-start.48 = (f32[4,48,384]{2,1,0:T(8,128)}, f32[4,48,384]{2,1,0:T(8,128)}, u32[]{:S(2)}, u32[]{:S(2)}) collective-permute-start(f32[4,48,384]{2,1,0:T(8,128)} %dynamic-slice_bitcast_fusion.18), channel_id=1, source_target_pairs={{0,16},{4,20},{8,24},{12,28},{16,0},{20,4},{24,8},{28,12},{1,17},{... | collective-permute-start | bytes 884744 | tf_op jit(solution)/shard_map/ppermute | solution.py:38
  525.7 11.2 %collective-permute-start.50 = (f32[4,72,384]{2,1,0:T(8,128)}, f32[4,72,384]{2,1,0:T(8,128)}, u32[]{:S(2)}, u32[]{:S(2)}) collective-permute-start(f32[4,72,384]{2,1,0:T(8,128)} %dynamic-slice_bitcast_fusion.14), channel_id=1, source_target_pairs={{0,8},{4,12},{8,0},{12,4},{16,24},{20,28},{24,16},{28,20},{1,9},{5... | collective-permute-start | bytes 1327112 | tf_op jit(solution)/shard_map/ppermute | solution.py:38
  526.9 11.3 %collective-permute-start.51 = (f32[4,72,384]{2,1,0:T(8,128)}, f32[4,72,384]{2,1,0:T(8,128)}, u32[]{:S(2)}, u32[]{:S(2)}) collective-permute-start(f32[4,72,384]{2,1,0:T(8,128)} %dynamic-slice_bitcast_fusion.13), channel_id=1, source_target_pairs={{0,16},{4,20},{8,24},{12,28},{16,0},{20,4},{24,8},{28,12},{1,17},{... | collective-permute-start | bytes 1327112 | tf_op jit(solution)/shard_map/ppermute | solution.py:38
  541.4 16.5 %collective-permute-start.53 = (f32[2,120,768]{2,1,0:T(8,128)}, f32[2,120,768]{2,1,0:T(8,128)S(1)}, u32[]{:S(2)}, u32[]{:S(2)}) collective-permute-start(f32[2,120,768]{2,1,0:T(8,128)} %dynamic-slice_bitcast_fusion.7), channel_id=1, source_target_pairs={{0,1},{1,0},{2,3},{3,2},{4,5},{5,4},{6,7},{7,6},{8,9},{9,8},{10,11... | collective-permute-start | bytes 2211848 | tf_op jit(solution)/shard_map/ppermute | solution.py:38
  559.2 21.4 %collective-permute-start.57 = (f32[1,120,768]{2,1,0:T(8,128)S(1)}, f32[1,120,768]{2,1,0:T(8,128)S(1)}, u32[]{:S(2)}, u32[]{:S(2)}) collective-permute-start(f32[1,120,768]{2,1,0:T(8,128)S(1)} %constant_dynamic-slice_fusion.1), channel_id=1, source_target_pairs={{0,2},{1,3},{2,0},{3,1},{4,6},{5,7},{6,4},{7,5},{8,10},{9,11},{10,... | collective-permute-start | bytes 1105928 | tf_op jit(solution)/shard_map/ppermute | solution.py:38
  560.6 7.1 collective-permute-start.58
  562.4 18.1 %collective-permute-start.59 = (f32[24,768]{1,0:T(8,128)S(1)}, f32[24,768]{1,0:T(8,128)S(1)}, u32[]{:S(2)}, u32[]{:S(2)}) collective-permute-start(f32[24,768]{1,0:T(8,128)S(1)} %add_add_fusion.3), channel_id=1, source_target_pairs={{0,2},{1,3},{2,0},{3,1},{4,6},{5,7},{6,4},{7,5},{8,10},{9,11},{10,... | collective-permute-start | bytes 221192 | tf_op jit(solution)/shard_map/ppermute | solution.py:38
  564.0 16.5 %collective-permute-start.60 = (f32[24,768]{1,0:T(8,128)S(1)}, f32[24,768]{1,0:T(8,128)S(1)}, u32[]{:S(2)}, u32[]{:S(2)}) collective-permute-start(f32[24,768]{1,0:T(8,128)S(1)} %add_add_fusion.3), channel_id=1, source_target_pairs={{0,3},{1,2},{2,1},{3,0},{4,7},{5,6},{6,5},{7,4},{8,11},{9,10},{10,... | collective-permute-start | bytes 221192 | tf_op jit(solution)/shard_map/ppermute | solution.py:38
  603.9 10.0 %collective-permute-start.68 = (f32[96,768]{1,0:T(8,128)S(1)}, f32[96,768]{1,0:T(8,128)S(1)}, u32[]{:S(2)}, u32[]{:S(2)}) collective-permute-start(f32[96,768]{1,0:T(8,128)S(1)} %get-tuple-element.261), channel_id=1, source_target_pairs={{0,8},{4,12},{8,0},{12,4},{16,24},{20,28},{24,16},{28,20},{1,9},{5... | collective-permute-start | bytes 884744 | tf_op jit(solution)/shard_map/ppermute | solution.py:38
  605.0 13.4 %collective-permute-start.69 = (f32[96,768]{1,0:T(8,128)S(1)}, f32[96,768]{1,0:T(8,128)S(1)}, u32[]{:S(2)}, u32[]{:S(2)}) collective-permute-start(f32[96,768]{1,0:T(8,128)S(1)} %get-tuple-element.260), channel_id=1, source_target_pairs={{0,16},{4,20},{8,24},{12,28},{16,0},{20,4},{24,8},{28,12},{1,17},{... | collective-permute-start | bytes 884744 | tf_op jit(solution)/shard_map/ppermute | solution.py:38
  605.9 12.6 %collective-permute-start.70 = (f32[96,768]{1,0:T(8,128)S(1)}, f32[96,768]{1,0:T(8,128)S(1)}, u32[]{:S(2)}, u32[]{:S(2)}) collective-permute-start(f32[96,768]{1,0:T(8,128)S(1)} %get-tuple-element.259), channel_id=1, source_target_pairs={{0,24},{4,28},{8,16},{12,20},{16,8},{20,12},{24,0},{28,4},{1,25},{... | collective-permute-start | bytes 884744 | tf_op jit(solution)/shard_map/ppermute | solution.py:38
  625.4 9.8 %collective-permute-start.72 = (f32[48,896]{1,0:T(8,128)}, f32[48,896]{1,0:T(8,128)S(1)}, u32[]{:S(2)}, u32[]{:S(2)}) collective-permute-start(f32[48,896]{1,0:T(8,128)} %get-tuple-element.282), channel_id=1, source_target_pairs={{0,1},{1,0},{2,3},{3,2},{4,5},{5,4},{6,7},{7,6},{8,9},{9,8},{10,11... | collective-permute-start | bytes 516104 | tf_op jit(solution)/shard_map/ppermute | solution.py:38
  625.5 15.8 %collective-permute-start.73 = (f32[48,896]{1,0:T(8,128)}, f32[48,896]{1,0:T(8,128)S(1)}, u32[]{:S(2)}, u32[]{:S(2)}) collective-permute-start(f32[48,896]{1,0:T(8,128)} %get-tuple-element.281), channel_id=1, source_target_pairs={{0,2},{1,3},{2,0},{3,1},{4,6},{5,7},{6,4},{7,5},{8,10},{9,11},{10,... | collective-permute-start | bytes 516104 | tf_op jit(solution)/shard_map/ppermute | solution.py:38
  628.5 12.8 %collective-permute-start.74 = (f32[48,896]{1,0:T(8,128)}, f32[48,896]{1,0:T(8,128)}, u32[]{:S(2)}, u32[]{:S(2)}) collective-permute-start(f32[48,896]{1,0:T(8,128)} %get-tuple-element.280), channel_id=1, source_target_pairs={{0,3},{1,2},{2,1},{3,0},{4,7},{5,6},{6,5},{7,4},{8,11},{9,10},{10,... | collective-permute-start | bytes 516104 | tf_op jit(solution)/shard_map/ppermute | solution.py:38
  642.4 7.7 %collective-permute-start.75 = (f32[48,896]{1,0:T(8,128)S(1)}, f32[48,896]{1,0:T(8,128)S(1)}, u32[]{:S(2)}, u32[]{:S(2)}) collective-permute-start(f32[48,896]{1,0:T(8,128)S(1)} %fusion.75), channel_id=1, source_target_pairs={{0,3},{1,2},{2,1},{3,0},{4,7},{5,6},{6,5},{7,4},{8,11},{9,10},{10,... | collective-permute-start | bytes 516104 | tf_op jit(solution)/shard_map/ppermute | solution.py:38
  644.9 15.4 %collective-permute-start.76 = (f32[48,896]{1,0:T(8,128)S(1)}, f32[48,896]{1,0:T(8,128)S(1)}, u32[]{:S(2)}, u32[]{:S(2)}) collective-permute-start(f32[48,896]{1,0:T(8,128)S(1)} %fusion.75), channel_id=1, source_target_pairs={{0,2},{1,3},{2,0},{3,1},{4,6},{5,7},{6,4},{7,5},{8,10},{9,11},{10,... | collective-permute-start | bytes 516104 | tf_op jit(solution)/shard_map/ppermute | solution.py:38
  647.5 12.8 %collective-permute-start.77 = (f32[48,896]{1,0:T(8,128)S(1)}, f32[48,896]{1,0:T(8,128)S(1)}, u32[]{:S(2)}, u32[]{:S(2)}) collective-permute-start(f32[48,896]{1,0:T(8,128)S(1)} %fusion.75), channel_id=1, source_target_pairs={{0,1},{1,0},{2,3},{3,2},{4,5},{5,4},{6,7},{7,6},{8,9},{9,8},{10,11... | collective-permute-start | bytes 516104 | tf_op jit(solution)/shard_map/ppermute | solution.py:38
  660.4 6.4 collective-permute-start.78
  684.3 10.8 %collective-permute-start.79 = (f32[96,768]{1,0:T(8,128)S(1)}, f32[96,768]{1,0:T(8,128)S(1)}, u32[]{:S(2)}, u32[]{:S(2)}) collective-permute-start(f32[96,768]{1,0:T(8,128)S(1)} %get-tuple-element.257), channel_id=1, source_target_pairs={{0,24},{4,28},{8,16},{12,20},{16,8},{20,12},{24,0},{28,4},{1,25},{... | collective-permute-start | bytes 884744 | tf_op jit(solution)/shard_map/ppermute | solution.py:38
  686.0 15.0 %collective-permute-start.80 = (f32[96,768]{1,0:T(8,128)S(1)}, f32[96,768]{1,0:T(8,128)S(1)}, u32[]{:S(2)}, u32[]{:S(2)}) collective-permute-start(f32[96,768]{1,0:T(8,128)S(1)} %get-tuple-element.256), channel_id=1, source_target_pairs={{0,16},{4,20},{8,24},{12,28},{16,0},{20,4},{24,8},{28,12},{1,17},{... | collective-permute-start | bytes 884744 | tf_op jit(solution)/shard_map/ppermute | solution.py:38
  686.7 14.3 %collective-permute-start.81 = (f32[96,768]{1,0:T(8,128)S(1)}, f32[96,768]{1,0:T(8,128)S(1)}, u32[]{:S(2)}, u32[]{:S(2)}) collective-permute-start(f32[96,768]{1,0:T(8,128)S(1)} %get-tuple-element.254), channel_id=1, source_target_pairs={{0,8},{4,12},{8,0},{12,4},{16,24},{20,28},{24,16},{28,20},{1,9},{5... | collective-permute-start | bytes 884744 | tf_op jit(solution)/shard_map/ppermute | solution.py:38
  (137 other events, 1355.1 us)
Sparse Core Ops, SparseCore 0:
  144.5 86.3 all-gather.2
  363.8 100.6 all-gather.4
  474.1 46.2 reduce-scatter.1

commit v7 on v6

--- a/solution.py
+++ b/solution.py
@@ -234,14 +234,15 @@
     return tree_sum(parts)
 
 
-def column_all_sum(value):
+def column_all_sum(value, beside):
     seq_place, count = lax.axis_index("seq"), lax.axis_size("seq")
     core = lax.axis_index("pack") & 1
     split = value.reshape(2, count, -1, value.shape[1])
     mine = pick(split, core) + swap(pick(split, 1 - core), "pack", 1)
     parts = [pick(mine, seq_place)] + [swap(pick(mine, seq_place ^ k), "seq", k) for k in range(1, count)]
-    mine = by_index(relative(tree_sum(parts), "seq"), seq_place)
-    return by_core(mine, swap(mine, "pack", 1), 0).reshape(value.shape)
+    total, *beside = hold(tree_sum(parts), *beside)
+    mine = by_index(relative(total, "seq"), seq_place)
+    return by_core(mine, swap(mine, "pack", 1), 0).reshape(value.shape), beside
 
 
 def fold(matrix):
@@ -552,9 +553,9 @@
     )
 
 
-def as_rows(value, width):
-    flat = value.reshape(1, -1)
-    return jnp.pad(flat, ((0, 7), (0, width - flat.shape[1])))
+def as_rows(width, *values):
+    rows = [jnp.pad(value.reshape(1, -1), ((0, 0), (0, width - value.size))) for value in values]
+    return jnp.pad(jnp.concatenate(rows), ((0, 8 - len(rows)), (0, 0)))
 
 
 def from_rows(cells, shape):
@@ -575,9 +576,10 @@
     return jnp.dot(left, right, precision=NS_PREC, preferred_element_type=F32)
 
 
-def ortho(columns):
+def ortho(columns, beside):
     gram_part = lax.dot_general(columns, columns, (TN, ((), ())), precision=NS_PREC, preferred_element_type=F32)
-    gram_mat, scale = unfold(column_all_sum(fold(gram_part)), columns.shape[1])
+    folded, beside = column_all_sum(fold(gram_part), beside)
+    gram_mat, scale = unfold(folded, columns.shape[1])
     iterate = columns * scale
     eye = jnp.eye(gram_mat.shape[0], dtype=F32)
     for step in range(NS_STEPS):
@@ -590,7 +592,7 @@
         else:
             first_pass = hmul(iterate, gram_mat)
             iterate = COEF_ONE * iterate + COEF_TWO * first_pass + COEF_THREE * hmul(first_pass, gram_mat)
-    return iterate
+    return iterate, beside
 
 
 def to_columns(shards):
@@ -722,8 +724,7 @@
         embed_weight.T,
         qkv_weight.T,
         output_weight.T,
-        as_rows(small_params, width),
-        as_rows(head_bias, width),
+        as_rows(width, small_params, head_bias),
     ]
     spots = [0]
     for piece in bundle:
@@ -742,13 +743,13 @@
     tokens = mm("rw,wi->ri", chosen, window).astype(LOW)
     tokens, up_gather.shard, *first.parts = hold(tokens, up_gather.shard, *first.parts)
     up_gather.send_seq()
-    embed_full, qkv_full, output_full, small_full, bias_full = first.pieces(spots)
+    embed_full, qkv_full, output_full, small_full = first.pieces(spots)
     embed_full, qkv_full, output_full = (
         value.reshape(-1, width) for value in (embed_full, qkv_full, output_full)
     )
     (gain_bias,) = hold(from_rows(small_full, small_params.shape).astype(F32))
-    bias_full = lax.dynamic_slice_in_dim(bias_full, pack_place * seq_count, seq_count, 0)
-    bias_full = bias_full[:, 0, : head_bias.shape[0]].reshape(-1)
+    bias_full = lax.dynamic_slice_in_dim(small_full, pack_place * seq_count, seq_count, 0)
+    bias_full = bias_full[:, 1, : head_bias.shape[0]].reshape(-1)
 
     rows = tokens.shape[0]
     query_id = group.reshape(rows // BLOCK, 1, BLOCK)
@@ -927,22 +928,23 @@
         for moment, share in zip((qkv_moment, output_moment, up_moment, down_moment), muon_shares)
     ]
     columns = to_columns(moments)
-    iterates = ortho(columns.reshape(-1, width)).reshape(columns.shape)
+    count_float = step_count[0].astype(F32)
+    iterates, (new_head, new_head_first, new_head_second) = ortho(
+        columns.reshape(-1, width),
+        adam_update(head_weight, head_first, head_second, head_grad, factor, count_float),
+    )
+    iterates = iterates.reshape(columns.shape)
     iterates = [iterate.T for iterate in from_columns(iterates, [m.shape[0] for m in moments])]
     moments = [moment.T for moment in moments]
     new_qkv = muon_update(qkv_weight, iterates[0])
     new_output = muon_update(output_weight, iterates[1])
     new_up = muon_update(up_weight, iterates[2])
     new_down = muon_update(down_weight, iterates[3])
-    count_float = step_count[0].astype(F32)
     new_embed, new_embed_first, new_embed_second = adam_update(
         embed_weight, embed_first, embed_second, embed_share, factor, count_float
     )
     new_small, new_small_first, new_small_second = adam_update(
         small_params, small_first, small_second, small_share, factor, count_float
-    )
-    new_head, new_head_first, new_head_second = adam_update(
-        head_weight, head_first, head_second, head_grad, factor, count_float
     )
     new_bias, new_bias_first, new_bias_second = adam_update(
         head_bias, bias_first, bias_second, bias_grad, factor, count_float

time: 717 us -> 713 us (level)
  waiting for transfers between devices: 161 us -> 153 us
    ppermute x80, waiting for transfers between devices: 138 us -> 129 us  [swap(): lax.ppermute(value, axis, [(i, i ^ bit) for i in range(lax.axis_size(axis...]
  transfers between devices with their start and end apart: 85 -> 85, of which waited for: 48 -> 42; matrix products, arithmetic and copies ran while one was open for 31% -> 31% of each run, Pallas kernels for 11% -> 11%
where the time goes in v7:
time: 713 us; the launch traced here: 707 us
  matrix products  185 us (26%)
  waiting for transfers between devices  153 us (21%)
  Pallas kernels  104 us (15%)
  other arithmetic  94.9 us (13%)
  starting transfers between devices  92 us (13%)
  local copies, waits for them, and re-layouts  54.7 us (8%)
  between operations  23 us (3%)
    dot_general x25, matrix products, mm(): return jnp.einsum(spec, left, right, preferred_element_type=F32)  165 us
    ppermute x80, waiting for transfers between devices, swap(): lax.ppermute(value, axis, [(i, i ^ bit) for i in range(lax.axis_size(axis...  129 us
    ppermute x80, starting transfers between devices, swap(): lax.ppermute(value, axis, [(i, i ^ bit) for i in range(lax.axis_size(axis...  88.9 us
    pallas_call x1, Pallas kernels, attend_back(): pl.pallas_call(lambda *refs: attend_back_kernel(width, blocks, *refs), gr...  47.2 us
    pallas_call x3, Pallas kernels, norm_back(): pl.pallas_call(lambda *refs: norm_back_kernel(groups, keep_sum, *refs), g...  34.3 us
    pallas_call x1, Pallas kernels, attend(): pl.pallas_call(lambda *refs: attend_kernel(width, blocks, *refs), grid=(b...  21.1 us
    add x14, other arithmetic, step(): self.value = self.keep + swap(sent, 'pack', self.bit)  18 us
    ppermute x1, waiting for transfers between devices, body(): lax.ppermute(patches[:, shard_len - MAXLEN:], 'seq', [(i, i + 1) for i in...  16.8 us
  transfers between devices with their start and end apart: 85, of which 42 were waited for; matrix products, arithmetic and copies ran while one was open for 31% of the time, Pallas kernels for 11%

profile of v7, /device:TPU:0, one launch (start us, length us, event | category | flops | bytes accessed | tf_op | source)
XLA Modules:
  0.0 706.9 jit_solution(16952964668765205640)
XLA Ops:
  10.7 5.1 collective-permute-start
  21.7 10.8 %collective-permute-done.1 = bf16[128,768]{1,0:T(8,128)(2,1)S(1)} collective-permute-done((bf16[128,768]{1,0:T(8,128)(2,1)S(1)}, bf16[128,768]{1,0:T(8,128)(2,1)S(1)}, u32[]{:S(2)}, u32[]{:S(2)}) %collective-permute-start.1) | collective-permute-done | bytes 196640 | tf_op jit(solution)/shard_map/ppermute | solution.py:38
  42.4 16.8 %collective-permute-done.3 = bf16[6,128,768]{2,1,0:T(8,128)(2,1)S(1)} collective-permute-done((bf16[6,128,768]{2,1,0:T(8,128)(2,1)S(1)}, bf16[6,128,768]{2,1,0:T(8,128)(2,1)S(1)}, u32[]{:S(2)}, u32[]{:S(2)}) %collective-permute-start.3) | collective-permute-done | bytes 1179680 | tf_op jit(solution)/shard_map/ppermute | solution.py:738
  59.2 4.2 collective-permute-done.4
  63.9 10.3 %fusion.23 = bf16[1664,768]{1,0:T(8,128)(2,1)} fusion(bf16[3072,768]{1,0:T(8,128)(2,1)S(1)} %bitcast.381, s32[1664]{0:T(1024)S(1)} %get-tuple-element.320), kind=kOutput, calls=%fused_computation.55 | convolution fusion | flops 7858126848 | bytes 7281152 | tf_op jit(solution)/shard_map/rw,wi->ri/dot_general | solution.py:568
  83.9 5.0 collective-permute-start.11
  97.6 4.5 convolution_add_fusion.1.refs_0_
  108.2 2.8 reduce_sum.243
  111.0 3.1 multiply_reduce_fusion.2
  117.1 3.0 collective-permute-start.10
  120.2 9.3 %add_convert_fusion.refs_0_ = bf16[1664,2304]{1,0:T(8,128)(2,1)} fusion(bf16[2304,768]{1,0:T(8,128)(2,1)S(1)} %bitcast.383, f32[2304]{0:T(1024)S(1)} %pad_maximum_fusion.16, f32[1664,768]{1,0:T(8,128)S(1)} %bitcast.361, f32[768]{0:T(1024)S(1)} %get-tuple-element.308, f32[768]{0:T(1024)S(1)} %get-tuple-element.316, f32[1664]{0:T(1024)S(1)} %add_rsqrt_fusion.2, ...), kind=kOutput, calls=%fused_computation.7 | convolution fusion | flops 5902860288 | bytes 16347136 | tf_op jit(solution)/shard_map/rd,ed->re/dot_general | solution.py:568
  136.7 3.0 pad_maximum_fusion.2
  139.8 21.1 %shard_map.435 = (bf16[1664,768]{1,0:T(8,128)(2,1)}, f32[13,6,256]{2,1,0:T(8,128)}) custom-call(bf16[1664,2304]{1,0:T(8,128)(2,1)} %add_convert_fusion.refs_0_, s32[13,1,128]{2,1,0:T(1,128)} %select_n.779.refs_1_.refs_3_, s32[1920,1]{1,0:T(8,128)} %broadcast_in_dim.210.refs_2_.refs_4_), custom_call_target="tpu_custom_call" | custom-call | tf_op jit(solution)/shard_map/pallas_call | solution.py:405
  161.2 5.7 fusion.138
  167.7 2.8 pad_maximum_fusion.3
  172.0 8.8 %multiply_convert_fusion.1 = (bf16[1664,1536]{1,0:T(8,128)(2,1)S(1)}, f32[1664,1536]{1,0:T(8,128)}) fusion(f32[1536]{0:T(1024)S(1)} %add.690, bf16[1664,768]{1,0:T(8,128)(2,1)S(1)} %add_convert_fusion.1, bf16[1536,768]{1,0:T(8,128)(2,1)} %bitcast.38), kind=kOutput, calls=%fused_computation.24 | convolution fusion | flops 3941203968 | bytes 20256768 | tf_op jit(solution)/shard_map/rd,fd->rf/dot_general | solution.py:568
  180.8 4.2 fusion.140
  185.0 8.9 %multiply_convert_fusion = (bf16[1664,1536]{1,0:T(8,128)(2,1)S(1)}, f32[1664,1536]{1,0:T(8,128)}) fusion(f32[1536]{0:T(1024)S(1)} %add.694, bf16[1664,768]{1,0:T(8,128)(2,1)S(1)} %add_convert_fusion.1, bf16[1536,768]{1,0:T(8,128)(2,1)} %bitcast.44), kind=kOutput, calls=%fused_computation.22 | convolution fusion | flops 3941203968 | bytes 20256768 | tf_op jit(solution)/shard_map/rd,fd->rf/dot_general | solution.py:568
  194.0 4.8 fusion.139
  201.2 3.0 fusion.59
  208.7 2.9 collective-permute-done.22
  211.6 3.0 collective-permute-done.24
  223.3 2.9 all-gather.3.cloned.1.call-done
  226.3 5.6 fusion.39
  244.6 3.6 collective-permute-start.35
  252.4 11.4 %shard_map.436 = (bf16[1664,768]{1,0:T(8,128)(2,1)}, f32[8,768]{1,0:T(8,128)}, f32[1664,768]{1,0:T(8,128)}) custom-call(f32[1664,768]{1,0:T(8,128)} %copy-done.4, f32[96,768]{1,0:T(8,128)} %maximum_divide_fusion.refs_1_, s32[1664,1]{1,0:T(8,128)} %select_n.862.refs_2_, f32[1,768]{1,0:T(1,128)} %get-tuple-element.305.refs_3_), custom_call_target="tpu_custom_call" | custom-call | tf_op jit(solution)/shard_map/pallas_call | solution.py:501
  263.9 7.5 %fusion.143 = f32[1536,768]{1,0:T(8,128)S(1)} fusion(bf16[1664,1536]{1,0:T(8,128)(2,1)} %copy-done.99, bf16[1664,768]{1,0:T(8,128)(2,1)} %get-tuple-element.132), kind=kOutput, calls=%fused_computation.403 | convolution fusion | flops 3925868544 | bytes 12386304 | tf_op jit(solution)/shard_map/rf,rd->fd/dot_general | solution.py:568
  271.4 9.4 %fusion.142 = f32[1536,768]{1,0:T(8,128)} fusion(bf16[1664,1536]{1,0:T(8,128)(2,1)} %copy-done.98, bf16[1664,768]{1,0:T(8,128)(2,1)S(1)} %copy-done.95), kind=kOutput, calls=%fused_computation.402 | convolution fusion | flops 3925868544 | bytes 12386304 | tf_op jit(solution)/shard_map/rf,rd->fd/dot_general | solution.py:568
  280.8 9.7 %fusion.6 = bf16[1664,1536]{1,0:T(8,128)(2,1)S(1)} fusion(bf16[1664,768]{1,0:T(8,128)(2,1)S(1)} %copy-done.95, bf16[1536,768]{1,0:T(8,128)(2,1)S(1)} %bitcast.390, f32[1664,1536]{1,0:T(8,128)} %get-tuple-element.333, f32[1536]{0:T(1024)S(1)} %add.690), kind=kOutput, calls=%fused_computation.13 | convolution fusion | flops 3953983488 | bytes 20256768 | tf_op jit(solution)/shard_map/rd,fd->rf/dot_general | solution.py:568
  290.5 4.7 fusion.145
  295.2 9.3 %fusion.12 = bf16[1664,1536]{1,0:T(8,128)(2,1)S(1)} fusion(bf16[1664,768]{1,0:T(8,128)(2,1)S(1)} %copy-done.95, bf16[1536,768]{1,0:T(8,128)(2,1)S(1)} %bitcast.423, f32[1664,1536]{1,0:T(8,128)} %get-tuple-element.335, f32[1536]{0:T(1024)S(1)} %add.694), kind=kOutput, calls=%fused_computation.19 | convolution fusion | flops 3953983488 | bytes 20256768 | tf_op jit(solution)/shard_map/rd,fd->rf/dot_general | solution.py:568
  304.5 4.6 fusion.144
  312.2 7.6 %fusion.146 = f32[1664,768]{1,0:T(8,128)} fusion(bf16[1664,1536]{1,0:T(8,128)(2,1)S(1)} %fusion.6, bf16[1536,768]{1,0:T(8,128)(2,1)} %bitcast.38), kind=kOutput, calls=%fused_computation.406 | convolution fusion | flops 3925868544 | bytes 12582912 | tf_op jit(solution)/shard_map/rf,fd->rd/dot_general | solution.py:568
  319.9 8.3 %convolution_add_fusion.2.refs_1_ = f32[1664,768]{1,0:T(8,128)} fusion(f32[1664,768]{1,0:T(8,128)} %fusion.146, bf16[1664,1536]{1,0:T(8,128)(2,1)S(1)} %fusion.12, bf16[1536,768]{1,0:T(8,128)(2,1)} %bitcast.44), kind=kOutput, calls=%fused_computation.50 | convolution fusion | flops 3927146496 | bytes 17694720 | tf_op jit(solution)/shard_map/rf,fd->rd/dot_general | solution.py:568
  330.3 2.9 copy_add_fusion
  339.8 12.1 %shard_map.437 = (bf16[1664,768]{1,0:T(8,128)(2,1)}, f32[8,768]{1,0:T(8,128)}, f32[1664,768]{1,0:T(8,128)}) custom-call(f32[1664,768]{1,0:T(8,128)} %copy-done.3, f32[1664,768]{1,0:T(8,128)} %convolution_add_fusion.2.refs_1_, f32[1664,768]{1,0:T(8,128)} %get-tuple-element.138.refs_2_, f32[1,768]{1,0:T(1,128)} %get-tuple-element.306.refs_3_), custom_call_target="tpu_custom_call" | custom-call | tf_op jit(solution)/shard_map/pallas_call | solution.py:501
  351.8 5.4 convolution_convert_fusion.refs_1_
  359.0 47.2 %shard_map.438 = bf16[1664,2304]{1,0:T(8,128)(2,1)} custom-call(bf16[1664,2304]{1,0:T(8,128)(2,1)} %add_convert_fusion.refs_0_, bf16[1664,768]{1,0:T(8,128)(2,1)} %convolution_convert_fusion.refs_1_, f32[13,6,256]{2,1,0:T(8,128)} %get-tuple-element.143.refs_2_, s32[13,1,128]{2,1,0:T(1,128)} %select_n.779.refs_1_.refs_3_, ...), custom_call_target="tpu_custom_call" | custom-call | tf_op jit(solution)/shard_map/pallas_call | solution.py:430
  406.1 4.9 fusion.147
  421.6 7.8 %fusion.148.refs_1_ = f32[1664,768]{1,0:T(8,128)} fusion(bf16[1664,2304]{1,0:T(8,128)(2,1)S(1)} %bitcast.363, bf16[2304,768]{1,0:T(8,128)(2,1)S(1)} %bitcast.384), kind=kOutput, calls=%fused_computation.408 | convolution fusion | flops 5888802816 | bytes 16318464 | tf_op jit(solution)/shard_map/re,ed->rd/dot_general | solution.py:568
  429.5 10.8 %shard_map.439 = (bf16[1664,768]{1,0:T(8,128)(2,1)}, f32[8,768]{1,0:T(8,128)}) custom-call(f32[1664,768]{1,0:T(8,128)} %convolution_add_fusion.1.refs_0_, f32[1664,768]{1,0:T(8,128)} %fusion.148.refs_1_, f32[1664,768]{1,0:T(8,128)} %get-tuple-element.147.refs_2_, f32[1,768]{1,0:T(1,128)} %get-tuple-element.304.refs_3_), custom_call_target="tpu_custom_call" | custom-call | tf_op jit(solution)/shard_map/pallas_call | solution.py:501
  440.3 4.9 fusion.149
  452.7 11.6 %fusion.121 = f32[2304,768]{1,0:T(8,128)S(1)} fusion(bf16[1664,2304]{1,0:T(8,128)(2,1)} %shard_map.438, f32[1664,768]{1,0:T(8,128)} %convolution_add_fusion.1.refs_0_, f32[768]{0:T(1024)S(1)} %copy-done.83, f32[768]{0:T(1024)S(1)} %copy-done.85, f32[1664]{0:T(1024)S(1)} %copy-done.78, f32[1664]{0:T(1024)S(1)} %copy-done.66), kind=kOutput, calls=%fused_computation.389 | convolution fusion | flops 5895192576 | bytes 19876864 | tf_op jit(solution)/shard_map/re,rd->ed/dot_general | solution.py:568
  470.4 2.9 convert_reduce_fusion.3
  476.6 3.5 bitcast_add_fusion
  484.4 5.3 collective-permute-done.45
  495.5 3.3 convert_reduce_fusion.2
  498.8 3.5 fusion.21
  502.3 4.4 convert_reduce_fusion
  508.3 6.6 collective-permute-done.46
  525.3 7.9 %collective-permute-done.50 = f32[4,72,384]{2,1,0:T(8,128)} collective-permute-done((f32[4,72,384]{2,1,0:T(8,128)}, f32[4,72,384]{2,1,0:T(8,128)}, u32[]{:S(2)}, u32[]{:S(2)}) %collective-permute-start.50) | collective-permute-done | bytes 442400 | tf_op jit(solution)/shard_map/ppermute | solution.py:38
  546.4 7.9 %collective-permute-done.53 = f32[2,120,768]{2,1,0:T(8,128)} collective-permute-done((f32[2,120,768]{2,1,0:T(8,128)}, f32[2,120,768]{2,1,0:T(8,128)}, u32[]{:S(2)}, u32[]{:S(2)}) %collective-permute-start.53) | collective-permute-done | bytes 737312 | tf_op jit(solution)/shard_map/ppermute | solution.py:38
  564.5 12.8 %collective-permute-done.59 = f32[24,768]{1,0:T(8,128)S(1)} collective-permute-done((f32[24,768]{1,0:T(8,128)S(1)}, f32[24,768]{1,0:T(8,128)S(1)}, u32[]{:S(2)}, u32[]{:S(2)}) %collective-permute-start.59) | collective-permute-done | bytes 73760 | tf_op jit(solution)/shard_map/ppermute | solution.py:38
  607.5 6.5 collective-permute-done.68
  614.0 4.7 collective-permute-done.69
  626.8 3.1 collective-permute-start.73
  631.0 5.6 multiply_subtract_fusion
  636.6 5.9 collective-permute-done.73
  650.2 10.1 %collective-permute-done.76 = f32[48,896]{1,0:T(8,128)S(1)} collective-permute-done((f32[48,896]{1,0:T(8,128)S(1)}, f32[48,896]{1,0:T(8,128)S(1)}, u32[]{:S(2)}, u32[]{:S(2)}) %collective-permute-start.76) | collective-permute-done | bytes 172064 | tf_op jit(solution)/shard_map/ppermute | solution.py:38
  663.3 3.0 fusion.150
  666.4 3.1 fusion.151
  669.5 3.5 fusion.30
  686.0 5.1 collective-permute-done.79
  691.1 5.4 collective-permute-done.80
  (602 shorter events, 234.3 us)
Async XLA Ops:
  7.2 219.1 %all-gather.3.cloned.1.call-start = ((), (), s32[]{:S(2)}) async-start(), calls=%async_computation.1 | async-start | bytes 5406720 | tf_op jit(solution)/shard_map/all_gather | solution.py:773
  10.7 11.0 %collective-permute-start = (bf16[128,768]{1,0:T(8,128)(2,1)S(1)}, bf16[128,768]{1,0:T(8,128)(2,1)S(1)}, u32[]{:S(2)}, u32[]{:S(2)}) collective-permute-start(bf16[128,768]{1,0:T(8,128)(2,1)S(1)} %fusion.76), channel_id=1, source_target_pairs={{0,3},{1,2},{2,1},{3,0},{4,7},{5,6},{6,5},{7,4},{8,11},{9,10},{10,... | collective-permute-start | bytes 589832 | tf_op jit(solution)/shard_map/ppermute | solution.py:38
  15.8 16.7 %collective-permute-start.1 = (bf16[128,768]{1,0:T(8,128)(2,1)S(1)}, bf16[128,768]{1,0:T(8,128)(2,1)S(1)}, u32[]{:S(2)}, u32[]{:S(2)}) collective-permute-start(bf16[128,768]{1,0:T(8,128)(2,1)S(1)} %fusion.76), channel_id=1, source_target_pairs={{0,2},{1,3},{2,0},{3,1},{4,6},{5,7},{6,4},{7,5},{8,10},{9,11},{10,... | collective-permute-start | bytes 589832 | tf_op jit(solution)/shard_map/ppermute | solution.py:38
  15.8 16.7 %collective-permute-start.2 = (bf16[128,768]{1,0:T(8,128)(2,1)S(1)}, bf16[128,768]{1,0:T(8,128)(2,1)S(1)}, u32[]{:S(2)}, u32[]{:S(2)}) collective-permute-start(bf16[128,768]{1,0:T(8,128)(2,1)S(1)} %fusion.76), channel_id=1, source_target_pairs={{0,1},{1,0},{2,3},{3,2},{4,5},{5,4},{6,7},{7,6},{8,9},{9,8},{10,11... | collective-permute-start | bytes 589832 | tf_op jit(solution)/shard_map/ppermute | solution.py:38
  33.1 26.1 %collective-permute-start.3 = (bf16[6,128,768]{2,1,0:T(8,128)(2,1)S(1)}, bf16[6,128,768]{2,1,0:T(8,128)(2,1)S(1)}, u32[]{:S(2)}, u32[]{:S(2)}) collective-permute-start(bf16[6,128,768]{2,1,0:T(8,128)(2,1)S(1)} %get-tuple-element.252), channel_id=1, source_target_pairs={{0,1},{1,2},{2,3},{4,5},{5,6},{6,7},{8,9},{9,10},{10,11},{12,13},{... | collective-permute-start | bytes 3538952 | tf_op jit(solution)/shard_map/ppermute | solution.py:738
  34.8 28.6 %collective-permute-start.4 = (bf16[6,128,768]{2,1,0:T(8,128)(2,1)S(1)}, bf16[6,128,768]{2,1,0:T(8,128)(2,1)S(1)}, u32[]{:S(2)}, u32[]{:S(2)}) collective-permute-start(bf16[6,128,768]{2,1,0:T(8,128)(2,1)S(1)} %get-tuple-element.253), channel_id=1, source_target_pairs={{1,0},{2,1},{3,2},{5,4},{6,5},{7,6},{9,8},{10,9},{11,10},{13,12},{... | collective-permute-start | bytes 3538952 | tf_op jit(solution)/shard_map/ppermute | solution.py:739
  38.9 35.3 %collective-permute-start.5 = (bf16[4,128,768]{2,1,0:T(8,128)(2,1)S(1)}, bf16[4,128,768]{2,1,0:T(8,128)(2,1)S(1)}, u32[]{:S(2)}, u32[]{:S(2)}) collective-permute-start(bf16[4,128,768]{2,1,0:T(8,128)(2,1)S(1)} %pad_maximum_fusion.10), channel_id=1, source_target_pairs={{0,8},{4,12},{8,0},{12,4},{16,24},{20,28},{24,16},{28,20},{1,9},{5... | collective-permute-start | bytes 2359304 | tf_op jit(solution)/shard_map/ppermute | solution.py:38
  40.4 34.9 %collective-permute-start.6 = (bf16[4,128,768]{2,1,0:T(8,128)(2,1)S(1)}, bf16[4,128,768]{2,1,0:T(8,128)(2,1)S(1)}, u32[]{:S(2)}, u32[]{:S(2)}) collective-permute-start(bf16[4,128,768]{2,1,0:T(8,128)(2,1)S(1)} %pad_maximum_fusion.10), channel_id=1, source_target_pairs={{0,16},{4,20},{8,24},{12,28},{16,0},{20,4},{24,8},{28,12},{1,17},{... | collective-permute-start | bytes 2359304 | tf_op jit(solution)/shard_map/ppermute | solution.py:38
  41.9 33.4 %collective-permute-start.7 = (bf16[4,128,768]{2,1,0:T(8,128)(2,1)S(1)}, bf16[4,128,768]{2,1,0:T(8,128)(2,1)S(1)}, u32[]{:S(2)}, u32[]{:S(2)}) collective-permute-start(bf16[4,128,768]{2,1,0:T(8,128)(2,1)S(1)} %pad_maximum_fusion.10), channel_id=1, source_target_pairs={{0,24},{4,28},{8,16},{12,20},{16,8},{20,12},{24,0},{28,4},{1,25},{... | collective-permute-start | bytes 2359304 | tf_op jit(solution)/shard_map/ppermute | solution.py:38
  76.1 15.8 %collective-permute-start.8 = (bf16[4,4,128,768]{3,2,1,0:T(8,128)(2,1)S(1)}, bf16[4,4,128,768]{3,2,1,0:T(8,128)(2,1)}, u32[]{:S(2)}, u32[]{:S(2)}) collective-permute-start(bf16[4,4,128,768]{3,2,1,0:T(8,128)(2,1)S(1)} %pad_maximum_fusion.1), channel_id=1, source_target_pairs={{0,4},{4,0},{8,12},{12,8},{16,20},{20,16},{24,28},{28,24},{1,5},{5... | collective-permute-start | bytes 9437192 | tf_op jit(solution)/shard_map/ppermute | solution.py:38
  83.9 18.2 %collective-permute-start.11 = (bf16[96,768]{1,0:T(8,128)(2,1)}, bf16[96,768]{1,0:T(8,128)(2,1)S(1)}, u32[]{:S(2)}, u32[]{:S(2)}) collective-permute-start(bf16[96,768]{1,0:T(8,128)(2,1)} %convert_bitcast_fusion.1), channel_id=1, source_target_pairs={{0,3},{1,2},{2,1},{3,0},{4,7},{5,6},{6,5},{7,4},{8,11},{9,10},{10,... | collective-permute-start | bytes 442376 | tf_op jit(solution)/shard_map/ppermute | solution.py:38
  88.9 13.2 %collective-permute-start.12 = (bf16[96,768]{1,0:T(8,128)(2,1)}, bf16[96,768]{1,0:T(8,128)(2,1)S(1)}, u32[]{:S(2)}, u32[]{:S(2)}) collective-permute-start(bf16[96,768]{1,0:T(8,128)(2,1)} %convert_bitcast_fusion.1), channel_id=1, source_target_pairs={{0,2},{1,3},{2,0},{3,1},{4,6},{5,7},{6,4},{7,5},{8,10},{9,11},{10,... | collective-permute-start | bytes 442376 | tf_op jit(solution)/shard_map/ppermute | solution.py:38
  88.9 13.2 %collective-permute-start.13 = (bf16[96,768]{1,0:T(8,128)(2,1)}, bf16[96,768]{1,0:T(8,128)(2,1)}, u32[]{:S(2)}, u32[]{:S(2)}) collective-permute-start(bf16[96,768]{1,0:T(8,128)(2,1)} %convert_bitcast_fusion.1), channel_id=1, source_target_pairs={{0,1},{1,0},{2,3},{3,2},{4,5},{5,4},{6,7},{7,6},{8,9},{9,8},{10,11... | collective-permute-start | bytes 442376 | tf_op jit(solution)/shard_map/ppermute | solution.py:38
  103.2 29.1 %collective-permute-start.14 = (bf16[4,96,768]{2,1,0:T(8,128)(2,1)S(1)}, bf16[4,96,768]{2,1,0:T(8,128)(2,1)S(1)}, u32[]{:S(2)}, u32[]{:S(2)}) collective-permute-start(bf16[4,96,768]{2,1,0:T(8,128)(2,1)S(1)} %pad_maximum_fusion.13), channel_id=1, source_target_pairs={{0,8},{4,12},{8,0},{12,4},{16,24},{20,28},{24,16},{28,20},{1,9},{5... | collective-permute-start | bytes 1769480 | tf_op jit(solution)/shard_map/ppermute | solution.py:38
  104.5 27.8 %collective-permute-start.15 = (bf16[4,96,768]{2,1,0:T(8,128)(2,1)S(1)}, bf16[4,96,768]{2,1,0:T(8,128)(2,1)}, u32[]{:S(2)}, u32[]{:S(2)}) collective-permute-start(bf16[4,96,768]{2,1,0:T(8,128)(2,1)S(1)} %pad_maximum_fusion.13), channel_id=1, source_target_pairs={{0,16},{4,20},{8,24},{12,28},{16,0},{20,4},{24,8},{28,12},{1,17},{... | collective-permute-start | bytes 1769480 | tf_op jit(solution)/shard_map/ppermute | solution.py:38
  105.3 27.0 %collective-permute-start.16 = (bf16[4,96,768]{2,1,0:T(8,128)(2,1)S(1)}, bf16[4,96,768]{2,1,0:T(8,128)(2,1)}, u32[]{:S(2)}, u32[]{:S(2)}) collective-permute-start(bf16[4,96,768]{2,1,0:T(8,128)(2,1)S(1)} %pad_maximum_fusion.13), channel_id=1, source_target_pairs={{0,24},{4,28},{8,16},{12,20},{16,8},{20,12},{24,0},{28,4},{1,25},{... | collective-permute-start | bytes 1769480 | tf_op jit(solution)/shard_map/ppermute | solution.py:38
  106.8 10.3 %collective-permute-start.9 = (bf16[1,96,768]{2,1,0:T(8,128)(2,1)S(1)}, bf16[1,96,768]{2,1,0:T(8,128)(2,1)S(1)}, u32[]{:S(2)}, u32[]{:S(2)}) collective-permute-start(bf16[1,96,768]{2,1,0:T(8,128)(2,1)S(1)} %bitcast.400), channel_id=1, source_target_pairs={{0,1},{1,0},{2,3},{3,2},{4,5},{5,4},{6,7},{7,6},{8,9},{9,8},{10,11... | collective-permute-start | bytes 442376 | tf_op jit(solution)/shard_map/ppermute | solution.py:38
  117.1 15.1 %collective-permute-start.10 = (bf16[2,96,768]{2,1,0:T(8,128)(2,1)S(1)}, bf16[2,96,768]{2,1,0:T(8,128)(2,1)S(1)}, u32[]{:S(2)}, u32[]{:S(2)}) collective-permute-start(bf16[2,96,768]{2,1,0:T(8,128)(2,1)S(1)} %maximum_select_fusion.6), channel_id=1, source_target_pairs={{0,2},{1,3},{2,0},{3,1},{4,6},{5,7},{6,4},{7,5},{8,10},{9,11},{10,... | collective-permute-start | bytes 884744 | tf_op jit(solution)/shard_map/ppermute | solution.py:38
  132.4 28.6 %collective-permute-start.17 = (bf16[4,96,768]{2,1,0:T(8,128)(2,1)S(1)}, bf16[4,96,768]{2,1,0:T(8,128)(2,1)}, u32[]{:S(2)}, u32[]{:S(2)}) collective-permute-start(bf16[4,96,768]{2,1,0:T(8,128)(2,1)S(1)} %maximum_select_fusion.4), channel_id=1, source_target_pairs={{0,8},{4,12},{8,0},{12,4},{16,24},{20,28},{24,16},{28,20},{1,9},{5... | collective-permute-start | bytes 1769480 | tf_op jit(solution)/shard_map/ppermute | solution.py:38
  133.7 27.3 %collective-permute-start.18 = (bf16[4,96,768]{2,1,0:T(8,128)(2,1)S(1)}, bf16[4,96,768]{2,1,0:T(8,128)(2,1)}, u32[]{:S(2)}, u32[]{:S(2)}) collective-permute-start(bf16[4,96,768]{2,1,0:T(8,128)(2,1)S(1)} %maximum_select_fusion.4), channel_id=1, source_target_pairs={{0,16},{4,20},{8,24},{12,28},{16,0},{20,4},{24,8},{28,12},{1,17},{... | collective-permute-start | bytes 1769480 | tf_op jit(solution)/shard_map/ppermute | solution.py:38
  134.5 26.7 %collective-permute-start.19 = (bf16[4,96,768]{2,1,0:T(8,128)(2,1)S(1)}, bf16[4,96,768]{2,1,0:T(8,128)(2,1)}, u32[]{:S(2)}, u32[]{:S(2)}) collective-permute-start(bf16[4,96,768]{2,1,0:T(8,128)(2,1)S(1)} %maximum_select_fusion.4), channel_id=1, source_target_pairs={{0,24},{4,28},{8,16},{12,20},{16,8},{20,12},{24,0},{28,4},{1,25},{... | collective-permute-start | bytes 1769480 | tf_op jit(solution)/shard_map/ppermute | solution.py:38
  139.7 45.3 %collective-permute-start.20 = (bf16[4,4,96,768]{3,2,1,0:T(8,128)(2,1)}, bf16[4,4,96,768]{3,2,1,0:T(8,128)(2,1)}, u32[]{:S(2)}, u32[]{:S(2)}) collective-permute-start(bf16[4,4,96,768]{3,2,1,0:T(8,128)(2,1)} %pad_maximum_fusion.2), channel_id=1, source_target_pairs={{0,4},{4,0},{8,12},{12,8},{16,20},{20,16},{24,28},{28,24},{1,5},{5... | collective-permute-start | bytes 7077896 | tf_op jit(solution)/shard_map/ppermute | solution.py:38
  139.7 330.1 %all-gather.5.cloned.1.call-start = ((), (), s32[]{:S(2)}) async-start(), calls=%async_computation.2 | async-start | bytes 6881280 | tf_op jit(solution)/shard_map/all_gather | solution.py:822
  170.5 23.4 %collective-permute-start.21 = (bf16[4,4,96,768]{3,2,1,0:T(8,128)(2,1)S(1)}, bf16[4,4,96,768]{3,2,1,0:T(8,128)(2,1)S(1)}, u32[]{:S(2)}, u32[]{:S(2)}) collective-permute-start(bf16[4,4,96,768]{3,2,1,0:T(8,128)(2,1)S(1)} %pad_maximum_fusion.3), channel_id=1, source_target_pairs={{0,4},{4,0},{8,12},{12,8},{16,20},{20,16},{24,28},{28,24},{1,5},{5... | collective-permute-start | bytes 7077896 | tf_op jit(solution)/shard_map/ppermute | solution.py:38
  204.2 7.4 %collective-permute-start.22 = (bf16[24,768]{1,0:T(8,128)(2,1)S(1)}, bf16[24,768]{1,0:T(8,128)(2,1)S(1)}, u32[]{:S(2)}, u32[]{:S(2)}) collective-permute-start(bf16[24,768]{1,0:T(8,128)(2,1)S(1)} %get-tuple-element.301), channel_id=1, source_target_pairs={{0,1},{1,0},{2,3},{3,2},{4,5},{5,4},{6,7},{7,6},{8,9},{9,8},{10,11... | collective-permute-start | bytes 110600 | tf_op jit(solution)/shard_map/ppermute | solution.py:38
  205.5 6.1 collective-permute-start.23
  208.1 6.5 collective-permute-start.24
  243.7 6.4 collective-permute-start.33
  244.6 7.0 collective-permute-start.34
  244.6 7.0 collective-permute-start.35
  311.7 16.4 %collective-permute-start.37 = (f32[2,2,4,96,768]{4,3,2,0,1:T(8,128)}, f32[2,2,4,96,768]{4,3,2,0,1:T(8,128)S(1)}, u32[]{:S(2)}, u32[]{:S(2)}) collective-permute-start(f32[2,2,4,96,768]{4,3,2,0,1:T(8,128)} %copy.84), channel_id=1, source_target_pairs={{0,4},{4,0},{8,12},{12,8},{16,20},{20,16},{24,28},{28,24},{1,5},{5... | collective-permute-start | bytes 14155784 | tf_op jit(solution)/shard_map/ppermute | solution.py:38
  311.7 23.2 %collective-permute-start.36 = (f32[2,2,4,96,768]{4,3,2,1,0:T(8,128)}, f32[2,2,4,96,768]{4,3,2,1,0:T(8,128)S(1)}, u32[]{:S(2)}, u32[]{:S(2)}) collective-permute-start(f32[2,2,4,96,768]{4,3,2,1,0:T(8,128)} %bitcast.421), channel_id=1, source_target_pairs={{0,4},{4,0},{8,12},{12,8},{16,20},{20,16},{24,28},{28,24},{1,5},{5... | collective-permute-start | bytes 14155784 | tf_op jit(solution)/shard_map/ppermute | solution.py:38
  357.2 55.0 %collective-permute-start.39 = (f32[2,4,96,768]{3,2,1,0:T(8,128)}, f32[2,4,96,768]{3,2,1,0:T(8,128)}, u32[]{:S(2)}, u32[]{:S(2)}) collective-permute-start(f32[2,4,96,768]{3,2,1,0:T(8,128)} %slice_bitcast_fusion.2), channel_id=1, source_target_pairs={{0,8},{4,12},{8,0},{12,4},{16,24},{20,28},{24,16},{28,20},{1,9},{5... | collective-permute-start | bytes 7077896 | tf_op jit(solution)/shard_map/ppermute | solution.py:38
  358.1 57.7 %collective-permute-start.38 = (f32[2,4,96,768]{3,2,1,0:T(8,128)}, f32[2,4,96,768]{3,2,1,0:T(8,128)}, u32[]{:S(2)}, u32[]{:S(2)}) collective-permute-start(f32[2,4,96,768]{3,2,1,0:T(8,128)} %slice_bitcast_fusion.3), channel_id=1, source_target_pairs={{0,16},{4,20},{8,24},{12,28},{16,0},{20,4},{24,8},{28,12},{1,17},{... | collective-permute-start | bytes 7077896 | tf_op jit(solution)/shard_map/ppermute | solution.py:38
  358.9 178.7 %reduce-scatter.2.cloned.1.call-start = ((), (), s32[]{:S(2)}) async-start(), calls=%async_computation.3 | async-start | bytes 2949120 | tf_op jit(solution)/shard_map/reduce_scatter | solution.py:864
  419.1 29.0 %collective-permute-start.40 = (f32[4,96,768]{2,1,0:T(8,128)}, f32[4,96,768]{2,1,0:T(8,128)}, u32[]{:S(2)}, u32[]{:S(2)}) collective-permute-start(f32[4,96,768]{2,1,0:T(8,128)} %slice_bitcast_fusion.9), channel_id=1, source_target_pairs={{0,8},{4,12},{8,0},{12,4},{16,24},{20,28},{24,16},{28,20},{1,9},{5... | collective-permute-start | bytes 3538952 | tf_op jit(solution)/shard_map/ppermute | solution.py:38
  420.3 29.2 %collective-permute-start.41 = (f32[4,96,768]{2,1,0:T(8,128)}, f32[4,96,768]{2,1,0:T(8,128)}, u32[]{:S(2)}, u32[]{:S(2)}) collective-permute-start(f32[4,96,768]{2,1,0:T(8,128)} %slice_bitcast_fusion.8), channel_id=1, source_target_pairs={{0,16},{4,20},{8,24},{12,28},{16,0},{20,4},{24,8},{28,12},{1,17},{... | collective-permute-start | bytes 3538952 | tf_op jit(solution)/shard_map/ppermute | solution.py:38
  452.6 15.5 %collective-permute-start.42 = (f32[2,2,4,48,768]{4,3,2,1,0:T(8,128)}, f32[2,2,4,48,768]{4,3,2,1,0:T(8,128)S(1)}, u32[]{:S(2)}, u32[]{:S(2)}) collective-permute-start(f32[2,2,4,48,768]{4,3,2,1,0:T(8,128)} %pad_maximum_fusion.4), channel_id=1, source_target_pairs={{0,4},{4,0},{8,12},{12,8},{16,20},{20,16},{24,28},{28,24},{1,5},{5... | collective-permute-start | bytes 7077896 | tf_op jit(solution)/shard_map/ppermute | solution.py:38
  469.8 6.8 collective-permute-start.43
  473.4 16.2 %collective-permute-start.45 = (f32[2,4,48,384]{3,2,1,0:T(8,128)S(1)}, f32[2,4,48,384]{3,2,1,0:T(8,128)S(1)}, u32[]{:S(2)}, u32[]{:S(2)}) collective-permute-start(f32[2,4,48,384]{3,2,1,0:T(8,128)S(1)} %get-tuple-element.166), channel_id=1, source_target_pairs={{0,16},{4,20},{8,24},{12,28},{16,0},{20,4},{24,8},{28,12},{1,17},{... | collective-permute-start | bytes 1769480 | tf_op jit(solution)/shard_map/ppermute | solution.py:38
  474.2 17.3 %collective-permute-start.47 = (f32[2,4,48,384]{3,2,1,0:T(8,128)}, f32[2,4,48,384]{3,2,1,0:T(8,128)S(1)}, u32[]{:S(2)}, u32[]{:S(2)}) collective-permute-start(f32[2,4,48,384]{3,2,1,0:T(8,128)} %get-tuple-element.168), channel_id=1, source_target_pairs={{0,8},{4,12},{8,0},{12,4},{16,24},{20,28},{24,16},{28,20},{1,9},{5... | collective-permute-start | bytes 1769480 | tf_op jit(solution)/shard_map/ppermute | solution.py:38
  482.8 35.0 %collective-permute-start.49 = (f32[2,4,72,384]{3,2,1,0:T(8,128)}, f32[2,4,72,384]{3,2,1,0:T(8,128)}, u32[]{:S(2)}, u32[]{:S(2)}) collective-permute-start(f32[2,4,72,384]{3,2,1,0:T(8,128)} %dynamic-slice_bitcast_fusion.5), channel_id=1, source_target_pairs={{0,8},{4,12},{8,0},{12,4},{16,24},{20,28},{24,16},{28,20},{1,9},{5... | collective-permute-start | bytes 2654216 | tf_op jit(solution)/shard_map/ppermute | solution.py:38
  483.6 36.2 %collective-permute-start.44 = (f32[2,4,72,384]{3,2,1,0:T(8,128)}, f32[2,4,72,384]{3,2,1,0:T(8,128)}, u32[]{:S(2)}, u32[]{:S(2)}) collective-permute-start(f32[2,4,72,384]{3,2,1,0:T(8,128)} %dynamic-slice_bitcast_fusion.6), channel_id=1, source_target_pairs={{0,16},{4,20},{8,24},{12,28},{16,0},{20,4},{24,8},{28,12},{1,17},{... | collective-permute-start | bytes 2654216 | tf_op jit(solution)/shard_map/ppermute | solution.py:38
  490.7 24.1 %collective-permute-start.46 = (f32[4,48,384]{2,1,0:T(8,128)}, f32[4,48,384]{2,1,0:T(8,128)}, u32[]{:S(2)}, u32[]{:S(2)}) collective-permute-start(f32[4,48,384]{2,1,0:T(8,128)} %dynamic-slice_bitcast_fusion.19), channel_id=1, source_target_pairs={{0,8},{4,12},{8,0},{12,4},{16,24},{20,28},{24,16},{28,20},{1,9},{5... | collective-permute-start | bytes 884744 | tf_op jit(solution)/shard_map/ppermute | solution.py:38
  493.2 22.6 %collective-permute-start.48 = (f32[4,48,384]{2,1,0:T(8,128)}, f32[4,48,384]{2,1,0:T(8,128)}, u32[]{:S(2)}, u32[]{:S(2)}) collective-permute-start(f32[4,48,384]{2,1,0:T(8,128)} %dynamic-slice_bitcast_fusion.18), channel_id=1, source_target_pairs={{0,16},{4,20},{8,24},{12,28},{16,0},{20,4},{24,8},{28,12},{1,17},{... | collective-permute-start | bytes 884744 | tf_op jit(solution)/shard_map/ppermute | solution.py:38
  521.9 11.2 %collective-permute-start.50 = (f32[4,72,384]{2,1,0:T(8,128)}, f32[4,72,384]{2,1,0:T(8,128)}, u32[]{:S(2)}, u32[]{:S(2)}) collective-permute-start(f32[4,72,384]{2,1,0:T(8,128)} %dynamic-slice_bitcast_fusion.14), channel_id=1, source_target_pairs={{0,8},{4,12},{8,0},{12,4},{16,24},{20,28},{24,16},{28,20},{1,9},{5... | collective-permute-start | bytes 1327112 | tf_op jit(solution)/shard_map/ppermute | solution.py:38
  522.8 11.6 %collective-permute-start.51 = (f32[4,72,384]{2,1,0:T(8,128)}, f32[4,72,384]{2,1,0:T(8,128)}, u32[]{:S(2)}, u32[]{:S(2)}) collective-permute-start(f32[4,72,384]{2,1,0:T(8,128)} %dynamic-slice_bitcast_fusion.13), channel_id=1, source_target_pairs={{0,16},{4,20},{8,24},{12,28},{16,0},{20,4},{24,8},{28,12},{1,17},{... | collective-permute-start | bytes 1327112 | tf_op jit(solution)/shard_map/ppermute | solution.py:38
  537.6 16.6 %collective-permute-start.53 = (f32[2,120,768]{2,1,0:T(8,128)}, f32[2,120,768]{2,1,0:T(8,128)}, u32[]{:S(2)}, u32[]{:S(2)}) collective-permute-start(f32[2,120,768]{2,1,0:T(8,128)} %dynamic-slice_bitcast_fusion.7), channel_id=1, source_target_pairs={{0,1},{1,0},{2,3},{3,2},{4,5},{5,4},{6,7},{7,6},{8,9},{9,8},{10,11... | collective-permute-start | bytes 2211848 | tf_op jit(solution)/shard_map/ppermute | solution.py:38
  555.7 21.6 %collective-permute-start.57 = (f32[1,120,768]{2,1,0:T(8,128)S(1)}, f32[1,120,768]{2,1,0:T(8,128)S(1)}, u32[]{:S(2)}, u32[]{:S(2)}) collective-permute-start(f32[1,120,768]{2,1,0:T(8,128)S(1)} %constant_dynamic-slice_fusion.1), channel_id=1, source_target_pairs={{0,2},{1,3},{2,0},{3,1},{4,6},{5,7},{6,4},{7,5},{8,10},{9,11},{10,... | collective-permute-start | bytes 1105928 | tf_op jit(solution)/shard_map/ppermute | solution.py:38
  557.4 7.1 %collective-permute-start.58 = (f32[24,768]{1,0:T(8,128)S(1)}, f32[24,768]{1,0:T(8,128)S(1)}, u32[]{:S(2)}, u32[]{:S(2)}) collective-permute-start(f32[24,768]{1,0:T(8,128)S(1)} %add_add_fusion.3), channel_id=1, source_target_pairs={{0,1},{1,0},{2,3},{3,2},{4,5},{5,4},{6,7},{7,6},{8,9},{9,8},{10,11... | collective-permute-start | bytes 221192 | tf_op jit(solution)/shard_map/ppermute | solution.py:38
  559.0 18.3 %collective-permute-start.59 = (f32[24,768]{1,0:T(8,128)S(1)}, f32[24,768]{1,0:T(8,128)S(1)}, u32[]{:S(2)}, u32[]{:S(2)}) collective-permute-start(f32[24,768]{1,0:T(8,128)S(1)} %add_add_fusion.3), channel_id=1, source_target_pairs={{0,2},{1,3},{2,0},{3,1},{4,6},{5,7},{6,4},{7,5},{8,10},{9,11},{10,... | collective-permute-start | bytes 221192 | tf_op jit(solution)/shard_map/ppermute | solution.py:38
  560.8 16.6 %collective-permute-start.60 = (f32[24,768]{1,0:T(8,128)S(1)}, f32[24,768]{1,0:T(8,128)S(1)}, u32[]{:S(2)}, u32[]{:S(2)}) collective-permute-start(f32[24,768]{1,0:T(8,128)S(1)} %add_add_fusion.3), channel_id=1, source_target_pairs={{0,3},{1,2},{2,1},{3,0},{4,7},{5,6},{6,5},{7,4},{8,11},{9,10},{10,... | collective-permute-start | bytes 221192 | tf_op jit(solution)/shard_map/ppermute | solution.py:38
  604.0 10.0 %collective-permute-start.68 = (f32[96,768]{1,0:T(8,128)S(1)}, f32[96,768]{1,0:T(8,128)S(1)}, u32[]{:S(2)}, u32[]{:S(2)}) collective-permute-start(f32[96,768]{1,0:T(8,128)S(1)} %get-tuple-element.265), channel_id=1, source_target_pairs={{0,8},{4,12},{8,0},{12,4},{16,24},{20,28},{24,16},{28,20},{1,9},{5... | collective-permute-start | bytes 884744 | tf_op jit(solution)/shard_map/ppermute | solution.py:38
  605.3 13.4 %collective-permute-start.69 = (f32[96,768]{1,0:T(8,128)S(1)}, f32[96,768]{1,0:T(8,128)S(1)}, u32[]{:S(2)}, u32[]{:S(2)}) collective-permute-start(f32[96,768]{1,0:T(8,128)S(1)} %get-tuple-element.264), channel_id=1, source_target_pairs={{0,16},{4,20},{8,24},{12,28},{16,0},{20,4},{24,8},{28,12},{1,17},{... | collective-permute-start | bytes 884744 | tf_op jit(solution)/shard_map/ppermute | solution.py:38
  605.9 12.8 %collective-permute-start.70 = (f32[96,768]{1,0:T(8,128)S(1)}, f32[96,768]{1,0:T(8,128)S(1)}, u32[]{:S(2)}, u32[]{:S(2)}) collective-permute-start(f32[96,768]{1,0:T(8,128)S(1)} %get-tuple-element.263), channel_id=1, source_target_pairs={{0,24},{4,28},{8,16},{12,20},{16,8},{20,12},{24,0},{28,4},{1,25},{... | collective-permute-start | bytes 884744 | tf_op jit(solution)/shard_map/ppermute | solution.py:38
  626.5 10.1 %collective-permute-start.72 = (f32[48,896]{1,0:T(8,128)S(1)}, f32[48,896]{1,0:T(8,128)S(1)}, u32[]{:S(2)}, u32[]{:S(2)}) collective-permute-start(f32[48,896]{1,0:T(8,128)S(1)} %get-tuple-element.285), channel_id=1, source_target_pairs={{0,1},{1,0},{2,3},{3,2},{4,5},{5,4},{6,7},{7,6},{8,9},{9,8},{10,11... | collective-permute-start | bytes 516104 | tf_op jit(solution)/shard_map/ppermute | solution.py:38
  626.8 15.8 %collective-permute-start.73 = (f32[48,896]{1,0:T(8,128)S(1)}, f32[48,896]{1,0:T(8,128)S(1)}, u32[]{:S(2)}, u32[]{:S(2)}) collective-permute-start(f32[48,896]{1,0:T(8,128)S(1)} %get-tuple-element.284), channel_id=1, source_target_pairs={{0,2},{1,3},{2,0},{3,1},{4,6},{5,7},{6,4},{7,5},{8,10},{9,11},{10,... | collective-permute-start | bytes 516104 | tf_op jit(solution)/shard_map/ppermute | solution.py:38
  629.9 12.6 %collective-permute-start.74 = (f32[48,896]{1,0:T(8,128)S(1)}, f32[48,896]{1,0:T(8,128)S(1)}, u32[]{:S(2)}, u32[]{:S(2)}) collective-permute-start(f32[48,896]{1,0:T(8,128)S(1)} %get-tuple-element.283), channel_id=1, source_target_pairs={{0,3},{1,2},{2,1},{3,0},{4,7},{5,6},{6,5},{7,4},{8,11},{9,10},{10,... | collective-permute-start | bytes 516104 | tf_op jit(solution)/shard_map/ppermute | solution.py:38
  642.6 7.6 %collective-permute-start.75 = (f32[48,896]{1,0:T(8,128)S(1)}, f32[48,896]{1,0:T(8,128)S(1)}, u32[]{:S(2)}, u32[]{:S(2)}) collective-permute-start(f32[48,896]{1,0:T(8,128)S(1)} %fusion.77), channel_id=1, source_target_pairs={{0,3},{1,2},{2,1},{3,0},{4,7},{5,6},{6,5},{7,4},{8,11},{9,10},{10,... | collective-permute-start | bytes 516104 | tf_op jit(solution)/shard_map/ppermute | solution.py:38
  645.1 15.2 %collective-permute-start.76 = (f32[48,896]{1,0:T(8,128)S(1)}, f32[48,896]{1,0:T(8,128)S(1)}, u32[]{:S(2)}, u32[]{:S(2)}) collective-permute-start(f32[48,896]{1,0:T(8,128)S(1)} %fusion.77), channel_id=1, source_target_pairs={{0,2},{1,3},{2,0},{3,1},{4,6},{5,7},{6,4},{7,5},{8,10},{9,11},{10,... | collective-permute-start | bytes 516104 | tf_op jit(solution)/shard_map/ppermute | solution.py:38
  647.6 12.8 %collective-permute-start.77 = (f32[48,896]{1,0:T(8,128)S(1)}, f32[48,896]{1,0:T(8,128)S(1)}, u32[]{:S(2)}, u32[]{:S(2)}) collective-permute-start(f32[48,896]{1,0:T(8,128)S(1)} %fusion.77), channel_id=1, source_target_pairs={{0,1},{1,0},{2,3},{3,2},{4,5},{5,4},{6,7},{7,6},{8,9},{9,8},{10,11... | collective-permute-start | bytes 516104 | tf_op jit(solution)/shard_map/ppermute | solution.py:38
  680.2 10.9 %collective-permute-start.79 = (f32[96,768]{1,0:T(8,128)S(1)}, f32[96,768]{1,0:T(8,128)S(1)}, u32[]{:S(2)}, u32[]{:S(2)}) collective-permute-start(f32[96,768]{1,0:T(8,128)S(1)} %get-tuple-element.261), channel_id=1, source_target_pairs={{0,24},{4,28},{8,16},{12,20},{16,8},{20,12},{24,0},{28,4},{1,25},{... | collective-permute-start | bytes 884744 | tf_op jit(solution)/shard_map/ppermute | solution.py:38
  681.5 15.1 %collective-permute-start.80 = (f32[96,768]{1,0:T(8,128)S(1)}, f32[96,768]{1,0:T(8,128)S(1)}, u32[]{:S(2)}, u32[]{:S(2)}) collective-permute-start(f32[96,768]{1,0:T(8,128)S(1)} %get-tuple-element.260), channel_id=1, source_target_pairs={{0,16},{4,20},{8,24},{12,28},{16,0},{20,4},{24,8},{28,12},{1,17},{... | collective-permute-start | bytes 884744 | tf_op jit(solution)/shard_map/ppermute | solution.py:38
  682.2 14.3 %collective-permute-start.81 = (f32[96,768]{1,0:T(8,128)S(1)}, f32[96,768]{1,0:T(8,128)S(1)}, u32[]{:S(2)}, u32[]{:S(2)}) collective-permute-start(f32[96,768]{1,0:T(8,128)S(1)} %get-tuple-element.258), channel_id=1, source_target_pairs={{0,8},{4,12},{8,0},{12,4},{16,24},{20,28},{24,16},{28,20},{1,9},{5... | collective-permute-start | bytes 884744 | tf_op jit(solution)/shard_map/ppermute | solution.py:38
  (132 other events, 1106.7 us)
Sparse Core Ops, SparseCore 0:
  139.8 86.3 all-gather.2
  359.0 100.9 all-gather.4
  470.5 45.6 reduce-scatter.1

commit v8 on v7

--- a/solution.py
+++ b/solution.py
@@ -448,8 +448,8 @@
     )(qkv_rows, grad_rows, log_total, query_id, key_id)
 
 
-def layer_norm(values, gain_row, bias_row):
-    centre = values - jnp.mean(values, axis=-1, keepdims=True)
+def layer_norm(values, gain_row, bias_row, mean=None):
+    centre = values - (jnp.mean(values, axis=-1, keepdims=True) if mean is None else mean)
     spread = jnp.mean(centre * centre, axis=-1, keepdims=True)
     return centre * lax.rsqrt(spread + 1e-06) * gain_row + bias_row
 
@@ -760,11 +760,14 @@
     ).astype(F32)
 
     embedded = mm("ri,di->rd", tokens, embed_full) + gain_bias[6]
-    embedded, up_gather.parts[0], down_gather.shard = hold(embedded, up_gather.parts[0], down_gather.shard)
+    mean_one = jnp.mean(embedded, axis=-1, keepdims=True)
+    embedded, mean_one, up_gather.parts[0], down_gather.shard = hold(
+        embedded, mean_one, up_gather.parts[0], down_gather.shard
+    )
     up_gather.join_seq()
     up_gather.in_plane()
     down_gather.doubling()
-    normed_one = layer_norm(embedded, gain_bias[0], gain_bias[1]).astype(LOW)
+    normed_one = layer_norm(embedded, gain_bias[0], gain_bias[1], mean_one).astype(LOW)
     qkv_bias = jnp.concatenate([gain_bias[7], jnp.zeros_like(gain_bias[7]), gain_bias[8]])
     qkv_rows = (mm("rd,ed->re", normed_one, qkv_full) + qkv_bias).astype(LOW)
     qkv_rows, down_gather.block, head_low, *up_gather.parts = hold(

time: 713 us -> 713 us (level)
  transfers between devices with their start and end apart: 85 -> 85, of which waited for: 42 -> 44; matrix products, arithmetic and copies ran while one was open for 31% -> 31% of each run, Pallas kernels for 11% -> 11%
where the time goes in v8:
time: 713 us; the launch traced here: 707 us
  matrix products  186 us (26%)
  waiting for transfers between devices  155 us (22%)
  Pallas kernels  104 us (15%)
  starting transfers between devices  92.8 us (13%)
  other arithmetic  92.1 us (13%)
  local copies, waits for them, and re-layouts  54.7 us (8%)
  between operations  23 us (3%)
    dot_general x25, matrix products, mm(): return jnp.einsum(spec, left, right, preferred_element_type=F32)  165 us
    ppermute x80, waiting for transfers between devices, swap(): lax.ppermute(value, axis, [(i, i ^ bit) for i in range(lax.axis_size(axis...  131 us
    ppermute x80, starting transfers between devices, swap(): lax.ppermute(value, axis, [(i, i ^ bit) for i in range(lax.axis_size(axis...  89.7 us
    pallas_call x1, Pallas kernels, attend_back(): pl.pallas_call(lambda *refs: attend_back_kernel(width, blocks, *refs), gr...  47.2 us
    pallas_call x3, Pallas kernels, norm_back(): pl.pallas_call(lambda *refs: norm_back_kernel(groups, keep_sum, *refs), g...  34.3 us
    pallas_call x1, Pallas kernels, attend(): pl.pallas_call(lambda *refs: attend_kernel(width, blocks, *refs), grid=(b...  21.2 us
    add x14, other arithmetic, step(): self.value = self.keep + swap(sent, 'pack', self.bit)  18 us
    ppermute x1, waiting for transfers between devices, body(): lax.ppermute(patches[:, shard_len - MAXLEN:], 'seq', [(i, i + 1) for i in...  16.8 us
  transfers between devices with their start and end apart: 85, of which 44 were waited for; matrix products, arithmetic and copies ran while one was open for 31% of the time, Pallas kernels for 11%

profile of v8, /device:TPU:0, one launch (start us, length us, event | category | flops | bytes accessed | tf_op | source)
XLA Modules:
  0.0 706.7 jit_solution(12940520631141421472)
XLA Ops:
  10.7 5.1 collective-permute-start
  21.7 10.8 %collective-permute-done.1 = bf16[128,768]{1,0:T(8,128)(2,1)S(1)} collective-permute-done((bf16[128,768]{1,0:T(8,128)(2,1)S(1)}, bf16[128,768]{1,0:T(8,128)(2,1)S(1)}, u32[]{:S(2)}, u32[]{:S(2)}) %collective-permute-start.1) | collective-permute-done | bytes 196640 | tf_op jit(solution)/shard_map/ppermute | solution.py:38
  42.4 16.8 %collective-permute-done.3 = bf16[6,128,768]{2,1,0:T(8,128)(2,1)S(1)} collective-permute-done((bf16[6,128,768]{2,1,0:T(8,128)(2,1)S(1)}, bf16[6,128,768]{2,1,0:T(8,128)(2,1)S(1)}, u32[]{:S(2)}, u32[]{:S(2)}) %collective-permute-start.3) | collective-permute-done | bytes 1179680 | tf_op jit(solution)/shard_map/ppermute | solution.py:738
  59.2 4.2 collective-permute-done.4
  63.9 10.3 %fusion.23 = bf16[1664,768]{1,0:T(8,128)(2,1)} fusion(bf16[3072,768]{1,0:T(8,128)(2,1)S(1)} %bitcast.381, s32[1664]{0:T(1024)S(1)} %get-tuple-element.322), kind=kOutput, calls=%fused_computation.55 | convolution fusion | flops 7858126848 | bytes 7281152 | tf_op jit(solution)/shard_map/rw,wi->ri/dot_general | solution.py:568
  76.2 2.7 convert_element_type.175
  83.9 5.0 collective-permute-start.11
  97.6 4.5 fusion.138
  108.3 3.1 multiply_reduce_fusion.2
  114.4 3.0 collective-permute-start.10
  117.4 9.3 %add_convert_fusion.refs_0_ = bf16[1664,2304]{1,0:T(8,128)(2,1)} fusion(bf16[2304,768]{1,0:T(8,128)(2,1)S(1)} %bitcast.383, f32[2304]{0:T(1024)S(1)} %pad_maximum_fusion.16, f32[1664,768]{1,0:T(8,128)S(1)} %bitcast.363, f32[768]{0:T(1024)S(1)} %get-tuple-element.310, f32[768]{0:T(1024)S(1)} %get-tuple-element.318, f32[1664]{0:T(1024)S(1)} %add_rsqrt_fusion.2, ...), kind=kOutput, calls=%fused_computation.7 | convolution fusion | flops 5902860288 | bytes 16347136 | tf_op jit(solution)/shard_map/rd,ed->re/dot_general | solution.py:568
  136.4 3.0 pad_maximum_fusion.2
  139.5 21.2 %shard_map.435 = (bf16[1664,768]{1,0:T(8,128)(2,1)}, f32[13,6,256]{2,1,0:T(8,128)}) custom-call(bf16[1664,2304]{1,0:T(8,128)(2,1)} %add_convert_fusion.refs_0_, s32[13,1,128]{2,1,0:T(1,128)} %select_n.779.refs_1_.refs_3_, s32[1920,1]{1,0:T(8,128)} %broadcast_in_dim.210.refs_2_.refs_4_), custom_call_target="tpu_custom_call" | custom-call | tf_op jit(solution)/shard_map/pallas_call | solution.py:405
  160.7 5.7 fusion.139
  167.2 2.8 pad_maximum_fusion.3
  171.7 8.8 %multiply_convert_fusion.1 = (bf16[1664,1536]{1,0:T(8,128)(2,1)S(1)}, f32[1664,1536]{1,0:T(8,128)}) fusion(f32[1536]{0:T(1024)S(1)} %add.690, bf16[1664,768]{1,0:T(8,128)(2,1)S(1)} %add_convert_fusion.1, bf16[1536,768]{1,0:T(8,128)(2,1)} %bitcast.38), kind=kOutput, calls=%fused_computation.24 | convolution fusion | flops 3941203968 | bytes 20256768 | tf_op jit(solution)/shard_map/rd,fd->rf/dot_general | solution.py:568
  180.6 4.2 fusion.141
  184.8 9.1 %multiply_convert_fusion = (bf16[1664,1536]{1,0:T(8,128)(2,1)S(1)}, f32[1664,1536]{1,0:T(8,128)}) fusion(f32[1536]{0:T(1024)S(1)} %add.694, bf16[1664,768]{1,0:T(8,128)(2,1)S(1)} %add_convert_fusion.1, bf16[1536,768]{1,0:T(8,128)(2,1)} %bitcast.44), kind=kOutput, calls=%fused_computation.22 | convolution fusion | flops 3941203968 | bytes 20256768 | tf_op jit(solution)/shard_map/rd,fd->rf/dot_general | solution.py:568
  194.0 4.8 fusion.140
  201.1 3.0 fusion.59
  205.7 2.6 collective-permute-start.23
  223.5 2.7 all-gather.3.cloned.1.call-done
  226.2 5.6 fusion.39
  244.6 3.6 collective-permute-start.35
  252.4 11.4 %shard_map.436 = (bf16[1664,768]{1,0:T(8,128)(2,1)}, f32[8,768]{1,0:T(8,128)}, f32[1664,768]{1,0:T(8,128)}) custom-call(f32[1664,768]{1,0:T(8,128)} %copy-done.4, f32[96,768]{1,0:T(8,128)} %maximum_divide_fusion.refs_1_, s32[1664,1]{1,0:T(8,128)} %select_n.862.refs_2_, f32[1,768]{1,0:T(1,128)} %get-tuple-element.307.refs_3_), custom_call_target="tpu_custom_call" | custom-call | tf_op jit(solution)/shard_map/pallas_call | solution.py:501
  263.8 7.5 %fusion.144 = f32[1536,768]{1,0:T(8,128)S(1)} fusion(bf16[1664,1536]{1,0:T(8,128)(2,1)} %copy-done.99, bf16[1664,768]{1,0:T(8,128)(2,1)} %get-tuple-element.134), kind=kOutput, calls=%fused_computation.404 | convolution fusion | flops 3925868544 | bytes 12386304 | tf_op jit(solution)/shard_map/rf,rd->fd/dot_general | solution.py:568
  271.3 9.4 %fusion.143 = f32[1536,768]{1,0:T(8,128)} fusion(bf16[1664,1536]{1,0:T(8,128)(2,1)} %copy-done.98, bf16[1664,768]{1,0:T(8,128)(2,1)S(1)} %copy-done.95), kind=kOutput, calls=%fused_computation.403 | convolution fusion | flops 3925868544 | bytes 12386304 | tf_op jit(solution)/shard_map/rf,rd->fd/dot_general | solution.py:568
  280.7 9.7 %fusion.6 = bf16[1664,1536]{1,0:T(8,128)(2,1)S(1)} fusion(bf16[1664,768]{1,0:T(8,128)(2,1)S(1)} %copy-done.95, bf16[1536,768]{1,0:T(8,128)(2,1)S(1)} %bitcast.390, f32[1664,1536]{1,0:T(8,128)} %get-tuple-element.337, f32[1536]{0:T(1024)S(1)} %add.690), kind=kOutput, calls=%fused_computation.13 | convolution fusion | flops 3953983488 | bytes 20256768 | tf_op jit(solution)/shard_map/rd,fd->rf/dot_general | solution.py:568
  290.4 4.7 fusion.146
  295.2 9.3 %fusion.12 = bf16[1664,1536]{1,0:T(8,128)(2,1)S(1)} fusion(bf16[1664,768]{1,0:T(8,128)(2,1)S(1)} %copy-done.95, bf16[1536,768]{1,0:T(8,128)(2,1)S(1)} %bitcast.423, f32[1664,1536]{1,0:T(8,128)} %get-tuple-element.339, f32[1536]{0:T(1024)S(1)} %add.694), kind=kOutput, calls=%fused_computation.19 | convolution fusion | flops 3953983488 | bytes 20256768 | tf_op jit(solution)/shard_map/rd,fd->rf/dot_general | solution.py:568
  304.5 4.6 fusion.145
  312.2 7.6 %fusion.147 = f32[1664,768]{1,0:T(8,128)} fusion(bf16[1664,1536]{1,0:T(8,128)(2,1)S(1)} %fusion.6, bf16[1536,768]{1,0:T(8,128)(2,1)} %bitcast.38), kind=kOutput, calls=%fused_computation.407 | convolution fusion | flops 3925868544 | bytes 12582912 | tf_op jit(solution)/shard_map/rf,fd->rd/dot_general | solution.py:568
  319.8 8.3 %convolution_add_fusion.2.refs_1_ = f32[1664,768]{1,0:T(8,128)} fusion(f32[1664,768]{1,0:T(8,128)} %fusion.147, bf16[1664,1536]{1,0:T(8,128)(2,1)S(1)} %fusion.12, bf16[1536,768]{1,0:T(8,128)(2,1)} %bitcast.44), kind=kOutput, calls=%fused_computation.50 | convolution fusion | flops 3927146496 | bytes 17694720 | tf_op jit(solution)/shard_map/rf,fd->rd/dot_general | solution.py:568
  330.2 2.9 copy_add_fusion
  339.7 12.1 %shard_map.437 = (bf16[1664,768]{1,0:T(8,128)(2,1)}, f32[8,768]{1,0:T(8,128)}, f32[1664,768]{1,0:T(8,128)}) custom-call(f32[1664,768]{1,0:T(8,128)} %copy-done.3, f32[1664,768]{1,0:T(8,128)} %convolution_add_fusion.2.refs_1_, f32[1664,768]{1,0:T(8,128)} %get-tuple-element.140.refs_2_, f32[1,768]{1,0:T(1,128)} %get-tuple-element.308.refs_3_), custom_call_target="tpu_custom_call" | custom-call | tf_op jit(solution)/shard_map/pallas_call | solution.py:501
  351.8 5.4 convolution_convert_fusion.refs_1_
  358.9 47.2 %shard_map.438 = bf16[1664,2304]{1,0:T(8,128)(2,1)} custom-call(bf16[1664,2304]{1,0:T(8,128)(2,1)} %add_convert_fusion.refs_0_, bf16[1664,768]{1,0:T(8,128)(2,1)} %convolution_convert_fusion.refs_1_, f32[13,6,256]{2,1,0:T(8,128)} %get-tuple-element.145.refs_2_, s32[13,1,128]{2,1,0:T(1,128)} %select_n.779.refs_1_.refs_3_, ...), custom_call_target="tpu_custom_call" | custom-call | tf_op jit(solution)/shard_map/pallas_call | solution.py:430
  406.0 4.9 fusion.148
  421.5 7.8 %fusion.149.refs_1_ = f32[1664,768]{1,0:T(8,128)} fusion(bf16[1664,2304]{1,0:T(8,128)(2,1)S(1)} %bitcast.361, bf16[2304,768]{1,0:T(8,128)(2,1)S(1)} %bitcast.384), kind=kOutput, calls=%fused_computation.409 | convolution fusion | flops 5888802816 | bytes 16318464 | tf_op jit(solution)/shard_map/re,ed->rd/dot_general | solution.py:568
  429.3 10.8 %shard_map.439 = (bf16[1664,768]{1,0:T(8,128)(2,1)}, f32[8,768]{1,0:T(8,128)}) custom-call(f32[1664,768]{1,0:T(8,128)} %get-tuple-element.115.refs_0_, f32[1664,768]{1,0:T(8,128)} %fusion.149.refs_1_, f32[1664,768]{1,0:T(8,128)} %get-tuple-element.149.refs_2_, f32[1,768]{1,0:T(1,128)} %get-tuple-element.306.refs_3_), custom_call_target="tpu_custom_call" | custom-call | tf_op jit(solution)/shard_map/pallas_call | solution.py:501
  440.1 4.9 fusion.150
  452.5 11.5 %fusion.121 = f32[2304,768]{1,0:T(8,128)S(1)} fusion(bf16[1664,2304]{1,0:T(8,128)(2,1)} %shard_map.438, f32[1664,768]{1,0:T(8,128)} %get-tuple-element.115.refs_0_, f32[768]{0:T(1024)S(1)} %copy-done.83, f32[768]{0:T(1024)S(1)} %copy-done.85, f32[1664]{0:T(1024)S(1)} %copy-done.78, f32[1664]{0:T(1024)S(1)} %copy-done.66), kind=kOutput, calls=%fused_computation.389 | convolution fusion | flops 5895192576 | bytes 19876864 | tf_op jit(solution)/shard_map/re,rd->ed/dot_general | solution.py:568
  470.2 2.9 convert_reduce_fusion.3
  476.4 3.5 bitcast_add_fusion
  484.2 5.2 collective-permute-done.45
  495.3 3.3 convert_reduce_fusion.2
  498.6 3.5 fusion.21
  502.2 4.4 convert_reduce_fusion
  508.1 6.4 collective-permute-done.46
  525.2 7.8 %collective-permute-done.50 = f32[4,72,384]{2,1,0:T(8,128)} collective-permute-done((f32[4,72,384]{2,1,0:T(8,128)}, f32[4,72,384]{2,1,0:T(8,128)}, u32[]{:S(2)}, u32[]{:S(2)}) %collective-permute-start.50) | collective-permute-done | bytes 442400 | tf_op jit(solution)/shard_map/ppermute | solution.py:38
  546.3 7.7 %collective-permute-done.53 = f32[2,120,768]{2,1,0:T(8,128)} collective-permute-done((f32[2,120,768]{2,1,0:T(8,128)}, f32[2,120,768]{2,1,0:T(8,128)}, u32[]{:S(2)}, u32[]{:S(2)}) %collective-permute-start.53) | collective-permute-done | bytes 737312 | tf_op jit(solution)/shard_map/ppermute | solution.py:38
  564.5 12.7 %collective-permute-done.59 = f32[24,768]{1,0:T(8,128)S(1)} collective-permute-done((f32[24,768]{1,0:T(8,128)S(1)}, f32[24,768]{1,0:T(8,128)S(1)}, u32[]{:S(2)}, u32[]{:S(2)}) %collective-permute-start.59) | collective-permute-done | bytes 73760 | tf_op jit(solution)/shard_map/ppermute | solution.py:38
  582.4 2.7 collective-permute-start.63
  607.4 6.5 collective-permute-done.68
  613.8 4.7 collective-permute-done.69
  626.6 3.2 collective-permute-start.73
  630.8 5.6 multiply_subtract_fusion
  636.4 6.0 collective-permute-done.73
  650.1 10.2 %collective-permute-done.76 = f32[48,896]{1,0:T(8,128)S(1)} collective-permute-done((f32[48,896]{1,0:T(8,128)S(1)}, f32[48,896]{1,0:T(8,128)S(1)}, u32[]{:S(2)}, u32[]{:S(2)}) %collective-permute-start.76) | collective-permute-done | bytes 172064 | tf_op jit(solution)/shard_map/ppermute | solution.py:38
  663.2 3.0 fusion.151
  666.2 3.1 fusion.152
  669.4 3.5 fusion.30
  685.9 5.1 collective-permute-done.79
  691.0 5.4 collective-permute-done.80
  (603 shorter events, 235.4 us)
Async XLA Ops:
  7.2 219.0 %all-gather.3.cloned.1.call-start = ((), (), s32[]{:S(2)}) async-start(), calls=%async_computation.1 | async-start | bytes 5406720 | tf_op jit(solution)/shard_map/all_gather | solution.py:776
  10.7 11.0 %collective-permute-start = (bf16[128,768]{1,0:T(8,128)(2,1)S(1)}, bf16[128,768]{1,0:T(8,128)(2,1)S(1)}, u32[]{:S(2)}, u32[]{:S(2)}) collective-permute-start(bf16[128,768]{1,0:T(8,128)(2,1)S(1)} %fusion.76), channel_id=1, source_target_pairs={{0,3},{1,2},{2,1},{3,0},{4,7},{5,6},{6,5},{7,4},{8,11},{9,10},{10,... | collective-permute-start | bytes 589832 | tf_op jit(solution)/shard_map/ppermute | solution.py:38
  15.8 16.7 %collective-permute-start.1 = (bf16[128,768]{1,0:T(8,128)(2,1)S(1)}, bf16[128,768]{1,0:T(8,128)(2,1)S(1)}, u32[]{:S(2)}, u32[]{:S(2)}) collective-permute-start(bf16[128,768]{1,0:T(8,128)(2,1)S(1)} %fusion.76), channel_id=1, source_target_pairs={{0,2},{1,3},{2,0},{3,1},{4,6},{5,7},{6,4},{7,5},{8,10},{9,11},{10,... | collective-permute-start | bytes 589832 | tf_op jit(solution)/shard_map/ppermute | solution.py:38
  15.8 16.7 %collective-permute-start.2 = (bf16[128,768]{1,0:T(8,128)(2,1)S(1)}, bf16[128,768]{1,0:T(8,128)(2,1)S(1)}, u32[]{:S(2)}, u32[]{:S(2)}) collective-permute-start(bf16[128,768]{1,0:T(8,128)(2,1)S(1)} %fusion.76), channel_id=1, source_target_pairs={{0,1},{1,0},{2,3},{3,2},{4,5},{5,4},{6,7},{7,6},{8,9},{9,8},{10,11... | collective-permute-start | bytes 589832 | tf_op jit(solution)/shard_map/ppermute | solution.py:38
  33.1 26.1 %collective-permute-start.3 = (bf16[6,128,768]{2,1,0:T(8,128)(2,1)S(1)}, bf16[6,128,768]{2,1,0:T(8,128)(2,1)S(1)}, u32[]{:S(2)}, u32[]{:S(2)}) collective-permute-start(bf16[6,128,768]{2,1,0:T(8,128)(2,1)S(1)} %get-tuple-element.254), channel_id=1, source_target_pairs={{0,1},{1,2},{2,3},{4,5},{5,6},{6,7},{8,9},{9,10},{10,11},{12,13},{... | collective-permute-start | bytes 3538952 | tf_op jit(solution)/shard_map/ppermute | solution.py:738
  34.8 28.6 %collective-permute-start.4 = (bf16[6,128,768]{2,1,0:T(8,128)(2,1)S(1)}, bf16[6,128,768]{2,1,0:T(8,128)(2,1)S(1)}, u32[]{:S(2)}, u32[]{:S(2)}) collective-permute-start(bf16[6,128,768]{2,1,0:T(8,128)(2,1)S(1)} %get-tuple-element.255), channel_id=1, source_target_pairs={{1,0},{2,1},{3,2},{5,4},{6,5},{7,6},{9,8},{10,9},{11,10},{13,12},{... | collective-permute-start | bytes 3538952 | tf_op jit(solution)/shard_map/ppermute | solution.py:739
  38.9 35.3 %collective-permute-start.5 = (bf16[4,128,768]{2,1,0:T(8,128)(2,1)S(1)}, bf16[4,128,768]{2,1,0:T(8,128)(2,1)S(1)}, u32[]{:S(2)}, u32[]{:S(2)}) collective-permute-start(bf16[4,128,768]{2,1,0:T(8,128)(2,1)S(1)} %pad_maximum_fusion.10), channel_id=1, source_target_pairs={{0,8},{4,12},{8,0},{12,4},{16,24},{20,28},{24,16},{28,20},{1,9},{5... | collective-permute-start | bytes 2359304 | tf_op jit(solution)/shard_map/ppermute | solution.py:38
  40.4 34.9 %collective-permute-start.6 = (bf16[4,128,768]{2,1,0:T(8,128)(2,1)S(1)}, bf16[4,128,768]{2,1,0:T(8,128)(2,1)S(1)}, u32[]{:S(2)}, u32[]{:S(2)}) collective-permute-start(bf16[4,128,768]{2,1,0:T(8,128)(2,1)S(1)} %pad_maximum_fusion.10), channel_id=1, source_target_pairs={{0,16},{4,20},{8,24},{12,28},{16,0},{20,4},{24,8},{28,12},{1,17},{... | collective-permute-start | bytes 2359304 | tf_op jit(solution)/shard_map/ppermute | solution.py:38
  41.9 33.4 %collective-permute-start.7 = (bf16[4,128,768]{2,1,0:T(8,128)(2,1)S(1)}, bf16[4,128,768]{2,1,0:T(8,128)(2,1)S(1)}, u32[]{:S(2)}, u32[]{:S(2)}) collective-permute-start(bf16[4,128,768]{2,1,0:T(8,128)(2,1)S(1)} %pad_maximum_fusion.10), channel_id=1, source_target_pairs={{0,24},{4,28},{8,16},{12,20},{16,8},{20,12},{24,0},{28,4},{1,25},{... | collective-permute-start | bytes 2359304 | tf_op jit(solution)/shard_map/ppermute | solution.py:38
  76.1 15.8 %collective-permute-start.8 = (bf16[4,4,128,768]{3,2,1,0:T(8,128)(2,1)S(1)}, bf16[4,4,128,768]{3,2,1,0:T(8,128)(2,1)}, u32[]{:S(2)}, u32[]{:S(2)}) collective-permute-start(bf16[4,4,128,768]{3,2,1,0:T(8,128)(2,1)S(1)} %pad_maximum_fusion.1), channel_id=1, source_target_pairs={{0,4},{4,0},{8,12},{12,8},{16,20},{20,16},{24,28},{28,24},{1,5},{5... | collective-permute-start | bytes 9437192 | tf_op jit(solution)/shard_map/ppermute | solution.py:38
  83.9 18.2 %collective-permute-start.11 = (bf16[96,768]{1,0:T(8,128)(2,1)}, bf16[96,768]{1,0:T(8,128)(2,1)S(1)}, u32[]{:S(2)}, u32[]{:S(2)}) collective-permute-start(bf16[96,768]{1,0:T(8,128)(2,1)} %convert_bitcast_fusion.1), channel_id=1, source_target_pairs={{0,3},{1,2},{2,1},{3,0},{4,7},{5,6},{6,5},{7,4},{8,11},{9,10},{10,... | collective-permute-start | bytes 442376 | tf_op jit(solution)/shard_map/ppermute | solution.py:38
  88.9 13.2 %collective-permute-start.12 = (bf16[96,768]{1,0:T(8,128)(2,1)}, bf16[96,768]{1,0:T(8,128)(2,1)S(1)}, u32[]{:S(2)}, u32[]{:S(2)}) collective-permute-start(bf16[96,768]{1,0:T(8,128)(2,1)} %convert_bitcast_fusion.1), channel_id=1, source_target_pairs={{0,2},{1,3},{2,0},{3,1},{4,6},{5,7},{6,4},{7,5},{8,10},{9,11},{10,... | collective-permute-start | bytes 442376 | tf_op jit(solution)/shard_map/ppermute | solution.py:38
  88.9 13.2 %collective-permute-start.13 = (bf16[96,768]{1,0:T(8,128)(2,1)}, bf16[96,768]{1,0:T(8,128)(2,1)}, u32[]{:S(2)}, u32[]{:S(2)}) collective-permute-start(bf16[96,768]{1,0:T(8,128)(2,1)} %convert_bitcast_fusion.1), channel_id=1, source_target_pairs={{0,1},{1,0},{2,3},{3,2},{4,5},{5,4},{6,7},{7,6},{8,9},{9,8},{10,11... | collective-permute-start | bytes 442376 | tf_op jit(solution)/shard_map/ppermute | solution.py:38
  103.2 26.4 %collective-permute-start.14 = (bf16[4,96,768]{2,1,0:T(8,128)(2,1)S(1)}, bf16[4,96,768]{2,1,0:T(8,128)(2,1)S(1)}, u32[]{:S(2)}, u32[]{:S(2)}) collective-permute-start(bf16[4,96,768]{2,1,0:T(8,128)(2,1)S(1)} %pad_maximum_fusion.13), channel_id=1, source_target_pairs={{0,8},{4,12},{8,0},{12,4},{16,24},{20,28},{24,16},{28,20},{1,9},{5... | collective-permute-start | bytes 1769480 | tf_op jit(solution)/shard_map/ppermute | solution.py:38
  104.5 25.9 %collective-permute-start.15 = (bf16[4,96,768]{2,1,0:T(8,128)(2,1)S(1)}, bf16[4,96,768]{2,1,0:T(8,128)(2,1)}, u32[]{:S(2)}, u32[]{:S(2)}) collective-permute-start(bf16[4,96,768]{2,1,0:T(8,128)(2,1)S(1)} %pad_maximum_fusion.13), channel_id=1, source_target_pairs={{0,16},{4,20},{8,24},{12,28},{16,0},{20,4},{24,8},{28,12},{1,17},{... | collective-permute-start | bytes 1769480 | tf_op jit(solution)/shard_map/ppermute | solution.py:38
  105.4 26.8 %collective-permute-start.16 = (bf16[4,96,768]{2,1,0:T(8,128)(2,1)S(1)}, bf16[4,96,768]{2,1,0:T(8,128)(2,1)}, u32[]{:S(2)}, u32[]{:S(2)}) collective-permute-start(bf16[4,96,768]{2,1,0:T(8,128)(2,1)S(1)} %pad_maximum_fusion.13), channel_id=1, source_target_pairs={{0,24},{4,28},{8,16},{12,20},{16,8},{20,12},{24,0},{28,4},{1,25},{... | collective-permute-start | bytes 1769480 | tf_op jit(solution)/shard_map/ppermute | solution.py:38
  106.8 7.5 %collective-permute-start.9 = (bf16[1,96,768]{2,1,0:T(8,128)(2,1)S(1)}, bf16[1,96,768]{2,1,0:T(8,128)(2,1)S(1)}, u32[]{:S(2)}, u32[]{:S(2)}) collective-permute-start(bf16[1,96,768]{2,1,0:T(8,128)(2,1)S(1)} %bitcast.400), channel_id=1, source_target_pairs={{0,1},{1,0},{2,3},{3,2},{4,5},{5,4},{6,7},{7,6},{8,9},{9,8},{10,11... | collective-permute-start | bytes 442376 | tf_op jit(solution)/shard_map/ppermute | solution.py:38
  114.4 15.1 %collective-permute-start.10 = (bf16[2,96,768]{2,1,0:T(8,128)(2,1)S(1)}, bf16[2,96,768]{2,1,0:T(8,128)(2,1)S(1)}, u32[]{:S(2)}, u32[]{:S(2)}) collective-permute-start(bf16[2,96,768]{2,1,0:T(8,128)(2,1)S(1)} %maximum_select_fusion.6), channel_id=1, source_target_pairs={{0,2},{1,3},{2,0},{3,1},{4,6},{5,7},{6,4},{7,5},{8,10},{9,11},{10,... | collective-permute-start | bytes 884744 | tf_op jit(solution)/shard_map/ppermute | solution.py:38
  132.1 28.5 %collective-permute-start.17 = (bf16[4,96,768]{2,1,0:T(8,128)(2,1)S(1)}, bf16[4,96,768]{2,1,0:T(8,128)(2,1)}, u32[]{:S(2)}, u32[]{:S(2)}) collective-permute-start(bf16[4,96,768]{2,1,0:T(8,128)(2,1)S(1)} %maximum_select_fusion.4), channel_id=1, source_target_pairs={{0,8},{4,12},{8,0},{12,4},{16,24},{20,28},{24,16},{28,20},{1,9},{5... | collective-permute-start | bytes 1769480 | tf_op jit(solution)/shard_map/ppermute | solution.py:38
  132.9 27.7 %collective-permute-start.18 = (bf16[4,96,768]{2,1,0:T(8,128)(2,1)S(1)}, bf16[4,96,768]{2,1,0:T(8,128)(2,1)}, u32[]{:S(2)}, u32[]{:S(2)}) collective-permute-start(bf16[4,96,768]{2,1,0:T(8,128)(2,1)S(1)} %maximum_select_fusion.4), channel_id=1, source_target_pairs={{0,16},{4,20},{8,24},{12,28},{16,0},{20,4},{24,8},{28,12},{1,17},{... | collective-permute-start | bytes 1769480 | tf_op jit(solution)/shard_map/ppermute | solution.py:38
  134.5 26.2 %collective-permute-start.19 = (bf16[4,96,768]{2,1,0:T(8,128)(2,1)S(1)}, bf16[4,96,768]{2,1,0:T(8,128)(2,1)}, u32[]{:S(2)}, u32[]{:S(2)}) collective-permute-start(bf16[4,96,768]{2,1,0:T(8,128)(2,1)S(1)} %maximum_select_fusion.4), channel_id=1, source_target_pairs={{0,24},{4,28},{8,16},{12,20},{16,8},{20,12},{24,0},{28,4},{1,25},{... | collective-permute-start | bytes 1769480 | tf_op jit(solution)/shard_map/ppermute | solution.py:38
  139.4 45.4 %collective-permute-start.20 = (bf16[4,4,96,768]{3,2,1,0:T(8,128)(2,1)}, bf16[4,4,96,768]{3,2,1,0:T(8,128)(2,1)}, u32[]{:S(2)}, u32[]{:S(2)}) collective-permute-start(bf16[4,4,96,768]{3,2,1,0:T(8,128)(2,1)} %pad_maximum_fusion.2), channel_id=1, source_target_pairs={{0,4},{4,0},{8,12},{12,8},{16,20},{20,16},{24,28},{28,24},{1,5},{5... | collective-permute-start | bytes 7077896 | tf_op jit(solution)/shard_map/ppermute | solution.py:38
  139.4 330.2 %all-gather.5.cloned.1.call-start = ((), (), s32[]{:S(2)}) async-start(), calls=%async_computation.2 | async-start | bytes 6881280 | tf_op jit(solution)/shard_map/all_gather | solution.py:825
  170.0 23.9 %collective-permute-start.21 = (bf16[4,4,96,768]{3,2,1,0:T(8,128)(2,1)S(1)}, bf16[4,4,96,768]{3,2,1,0:T(8,128)(2,1)S(1)}, u32[]{:S(2)}, u32[]{:S(2)}) collective-permute-start(bf16[4,4,96,768]{3,2,1,0:T(8,128)(2,1)S(1)} %pad_maximum_fusion.3), channel_id=1, source_target_pairs={{0,4},{4,0},{8,12},{12,8},{16,20},{20,16},{24,28},{28,24},{1,5},{5... | collective-permute-start | bytes 7077896 | tf_op jit(solution)/shard_map/ppermute | solution.py:38
  204.2 6.8 collective-permute-start.22
  205.7 6.8 collective-permute-start.23
  208.3 6.5 collective-permute-start.24
  243.7 6.3 collective-permute-start.33
  244.6 6.9 collective-permute-start.34
  244.6 6.9 collective-permute-start.35
  311.7 16.4 %collective-permute-start.37 = (f32[2,2,4,96,768]{4,3,2,0,1:T(8,128)}, f32[2,2,4,96,768]{4,3,2,0,1:T(8,128)S(1)}, u32[]{:S(2)}, u32[]{:S(2)}) collective-permute-start(f32[2,2,4,96,768]{4,3,2,0,1:T(8,128)} %copy.87), channel_id=1, source_target_pairs={{0,4},{4,0},{8,12},{12,8},{16,20},{20,16},{24,28},{28,24},{1,5},{5... | collective-permute-start | bytes 14155784 | tf_op jit(solution)/shard_map/ppermute | solution.py:38
  311.7 23.1 %collective-permute-start.36 = (f32[2,2,4,96,768]{4,3,2,1,0:T(8,128)}, f32[2,2,4,96,768]{4,3,2,1,0:T(8,128)S(1)}, u32[]{:S(2)}, u32[]{:S(2)}) collective-permute-start(f32[2,2,4,96,768]{4,3,2,1,0:T(8,128)} %bitcast.421), channel_id=1, source_target_pairs={{0,4},{4,0},{8,12},{12,8},{16,20},{20,16},{24,28},{28,24},{1,5},{5... | collective-permute-start | bytes 14155784 | tf_op jit(solution)/shard_map/ppermute | solution.py:38
  357.2 55.0 %collective-permute-start.39 = (f32[2,4,96,768]{3,2,1,0:T(8,128)}, f32[2,4,96,768]{3,2,1,0:T(8,128)}, u32[]{:S(2)}, u32[]{:S(2)}) collective-permute-start(f32[2,4,96,768]{3,2,1,0:T(8,128)} %slice_bitcast_fusion.2), channel_id=1, source_target_pairs={{0,8},{4,12},{8,0},{12,4},{16,24},{20,28},{24,16},{28,20},{1,9},{5... | collective-permute-start | bytes 7077896 | tf_op jit(solution)/shard_map/ppermute | solution.py:38
  358.0 57.7 %collective-permute-start.38 = (f32[2,4,96,768]{3,2,1,0:T(8,128)}, f32[2,4,96,768]{3,2,1,0:T(8,128)}, u32[]{:S(2)}, u32[]{:S(2)}) collective-permute-start(f32[2,4,96,768]{3,2,1,0:T(8,128)} %slice_bitcast_fusion.3), channel_id=1, source_target_pairs={{0,16},{4,20},{8,24},{12,28},{16,0},{20,4},{24,8},{28,12},{1,17},{... | collective-permute-start | bytes 7077896 | tf_op jit(solution)/shard_map/ppermute | solution.py:38
  358.8 178.6 %reduce-scatter.2.cloned.1.call-start = ((), (), s32[]{:S(2)}) async-start(), calls=%async_computation.3 | async-start | bytes 2949120 | tf_op jit(solution)/shard_map/reduce_scatter | solution.py:867
  419.1 28.9 %collective-permute-start.40 = (f32[4,96,768]{2,1,0:T(8,128)}, f32[4,96,768]{2,1,0:T(8,128)}, u32[]{:S(2)}, u32[]{:S(2)}) collective-permute-start(f32[4,96,768]{2,1,0:T(8,128)} %slice_bitcast_fusion.9), channel_id=1, source_target_pairs={{0,8},{4,12},{8,0},{12,4},{16,24},{20,28},{24,16},{28,20},{1,9},{5... | collective-permute-start | bytes 3538952 | tf_op jit(solution)/shard_map/ppermute | solution.py:38
  420.2 29.2 %collective-permute-start.41 = (f32[4,96,768]{2,1,0:T(8,128)}, f32[4,96,768]{2,1,0:T(8,128)}, u32[]{:S(2)}, u32[]{:S(2)}) collective-permute-start(f32[4,96,768]{2,1,0:T(8,128)} %slice_bitcast_fusion.8), channel_id=1, source_target_pairs={{0,16},{4,20},{8,24},{12,28},{16,0},{20,4},{24,8},{28,12},{1,17},{... | collective-permute-start | bytes 3538952 | tf_op jit(solution)/shard_map/ppermute | solution.py:38
  452.5 15.4 %collective-permute-start.42 = (f32[2,2,4,48,768]{4,3,2,1,0:T(8,128)}, f32[2,2,4,48,768]{4,3,2,1,0:T(8,128)S(1)}, u32[]{:S(2)}, u32[]{:S(2)}) collective-permute-start(f32[2,2,4,48,768]{4,3,2,1,0:T(8,128)} %pad_maximum_fusion.4), channel_id=1, source_target_pairs={{0,4},{4,0},{8,12},{12,8},{16,20},{20,16},{24,28},{28,24},{1,5},{5... | collective-permute-start | bytes 7077896 | tf_op jit(solution)/shard_map/ppermute | solution.py:38
  469.6 6.7 collective-permute-start.43
  473.2 16.2 %collective-permute-start.45 = (f32[2,4,48,384]{3,2,1,0:T(8,128)S(1)}, f32[2,4,48,384]{3,2,1,0:T(8,128)S(1)}, u32[]{:S(2)}, u32[]{:S(2)}) collective-permute-start(f32[2,4,48,384]{3,2,1,0:T(8,128)S(1)} %get-tuple-element.168), channel_id=1, source_target_pairs={{0,16},{4,20},{8,24},{12,28},{16,0},{20,4},{24,8},{28,12},{1,17},{... | collective-permute-start | bytes 1769480 | tf_op jit(solution)/shard_map/ppermute | solution.py:38
  474.0 17.4 %collective-permute-start.47 = (f32[2,4,48,384]{3,2,1,0:T(8,128)}, f32[2,4,48,384]{3,2,1,0:T(8,128)S(1)}, u32[]{:S(2)}, u32[]{:S(2)}) collective-permute-start(f32[2,4,48,384]{3,2,1,0:T(8,128)} %get-tuple-element.170), channel_id=1, source_target_pairs={{0,8},{4,12},{8,0},{12,4},{16,24},{20,28},{24,16},{28,20},{1,9},{5... | collective-permute-start | bytes 1769480 | tf_op jit(solution)/shard_map/ppermute | solution.py:38
  482.5 34.9 %collective-permute-start.49 = (f32[2,4,72,384]{3,2,1,0:T(8,128)}, f32[2,4,72,384]{3,2,1,0:T(8,128)}, u32[]{:S(2)}, u32[]{:S(2)}) collective-permute-start(f32[2,4,72,384]{3,2,1,0:T(8,128)} %dynamic-slice_bitcast_fusion.5), channel_id=1, source_target_pairs={{0,8},{4,12},{8,0},{12,4},{16,24},{20,28},{24,16},{28,20},{1,9},{5... | collective-permute-start | bytes 2654216 | tf_op jit(solution)/shard_map/ppermute | solution.py:38
  483.4 36.1 %collective-permute-start.44 = (f32[2,4,72,384]{3,2,1,0:T(8,128)}, f32[2,4,72,384]{3,2,1,0:T(8,128)}, u32[]{:S(2)}, u32[]{:S(2)}) collective-permute-start(f32[2,4,72,384]{3,2,1,0:T(8,128)} %dynamic-slice_bitcast_fusion.6), channel_id=1, source_target_pairs={{0,16},{4,20},{8,24},{12,28},{16,0},{20,4},{24,8},{28,12},{1,17},{... | collective-permute-start | bytes 2654216 | tf_op jit(solution)/shard_map/ppermute | solution.py:38
  490.5 24.1 %collective-permute-start.46 = (f32[4,48,384]{2,1,0:T(8,128)}, f32[4,48,384]{2,1,0:T(8,128)}, u32[]{:S(2)}, u32[]{:S(2)}) collective-permute-start(f32[4,48,384]{2,1,0:T(8,128)} %dynamic-slice_bitcast_fusion.19), channel_id=1, source_target_pairs={{0,8},{4,12},{8,0},{12,4},{16,24},{20,28},{24,16},{28,20},{1,9},{5... | collective-permute-start | bytes 884744 | tf_op jit(solution)/shard_map/ppermute | solution.py:38
  493.0 22.6 %collective-permute-start.48 = (f32[4,48,384]{2,1,0:T(8,128)}, f32[4,48,384]{2,1,0:T(8,128)}, u32[]{:S(2)}, u32[]{:S(2)}) collective-permute-start(f32[4,48,384]{2,1,0:T(8,128)} %dynamic-slice_bitcast_fusion.18), channel_id=1, source_target_pairs={{0,16},{4,20},{8,24},{12,28},{16,0},{20,4},{24,8},{28,12},{1,17},{... | collective-permute-start | bytes 884744 | tf_op jit(solution)/shard_map/ppermute | solution.py:38
  521.7 11.2 %collective-permute-start.50 = (f32[4,72,384]{2,1,0:T(8,128)}, f32[4,72,384]{2,1,0:T(8,128)}, u32[]{:S(2)}, u32[]{:S(2)}) collective-permute-start(f32[4,72,384]{2,1,0:T(8,128)} %dynamic-slice_bitcast_fusion.14), channel_id=1, source_target_pairs={{0,8},{4,12},{8,0},{12,4},{16,24},{20,28},{24,16},{28,20},{1,9},{5... | collective-permute-start | bytes 1327112 | tf_op jit(solution)/shard_map/ppermute | solution.py:38
  522.6 11.5 %collective-permute-start.51 = (f32[4,72,384]{2,1,0:T(8,128)}, f32[4,72,384]{2,1,0:T(8,128)}, u32[]{:S(2)}, u32[]{:S(2)}) collective-permute-start(f32[4,72,384]{2,1,0:T(8,128)} %dynamic-slice_bitcast_fusion.13), channel_id=1, source_target_pairs={{0,16},{4,20},{8,24},{12,28},{16,0},{20,4},{24,8},{28,12},{1,17},{... | collective-permute-start | bytes 1327112 | tf_op jit(solution)/shard_map/ppermute | solution.py:38
  537.4 16.6 %collective-permute-start.53 = (f32[2,120,768]{2,1,0:T(8,128)}, f32[2,120,768]{2,1,0:T(8,128)}, u32[]{:S(2)}, u32[]{:S(2)}) collective-permute-start(f32[2,120,768]{2,1,0:T(8,128)} %dynamic-slice_bitcast_fusion.7), channel_id=1, source_target_pairs={{0,1},{1,0},{2,3},{3,2},{4,5},{5,4},{6,7},{7,6},{8,9},{9,8},{10,11... | collective-permute-start | bytes 2211848 | tf_op jit(solution)/shard_map/ppermute | solution.py:38
  555.5 21.8 %collective-permute-start.57 = (f32[1,120,768]{2,1,0:T(8,128)S(1)}, f32[1,120,768]{2,1,0:T(8,128)S(1)}, u32[]{:S(2)}, u32[]{:S(2)}) collective-permute-start(f32[1,120,768]{2,1,0:T(8,128)S(1)} %constant_dynamic-slice_fusion.1), channel_id=1, source_target_pairs={{0,2},{1,3},{2,0},{3,1},{4,6},{5,7},{6,4},{7,5},{8,10},{9,11},{10,... | collective-permute-start | bytes 1105928 | tf_op jit(solution)/shard_map/ppermute | solution.py:38
  557.4 7.1 %collective-permute-start.58 = (f32[24,768]{1,0:T(8,128)S(1)}, f32[24,768]{1,0:T(8,128)S(1)}, u32[]{:S(2)}, u32[]{:S(2)}) collective-permute-start(f32[24,768]{1,0:T(8,128)S(1)} %add_add_fusion.3), channel_id=1, source_target_pairs={{0,1},{1,0},{2,3},{3,2},{4,5},{5,4},{6,7},{7,6},{8,9},{9,8},{10,11... | collective-permute-start | bytes 221192 | tf_op jit(solution)/shard_map/ppermute | solution.py:38
  558.9 18.4 %collective-permute-start.59 = (f32[24,768]{1,0:T(8,128)S(1)}, f32[24,768]{1,0:T(8,128)S(1)}, u32[]{:S(2)}, u32[]{:S(2)}) collective-permute-start(f32[24,768]{1,0:T(8,128)S(1)} %add_add_fusion.3), channel_id=1, source_target_pairs={{0,2},{1,3},{2,0},{3,1},{4,6},{5,7},{6,4},{7,5},{8,10},{9,11},{10,... | collective-permute-start | bytes 221192 | tf_op jit(solution)/shard_map/ppermute | solution.py:38
  560.7 16.6 %collective-permute-start.60 = (f32[24,768]{1,0:T(8,128)S(1)}, f32[24,768]{1,0:T(8,128)S(1)}, u32[]{:S(2)}, u32[]{:S(2)}) collective-permute-start(f32[24,768]{1,0:T(8,128)S(1)} %add_add_fusion.3), channel_id=1, source_target_pairs={{0,3},{1,2},{2,1},{3,0},{4,7},{5,6},{6,5},{7,4},{8,11},{9,10},{10,... | collective-permute-start | bytes 221192 | tf_op jit(solution)/shard_map/ppermute | solution.py:38
  603.8 10.0 %collective-permute-start.68 = (f32[96,768]{1,0:T(8,128)S(1)}, f32[96,768]{1,0:T(8,128)S(1)}, u32[]{:S(2)}, u32[]{:S(2)}) collective-permute-start(f32[96,768]{1,0:T(8,128)S(1)} %get-tuple-element.267), channel_id=1, source_target_pairs={{0,8},{4,12},{8,0},{12,4},{16,24},{20,28},{24,16},{28,20},{1,9},{5... | collective-permute-start | bytes 884744 | tf_op jit(solution)/shard_map/ppermute | solution.py:38
  605.1 13.4 %collective-permute-start.69 = (f32[96,768]{1,0:T(8,128)S(1)}, f32[96,768]{1,0:T(8,128)S(1)}, u32[]{:S(2)}, u32[]{:S(2)}) collective-permute-start(f32[96,768]{1,0:T(8,128)S(1)} %get-tuple-element.266), channel_id=1, source_target_pairs={{0,16},{4,20},{8,24},{12,28},{16,0},{20,4},{24,8},{28,12},{1,17},{... | collective-permute-start | bytes 884744 | tf_op jit(solution)/shard_map/ppermute | solution.py:38
  605.8 12.7 %collective-permute-start.70 = (f32[96,768]{1,0:T(8,128)S(1)}, f32[96,768]{1,0:T(8,128)S(1)}, u32[]{:S(2)}, u32[]{:S(2)}) collective-permute-start(f32[96,768]{1,0:T(8,128)S(1)} %get-tuple-element.265), channel_id=1, source_target_pairs={{0,24},{4,28},{8,16},{12,20},{16,8},{20,12},{24,0},{28,4},{1,25},{... | collective-permute-start | bytes 884744 | tf_op jit(solution)/shard_map/ppermute | solution.py:38
  626.4 10.1 %collective-permute-start.72 = (f32[48,896]{1,0:T(8,128)S(1)}, f32[48,896]{1,0:T(8,128)S(1)}, u32[]{:S(2)}, u32[]{:S(2)}) collective-permute-start(f32[48,896]{1,0:T(8,128)S(1)} %get-tuple-element.287), channel_id=1, source_target_pairs={{0,1},{1,0},{2,3},{3,2},{4,5},{5,4},{6,7},{7,6},{8,9},{9,8},{10,11... | collective-permute-start | bytes 516104 | tf_op jit(solution)/shard_map/ppermute | solution.py:38
  626.6 15.8 %collective-permute-start.73 = (f32[48,896]{1,0:T(8,128)S(1)}, f32[48,896]{1,0:T(8,128)S(1)}, u32[]{:S(2)}, u32[]{:S(2)}) collective-permute-start(f32[48,896]{1,0:T(8,128)S(1)} %get-tuple-element.286), channel_id=1, source_target_pairs={{0,2},{1,3},{2,0},{3,1},{4,6},{5,7},{6,4},{7,5},{8,10},{9,11},{10,... | collective-permute-start | bytes 516104 | tf_op jit(solution)/shard_map/ppermute | solution.py:38
  629.8 12.6 %collective-permute-start.74 = (f32[48,896]{1,0:T(8,128)S(1)}, f32[48,896]{1,0:T(8,128)S(1)}, u32[]{:S(2)}, u32[]{:S(2)}) collective-permute-start(f32[48,896]{1,0:T(8,128)S(1)} %get-tuple-element.285), channel_id=1, source_target_pairs={{0,3},{1,2},{2,1},{3,0},{4,7},{5,6},{6,5},{7,4},{8,11},{9,10},{10,... | collective-permute-start | bytes 516104 | tf_op jit(solution)/shard_map/ppermute | solution.py:38
  642.5 7.6 %collective-permute-start.75 = (f32[48,896]{1,0:T(8,128)S(1)}, f32[48,896]{1,0:T(8,128)S(1)}, u32[]{:S(2)}, u32[]{:S(2)}) collective-permute-start(f32[48,896]{1,0:T(8,128)S(1)} %fusion.77), channel_id=1, source_target_pairs={{0,3},{1,2},{2,1},{3,0},{4,7},{5,6},{6,5},{7,4},{8,11},{9,10},{10,... | collective-permute-start | bytes 516104 | tf_op jit(solution)/shard_map/ppermute | solution.py:38
  645.0 15.2 %collective-permute-start.76 = (f32[48,896]{1,0:T(8,128)S(1)}, f32[48,896]{1,0:T(8,128)S(1)}, u32[]{:S(2)}, u32[]{:S(2)}) collective-permute-start(f32[48,896]{1,0:T(8,128)S(1)} %fusion.77), channel_id=1, source_target_pairs={{0,2},{1,3},{2,0},{3,1},{4,6},{5,7},{6,4},{7,5},{8,10},{9,11},{10,... | collective-permute-start | bytes 516104 | tf_op jit(solution)/shard_map/ppermute | solution.py:38
  647.4 12.8 %collective-permute-start.77 = (f32[48,896]{1,0:T(8,128)S(1)}, f32[48,896]{1,0:T(8,128)S(1)}, u32[]{:S(2)}, u32[]{:S(2)}) collective-permute-start(f32[48,896]{1,0:T(8,128)S(1)} %fusion.77), channel_id=1, source_target_pairs={{0,1},{1,0},{2,3},{3,2},{4,5},{5,4},{6,7},{7,6},{8,9},{9,8},{10,11... | collective-permute-start | bytes 516104 | tf_op jit(solution)/shard_map/ppermute | solution.py:38
  680.1 10.9 %collective-permute-start.79 = (f32[96,768]{1,0:T(8,128)S(1)}, f32[96,768]{1,0:T(8,128)S(1)}, u32[]{:S(2)}, u32[]{:S(2)}) collective-permute-start(f32[96,768]{1,0:T(8,128)S(1)} %get-tuple-element.263), channel_id=1, source_target_pairs={{0,24},{4,28},{8,16},{12,20},{16,8},{20,12},{24,0},{28,4},{1,25},{... | collective-permute-start | bytes 884744 | tf_op jit(solution)/shard_map/ppermute | solution.py:38
  681.3 15.1 %collective-permute-start.80 = (f32[96,768]{1,0:T(8,128)S(1)}, f32[96,768]{1,0:T(8,128)S(1)}, u32[]{:S(2)}, u32[]{:S(2)}) collective-permute-start(f32[96,768]{1,0:T(8,128)S(1)} %get-tuple-element.262), channel_id=1, source_target_pairs={{0,16},{4,20},{8,24},{12,28},{16,0},{20,4},{24,8},{28,12},{1,17},{... | collective-permute-start | bytes 884744 | tf_op jit(solution)/shard_map/ppermute | solution.py:38
  682.1 14.3 %collective-permute-start.81 = (f32[96,768]{1,0:T(8,128)S(1)}, f32[96,768]{1,0:T(8,128)S(1)}, u32[]{:S(2)}, u32[]{:S(2)}) collective-permute-start(f32[96,768]{1,0:T(8,128)S(1)} %get-tuple-element.260), channel_id=1, source_target_pairs={{0,8},{4,12},{8,0},{12,4},{16,24},{20,28},{24,16},{28,20},{1,9},{5... | collective-permute-start | bytes 884744 | tf_op jit(solution)/shard_map/ppermute | solution.py:38
  (132 other events, 1104.4 us)
Sparse Core Ops, SparseCore 0:
  139.5 86.6 all-gather.2
  358.9 101.0 all-gather.4
  470.3 45.7 reduce-scatter.1
